TPU v7x, 32 devices: a whole 2x2x4 slice. The times are simulated.
32 devices in a mesh: layer: 4 (over z), row: 4 (over x, core), col: 2 (over y).
Axes of the slice: x: 2, y: 2, z: 4, core: 2. Of those that a mesh axis runs over, the one named last changes fastest.
Arguments:
- c_states: float32 [4, 64, 32, 256], P('layer', None, 'row', 'col'), may hold values from -6 to 6
- c_adjoints: float32 [4, 64, 32, 256], P('layer', None, 'row', 'col'), may hold values from -6 to 6
- weights: bfloat16 [16, 64, 576], P('layer'), may hold values from -0.25 to 0.25
Outputs:
- new_states: float32 [4, 64, 32, 256], P('layer', None, 'row', 'col')
- new_adjoints: float32 [4, 64, 32, 256], P('layer', None, 'row', 'col')
- weight_grads: float32 [16, 64, 576], P('layer')
All inputs are finite; a program needn't handle non-finite values.
Results may differ from a plain program's by a relative error of at most 0.006.
Values may be sent and summed in bfloat16 or wider, within the bound.
No kernel may reach another device: no remote copies, remote signals or barrier semaphores. Data moves between devices by JAX's collectives and lax.ppermute only.
A program may use at most 64 MiB of HBM per device.

v0:
```python
import jax
import jax.numpy as jnp
from jax import lax
from jax.sharding import PartitionSpec as P

step_size = 0.2


def with_halo(cells, sides, width):
    for axis, dim in sides:
        count = lax.axis_size(axis)
        ends = count - 1
        head = lax.slice_in_dim(cells, 0, width, axis=dim)
        tail = lax.slice_in_dim(cells, cells.shape[dim] - width, cells.shape[dim], axis=dim)
        cells = jnp.concatenate(
            [
                lax.ppermute(tail, axis, [(i, (i + 1) % count) for i in range(ends)]),
                cells,
                lax.ppermute(head, axis, [((i + 1) % count, i) for i in range(ends)]),
            ],
            axis=dim,
        )
    return cells


def from_behind(array, axis, by):
    devices = lax.axis_size(axis)
    pairs = [(i, i + by) for i in range(devices) if 0 <= i + by < devices]
    return lax.ppermute(array, axis, pairs)


def tile_patches(padded, tile_rows, tile_cols):
    shifted = [
        padded[:, row_off : row_off + tile_rows, col_off : col_off + tile_cols].reshape(
            padded.shape[0], tile_rows * tile_cols
        )
        for row_off in range(3)
        for col_off in range(3)
    ]
    return jnp.concatenate(shifted, 0)


def exact_dot(left_mat, right_mat):
    return jnp.dot(
        left_mat, right_mat, precision=lax.Precision.HIGHEST, preferred_element_type=jnp.float32
    )


def flipped(weight_mat):
    channels = weight_mat.shape[0]
    return jnp.transpose(weight_mat.reshape(channels, 9, channels)[:, ::-1, :], (2, 1, 0)).reshape(
        channels, 9 * channels
    )


def local(c_states, c_adjoints, weights):
    group_index = lax.axis_index("layer")
    group_count = lax.axis_size("layer")
    channels, tile_rows, tile_cols = c_states.shape[1:]
    pixels = tile_rows * tile_cols
    depth = weights.shape[0]
    initial_flat = c_states[0].reshape(channels, pixels)
    guess_flat = c_adjoints[0].reshape(channels, pixels)

    def advance(state, weight_mat):
        active = state.astype(jnp.bfloat16).reshape(channels, tile_rows, tile_cols)
        padded = with_halo(active, (("row", 1), ("col", 2)), 1)
        preact = jnp.dot(
            weight_mat,
            tile_patches(padded, tile_rows, tile_cols),
            preferred_element_type=jnp.float32,
        )
        return (state + step_size * jnp.tanh(preact), padded, preact)

    state = initial_flat
    for layer_pos in range(depth):
        state, _, _ = advance(state, weights[layer_pos])
    group_end = state
    summed = jnp.sum(weights[0].astype(jnp.float32).reshape(channels, 9, channels), axis=1)
    coarse_map = jnp.eye(channels, dtype=jnp.float32) + step_size * summed
    is_first = group_index == 0
    is_last = group_index == group_count - 1
    zero_map = jnp.zeros_like(coarse_map)
    blank = jnp.zeros((channels, pixels), jnp.float32)
    fwd_map = jnp.where(is_first, zero_map, coarse_map)
    fwd_offset = jnp.where(is_first, group_end, group_end - exact_dot(coarse_map, initial_flat))

    def state_turn(turn_number, carried):
        return from_behind(exact_dot(fwd_map, carried) + fwd_offset, "layer", 1)

    arrived = lax.fori_loop(0, group_count - 1, state_turn, blank)
    corrected = jnp.where(is_first, initial_flat, arrived)
    state = corrected
    trail = []
    for layer_pos in range(depth):
        state, padded, preact = advance(state, weights[layer_pos])
        trail.append((padded, preact))
    adjoint = guess_flat
    grad_list = [None] * depth
    for layer_pos in reversed(range(depth)):
        padded, preact = trail[layer_pos]
        slope = jnp.tanh(preact)
        source = (adjoint * step_size * (1.0 - slope * slope)).astype(jnp.bfloat16)
        source_pad = with_halo(
            source.reshape(channels, tile_rows, tile_cols), (("row", 1), ("col", 2)), 1
        )
        grad_list[layer_pos] = lax.dot_general(
            source,
            tile_patches(padded, tile_rows, tile_cols),
            (((1,), (1,)), ((), ())),
            preferred_element_type=jnp.float32,
        )
        back = jnp.dot(
            flipped(weights[layer_pos]),
            tile_patches(source_pad, tile_rows, tile_cols),
            preferred_element_type=jnp.float32,
        )
        adjoint = adjoint + back
    weight_grads = lax.psum(jnp.stack(grad_list, 0), ("row", "col"))
    transposed = coarse_map.T
    back_map = jnp.where(is_last, zero_map, transposed)
    back_offset = jnp.where(is_last, adjoint, adjoint - exact_dot(transposed, guess_flat))

    def adjoint_turn(turn_number, carried):
        return from_behind(exact_dot(back_map, carried) + back_offset, "layer", -1)

    returned = lax.fori_loop(0, group_count - 1, adjoint_turn, blank)
    new_adjoint = jnp.where(is_last, guess_flat, returned)
    out_shape = (1, channels, tile_rows, tile_cols)
    return (corrected.reshape(out_shape), new_adjoint.reshape(out_shape), weight_grads)


def solution(mesh):
    placed = (
        P("layer", None, "row", "col"),
        P("layer", None, "row", "col"),
        P("layer", None, None),
    )
    return jax.shard_map(
        local,
        mesh=mesh,
        in_specs=placed,
        out_specs=(
            P("layer", None, "row", "col"),
            P("layer", None, "row", "col"),
            P("layer", None, None),
        ),
        check_vma=False,
    )
```

profile of v0, /device:TPU:19, one launch (start us, length us, event | category | flops | bytes accessed | tf_op | source)
XLA Modules:
  0.0 351.6 jit_solution(8940493227506223574)
XLA Ops:
  9.5 3.2 collective-permute-start.3
  20.9 3.3 collective-permute-done.5
  27.6 6.4 %collective-permute-start.7 = (bf16[64,1,128]{2,1,0:T(2,128)(2,1)S(1)}, bf16[64,1,128]{2,1,0:T(2,128)(2,1)S(1)}, u32[]{:S(2)}, u32[]{:S(2)}) collective-permute-start(bf16[64,1,128]{2,1,0:T(2,128)(2,1)S(1)} %get-tuple-element.222), channel_id=1, source_target_pairs={{2,0},{4,2},{6,4},{3,1},{5,3},{7,5},{10,8},{12,10},{14,12},{11,9},... | collective-permute-start | bytes 49160 | tf_op jit(solution)/shard_map/ppermute | solution.py:19
  40.3 3.3 collective-permute-done.9
  46.3 6.6 %collective-permute-start.11 = (bf16[64,1,128]{2,1,0:T(2,128)(2,1)S(1)}, bf16[64,1,128]{2,1,0:T(2,128)(2,1)S(1)}, u32[]{:S(2)}, u32[]{:S(2)}) collective-permute-start(bf16[64,1,128]{2,1,0:T(2,128)(2,1)S(1)} %get-tuple-element.220), channel_id=1, source_target_pairs={{2,0},{4,2},{6,4},{3,1},{5,3},{7,5},{10,8},{12,10},{14,12},{11,9},... | collective-permute-start | bytes 49160 | tf_op jit(solution)/shard_map/ppermute | solution.py:19
  59.2 4.2 %collective-permute-done.13 = bf16[64,10,1]{2,1,0:T(8,128)(2,1)S(1)} collective-permute-done((bf16[64,10,1]{2,1,0:T(8,128)(2,1)S(1)}, bf16[64,10,1]{2,1,0:T(8,128)(2,1)S(1)}, u32[]{:S(2)}, u32[]{:S(2)}) %collective-permute-start.13) | collective-permute-done | bytes 1312 | tf_op jit(solution)/shard_map/ppermute | solution.py:19
  66.0 7.1 %collective-permute-start.15 = (bf16[64,1,128]{2,1,0:T(2,128)(2,1)S(1)}, bf16[64,1,128]{2,1,0:T(2,128)(2,1)S(1)}, u32[]{:S(2)}, u32[]{:S(2)}) collective-permute-start(bf16[64,1,128]{2,1,0:T(2,128)(2,1)S(1)} %get-tuple-element.218), channel_id=1, source_target_pairs={{2,0},{4,2},{6,4},{3,1},{5,3},{7,5},{10,8},{12,10},{14,12},{11,9},... | collective-permute-start | bytes 49160 | tf_op jit(solution)/shard_map/ppermute | solution.py:19
  79.4 3.4 collective-permute-done.17
  84.5 24.2 %while.20 = (s32[]{:T(128)}, f32[64,1024]{1,0:T(8,128)S(1)}, f32[64,64]{1,0:T(8,128)S(1)}, f32[64,1024]{1,0:T(8,128)S(1)}, s32[]{:T(128)}) while((s32[]{:T(128)}, f32[64,1024]{1,0:T(8,128)S(1)}, f32[64,64]{1,0:T(8,128)S(1)}, f32[64,1024]{1,0:T(8,128)S(1)}, s32[]{:T(128)}) %tuple.143), condition=%wide.region_2.3_spmd, body=%wide.region_1.2_spmd.sunk | while | flops 50397184 | bytes 1851493 | solution.py:91
  88.1 3.9 %collective-permute-done = f32[64,1024]{1,0:T(8,128)S(1)} collective-permute-done((f32[64,1024]{1,0:T(8,128)S(1)}, f32[64,1024]{1,0:T(8,128)S(1)}, u32[]{:S(2)}, u32[]{:S(2)}) %collective-permute-start) | collective-permute-done | bytes 262176 | tf_op jit(solution)/shard_map/while/body/eval_jaxpr/ppermute | solution.py:29
  95.5 4.3 %collective-permute-done = f32[64,1024]{1,0:T(8,128)S(1)} collective-permute-done((f32[64,1024]{1,0:T(8,128)S(1)}, f32[64,1024]{1,0:T(8,128)S(1)}, u32[]{:S(2)}, u32[]{:S(2)}) %collective-permute-start) | collective-permute-done | bytes 262176 | tf_op jit(solution)/shard_map/while/body/eval_jaxpr/ppermute | solution.py:29
  103.4 5.3 %collective-permute-done = f32[64,1024]{1,0:T(8,128)S(1)} collective-permute-done((f32[64,1024]{1,0:T(8,128)S(1)}, f32[64,1024]{1,0:T(8,128)S(1)}, u32[]{:S(2)}, u32[]{:S(2)}) %collective-permute-start) | collective-permute-done | bytes 262176 | tf_op jit(solution)/shard_map/while/body/eval_jaxpr/ppermute | solution.py:29
  110.2 10.4 %collective-permute-start.19 = (bf16[64,1,128]{2,1,0:T(2,128)(2,1)S(1)}, bf16[64,1,128]{2,1,0:T(2,128)(2,1)S(1)}, u32[]{:S(2)}, u32[]{:S(2)}) collective-permute-start(bf16[64,1,128]{2,1,0:T(2,128)(2,1)S(1)} %get-tuple-element.216), channel_id=1, source_target_pairs={{2,0},{4,2},{6,4},{3,1},{5,3},{7,5},{10,8},{12,10},{14,12},{11,9},... | collective-permute-start | bytes 49160 | tf_op jit(solution)/shard_map/ppermute | solution.py:19
  126.9 3.3 collective-permute-done.21
  132.8 8.6 %collective-permute-start.23 = (bf16[64,1,128]{2,1,0:T(2,128)(2,1)S(1)}, bf16[64,1,128]{2,1,0:T(2,128)(2,1)S(1)}, u32[]{:S(2)}, u32[]{:S(2)}) collective-permute-start(bf16[64,1,128]{2,1,0:T(2,128)(2,1)S(1)} %get-tuple-element.214), channel_id=1, source_target_pairs={{2,0},{4,2},{6,4},{3,1},{5,3},{7,5},{10,8},{12,10},{14,12},{11,9},... | collective-permute-start | bytes 49160 | tf_op jit(solution)/shard_map/ppermute | solution.py:19
  147.7 3.3 collective-permute-done.25
  154.5 7.9 %collective-permute-start.27 = (bf16[64,1,128]{2,1,0:T(2,128)(2,1)S(1)}, bf16[64,1,128]{2,1,0:T(2,128)(2,1)S(1)}, u32[]{:S(2)}, u32[]{:S(2)}) collective-permute-start(bf16[64,1,128]{2,1,0:T(2,128)(2,1)S(1)} %get-tuple-element.212), channel_id=1, source_target_pairs={{2,0},{4,2},{6,4},{3,1},{5,3},{7,5},{10,8},{12,10},{14,12},{11,9},... | collective-permute-start | bytes 49160 | tf_op jit(solution)/shard_map/ppermute | solution.py:19
  177.0 7.1 %collective-permute-start.31 = (bf16[64,1,128]{2,1,0:T(2,128)(2,1)S(1)}, bf16[64,1,128]{2,1,0:T(2,128)(2,1)S(1)}, u32[]{:S(2)}, u32[]{:S(2)}) collective-permute-start(bf16[64,1,128]{2,1,0:T(2,128)(2,1)S(1)} %get-tuple-element.210), channel_id=1, source_target_pairs={{2,0},{4,2},{6,4},{3,1},{5,3},{7,5},{10,8},{12,10},{14,12},{11,9},... | collective-permute-start | bytes 49160 | tf_op jit(solution)/shard_map/ppermute | solution.py:19
  192.6 3.5 collective-permute-done.33
  201.4 7.8 %collective-permute-start.35 = (bf16[64,1,128]{2,1,0:T(2,128)(2,1)}, bf16[64,1,128]{2,1,0:T(2,128)(2,1)}, u32[]{:S(2)}, u32[]{:S(2)}) collective-permute-start(bf16[64,1,128]{2,1,0:T(2,128)(2,1)} %get-tuple-element.208), channel_id=1, source_target_pairs={{2,0},{4,2},{6,4},{3,1},{5,3},{7,5},{10,8},{12,10},{14,12},{11,9},... | collective-permute-start | bytes 49160 | tf_op jit(solution)/shard_map/ppermute | solution.py:19
  221.9 4.3 %collective-permute-done.37 = bf16[64,10,1]{2,1,0:T(8,128)(2,1)S(1)} collective-permute-done((bf16[64,10,1]{2,1,0:T(8,128)(2,1)}, bf16[64,10,1]{2,1,0:T(8,128)(2,1)S(1)}, u32[]{:S(2)}, u32[]{:S(2)}) %collective-permute-start.37) | collective-permute-done | bytes 1312 | tf_op jit(solution)/shard_map/ppermute | solution.py:19
  231.8 6.0 %collective-permute-start.39 = (bf16[64,1,128]{2,1,0:T(2,128)(2,1)}, bf16[64,1,128]{2,1,0:T(2,128)(2,1)S(1)}, u32[]{:S(2)}, u32[]{:S(2)}) collective-permute-start(bf16[64,1,128]{2,1,0:T(2,128)(2,1)} %get-tuple-element.206), channel_id=1, source_target_pairs={{2,0},{4,2},{6,4},{3,1},{5,3},{7,5},{10,8},{12,10},{14,12},{11,9},... | collective-permute-start | bytes 49160 | tf_op jit(solution)/shard_map/ppermute | solution.py:19
  248.9 3.8 %collective-permute-done.41 = bf16[64,10,1]{2,1,0:T(8,128)(2,1)S(1)} collective-permute-done((bf16[64,10,1]{2,1,0:T(8,128)(2,1)S(1)}, bf16[64,10,1]{2,1,0:T(8,128)(2,1)S(1)}, u32[]{:S(2)}, u32[]{:S(2)}) %collective-permute-start.41) | collective-permute-done | bytes 1312 | tf_op jit(solution)/shard_map/ppermute | solution.py:19
  256.3 6.5 %collective-permute-start.43 = (bf16[64,1,128]{2,1,0:T(2,128)(2,1)S(1)}, bf16[64,1,128]{2,1,0:T(2,128)(2,1)S(1)}, u32[]{:S(2)}, u32[]{:S(2)}) collective-permute-start(bf16[64,1,128]{2,1,0:T(2,128)(2,1)S(1)} %get-tuple-element.204), channel_id=1, source_target_pairs={{2,0},{4,2},{6,4},{3,1},{5,3},{7,5},{10,8},{12,10},{14,12},{11,9},... | collective-permute-start | bytes 49160 | tf_op jit(solution)/shard_map/ppermute | solution.py:19
  269.0 3.8 %collective-permute-done.45 = bf16[64,10,1]{2,1,0:T(8,128)(2,1)S(1)} collective-permute-done((bf16[64,10,1]{2,1,0:T(8,128)(2,1)S(1)}, bf16[64,10,1]{2,1,0:T(8,128)(2,1)S(1)}, u32[]{:S(2)}, u32[]{:S(2)}) %collective-permute-start.45) | collective-permute-done | bytes 1312 | tf_op jit(solution)/shard_map/ppermute | solution.py:19
  276.3 6.6 %collective-permute-start.47 = (bf16[64,1,128]{2,1,0:T(2,128)(2,1)S(1)}, bf16[64,1,128]{2,1,0:T(2,128)(2,1)S(1)}, u32[]{:S(2)}, u32[]{:S(2)}) collective-permute-start(bf16[64,1,128]{2,1,0:T(2,128)(2,1)S(1)} %get-tuple-element.202), channel_id=1, source_target_pairs={{2,0},{4,2},{6,4},{3,1},{5,3},{7,5},{10,8},{12,10},{14,12},{11,9},... | collective-permute-start | bytes 49160 | tf_op jit(solution)/shard_map/ppermute | solution.py:19
  289.2 4.2 %collective-permute-done.49 = bf16[64,10,1]{2,1,0:T(8,128)(2,1)S(1)} collective-permute-done((bf16[64,10,1]{2,1,0:T(8,128)(2,1)S(1)}, bf16[64,10,1]{2,1,0:T(8,128)(2,1)S(1)}, u32[]{:S(2)}, u32[]{:S(2)}) %collective-permute-start.49) | collective-permute-done | bytes 1312 | tf_op jit(solution)/shard_map/ppermute | solution.py:19
  295.8 25.6 %while.21 = (s32[]{:T(128)}, f32[64,1024]{1,0:T(8,128)S(1)}, f32[64,64]{1,0:T(8,128)S(1)}, f32[64,1024]{1,0:T(8,128)S(1)}, s32[]{:T(128)}) while((s32[]{:T(128)}, f32[64,1024]{1,0:T(8,128)S(1)}, f32[64,64]{1,0:T(8,128)S(1)}, f32[64,1024]{1,0:T(8,128)S(1)}, s32[]{:T(128)}) %tuple.146), condition=%wide.region_4.5_spmd, body=%wide.region_3.4_spmd.sunk | while | flops 50397184 | bytes 1851493 | solution.py:127
  298.3 5.4 %collective-permute-done.1 = f32[64,1024]{1,0:T(8,128)S(1)} collective-permute-done((f32[64,1024]{1,0:T(8,128)S(1)}, f32[64,1024]{1,0:T(8,128)S(1)}, u32[]{:S(2)}, u32[]{:S(2)}) %collective-permute-start.1) | collective-permute-done | bytes 262176 | tf_op jit(solution)/shard_map/while/body/eval_jaxpr/ppermute | solution.py:29
  306.1 6.0 %collective-permute-done.1 = f32[64,1024]{1,0:T(8,128)S(1)} collective-permute-done((f32[64,1024]{1,0:T(8,128)S(1)}, f32[64,1024]{1,0:T(8,128)S(1)}, u32[]{:S(2)}, u32[]{:S(2)}) %collective-permute-start.1) | collective-permute-done | bytes 262176 | tf_op jit(solution)/shard_map/while/body/eval_jaxpr/ppermute | solution.py:29
  314.4 7.0 %collective-permute-done.1 = f32[64,1024]{1,0:T(8,128)S(1)} collective-permute-done((f32[64,1024]{1,0:T(8,128)S(1)}, f32[64,1024]{1,0:T(8,128)S(1)}, u32[]{:S(2)}, u32[]{:S(2)}) %collective-permute-start.1) | collective-permute-done | bytes 262176 | tf_op jit(solution)/shard_map/while/body/eval_jaxpr/ppermute | solution.py:29
  322.3 20.5 %all-reduce.2.cloned.1.call-done = f32[4,64,576]{2,1,0:T(8,128)} async-done(((f32[4,64,576]{2,1,0:T(8,128)}), f32[4,64,576]{2,1,0:T(8,128)}) %all-reduce.2.cloned.1.call-update) | async-done | bytes 589840 | tf_op jit(solution)/shard_map/psum | solution.py:119
  (368 shorter events, 158.0 us)
Async XLA Ops:
  7.2 335.6 %all-reduce.2.cloned.1.call-start = ((), (), s32[]{:S(2)}) async-start(), calls=%async_computation | async-start | bytes 1310720 | tf_op jit(solution)/shard_map/psum | solution.py:119
  26.3 7.7 %collective-permute-start.6 = (bf16[64,1,128]{2,1,0:T(2,128)(2,1)S(1)}, bf16[64,1,128]{2,1,0:T(2,128)(2,1)S(1)}, u32[]{:S(2)}, u32[]{:S(2)}) collective-permute-start(bf16[64,1,128]{2,1,0:T(2,128)(2,1)S(1)} %get-tuple-element.221), channel_id=1, source_target_pairs={{0,2},{2,4},{4,6},{1,3},{3,5},{5,7},{8,10},{10,12},{12,14},{9,11},... | collective-permute-start | bytes 49160 | tf_op jit(solution)/shard_map/ppermute | solution.py:17
  27.6 7.3 %collective-permute-start.7 = (bf16[64,1,128]{2,1,0:T(2,128)(2,1)S(1)}, bf16[64,1,128]{2,1,0:T(2,128)(2,1)S(1)}, u32[]{:S(2)}, u32[]{:S(2)}) collective-permute-start(bf16[64,1,128]{2,1,0:T(2,128)(2,1)S(1)} %get-tuple-element.222), channel_id=1, source_target_pairs={{2,0},{4,2},{6,4},{3,1},{5,3},{7,5},{10,8},{12,10},{14,12},{11,9},... | collective-permute-start | bytes 49160 | tf_op jit(solution)/shard_map/ppermute | solution.py:19
  45.0 7.9 %collective-permute-start.10 = (bf16[64,1,128]{2,1,0:T(2,128)(2,1)S(1)}, bf16[64,1,128]{2,1,0:T(2,128)(2,1)S(1)}, u32[]{:S(2)}, u32[]{:S(2)}) collective-permute-start(bf16[64,1,128]{2,1,0:T(2,128)(2,1)S(1)} %get-tuple-element.219), channel_id=1, source_target_pairs={{0,2},{2,4},{4,6},{1,3},{3,5},{5,7},{8,10},{10,12},{12,14},{9,11},... | collective-permute-start | bytes 49160 | tf_op jit(solution)/shard_map/ppermute | solution.py:17
  46.3 7.5 %collective-permute-start.11 = (bf16[64,1,128]{2,1,0:T(2,128)(2,1)S(1)}, bf16[64,1,128]{2,1,0:T(2,128)(2,1)S(1)}, u32[]{:S(2)}, u32[]{:S(2)}) collective-permute-start(bf16[64,1,128]{2,1,0:T(2,128)(2,1)S(1)} %get-tuple-element.220), channel_id=1, source_target_pairs={{2,0},{4,2},{6,4},{3,1},{5,3},{7,5},{10,8},{12,10},{14,12},{11,9},... | collective-permute-start | bytes 49160 | tf_op jit(solution)/shard_map/ppermute | solution.py:19
  64.7 8.5 %collective-permute-start.14 = (bf16[64,1,128]{2,1,0:T(2,128)(2,1)S(1)}, bf16[64,1,128]{2,1,0:T(2,128)(2,1)S(1)}, u32[]{:S(2)}, u32[]{:S(2)}) collective-permute-start(bf16[64,1,128]{2,1,0:T(2,128)(2,1)S(1)} %get-tuple-element.217), channel_id=1, source_target_pairs={{0,2},{2,4},{4,6},{1,3},{3,5},{5,7},{8,10},{10,12},{12,14},{9,11},... | collective-permute-start | bytes 49160 | tf_op jit(solution)/shard_map/ppermute | solution.py:17
  66.0 8.0 %collective-permute-start.15 = (bf16[64,1,128]{2,1,0:T(2,128)(2,1)S(1)}, bf16[64,1,128]{2,1,0:T(2,128)(2,1)S(1)}, u32[]{:S(2)}, u32[]{:S(2)}) collective-permute-start(bf16[64,1,128]{2,1,0:T(2,128)(2,1)S(1)} %get-tuple-element.218), channel_id=1, source_target_pairs={{2,0},{4,2},{6,4},{3,1},{5,3},{7,5},{10,8},{12,10},{14,12},{11,9},... | collective-permute-start | bytes 49160 | tf_op jit(solution)/shard_map/ppermute | solution.py:19
  92.3 7.5 %collective-permute-start = (f32[64,1024]{1,0:T(8,128)S(1)}, f32[64,1024]{1,0:T(8,128)S(1)}, u32[]{:S(2)}, u32[]{:S(2)}) collective-permute-start(f32[64,1024]{1,0:T(8,128)S(1)} %convolution_add_fusion.4), channel_id=1, source_target_pairs={{0,8},{8,16},{16,24},{1,9},{9,17},{17,25},{2,10},{10,18},{18,26},{... | collective-permute-start | bytes 786440 | tf_op jit(solution)/shard_map/while/body/eval_jaxpr/ppermute | solution.py:29
  100.2 8.5 %collective-permute-start = (f32[64,1024]{1,0:T(8,128)S(1)}, f32[64,1024]{1,0:T(8,128)S(1)}, u32[]{:S(2)}, u32[]{:S(2)}) collective-permute-start(f32[64,1024]{1,0:T(8,128)S(1)} %convolution_add_fusion.4), channel_id=1, source_target_pairs={{0,8},{8,16},{16,24},{1,9},{9,17},{17,25},{2,10},{10,18},{18,26},{... | collective-permute-start | bytes 786440 | tf_op jit(solution)/shard_map/while/body/eval_jaxpr/ppermute | solution.py:29
  108.9 11.7 %collective-permute-start.18 = (bf16[64,1,128]{2,1,0:T(2,128)(2,1)S(1)}, bf16[64,1,128]{2,1,0:T(2,128)(2,1)S(1)}, u32[]{:S(2)}, u32[]{:S(2)}) collective-permute-start(bf16[64,1,128]{2,1,0:T(2,128)(2,1)S(1)} %get-tuple-element.215), channel_id=1, source_target_pairs={{0,2},{2,4},{4,6},{1,3},{3,5},{5,7},{8,10},{10,12},{12,14},{9,11},... | collective-permute-start | bytes 49160 | tf_op jit(solution)/shard_map/ppermute | solution.py:17
  110.2 11.3 %collective-permute-start.19 = (bf16[64,1,128]{2,1,0:T(2,128)(2,1)S(1)}, bf16[64,1,128]{2,1,0:T(2,128)(2,1)S(1)}, u32[]{:S(2)}, u32[]{:S(2)}) collective-permute-start(bf16[64,1,128]{2,1,0:T(2,128)(2,1)S(1)} %get-tuple-element.216), channel_id=1, source_target_pairs={{2,0},{4,2},{6,4},{3,1},{5,3},{7,5},{10,8},{12,10},{14,12},{11,9},... | collective-permute-start | bytes 49160 | tf_op jit(solution)/shard_map/ppermute | solution.py:19
  131.5 9.9 %collective-permute-start.22 = (bf16[64,1,128]{2,1,0:T(2,128)(2,1)S(1)}, bf16[64,1,128]{2,1,0:T(2,128)(2,1)S(1)}, u32[]{:S(2)}, u32[]{:S(2)}) collective-permute-start(bf16[64,1,128]{2,1,0:T(2,128)(2,1)S(1)} %get-tuple-element.213), channel_id=1, source_target_pairs={{0,2},{2,4},{4,6},{1,3},{3,5},{5,7},{8,10},{10,12},{12,14},{9,11},... | collective-permute-start | bytes 49160 | tf_op jit(solution)/shard_map/ppermute | solution.py:17
  132.8 9.5 %collective-permute-start.23 = (bf16[64,1,128]{2,1,0:T(2,128)(2,1)S(1)}, bf16[64,1,128]{2,1,0:T(2,128)(2,1)S(1)}, u32[]{:S(2)}, u32[]{:S(2)}) collective-permute-start(bf16[64,1,128]{2,1,0:T(2,128)(2,1)S(1)} %get-tuple-element.214), channel_id=1, source_target_pairs={{2,0},{4,2},{6,4},{3,1},{5,3},{7,5},{10,8},{12,10},{14,12},{11,9},... | collective-permute-start | bytes 49160 | tf_op jit(solution)/shard_map/ppermute | solution.py:19
  153.2 9.2 %collective-permute-start.26 = (bf16[64,1,128]{2,1,0:T(2,128)(2,1)S(1)}, bf16[64,1,128]{2,1,0:T(2,128)(2,1)S(1)}, u32[]{:S(2)}, u32[]{:S(2)}) collective-permute-start(bf16[64,1,128]{2,1,0:T(2,128)(2,1)S(1)} %get-tuple-element.211), channel_id=1, source_target_pairs={{0,2},{2,4},{4,6},{1,3},{3,5},{5,7},{8,10},{10,12},{12,14},{9,11},... | collective-permute-start | bytes 49160 | tf_op jit(solution)/shard_map/ppermute | solution.py:17
  154.5 8.7 %collective-permute-start.27 = (bf16[64,1,128]{2,1,0:T(2,128)(2,1)S(1)}, bf16[64,1,128]{2,1,0:T(2,128)(2,1)S(1)}, u32[]{:S(2)}, u32[]{:S(2)}) collective-permute-start(bf16[64,1,128]{2,1,0:T(2,128)(2,1)S(1)} %get-tuple-element.212), channel_id=1, source_target_pairs={{2,0},{4,2},{6,4},{3,1},{5,3},{7,5},{10,8},{12,10},{14,12},{11,9},... | collective-permute-start | bytes 49160 | tf_op jit(solution)/shard_map/ppermute | solution.py:19
  166.2 7.3 %collective-permute-start.29 = (bf16[64,10,1]{2,1,0:T(8,128)(2,1)}, bf16[64,10,1]{2,1,0:T(8,128)(2,1)S(1)}, u32[]{:S(2)}, u32[]{:S(2)}) collective-permute-start(bf16[64,10,1]{2,1,0:T(8,128)(2,1)} %get-tuple-element.163), channel_id=1, source_target_pairs={{1,0},{3,2},{5,4},{7,6},{9,8},{11,10},{13,12},{15,14},{17,16},{19,... | collective-permute-start | bytes 3848 | tf_op jit(solution)/shard_map/ppermute | solution.py:19
  175.6 8.6 %collective-permute-start.30 = (bf16[64,1,128]{2,1,0:T(2,128)(2,1)S(1)}, bf16[64,1,128]{2,1,0:T(2,128)(2,1)S(1)}, u32[]{:S(2)}, u32[]{:S(2)}) collective-permute-start(bf16[64,1,128]{2,1,0:T(2,128)(2,1)S(1)} %get-tuple-element.209), channel_id=1, source_target_pairs={{0,2},{2,4},{4,6},{1,3},{3,5},{5,7},{8,10},{10,12},{12,14},{9,11},... | collective-permute-start | bytes 49160 | tf_op jit(solution)/shard_map/ppermute | solution.py:17
  177.0 7.9 %collective-permute-start.31 = (bf16[64,1,128]{2,1,0:T(2,128)(2,1)S(1)}, bf16[64,1,128]{2,1,0:T(2,128)(2,1)S(1)}, u32[]{:S(2)}, u32[]{:S(2)}) collective-permute-start(bf16[64,1,128]{2,1,0:T(2,128)(2,1)S(1)} %get-tuple-element.210), channel_id=1, source_target_pairs={{2,0},{4,2},{6,4},{3,1},{5,3},{7,5},{10,8},{12,10},{14,12},{11,9},... | collective-permute-start | bytes 49160 | tf_op jit(solution)/shard_map/ppermute | solution.py:19
  188.8 7.3 %collective-permute-start.33 = (bf16[64,10,1]{2,1,0:T(8,128)(2,1)}, bf16[64,10,1]{2,1,0:T(8,128)(2,1)S(1)}, u32[]{:S(2)}, u32[]{:S(2)}) collective-permute-start(bf16[64,10,1]{2,1,0:T(8,128)(2,1)} %get-tuple-element.161), channel_id=1, source_target_pairs={{1,0},{3,2},{5,4},{7,6},{9,8},{11,10},{13,12},{15,14},{17,16},{19,... | collective-permute-start | bytes 3848 | tf_op jit(solution)/shard_map/ppermute | solution.py:19
  200.1 10.8 %collective-permute-start.34 = (bf16[64,1,128]{2,1,0:T(2,128)(2,1)}, bf16[64,1,128]{2,1,0:T(2,128)(2,1)S(1)}, u32[]{:S(2)}, u32[]{:S(2)}) collective-permute-start(bf16[64,1,128]{2,1,0:T(2,128)(2,1)} %get-tuple-element.207), channel_id=1, source_target_pairs={{0,2},{2,4},{4,6},{1,3},{3,5},{5,7},{8,10},{10,12},{12,14},{9,11},... | collective-permute-start | bytes 49160 | tf_op jit(solution)/shard_map/ppermute | solution.py:17
  201.4 9.5 %collective-permute-start.35 = (bf16[64,1,128]{2,1,0:T(2,128)(2,1)}, bf16[64,1,128]{2,1,0:T(2,128)(2,1)}, u32[]{:S(2)}, u32[]{:S(2)}) collective-permute-start(bf16[64,1,128]{2,1,0:T(2,128)(2,1)} %get-tuple-element.208), channel_id=1, source_target_pairs={{2,0},{4,2},{6,4},{3,1},{5,3},{7,5},{10,8},{12,10},{14,12},{11,9},... | collective-permute-start | bytes 49160 | tf_op jit(solution)/shard_map/ppermute | solution.py:19
  212.7 7.4 %collective-permute-start.36 = (bf16[64,10,1]{2,1,0:T(8,128)(2,1)}, bf16[64,10,1]{2,1,0:T(8,128)(2,1)}, u32[]{:S(2)}, u32[]{:S(2)}) collective-permute-start(bf16[64,10,1]{2,1,0:T(8,128)(2,1)} %get-tuple-element.160), channel_id=1, source_target_pairs={{0,1},{2,3},{4,5},{6,7},{8,9},{10,11},{12,13},{14,15},{16,17},{18,... | collective-permute-start | bytes 3848 | tf_op jit(solution)/shard_map/ppermute | solution.py:17
  218.8 7.3 %collective-permute-start.37 = (bf16[64,10,1]{2,1,0:T(8,128)(2,1)}, bf16[64,10,1]{2,1,0:T(8,128)(2,1)S(1)}, u32[]{:S(2)}, u32[]{:S(2)}) collective-permute-start(bf16[64,10,1]{2,1,0:T(8,128)(2,1)} %get-tuple-element.159), channel_id=1, source_target_pairs={{1,0},{3,2},{5,4},{7,6},{9,8},{11,10},{13,12},{15,14},{17,16},{19,... | collective-permute-start | bytes 3848 | tf_op jit(solution)/shard_map/ppermute | solution.py:19
  230.5 13.0 %collective-permute-start.38 = (bf16[64,1,128]{2,1,0:T(2,128)(2,1)}, bf16[64,1,128]{2,1,0:T(2,128)(2,1)S(1)}, u32[]{:S(2)}, u32[]{:S(2)}) collective-permute-start(bf16[64,1,128]{2,1,0:T(2,128)(2,1)} %get-tuple-element.205), channel_id=1, source_target_pairs={{0,2},{2,4},{4,6},{1,3},{3,5},{5,7},{8,10},{10,12},{12,14},{9,11},... | collective-permute-start | bytes 49160 | tf_op jit(solution)/shard_map/ppermute | solution.py:17
  231.8 11.7 %collective-permute-start.39 = (bf16[64,1,128]{2,1,0:T(2,128)(2,1)}, bf16[64,1,128]{2,1,0:T(2,128)(2,1)S(1)}, u32[]{:S(2)}, u32[]{:S(2)}) collective-permute-start(bf16[64,1,128]{2,1,0:T(2,128)(2,1)} %get-tuple-element.206), channel_id=1, source_target_pairs={{2,0},{4,2},{6,4},{3,1},{5,3},{7,5},{10,8},{12,10},{14,12},{11,9},... | collective-permute-start | bytes 49160 | tf_op jit(solution)/shard_map/ppermute | solution.py:19
  255.0 8.3 %collective-permute-start.42 = (bf16[64,1,128]{2,1,0:T(2,128)(2,1)S(1)}, bf16[64,1,128]{2,1,0:T(2,128)(2,1)S(1)}, u32[]{:S(2)}, u32[]{:S(2)}) collective-permute-start(bf16[64,1,128]{2,1,0:T(2,128)(2,1)S(1)} %get-tuple-element.203), channel_id=1, source_target_pairs={{0,2},{2,4},{4,6},{1,3},{3,5},{5,7},{8,10},{10,12},{12,14},{9,11},... | collective-permute-start | bytes 49160 | tf_op jit(solution)/shard_map/ppermute | solution.py:17
  256.3 7.3 %collective-permute-start.43 = (bf16[64,1,128]{2,1,0:T(2,128)(2,1)S(1)}, bf16[64,1,128]{2,1,0:T(2,128)(2,1)S(1)}, u32[]{:S(2)}, u32[]{:S(2)}) collective-permute-start(bf16[64,1,128]{2,1,0:T(2,128)(2,1)S(1)} %get-tuple-element.204), channel_id=1, source_target_pairs={{2,0},{4,2},{6,4},{3,1},{5,3},{7,5},{10,8},{12,10},{14,12},{11,9},... | collective-permute-start | bytes 49160 | tf_op jit(solution)/shard_map/ppermute | solution.py:19
  275.0 8.4 %collective-permute-start.46 = (bf16[64,1,128]{2,1,0:T(2,128)(2,1)S(1)}, bf16[64,1,128]{2,1,0:T(2,128)(2,1)S(1)}, u32[]{:S(2)}, u32[]{:S(2)}) collective-permute-start(bf16[64,1,128]{2,1,0:T(2,128)(2,1)S(1)} %get-tuple-element.201), channel_id=1, source_target_pairs={{0,2},{2,4},{4,6},{1,3},{3,5},{5,7},{8,10},{10,12},{12,14},{9,11},... | collective-permute-start | bytes 49160 | tf_op jit(solution)/shard_map/ppermute | solution.py:17
  276.3 7.5 %collective-permute-start.47 = (bf16[64,1,128]{2,1,0:T(2,128)(2,1)S(1)}, bf16[64,1,128]{2,1,0:T(2,128)(2,1)S(1)}, u32[]{:S(2)}, u32[]{:S(2)}) collective-permute-start(bf16[64,1,128]{2,1,0:T(2,128)(2,1)S(1)} %get-tuple-element.202), channel_id=1, source_target_pairs={{2,0},{4,2},{6,4},{3,1},{5,3},{7,5},{10,8},{12,10},{14,12},{11,9},... | collective-permute-start | bytes 49160 | tf_op jit(solution)/shard_map/ppermute | solution.py:19
  296.2 7.5 %collective-permute-start.1 = (f32[64,1024]{1,0:T(8,128)S(1)}, f32[64,1024]{1,0:T(8,128)S(1)}, u32[]{:S(2)}, u32[]{:S(2)}) collective-permute-start(f32[64,1024]{1,0:T(8,128)S(1)} %convolution_add_fusion.5), channel_id=1, source_target_pairs={{8,0},{16,8},{24,16},{9,1},{17,9},{25,17},{10,2},{18,10},{26,18},{... | collective-permute-start | bytes 786440 | tf_op jit(solution)/shard_map/while/body/eval_jaxpr/ppermute | solution.py:29
  304.1 8.0 %collective-permute-start.1 = (f32[64,1024]{1,0:T(8,128)S(1)}, f32[64,1024]{1,0:T(8,128)S(1)}, u32[]{:S(2)}, u32[]{:S(2)}) collective-permute-start(f32[64,1024]{1,0:T(8,128)S(1)} %convolution_add_fusion.5), channel_id=1, source_target_pairs={{8,0},{16,8},{24,16},{9,1},{17,9},{25,17},{10,2},{18,10},{26,18},{... | collective-permute-start | bytes 786440 | tf_op jit(solution)/shard_map/while/body/eval_jaxpr/ppermute | solution.py:29
  312.4 9.0 %collective-permute-start.1 = (f32[64,1024]{1,0:T(8,128)S(1)}, f32[64,1024]{1,0:T(8,128)S(1)}, u32[]{:S(2)}, u32[]{:S(2)}) collective-permute-start(f32[64,1024]{1,0:T(8,128)S(1)} %convolution_add_fusion.5), channel_id=1, source_target_pairs={{8,0},{16,8},{24,16},{9,1},{17,9},{25,17},{10,2},{18,10},{26,18},{... | collective-permute-start | bytes 786440 | tf_op jit(solution)/shard_map/while/body/eval_jaxpr/ppermute | solution.py:29
  (50 other events, 303.9 us)
Sparse Core Ops, SparseCore 0:
  286.4 56.3 all-reduce.1
where the time goes:
time: 357 us; the launch traced here: 352 us
  starting transfers between devices  151 us (42%)
  waiting for transfers between devices  120 us (34%)
  local copies, waits for them, and re-layouts  28.5 us (8%)
  other arithmetic  24.9 us (7%)
  between operations  16.1 us (5%)
  matrix products  10.8 us (3%)
    ppermute x24, starting transfers between devices, with_halo(): lax.ppermute(head, axis, [((i + 1) % count, i) for i in range(ends)])  100 us
    ppermute x24, waiting for transfers between devices, with_halo(): lax.ppermute(head, axis, [((i + 1) % count, i) for i in range(ends)])  50.5 us
    ppermute x24, starting transfers between devices, with_halo(): lax.ppermute(tail, axis, [(i, (i + 1) % count) for i in range(ends)])  35.2 us
    ppermute x6, waiting for transfers between devices, from_behind(): return lax.ppermute(array, axis, pairs)  31.9 us
    concatenate x36, other arithmetic, with_halo(): jnp.concatenate([lax.ppermute(tail, axis, [(i, (i + 1) % count) for i in...  21.9 us
    psum x1, waiting for transfers between devices, local(): weight_grads = lax.psum(jnp.stack(grad_list, 0), ('row', 'col'))  20.5 us
    ppermute x24, waiting for transfers between devices, with_halo(): lax.ppermute(tail, axis, [(i, (i + 1) % count) for i in range(ends)])  17.3 us
    ppermute x6, starting transfers between devices, from_behind(): return lax.ppermute(array, axis, pairs)  15.6 us
  transfers between devices with their start and end apart: 55, of which 40 were waited for; matrix products, arithmetic and copies ran while one was open for 8% of the time, Pallas kernels for 0%

commit v1 on v0

v1 whole, which is shorter than its diff:
```python
import functools

import jax
import jax.numpy as jnp
from jax import lax
from jax.experimental import pallas as pl
from jax.experimental.pallas import tpu as pltpu
from jax.sharding import PartitionSpec as P

step_size = 0.2
EDGE = 8
VMEM_BYTES = 40 * 1024 * 1024
f32 = jnp.float32
bf16 = jnp.bfloat16


def call(body, out_shape, scratch=(), flops=0, moved=0):
    return pl.pallas_call(
        body,
        out_shape=out_shape,
        scratch_shapes=list(scratch),
        cost_estimate=pl.CostEstimate(
            flops=int(flops), bytes_accessed=int(moved), transcendentals=0
        ),
        compiler_params=pltpu.CompilerParams(vmem_limit_bytes=VMEM_BYTES),
    )


def row_of(ref, row, channels, rows):
    return ref[pl.ds(row, channels, stride=rows), :]


def lanes_of(shape):
    return lax.broadcasted_iota(jnp.int32, shape, 1)


def fold_edges(rows_list):
    shape = rows_list[0].shape
    slot = lanes_of(shape) // (2 * EDGE)
    total = jnp.zeros(shape, f32)
    for place, row in enumerate(rows_list):
        turned = pltpu.roll(row, (2 * EDGE * place + EDGE) % shape[1], 1)
        total = jnp.where(slot == place, turned, total)
    return total


def join_edges(from_left, from_right, has_left, has_right):
    lanes = lanes_of(from_left.shape)
    return jnp.where(
        lanes % (2 * EDGE) >= EDGE,
        from_right.astype(f32) * has_right,
        from_left.astype(f32) * has_left,
    )


def side_lanes(joined, place):
    cols = joined.shape[1]
    return pltpu.roll(joined, (cols - (2 * EDGE * place + EDGE)) % cols, 1)


def convolved(weights, slab):
    channels = slab.shape[1]
    lanes = slab.shape[2]
    product = jnp.dot(
        weights, slab.reshape(3 * channels, lanes), preferred_element_type=f32
    )
    return (
        pltpu.roll(product[:channels], 1, 1)
        + product[channels : 2 * channels]
        + pltpu.roll(product[2 * channels :], lanes - 1, 1)
    )


def flags():
    row, col = lax.axis_index("row"), lax.axis_index("col")
    up = (row > 0).astype(f32)
    down = (row < lax.axis_size("row") - 1).astype(f32)
    left = (col > 0).astype(f32)
    right = (col < lax.axis_size("col") - 1).astype(f32)
    return up, down, left, right


def lane_mask(cols, left, right):
    lanes = lax.broadcasted_iota(jnp.int32, (1, 2 * cols), 1)
    return jnp.where(lanes < cols, 1.0, jnp.where(lanes < cols + cols // 2, right, left))


def pack_body(c_ref, q_ref, top_ref, bottom_ref, edge_ref, *, channels, rows, depth):
    for which, ref in enumerate((c_ref, q_ref)):
        image = [row_of(ref, row, channels, rows) for row in range(rows)]
        for row in range(depth):
            top_ref[which * depth + row] = image[row].astype(bf16)
            bottom_ref[which * depth + row] = image[rows - depth + row].astype(bf16)
        edge_ref[which] = fold_edges(image).astype(bf16)


def load_halo(dest, first, side_ref, count, halo, joined, offset):
    for row in range(count):
        dest(
            first + row,
            halo[row].astype(f32),
            side_lanes(joined, offset + row),
        )


def layer_rows(low, high, body):
    def two(turn, carry):
        body(low + 2 * turn)
        body(low + 2 * turn + 1)
        return carry

    lax.fori_loop(0, (high - low) // 2, two, 0)


def row_flag(index, halo, rows, up, down):
    return jnp.where(index < halo, up, jnp.where(index >= halo + rows, down, 1.0))


def first_body(
    c_ref, above_ref, below_ref, left_ref, right_ref, w_ref, f_ref, fb_ref, x_ref, a_ref,
    *, channels, rows, depth,
):
    cols = c_ref.shape[1]
    up, down, left, right = flags()
    mask = lane_mask(cols, left, right)
    halo = depth

    def put(index, own, beyond):
        x_ref[index, :, :cols] = own
        x_ref[index, :, cols:] = beyond
        a_ref[0, index, :, :cols] = own.astype(bf16)
        a_ref[0, index, :, cols:] = beyond.astype(bf16)

    joined = [join_edges(left_ref[j], right_ref[j], left, right) for j in range(3)]
    for row in range(rows):
        put(halo + row, row_of(c_ref, row, channels, rows), side_lanes(joined[1], row))
    for row in range(depth):
        put(row, above_ref[row].astype(f32), side_lanes(joined[0], rows - depth + row))
        put(halo + rows + row, below_ref[row].astype(f32), side_lanes(joined[2], row))

    total = rows + 2 * halo
    for layer in range(depth):
        now, later = layer % 2, (layer + 1) % 2

        def step(index, layer=layer, now=now, later=later):
            z = convolved(w_ref[layer], a_ref[now, pl.ds(index - 1, 3)])
            gain = mask * (step_size * row_flag(index, halo, rows, up, down))
            x = x_ref[index] + gain * jnp.tanh(z)
            x_ref[index] = x
            a_ref[later, index] = x.astype(bf16)

        layer_rows(layer + 1, total - layer - 1, step)
    for row in range(rows):
        value = x_ref[halo + row, :, :cols]
        f_ref[row] = value
        fb_ref[row] = value.astype(bf16)


def hop_body(s_ref, c_ref, f_ref, m_ref, out_ref, *, channels, rows):
    for row in range(rows):
        e = s_ref[row].astype(f32) - row_of(c_ref, row, channels, rows)
        high = e.astype(bf16)
        low = (e - high.astype(f32)).astype(bf16)
        stacked = jnp.concatenate([high, high, low], 0)
        moved = jnp.dot(m_ref[...], stacked, preferred_element_type=f32)
        out_ref[row] = (f_ref[row] + e + moved).astype(bf16)


def settle_body(*refs, channels, rows):
    c_ref, arrived, s_ref, edge_ref = refs[0], refs[1:-2], refs[-2], refs[-1]
    first = lax.axis_index("layer") == 0
    image = []
    for row in range(rows):
        value = sum(ref[row].astype(f32) for ref in arrived)
        value = jnp.where(first, row_of(c_ref, row, channels, rows), value)
        s_ref[row] = value.astype(bf16)
        image.append(value)
    edge_ref[0] = fold_edges(image).astype(bf16)


def second_body(
    c_ref, q_ref, s_ref, s_above_ref, s_below_ref, s_left_ref, s_right_ref,
    q_above_ref, q_below_ref, q_left_ref, q_right_ref, w_ref, wt_ref,
    state_ref, g_ref, gb_ref, grad_ref,
    x_ref, a_ref, keep_ref, slope_ref, adj_ref, src_ref,
    *, channels, rows, depth,
):
    cols = c_ref.shape[1]
    up, down, left, right = flags()
    mask = lane_mask(cols, left, right)
    halo = 2 * depth
    total = rows + 2 * halo
    first = lax.axis_index("layer") == 0

    def put(index, own, beyond):
        x_ref[index, :, :cols] = own
        x_ref[index, :, cols:] = beyond
        a_ref[0, index, :, :cols] = own.astype(bf16)
        a_ref[0, index, :, cols:] = beyond.astype(bf16)

    joined = [join_edges(s_left_ref[j], s_right_ref[j], left, right) for j in range(3)]
    for row in range(rows):
        own = jnp.where(first, row_of(c_ref, row, channels, rows), s_ref[row].astype(f32))
        state_ref[pl.ds(row, channels, stride=rows), :] = own
        put(halo + row, own, side_lanes(joined[1], row))
    for row in range(halo):
        put(row, s_above_ref[rows - halo + row].astype(f32), side_lanes(joined[0], rows - halo + row))
        put(halo + rows + row, s_below_ref[row].astype(f32), side_lanes(joined[2], row))

    def put_adj(index, own, beyond):
        adj_ref[index, :, :cols] = own
        adj_ref[index, :, cols:] = beyond

    joined = [join_edges(q_left_ref[j], q_right_ref[j], left, right) for j in range(3)]
    for row in range(rows):
        put_adj(halo + row, row_of(q_ref, row, channels, rows), side_lanes(joined[1], row))
    for row in range(depth):
        put_adj(halo - depth + row, q_above_ref[row].astype(f32), side_lanes(joined[0], rows - depth + row))
        put_adj(halo + rows + row, q_below_ref[row].astype(f32), side_lanes(joined[2], row))

    def keep(layer):
        for row in range(rows):
            x = x_ref[halo + row]
            lanes = 2 * cols
            keep_ref[layer, :, pl.ds(row * cols, cols)] = jnp.concatenate(
                [
                    pltpu.roll(x, 1, 1)[:, :cols],
                    x[:, :cols],
                    pltpu.roll(x, lanes - 1, 1)[:, :cols],
                ],
                0,
            ).astype(bf16)

    for layer in range(depth):
        now, later = layer % 2, (layer + 1) % 2
        keep(layer)

        def step(index, layer=layer, now=now, later=later):
            z = convolved(w_ref[layer], a_ref[now, pl.ds(index - 1, 3)])
            gain = mask * (step_size * row_flag(index, halo, rows, up, down))
            t = jnp.tanh(z)
            slope_ref[layer, index] = gain * (1.0 - t * t)
            if layer < depth - 1:
                x = x_ref[index] + gain * t
                x_ref[index] = x
                a_ref[later, index] = x.astype(bf16)

        layer_rows(layer + 1, total - layer - 1, step)

    for layer in reversed(range(depth)):
        reach = layer + 1

        def source(index, layer=layer):
            src_ref[index] = (adj_ref[index] * slope_ref[layer, index]).astype(bf16)

        layer_rows(halo - reach, halo + rows + reach, source)

        def back(index, layer=layer):
            adj_ref[index] += convolved(wt_ref[layer], src_ref[pl.ds(index - 1, 3)])

        layer_rows(halo - layer, halo + rows + layer, back)
        stacked = jnp.concatenate(
            [
                src_ref[pl.ds(halo + row - 1, 3)].reshape(3 * channels, 2 * cols)[:, :cols]
                for row in range(rows)
            ],
            1,
        )
        grad = lax.dot_general(
            stacked, keep_ref[layer], (((1,), (1,)), ((), ())), preferred_element_type=f32
        )
        for tap in range(3):
            grad_ref[layer, :, pl.ds(tap * 3 * channels, 3 * channels)] = grad[
                (2 - tap) * channels : (3 - tap) * channels
            ]
    for row in range(rows):
        value = adj_ref[halo + row, :, :cols]
        g_ref[row] = value
        gb_ref[row] = value.astype(bf16)


def last_body(*refs, channels, rows):
    q_ref, arrived, out_ref = refs[0], refs[1:-1], refs[-1]
    last = lax.axis_index("layer") == lax.axis_size("layer") - 1
    for row in range(rows):
        value = sum(ref[row].astype(f32) for ref in arrived)
        value = jnp.where(last, row_of(q_ref, row, channels, rows), value)
        out_ref[pl.ds(row, channels, stride=rows), :] = value


def shifted(array, row_by, col_by):
    rows, cols = lax.axis_size("row"), lax.axis_size("col")
    pairs = [
        (r * cols + c, (r + row_by) * cols + c + col_by)
        for r in range(rows)
        for c in range(cols)
        if 0 <= r + row_by < rows and 0 <= c + col_by < cols
    ]
    return lax.ppermute(array, ("row", "col"), pairs)


def swapped(array, row_by):
    rows = lax.axis_size("row")
    pairs = [
        (r * 2 + c, (r + row_by) * 2 + 1 - c)
        for r in range(rows)
        for c in range(2)
        if 0 <= r + row_by < rows
    ]
    return lax.ppermute(array, ("row", "col"), pairs)


def around(edges):
    if lax.axis_size("col") == 2:
        parts = [swapped(edges, by) for by in (1, 0, -1)]
        both = jnp.stack(parts, 0)
        return both, both
    return (
        jnp.stack([shifted(edges, by, 1) for by in (1, 0, -1)], 0),
        jnp.stack([shifted(edges, by, -1) for by in (1, 0, -1)], 0),
    )


def total_over_tiles(grads):
    rows, cols = lax.axis_size("row"), lax.axis_size("col")
    depth = grads.shape[0]
    half = depth // 2
    odd = lax.axis_index("row") % 2 == 1
    sent = jnp.where(odd, grads[:half], grads[half:]).astype(bf16)
    own = jnp.where(odd, grads[half:], grads[:half])
    pair = [(r, r ^ 1) for r in range(rows)]
    value = own + lax.ppermute(sent, "row", pair).astype(f32)

    def add(value, axis, pairs):
        rounded = value.astype(bf16)
        return rounded.astype(f32) + lax.ppermute(rounded, axis, pairs).astype(f32)

    bit = 2
    while bit < rows:
        value = add(value, "row", [(r, r ^ bit) for r in range(rows)])
        bit *= 2
    bit = 1
    while bit < cols:
        value = add(value, "col", [(c, c ^ bit) for c in range(cols)])
        bit *= 2
    rounded = value.astype(bf16)
    other = lax.ppermute(rounded, "row", pair)
    first = jnp.where(odd, other, rounded)
    second = jnp.where(odd, rounded, other)
    return jnp.concatenate([first, second], 0).astype(f32)


def local(c_states, c_adjoints, weights):
    groups = lax.axis_size("layer")
    channels, rows, cols = c_states.shape[1:]
    depth = weights.shape[0]
    flat = (channels * rows, cols)
    c_flat, q_flat = c_states.reshape(flat), c_adjoints.reshape(flat)
    sizes = dict(channels=channels, rows=rows)
    tile_b = jax.ShapeDtypeStruct((rows, channels, cols), bf16)
    tile_f = jax.ShapeDtypeStruct((rows, channels, cols), f32)

    top, bottom, edges = call(
        functools.partial(pack_body, depth=depth, **sizes),
        (
            jax.ShapeDtypeStruct((2 * depth, channels, cols), bf16),
            jax.ShapeDtypeStruct((2 * depth, channels, cols), bf16),
            jax.ShapeDtypeStruct((2, channels, cols), bf16),
        ),
    )(c_flat, q_flat)
    above = shifted(bottom, 1, 0)
    below = shifted(top, -1, 0)
    left, right = around(edges)

    taps = weights.reshape(depth, channels, 3, 3, channels)
    w_fwd = jnp.transpose(taps, (0, 3, 1, 2, 4)).reshape(depth, 3 * channels, 3 * channels)
    w_back = jnp.transpose(taps[:, :, ::-1, ::-1, :], (0, 3, 4, 2, 1)).reshape(
        depth, 3 * channels, 3 * channels
    )
    coarse = step_size * jnp.sum(weights[0].astype(f32).reshape(channels, 9, channels), axis=1)
    high = coarse.astype(bf16)
    low = (coarse - high.astype(f32)).astype(bf16)
    m_fwd = jnp.concatenate([high, low, high], 1)
    m_back = jnp.concatenate([high.T, low.T, high.T], 1)

    lanes = 2 * cols
    mac = 2 * 9 * channels * channels * lanes
    total = rows + 2 * depth
    f, sending = call(
        functools.partial(first_body, depth=depth, **sizes),
        (tile_f, tile_b),
        [
            pltpu.VMEM((total, channels, lanes), f32),
            pltpu.VMEM((2, total, channels, lanes), bf16),
        ],
        flops=mac * 44,
    )(c_flat, above[:depth], below[:depth], left[:, 0], right[:, 0], w_fwd)

    def chain(sending, base, target, matrix, order):
        arrivals = []
        for place, (source, goal) in enumerate(order):
            arrived = lax.ppermute(sending, "layer", [(source, goal)])
            arrivals.append(arrived)
            if place < len(order) - 1:
                sending = call(functools.partial(hop_body, **sizes), tile_b)(
                    arrived, base, target, matrix
                )
        return arrivals

    arrivals = chain(sending, c_flat, f, m_fwd, [(k, k + 1) for k in range(groups - 1)])
    s, s_edges = call(
        functools.partial(settle_body, **sizes),
        (tile_b, jax.ShapeDtypeStruct((1, channels, cols), bf16)),
    )(c_flat, *arrivals)
    s_above = shifted(s, 1, 0)
    s_below = shifted(s, -1, 0)
    s_left, s_right = around(s_edges)

    total = rows + 4 * depth
    state, g, sending, grads = call(
        functools.partial(second_body, depth=depth, **sizes),
        (
            jax.ShapeDtypeStruct(flat, f32),
            tile_f,
            tile_b,
            jax.ShapeDtypeStruct((depth, channels, 9 * channels), f32),
        ),
        [
            pltpu.VMEM((total, channels, lanes), f32),
            pltpu.VMEM((2, total, channels, lanes), bf16),
            pltpu.VMEM((depth, 3 * channels, rows * cols), bf16),
            pltpu.VMEM((depth, total, channels, lanes), f32),
            pltpu.VMEM((total, channels, lanes), f32),
            pltpu.VMEM((total, channels, lanes), bf16),
        ],
        flops=mac * 136,
    )(
        c_flat, q_flat, s, s_above, s_below, s_left[:, 0], s_right[:, 0],
        above[depth:], below[depth:], left[:, 1], right[:, 1], w_fwd, w_back,
    )
    returned = chain(
        sending, q_flat, g, m_back, [(k, k - 1) for k in range(groups - 1, 0, -1)]
    )
    weight_grads = total_over_tiles(grads)
    adjoint = call(
        functools.partial(last_body, **sizes), jax.ShapeDtypeStruct(flat, f32)
    )(q_flat, *returned)
    return state.reshape(c_states.shape), adjoint.reshape(c_states.shape), weight_grads


def solution(mesh):
    placed = (
        P("layer", None, "row", "col"),
        P("layer", None, "row", "col"),
        P("layer", None, None),
    )
    return jax.shard_map(
        local, mesh=mesh, in_specs=placed, out_specs=placed, check_vma=False
    )
```

time: 357 us -> 104 us (0.29)
  the two profiles are of different devices: /device:TPU:19 before, /device:TPU:0 now
where the time goes in v1:
time: 104 us; the launch traced here: 103 us
  starting transfers between devices  39.7 us (38%)
  Pallas kernels  30.6 us (29%)
  waiting for transfers between devices  25.5 us (25%)
  local copies, waits for them, and re-layouts  5.18 us (5%)
  other arithmetic  1.26 us (1%)
  between operations  1.07 us (1%)
    pallas_call x1, Pallas kernels, local(): call(functools.partial(second_body, depth=depth, **sizes), (jax.ShapeDtyp...  21.5 us
    ppermute x6, waiting for transfers between devices, chain(): arrived = lax.ppermute(sending, 'layer', [(source, goal)])  16.9 us
    ppermute x6, starting transfers between devices, swapped(): return lax.ppermute(array, ('row', 'col'), pairs)  15.8 us
    ppermute x4, starting transfers between devices, shifted(): return lax.ppermute(array, ('row', 'col'), pairs)  9.85 us
    ppermute x6, starting transfers between devices, chain(): arrived = lax.ppermute(sending, 'layer', [(source, goal)])  7.44 us
    ppermute x2, waiting for transfers between devices, add(): return rounded.astype(f32) + lax.ppermute(rounded, axis, pairs).astype(f32)  7.01 us
    pallas_call x1, Pallas kernels, local(): call(functools.partial(first_body, depth=depth, **sizes), (tile_f, tile_b...  6.94 us
    ppermute x2, starting transfers between devices, add(): return rounded.astype(f32) + lax.ppermute(rounded, axis, pairs).astype(f32)  4.39 us
  transfers between devices with their start and end apart: 20, of which 6 were waited for; matrix products, arithmetic and copies ran while one was open for 3% of the time, Pallas kernels for 1%

profile of v1, /device:TPU:0, one launch (start us, length us, event | category | flops | bytes accessed | tf_op | source)
XLA Modules:
  0.0 103.3 jit_solution(2960812588978408640)
XLA Ops:
  0.6 0.9 copy-done
  1.6 0.9 copy-done.2
  2.7 1.3 %collective-permute-start.4 = (bf16[2,64,128]{2,1,0:T(8,128)(2,1)S(1)}, bf16[2,64,128]{2,1,0:T(8,128)(2,1)S(1)}, u32[]{:S(2)}, u32[]{:S(2)}) collective-permute-start(bf16[2,64,128]{2,1,0:T(8,128)(2,1)S(1)} %get-tuple-element.16), channel_id=1, source_target_pairs={{2,1},{3,0},{4,3},{5,2},{6,5},{7,4},{10,9},{11,8},{12,11},{13,10},... | collective-permute-start | bytes 98312 | tf_op jit(solution)/shard_map/ppermute | solution.py:310
  4.0 3.0 %collective-permute-start.3 = (bf16[2,64,128]{2,1,0:T(8,128)(2,1)S(1)}, bf16[2,64,128]{2,1,0:T(8,128)(2,1)S(1)}, u32[]{:S(2)}, u32[]{:S(2)}) collective-permute-start(bf16[2,64,128]{2,1,0:T(8,128)(2,1)S(1)} %get-tuple-element.16), channel_id=1, source_target_pairs={{0,1},{1,0},{2,3},{3,2},{4,5},{5,4},{6,7},{7,6},{8,9},{9,8},{10,11... | collective-permute-start | bytes 98312 | tf_op jit(solution)/shard_map/ppermute | solution.py:310
  7.0 4.0 %collective-permute-start.2 = (bf16[2,64,128]{2,1,0:T(8,128)(2,1)S(1)}, bf16[2,64,128]{2,1,0:T(8,128)(2,1)S(1)}, u32[]{:S(2)}, u32[]{:S(2)}) collective-permute-start(bf16[2,64,128]{2,1,0:T(8,128)(2,1)S(1)} %get-tuple-element.16), channel_id=1, source_target_pairs={{0,3},{1,2},{2,5},{3,4},{4,7},{5,6},{8,11},{9,10},{10,13},{11,12},... | collective-permute-start | bytes 98312 | tf_op jit(solution)/shard_map/ppermute | solution.py:310
  11.0 2.9 %collective-permute-start = (bf16[8,64,128]{2,1,0:T(8,128)(2,1)S(1)}, bf16[8,64,128]{2,1,0:T(8,128)(2,1)S(1)}, u32[]{:S(2)}, u32[]{:S(2)}) collective-permute-start(bf16[8,64,128]{2,1,0:T(8,128)(2,1)S(1)} %get-tuple-element.14), channel_id=1, source_target_pairs={{0,2},{1,3},{2,4},{3,5},{4,6},{5,7},{8,10},{9,11},{10,12},{11,13},... | collective-permute-start | bytes 393224 | tf_op jit(solution)/shard_map/ppermute | solution.py:299
  13.9 1.3 %collective-permute-start.1 = (bf16[8,64,128]{2,1,0:T(8,128)(2,1)S(1)}, bf16[8,64,128]{2,1,0:T(8,128)(2,1)S(1)}, u32[]{:S(2)}, u32[]{:S(2)}) collective-permute-start(bf16[8,64,128]{2,1,0:T(8,128)(2,1)S(1)} %get-tuple-element.15), channel_id=1, source_target_pairs={{2,0},{3,1},{4,2},{5,3},{6,4},{7,5},{10,8},{11,9},{12,10},{13,11},... | collective-permute-start | bytes 393224 | tf_op jit(solution)/shard_map/ppermute | solution.py:299
  15.6 0.6 copy.11
  17.7 6.9 %shard_map.59 = (f32[8,64,128]{2,1,0:T(8,128)S(1)}, bf16[8,64,128]{2,1,0:T(8,128)(2,1)S(1)}) custom-call(f32[512,128]{1,0:T(8,128)S(1)} %bitcast.36, bf16[4,64,128]{2,1,0:T(8,128)(2,1)S(1)} %get-tuple-element.30.above_ref, bf16[4,64,128]{2,1,0:T(8,128)(2,1)S(1)} %get-tuple-element.28.below_ref, bf16[3,64,128]{2,1,0:T(8,128)(2,1)S(1)} %get-tuple-element.32.left_ref.right_ref, ...), custom_call_target="tpu_custom_call" | custom-call | flops 830472192 | tf_op jit(solution)/shard_map/pallas_call | solution.py:389
  24.6 3.5 %collective-permute-start.5 = (bf16[8,64,128]{2,1,0:T(8,128)(2,1)S(1)}, bf16[8,64,128]{2,1,0:T(8,128)(2,1)S(1)}, u32[]{:S(2)}, u32[]{:S(2)}) collective-permute-start(bf16[8,64,128]{2,1,0:T(8,128)(2,1)S(1)} %get-tuple-element.17), channel_id=1, source_target_pairs={{0,8},{1,9},{2,10},{3,11},{4,12},{5,13},{6,14},{7,15}} | collective-permute-start | bytes 393224 | tf_op jit(solution)/shard_map/ppermute | solution.py:402
  28.3 2.4 %collective-permute-done.5.s_ref.refs_1_ = bf16[8,64,128]{2,1,0:T(8,128)(2,1)S(1)} collective-permute-done((bf16[8,64,128]{2,1,0:T(8,128)(2,1)S(1)}, bf16[8,64,128]{2,1,0:T(8,128)(2,1)S(1)}, u32[]{:S(2)}, u32[]{:S(2)}) %collective-permute-start.5) | collective-permute-done | bytes 131104 | tf_op jit(solution)/shard_map/ppermute | solution.py:402
  30.9 0.7 collective-permute-start.6
  31.9 0.7 collective-permute-start.7
  32.7 1.3 %collective-permute-start.12 = (bf16[1,64,128]{2,1,0:T(8,128)(2,1)S(1)}, bf16[1,64,128]{2,1,0:T(8,128)(2,1)S(1)}, u32[]{:S(2)}, u32[]{:S(2)}) collective-permute-start(bf16[1,64,128]{2,1,0:T(8,128)(2,1)S(1)} %get-tuple-element.20), channel_id=1, source_target_pairs={{2,1},{3,0},{4,3},{5,2},{6,5},{7,4},{10,9},{11,8},{12,11},{13,10},... | collective-permute-start | bytes 49160 | tf_op jit(solution)/shard_map/ppermute | solution.py:310
  34.0 0.7 collective-permute-start.11
  34.7 5.6 %collective-permute-start.10 = (bf16[1,64,128]{2,1,0:T(8,128)(2,1)S(1)}, bf16[1,64,128]{2,1,0:T(8,128)(2,1)S(1)}, u32[]{:S(2)}, u32[]{:S(2)}) collective-permute-start(bf16[1,64,128]{2,1,0:T(8,128)(2,1)S(1)} %get-tuple-element.20), channel_id=1, source_target_pairs={{0,3},{1,2},{2,5},{3,4},{4,7},{5,6},{8,11},{9,10},{10,13},{11,12},... | collective-permute-start | bytes 49160 | tf_op jit(solution)/shard_map/ppermute | solution.py:310
  40.3 1.3 %collective-permute-start.9 = (bf16[8,64,128]{2,1,0:T(8,128)(2,1)S(1)}, bf16[8,64,128]{2,1,0:T(8,128)(2,1)S(1)}, u32[]{:S(2)}, u32[]{:S(2)}) collective-permute-start(bf16[8,64,128]{2,1,0:T(8,128)(2,1)S(1)} %get-tuple-element.19.s_ref), channel_id=1, source_target_pairs={{2,0},{3,1},{4,2},{5,3},{6,4},{7,5},{10,8},{11,9},{12,10},{13,11},... | collective-permute-start | bytes 393224 | tf_op jit(solution)/shard_map/ppermute | solution.py:299
  41.6 4.3 %collective-permute-start.8 = (bf16[8,64,128]{2,1,0:T(8,128)(2,1)S(1)}, bf16[8,64,128]{2,1,0:T(8,128)(2,1)S(1)}, u32[]{:S(2)}, u32[]{:S(2)}) collective-permute-start(bf16[8,64,128]{2,1,0:T(8,128)(2,1)S(1)} %get-tuple-element.19.s_ref), channel_id=1, source_target_pairs={{0,2},{1,3},{2,4},{3,5},{4,6},{5,7},{8,10},{9,11},{10,12},{11,13},... | collective-permute-start | bytes 393224 | tf_op jit(solution)/shard_map/ppermute | solution.py:299
  46.0 0.5 copy.15
  47.4 21.5 %shard_map.63 = (f32[512,128]{1,0:T(8,128)}, f32[8,64,128]{2,1,0:T(8,128)S(1)}, bf16[8,64,128]{2,1,0:T(8,128)(2,1)S(1)}, f32[4,64,576]{2,1,0:T(8,128)S(1)}) custom-call(f32[512,128]{1,0:T(8,128)S(1)} %bitcast.40, f32[512,128]{1,0:T(8,128)S(1)} %bitcast.31, bf16[8,64,128]{2,1,0:T(8,128)(2,1)S(1)} %get-tuple-element.19.s_ref, ...), custom_call_target="tpu_custom_call" | custom-call | flops 2566914048 | tf_op jit(solution)/shard_map/pallas_call | solution.py:420
  69.0 2.1 %collective-permute-start.16 = (bf16[2,64,576]{2,1,0:T(8,128)(2,1)S(1)}, bf16[2,64,576]{2,1,0:T(8,128)(2,1)S(1)}, u32[]{:S(2)}, u32[]{:S(2)}) collective-permute-start(bf16[2,64,576]{2,1,0:T(8,128)(2,1)S(1)} %select_convert_fusion), channel_id=1, source_target_pairs={{0,2},{2,0},{4,6},{6,4},{1,3},{3,1},{5,7},{7,5},{8,10},{10,8},{12,... | collective-permute-start | bytes 442376 | tf_op jit(solution)/shard_map/ppermute | solution.py:332
  71.1 1.0 collective-permute-done.16
  72.2 2.8 %collective-permute-start.17 = (bf16[2,64,576]{2,1,0:T(8,128)(2,1)S(1)}, bf16[2,64,576]{2,1,0:T(8,128)(2,1)S(1)}, u32[]{:S(2)}, u32[]{:S(2)}) collective-permute-start(bf16[2,64,576]{2,1,0:T(8,128)(2,1)S(1)} %add_convert_fusion.2), channel_id=1, source_target_pairs={{0,4},{2,6},{4,0},{6,2},{1,5},{3,7},{5,1},{7,3},{8,12},{10,14},{12... | collective-permute-start | bytes 442376 | tf_op jit(solution)/shard_map/ppermute | solution.py:336
  75.0 0.7 collective-permute-start.13
  75.7 3.8 %collective-permute-done.17 = bf16[2,64,576]{2,1,0:T(8,128)(2,1)S(1)} collective-permute-done((bf16[2,64,576]{2,1,0:T(8,128)(2,1)S(1)}, bf16[2,64,576]{2,1,0:T(8,128)(2,1)S(1)}, u32[]{:S(2)}, u32[]{:S(2)}) %collective-permute-start.17) | collective-permute-done | bytes 147488 | tf_op jit(solution)/shard_map/ppermute | solution.py:336
  79.5 1.6 %collective-permute-start.18 = (bf16[2,64,576]{2,1,0:T(8,128)(2,1)S(1)}, bf16[2,64,576]{2,1,0:T(8,128)(2,1)S(1)}, u32[]{:S(2)}, u32[]{:S(2)}) collective-permute-start(bf16[2,64,576]{2,1,0:T(8,128)(2,1)S(1)} %add_convert_fusion.1), channel_id=1, source_target_pairs={{0,1},{1,0},{2,3},{3,2},{4,5},{5,4},{6,7},{7,6},{8,9},{9,8},{10,11... | collective-permute-start | bytes 442376 | tf_op jit(solution)/shard_map/ppermute | solution.py:336
  81.5 0.7 collective-permute-start.14
  82.2 3.2 %collective-permute-done.18 = bf16[2,64,576]{2,1,0:T(8,128)(2,1)S(1)} collective-permute-done((bf16[2,64,576]{2,1,0:T(8,128)(2,1)S(1)}, bf16[2,64,576]{2,1,0:T(8,128)(2,1)S(1)}, u32[]{:S(2)}, u32[]{:S(2)}) %collective-permute-start.18) | collective-permute-done | bytes 147488 | tf_op jit(solution)/shard_map/ppermute | solution.py:336
  85.7 1.3 %collective-permute-start.15 = (bf16[8,64,128]{2,1,0:T(8,128)(2,1)S(1)}, bf16[8,64,128]{2,1,0:T(8,128)(2,1)S(1)}, u32[]{:S(2)}, u32[]{:S(2)}) collective-permute-start(bf16[8,64,128]{2,1,0:T(8,128)(2,1)S(1)} %shard_map.65), channel_id=1, source_target_pairs={{8,0},{9,1},{10,2},{11,3},{12,4},{13,5},{14,6},{15,7}} | collective-permute-start | bytes 393224 | tf_op jit(solution)/shard_map/ppermute | solution.py:402
  87.0 14.5 %collective-permute-done.15.refs_3_ = bf16[8,64,128]{2,1,0:T(8,128)(2,1)S(1)} collective-permute-done((bf16[8,64,128]{2,1,0:T(8,128)(2,1)S(1)}, bf16[8,64,128]{2,1,0:T(8,128)(2,1)S(1)}, u32[]{:S(2)}, u32[]{:S(2)}) %collective-permute-start.15) | collective-permute-done | bytes 131104 | tf_op jit(solution)/shard_map/ppermute | solution.py:402
  101.6 0.8 shard_map.66
  102.4 0.9 maximum_convert_fusion
  (51 shorter events, 4.5 us)
Async XLA Ops:
  0.6 1.0 copy-start
  1.6 0.9 copy-start.2
  2.5 12.7 %copy-start.4 = (bf16[4,64,576]{2,1,0:T(8,128)(2,1)S(1)}, bf16[4,64,576]{2,1,0:T(8,128)(2,1)}, u32[]{:S(2)}) copy-start(bf16[4,64,576]{2,1,0:T(8,128)(2,1)} %param.5) | copy-start | bytes 884740
  2.7 14.0 %collective-permute-start.4 = (bf16[2,64,128]{2,1,0:T(8,128)(2,1)S(1)}, bf16[2,64,128]{2,1,0:T(8,128)(2,1)S(1)}, u32[]{:S(2)}, u32[]{:S(2)}) collective-permute-start(bf16[2,64,128]{2,1,0:T(8,128)(2,1)S(1)} %get-tuple-element.16), channel_id=1, source_target_pairs={{2,1},{3,0},{4,3},{5,2},{6,5},{7,4},{10,9},{11,8},{12,11},{13,10},... | collective-permute-start | bytes 98312 | tf_op jit(solution)/shard_map/ppermute | solution.py:310
  4.0 12.7 %collective-permute-start.3 = (bf16[2,64,128]{2,1,0:T(8,128)(2,1)S(1)}, bf16[2,64,128]{2,1,0:T(8,128)(2,1)S(1)}, u32[]{:S(2)}, u32[]{:S(2)}) collective-permute-start(bf16[2,64,128]{2,1,0:T(8,128)(2,1)S(1)} %get-tuple-element.16), channel_id=1, source_target_pairs={{0,1},{1,0},{2,3},{3,2},{4,5},{5,4},{6,7},{7,6},{8,9},{9,8},{10,11... | collective-permute-start | bytes 98312 | tf_op jit(solution)/shard_map/ppermute | solution.py:310
  7.0 9.7 %collective-permute-start.2 = (bf16[2,64,128]{2,1,0:T(8,128)(2,1)S(1)}, bf16[2,64,128]{2,1,0:T(8,128)(2,1)S(1)}, u32[]{:S(2)}, u32[]{:S(2)}) collective-permute-start(bf16[2,64,128]{2,1,0:T(8,128)(2,1)S(1)} %get-tuple-element.16), channel_id=1, source_target_pairs={{0,3},{1,2},{2,5},{3,4},{4,7},{5,6},{8,11},{9,10},{10,13},{11,12},... | collective-permute-start | bytes 98312 | tf_op jit(solution)/shard_map/ppermute | solution.py:310
  11.0 5.7 %collective-permute-start = (bf16[8,64,128]{2,1,0:T(8,128)(2,1)S(1)}, bf16[8,64,128]{2,1,0:T(8,128)(2,1)S(1)}, u32[]{:S(2)}, u32[]{:S(2)}) collective-permute-start(bf16[8,64,128]{2,1,0:T(8,128)(2,1)S(1)} %get-tuple-element.14), channel_id=1, source_target_pairs={{0,2},{1,3},{2,4},{3,5},{4,6},{5,7},{8,10},{9,11},{10,12},{11,13},... | collective-permute-start | bytes 393224 | tf_op jit(solution)/shard_map/ppermute | solution.py:299
  13.9 3.3 %collective-permute-start.1 = (bf16[8,64,128]{2,1,0:T(8,128)(2,1)S(1)}, bf16[8,64,128]{2,1,0:T(8,128)(2,1)S(1)}, u32[]{:S(2)}, u32[]{:S(2)}) collective-permute-start(bf16[8,64,128]{2,1,0:T(8,128)(2,1)S(1)} %get-tuple-element.15), channel_id=1, source_target_pairs={{2,0},{3,1},{4,2},{5,3},{6,4},{7,5},{10,8},{11,9},{12,10},{13,11},... | collective-permute-start | bytes 393224 | tf_op jit(solution)/shard_map/ppermute | solution.py:299
  16.7 1.0 copy-start.3
  24.6 6.0 %collective-permute-start.5 = (bf16[8,64,128]{2,1,0:T(8,128)(2,1)S(1)}, bf16[8,64,128]{2,1,0:T(8,128)(2,1)S(1)}, u32[]{:S(2)}, u32[]{:S(2)}) collective-permute-start(bf16[8,64,128]{2,1,0:T(8,128)(2,1)S(1)} %get-tuple-element.17), channel_id=1, source_target_pairs={{0,8},{1,9},{2,10},{3,11},{4,12},{5,13},{6,14},{7,15}} | collective-permute-start | bytes 393224 | tf_op jit(solution)/shard_map/ppermute | solution.py:402
  30.9 0.7 collective-permute-start.6
  31.9 0.7 collective-permute-start.7
  32.7 14.2 %collective-permute-start.12 = (bf16[1,64,128]{2,1,0:T(8,128)(2,1)S(1)}, bf16[1,64,128]{2,1,0:T(8,128)(2,1)S(1)}, u32[]{:S(2)}, u32[]{:S(2)}) collective-permute-start(bf16[1,64,128]{2,1,0:T(8,128)(2,1)S(1)} %get-tuple-element.20), channel_id=1, source_target_pairs={{2,1},{3,0},{4,3},{5,2},{6,5},{7,4},{10,9},{11,8},{12,11},{13,10},... | collective-permute-start | bytes 49160 | tf_op jit(solution)/shard_map/ppermute | solution.py:310
  34.0 13.0 %collective-permute-start.11 = (bf16[1,64,128]{2,1,0:T(8,128)(2,1)S(1)}, bf16[1,64,128]{2,1,0:T(8,128)(2,1)S(1)}, u32[]{:S(2)}, u32[]{:S(2)}) collective-permute-start(bf16[1,64,128]{2,1,0:T(8,128)(2,1)S(1)} %get-tuple-element.20), channel_id=1, source_target_pairs={{0,1},{1,0},{2,3},{3,2},{4,5},{5,4},{6,7},{7,6},{8,9},{9,8},{10,11... | collective-permute-start | bytes 49160 | tf_op jit(solution)/shard_map/ppermute | solution.py:310
  34.7 12.3 %collective-permute-start.10 = (bf16[1,64,128]{2,1,0:T(8,128)(2,1)S(1)}, bf16[1,64,128]{2,1,0:T(8,128)(2,1)S(1)}, u32[]{:S(2)}, u32[]{:S(2)}) collective-permute-start(bf16[1,64,128]{2,1,0:T(8,128)(2,1)S(1)} %get-tuple-element.20), channel_id=1, source_target_pairs={{0,3},{1,2},{2,5},{3,4},{4,7},{5,6},{8,11},{9,10},{10,13},{11,12},... | collective-permute-start | bytes 49160 | tf_op jit(solution)/shard_map/ppermute | solution.py:310
  40.3 6.7 %collective-permute-start.9 = (bf16[8,64,128]{2,1,0:T(8,128)(2,1)S(1)}, bf16[8,64,128]{2,1,0:T(8,128)(2,1)S(1)}, u32[]{:S(2)}, u32[]{:S(2)}) collective-permute-start(bf16[8,64,128]{2,1,0:T(8,128)(2,1)S(1)} %get-tuple-element.19.s_ref), channel_id=1, source_target_pairs={{2,0},{3,1},{4,2},{5,3},{6,4},{7,5},{10,8},{11,9},{12,10},{13,11},... | collective-permute-start | bytes 393224 | tf_op jit(solution)/shard_map/ppermute | solution.py:299
  41.6 5.4 %collective-permute-start.8 = (bf16[8,64,128]{2,1,0:T(8,128)(2,1)S(1)}, bf16[8,64,128]{2,1,0:T(8,128)(2,1)S(1)}, u32[]{:S(2)}, u32[]{:S(2)}) collective-permute-start(bf16[8,64,128]{2,1,0:T(8,128)(2,1)S(1)} %get-tuple-element.19.s_ref), channel_id=1, source_target_pairs={{0,2},{1,3},{2,4},{3,5},{4,6},{5,7},{8,10},{9,11},{10,12},{11,13},... | collective-permute-start | bytes 393224 | tf_op jit(solution)/shard_map/ppermute | solution.py:299
  46.5 1.0 copy-start.1
  69.0 3.2 %collective-permute-start.16 = (bf16[2,64,576]{2,1,0:T(8,128)(2,1)S(1)}, bf16[2,64,576]{2,1,0:T(8,128)(2,1)S(1)}, u32[]{:S(2)}, u32[]{:S(2)}) collective-permute-start(bf16[2,64,576]{2,1,0:T(8,128)(2,1)S(1)} %select_convert_fusion), channel_id=1, source_target_pairs={{0,2},{2,0},{4,6},{6,4},{1,3},{3,1},{5,7},{7,5},{8,10},{10,8},{12,... | collective-permute-start | bytes 442376 | tf_op jit(solution)/shard_map/ppermute | solution.py:332
  72.2 7.3 %collective-permute-start.17 = (bf16[2,64,576]{2,1,0:T(8,128)(2,1)S(1)}, bf16[2,64,576]{2,1,0:T(8,128)(2,1)S(1)}, u32[]{:S(2)}, u32[]{:S(2)}) collective-permute-start(bf16[2,64,576]{2,1,0:T(8,128)(2,1)S(1)} %add_convert_fusion.2), channel_id=1, source_target_pairs={{0,4},{2,6},{4,0},{6,2},{1,5},{3,7},{5,1},{7,3},{8,12},{10,14},{12... | collective-permute-start | bytes 442376 | tf_op jit(solution)/shard_map/ppermute | solution.py:336
  75.0 6.2 %collective-permute-start.13 = (bf16[8,64,128]{2,1,0:T(8,128)(2,1)S(1)}, bf16[8,64,128]{2,1,0:T(8,128)(2,1)S(1)}, u32[]{:S(2)}, u32[]{:S(2)}) collective-permute-start(bf16[8,64,128]{2,1,0:T(8,128)(2,1)S(1)} %get-tuple-element.22), channel_id=1, source_target_pairs={{24,16},{25,17},{26,18},{27,19},{28,20},{29,21},{30,22},{31,23}} | collective-permute-start | bytes 393224 | tf_op jit(solution)/shard_map/ppermute | solution.py:402
  79.5 5.8 %collective-permute-start.18 = (bf16[2,64,576]{2,1,0:T(8,128)(2,1)S(1)}, bf16[2,64,576]{2,1,0:T(8,128)(2,1)S(1)}, u32[]{:S(2)}, u32[]{:S(2)}) collective-permute-start(bf16[2,64,576]{2,1,0:T(8,128)(2,1)S(1)} %add_convert_fusion.1), channel_id=1, source_target_pairs={{0,1},{1,0},{2,3},{3,2},{4,5},{5,4},{6,7},{7,6},{8,9},{9,8},{10,11... | collective-permute-start | bytes 442376 | tf_op jit(solution)/shard_map/ppermute | solution.py:336
  81.5 4.0 %collective-permute-start.14 = (bf16[8,64,128]{2,1,0:T(8,128)(2,1)S(1)}, bf16[8,64,128]{2,1,0:T(8,128)(2,1)S(1)}, u32[]{:S(2)}, u32[]{:S(2)}) collective-permute-start(bf16[8,64,128]{2,1,0:T(8,128)(2,1)S(1)} %shard_map.64), channel_id=1, source_target_pairs={{16,8},{17,9},{18,10},{19,11},{20,12},{21,13},{22,14},{23,15}} | collective-permute-start | bytes 393224 | tf_op jit(solution)/shard_map/ppermute | solution.py:402
  85.4 17.0 %collective-permute-start.19 = (bf16[2,64,576]{2,1,0:T(8,128)(2,1)S(1)}, bf16[2,64,576]{2,1,0:T(8,128)(2,1)S(1)}, u32[]{:S(2)}, u32[]{:S(2)}) collective-permute-start(bf16[2,64,576]{2,1,0:T(8,128)(2,1)S(1)} %add_convert_fusion), channel_id=1, source_target_pairs={{0,2},{2,0},{4,6},{6,4},{1,3},{3,1},{5,7},{7,5},{8,10},{10,8},{12,... | collective-permute-start | bytes 442376 | tf_op jit(solution)/shard_map/ppermute | solution.py:347
  85.7 15.8 %collective-permute-start.15 = (bf16[8,64,128]{2,1,0:T(8,128)(2,1)S(1)}, bf16[8,64,128]{2,1,0:T(8,128)(2,1)S(1)}, u32[]{:S(2)}, u32[]{:S(2)}) collective-permute-start(bf16[8,64,128]{2,1,0:T(8,128)(2,1)S(1)} %shard_map.65), channel_id=1, source_target_pairs={{8,0},{9,1},{10,2},{11,3},{12,4},{13,5},{14,6},{15,7}} | collective-permute-start | bytes 393224 | tf_op jit(solution)/shard_map/ppermute | solution.py:402

commit v2 on v1

--- a/solution.py
+++ b/solution.py
@@ -103,13 +103,22 @@
         )
 
 
-def layer_rows(low, high, body):
-    def two(turn, carry):
-        body(low + 2 * turn)
-        body(low + 2 * turn + 1)
+def row_blocks(low, high, body, size=4):
+    turns, rest = divmod(high - low, size)
+
+    def turn(number, carry):
+        body(low + size * number, size)
         return carry
 
-    lax.fori_loop(0, (high - low) // 2, two, 0)
+    if turns > 0:
+        lax.fori_loop(0, turns, turn, 0)
+    if rest > 0:
+        body(low + size * turns, rest)
+
+
+def convolved_rows(weights, ref, first, count):
+    slab = ref[pl.ds(first - 1, count + 2)]
+    return [convolved(weights, slab[place : place + 3]) for place in range(count)]
 
 
 def row_flag(index, halo, rows, up, down):
@@ -117,7 +126,7 @@
 
 
 def first_body(
-    c_ref, above_ref, below_ref, left_ref, right_ref, w_ref, f_ref, fb_ref, x_ref, a_ref,
+    c_ref, above_ref, below_ref, left_ref, right_ref, w_ref, f_ref, fb_ref, x_ref, a_ref, a2_ref,
     *, channels, rows, depth,
 ):
     cols = c_ref.shape[1]
@@ -128,8 +137,8 @@
     def put(index, own, beyond):
         x_ref[index, :, :cols] = own
         x_ref[index, :, cols:] = beyond
-        a_ref[0, index, :, :cols] = own.astype(bf16)
-        a_ref[0, index, :, cols:] = beyond.astype(bf16)
+        a_ref[index, :, :cols] = own.astype(bf16)
+        a_ref[index, :, cols:] = beyond.astype(bf16)
 
     joined = [join_edges(left_ref[j], right_ref[j], left, right) for j in range(3)]
     for row in range(rows):
@@ -140,16 +149,20 @@
 
     total = rows + 2 * halo
     for layer in range(depth):
-        now, later = layer % 2, (layer + 1) % 2
-
-        def step(index, layer=layer, now=now, later=later):
-            z = convolved(w_ref[layer], a_ref[now, pl.ds(index - 1, 3)])
-            gain = mask * (step_size * row_flag(index, halo, rows, up, down))
-            x = x_ref[index] + gain * jnp.tanh(z)
-            x_ref[index] = x
-            a_ref[later, index] = x.astype(bf16)
-
-        layer_rows(layer + 1, total - layer - 1, step)
+        now, later = (a_ref, a2_ref) if layer % 2 == 0 else (a2_ref, a_ref)
+
+        def step(first, count, layer=layer, now=now, later=later):
+            states = x_ref[pl.ds(first, count)]
+            done = []
+            for place, z in enumerate(convolved_rows(w_ref[layer], now, first, count)):
+                gain = mask * (step_size * row_flag(first + place, halo, rows, up, down))
+                done.append(states[place] + gain * jnp.tanh(z))
+            for place, x in enumerate(done):
+                x_ref[first + place] = x
+                if layer < depth - 1:
+                    later[first + place] = x.astype(bf16)
+
+        row_blocks(layer + 1, total - layer - 1, step)
     for row in range(rows):
         value = x_ref[halo + row, :, :cols]
         f_ref[row] = value
@@ -182,7 +195,7 @@
     c_ref, q_ref, s_ref, s_above_ref, s_below_ref, s_left_ref, s_right_ref,
     q_above_ref, q_below_ref, q_left_ref, q_right_ref, w_ref, wt_ref,
     state_ref, g_ref, gb_ref, grad_ref,
-    x_ref, a_ref, keep_ref, slope_ref, adj_ref, src_ref,
+    x_ref, a_ref, a2_ref, keep_ref, slope_ref, adj_ref, src_ref,
     *, channels, rows, depth,
 ):
     cols = c_ref.shape[1]
@@ -195,8 +208,8 @@
     def put(index, own, beyond):
         x_ref[index, :, :cols] = own
         x_ref[index, :, cols:] = beyond
-        a_ref[0, index, :, :cols] = own.astype(bf16)
-        a_ref[0, index, :, cols:] = beyond.astype(bf16)
+        a_ref[index, :, :cols] = own.astype(bf16)
+        a_ref[index, :, cols:] = beyond.astype(bf16)
 
     joined = [join_edges(s_left_ref[j], s_right_ref[j], left, right) for j in range(3)]
     for row in range(rows):
@@ -232,33 +245,40 @@
             ).astype(bf16)
 
     for layer in range(depth):
-        now, later = layer % 2, (layer + 1) % 2
+        now, later = (a_ref, a2_ref) if layer % 2 == 0 else (a2_ref, a_ref)
         keep(layer)
 
-        def step(index, layer=layer, now=now, later=later):
-            z = convolved(w_ref[layer], a_ref[now, pl.ds(index - 1, 3)])
-            gain = mask * (step_size * row_flag(index, halo, rows, up, down))
-            t = jnp.tanh(z)
-            slope_ref[layer, index] = gain * (1.0 - t * t)
-            if layer < depth - 1:
-                x = x_ref[index] + gain * t
-                x_ref[index] = x
-                a_ref[later, index] = x.astype(bf16)
-
-        layer_rows(layer + 1, total - layer - 1, step)
+        def step(first, count, layer=layer, now=now, later=later):
+            states = x_ref[pl.ds(first, count)]
+            done = []
+            for place, z in enumerate(convolved_rows(w_ref[layer], now, first, count)):
+                gain = mask * (step_size * row_flag(first + place, halo, rows, up, down))
+                t = jnp.tanh(z)
+                done.append((gain * (1.0 - t * t), states[place] + gain * t))
+            for place, (slope, x) in enumerate(done):
+                slope_ref[layer, first + place] = slope
+                if layer < depth - 1:
+                    x_ref[first + place] = x
+                    later[first + place] = x.astype(bf16)
+
+        row_blocks(layer + 1, total - layer - 1, step)
 
     for layer in reversed(range(depth)):
         reach = layer + 1
 
-        def source(index, layer=layer):
-            src_ref[index] = (adj_ref[index] * slope_ref[layer, index]).astype(bf16)
-
-        layer_rows(halo - reach, halo + rows + reach, source)
-
-        def back(index, layer=layer):
-            adj_ref[index] += convolved(wt_ref[layer], src_ref[pl.ds(index - 1, 3)])
-
-        layer_rows(halo - layer, halo + rows + layer, back)
+        def source(first, count, layer=layer):
+            part = pl.ds(first, count)
+            src_ref[part] = (adj_ref[part] * slope_ref[layer, part]).astype(bf16)
+
+        row_blocks(halo - reach, halo + rows + reach, source, 2)
+
+        def back(first, count, layer=layer):
+            adjoints = adj_ref[pl.ds(first, count)]
+            moved = convolved_rows(wt_ref[layer], src_ref, first, count)
+            for place in range(count):
+                adj_ref[first + place] = adjoints[place] + moved[place]
+
+        row_blocks(halo - layer, halo + rows + layer, back)
         stacked = jnp.concatenate(
             [
                 src_ref[pl.ds(halo + row - 1, 3)].reshape(3 * channels, 2 * cols)[:, :cols]
@@ -326,10 +346,10 @@
     depth = grads.shape[0]
     half = depth // 2
     odd = lax.axis_index("row") % 2 == 1
-    sent = jnp.where(odd, grads[:half], grads[half:]).astype(bf16)
+    sent = jnp.where(odd, grads[:half], grads[half:])
     own = jnp.where(odd, grads[half:], grads[:half])
     pair = [(r, r ^ 1) for r in range(rows)]
-    value = own + lax.ppermute(sent, "row", pair).astype(f32)
+    value = own + lax.ppermute(sent, "row", pair)
 
     def add(value, axis, pairs):
         rounded = value.astype(bf16)
@@ -343,11 +363,10 @@
     while bit < cols:
         value = add(value, "col", [(c, c ^ bit) for c in range(cols)])
         bit *= 2
-    rounded = value.astype(bf16)
-    other = lax.ppermute(rounded, "row", pair)
-    first = jnp.where(odd, other, rounded)
-    second = jnp.where(odd, rounded, other)
-    return jnp.concatenate([first, second], 0).astype(f32)
+    other = lax.ppermute(value, "row", pair)
+    first = jnp.where(odd, other, value)
+    second = jnp.where(odd, value, other)
+    return jnp.concatenate([first, second], 0)
 
 
 def local(c_states, c_adjoints, weights):
@@ -391,7 +410,8 @@
         (tile_f, tile_b),
         [
             pltpu.VMEM((total, channels, lanes), f32),
-            pltpu.VMEM((2, total, channels, lanes), bf16),
+            pltpu.VMEM((total, channels, lanes), bf16),
+            pltpu.VMEM((total, channels, lanes), bf16),
         ],
         flops=mac * 44,
     )(c_flat, above[:depth], below[:depth], left[:, 0], right[:, 0], w_fwd)
@@ -402,7 +422,7 @@
             arrived = lax.ppermute(sending, "layer", [(source, goal)])
             arrivals.append(arrived)
             if place < len(order) - 1:
-                sending = call(functools.partial(hop_body, **sizes), tile_b)(
+                sending = call(functools.partial(hop_body, **sizes), tile_b, flops=10**10)(
                     arrived, base, target, matrix
                 )
         return arrivals
@@ -427,7 +447,8 @@
         ),
         [
             pltpu.VMEM((total, channels, lanes), f32),
-            pltpu.VMEM((2, total, channels, lanes), bf16),
+            pltpu.VMEM((total, channels, lanes), bf16),
+            pltpu.VMEM((total, channels, lanes), bf16),
             pltpu.VMEM((depth, 3 * channels, rows * cols), bf16),
             pltpu.VMEM((depth, total, channels, lanes), f32),
             pltpu.VMEM((total, channels, lanes), f32),
@@ -443,7 +464,7 @@
     )
     weight_grads = total_over_tiles(grads)
     adjoint = call(
-        functools.partial(last_body, **sizes), jax.ShapeDtypeStruct(flat, f32)
+        functools.partial(last_body, **sizes), jax.ShapeDtypeStruct(flat, f32), flops=10**10
     )(q_flat, *returned)
     return state.reshape(c_states.shape), adjoint.reshape(c_states.shape), weight_grads
 

time: 104 us -> 90.8 us (0.87)
  the two profiles are of different devices: /device:TPU:0 before, /device:TPU:2 now
where the time goes in v2:
time: 90.8 us; the launch traced here: 90.4 us
  starting transfers between devices  33.5 us (37%)
  waiting for transfers between devices  29.2 us (32%)
  Pallas kernels  20.9 us (23%)
  local copies, waits for them, and re-layouts  4.37 us (5%)
  other arithmetic  1.27 us (1%)
  between operations  1.08 us (1%)
    ppermute x6, waiting for transfers between devices, chain(): arrived = lax.ppermute(sending, 'layer', [(source, goal)])  16.5 us
    pallas_call x1, Pallas kernels, local(): call(functools.partial(second_body, depth=depth, **sizes), (jax.ShapeDtyp...  14.1 us
    ppermute x6, starting transfers between devices, swapped(): return lax.ppermute(array, ('row', 'col'), pairs)  13.2 us
    ppermute x4, starting transfers between devices, shifted(): return lax.ppermute(array, ('row', 'col'), pairs)  11.1 us
    ppermute x2, waiting for transfers between devices, add(): return rounded.astype(f32) + lax.ppermute(rounded, axis, pairs).astype(f32)  7.59 us
    ppermute x6, starting transfers between devices, chain(): arrived = lax.ppermute(sending, 'layer', [(source, goal)])  7.45 us
    pallas_call x1, Pallas kernels, local(): call(functools.partial(first_body, depth=depth, **sizes), (tile_f, tile_b...  4.62 us
    ppermute x4, waiting for transfers between devices, shifted(): return lax.ppermute(array, ('row', 'col'), pairs)  4.24 us
  transfers between devices with their start and end apart: 20, of which 7 were waited for; matrix products, arithmetic and copies ran while one was open for 3% of the time, Pallas kernels for 1%

profile of v2, /device:TPU:2, one launch (start us, length us, event | category | flops | bytes accessed | tf_op | source)
XLA Modules:
  0.0 90.4 jit_solution(17818188635870458419)
XLA Ops:
  0.6 0.9 %copy-done = f32[1,64,8,128]{3,2,1,0:T(8,128)S(1)} copy-done((f32[1,64,8,128]{3,2,1,0:T(8,128)S(1)}, f32[1,64,8,128]{3,2,1,0:T(8,128)}, u32[]{:S(2)}) %copy-start) | copy-done | bytes 262168
  1.6 0.9 %copy-done.2 = f32[1,64,8,128]{3,2,1,0:T(8,128)S(1)} copy-done((f32[1,64,8,128]{3,2,1,0:T(8,128)S(1)}, f32[1,64,8,128]{3,2,1,0:T(8,128)}, u32[]{:S(2)}) %copy-start.2) | copy-done | bytes 262168
  2.7 2.8 %collective-permute-start.4 = (bf16[2,64,128]{2,1,0:T(8,128)(2,1)S(1)}, bf16[2,64,128]{2,1,0:T(8,128)(2,1)S(1)}, u32[]{:S(2)}, u32[]{:S(2)}) collective-permute-start(bf16[2,64,128]{2,1,0:T(8,128)(2,1)S(1)} %get-tuple-element.16), channel_id=1, source_target_pairs={{2,1},{3,0},{4,3},{5,2},{6,5},{7,4},{10,9},{11,8},{12,11},{13,10},... | collective-permute-start | bytes 98312 | tf_op jit(solution)/shard_map/ppermute | solution.py:330
  5.5 0.7 collective-permute-start.3
  6.2 3.3 %collective-permute-start.2 = (bf16[2,64,128]{2,1,0:T(8,128)(2,1)S(1)}, bf16[2,64,128]{2,1,0:T(8,128)(2,1)S(1)}, u32[]{:S(2)}, u32[]{:S(2)}) collective-permute-start(bf16[2,64,128]{2,1,0:T(8,128)(2,1)S(1)} %get-tuple-element.16), channel_id=1, source_target_pairs={{0,3},{1,2},{2,5},{3,4},{4,7},{5,6},{8,11},{9,10},{10,13},{11,12},... | collective-permute-start | bytes 98312 | tf_op jit(solution)/shard_map/ppermute | solution.py:330
  9.6 1.9 %collective-permute-start = (bf16[8,64,128]{2,1,0:T(8,128)(2,1)S(1)}, bf16[8,64,128]{2,1,0:T(8,128)(2,1)S(1)}, u32[]{:S(2)}, u32[]{:S(2)}) collective-permute-start(bf16[8,64,128]{2,1,0:T(8,128)(2,1)S(1)} %get-tuple-element.14), channel_id=1, source_target_pairs={{0,2},{1,3},{2,4},{3,5},{4,6},{5,7},{8,10},{9,11},{10,12},{11,13},... | collective-permute-start | bytes 393224 | tf_op jit(solution)/shard_map/ppermute | solution.py:319
  11.5 3.6 %collective-permute-start.1 = (bf16[8,64,128]{2,1,0:T(8,128)(2,1)S(1)}, bf16[8,64,128]{2,1,0:T(8,128)(2,1)S(1)}, u32[]{:S(2)}, u32[]{:S(2)}) collective-permute-start(bf16[8,64,128]{2,1,0:T(8,128)(2,1)S(1)} %get-tuple-element.15), channel_id=1, source_target_pairs={{2,0},{3,1},{4,2},{5,3},{6,4},{7,5},{10,8},{11,9},{12,10},{13,11},... | collective-permute-start | bytes 393224 | tf_op jit(solution)/shard_map/ppermute | solution.py:319
  15.5 0.6 copy.11
  16.7 1.0 %collective-permute-done.1 = bf16[8,64,128]{2,1,0:T(8,128)(2,1)S(1)} collective-permute-done((bf16[8,64,128]{2,1,0:T(8,128)(2,1)S(1)}, bf16[8,64,128]{2,1,0:T(8,128)(2,1)S(1)}, u32[]{:S(2)}, u32[]{:S(2)}) %collective-permute-start.1) | collective-permute-done | bytes 131104 | tf_op jit(solution)/shard_map/ppermute | solution.py:319
  17.7 4.6 %shard_map.59 = (f32[8,64,128]{2,1,0:T(8,128)S(1)}, bf16[8,64,128]{2,1,0:T(8,128)(2,1)S(1)}) custom-call(f32[512,128]{1,0:T(8,128)S(1)} %bitcast.31, bf16[4,64,128]{2,1,0:T(8,128)(2,1)S(1)} %get-tuple-element.30.above_ref, bf16[4,64,128]{2,1,0:T(8,128)(2,1)S(1)} %get-tuple-element.28.below_ref, bf16[3,64,128]{2,1,0:T(8,128)(2,1)S(1)} %get-tuple-element.32.left_ref.right_ref, ...), custom_call_target="tpu_custom_call" | custom-call | flops 830472192 | tf_op jit(solution)/shard_map/pallas_call | solution.py:408
  22.3 3.5 %collective-permute-start.5 = (bf16[8,64,128]{2,1,0:T(8,128)(2,1)S(1)}, bf16[8,64,128]{2,1,0:T(8,128)(2,1)S(1)}, u32[]{:S(2)}, u32[]{:S(2)}) collective-permute-start(bf16[8,64,128]{2,1,0:T(8,128)(2,1)S(1)} %get-tuple-element.17), channel_id=1, source_target_pairs={{0,8},{1,9},{2,10},{3,11},{4,12},{5,13},{6,14},{7,15}} | collective-permute-start | bytes 393224 | tf_op jit(solution)/shard_map/ppermute | solution.py:422
  25.9 2.4 %collective-permute-done.5.s_ref.refs_1_ = bf16[8,64,128]{2,1,0:T(8,128)(2,1)S(1)} collective-permute-done((bf16[8,64,128]{2,1,0:T(8,128)(2,1)S(1)}, bf16[8,64,128]{2,1,0:T(8,128)(2,1)S(1)}, u32[]{:S(2)}, u32[]{:S(2)}) %collective-permute-start.5) | collective-permute-done | bytes 131104 | tf_op jit(solution)/shard_map/ppermute | solution.py:422
  28.6 0.7 collective-permute-start.6
  29.5 0.7 collective-permute-start.7
  30.4 2.9 %collective-permute-start.12 = (bf16[1,64,128]{2,1,0:T(8,128)(2,1)S(1)}, bf16[1,64,128]{2,1,0:T(8,128)(2,1)S(1)}, u32[]{:S(2)}, u32[]{:S(2)}) collective-permute-start(bf16[1,64,128]{2,1,0:T(8,128)(2,1)S(1)} %get-tuple-element.20), channel_id=1, source_target_pairs={{2,1},{3,0},{4,3},{5,2},{6,5},{7,4},{10,9},{11,8},{12,11},{13,10},... | collective-permute-start | bytes 49160 | tf_op jit(solution)/shard_map/ppermute | solution.py:330
  33.2 1.6 %collective-permute-start.11 = (bf16[1,64,128]{2,1,0:T(8,128)(2,1)S(1)}, bf16[1,64,128]{2,1,0:T(8,128)(2,1)S(1)}, u32[]{:S(2)}, u32[]{:S(2)}) collective-permute-start(bf16[1,64,128]{2,1,0:T(8,128)(2,1)S(1)} %get-tuple-element.20), channel_id=1, source_target_pairs={{0,1},{1,0},{2,3},{3,2},{4,5},{5,4},{6,7},{7,6},{8,9},{9,8},{10,11... | collective-permute-start | bytes 49160 | tf_op jit(solution)/shard_map/ppermute | solution.py:330
  34.8 1.9 %collective-permute-start.10 = (bf16[1,64,128]{2,1,0:T(8,128)(2,1)S(1)}, bf16[1,64,128]{2,1,0:T(8,128)(2,1)S(1)}, u32[]{:S(2)}, u32[]{:S(2)}) collective-permute-start(bf16[1,64,128]{2,1,0:T(8,128)(2,1)S(1)} %get-tuple-element.20), channel_id=1, source_target_pairs={{0,3},{1,2},{2,5},{3,4},{4,7},{5,6},{8,11},{9,10},{10,13},{11,12},... | collective-permute-start | bytes 49160 | tf_op jit(solution)/shard_map/ppermute | solution.py:330
  36.7 3.6 %collective-permute-start.9 = (bf16[8,64,128]{2,1,0:T(8,128)(2,1)S(1)}, bf16[8,64,128]{2,1,0:T(8,128)(2,1)S(1)}, u32[]{:S(2)}, u32[]{:S(2)}) collective-permute-start(bf16[8,64,128]{2,1,0:T(8,128)(2,1)S(1)} %get-tuple-element.19.s_ref), channel_id=1, source_target_pairs={{2,0},{3,1},{4,2},{5,3},{6,4},{7,5},{10,8},{11,9},{12,10},{13,11},... | collective-permute-start | bytes 393224 | tf_op jit(solution)/shard_map/ppermute | solution.py:319
  40.3 1.9 %collective-permute-start.8 = (bf16[8,64,128]{2,1,0:T(8,128)(2,1)S(1)}, bf16[8,64,128]{2,1,0:T(8,128)(2,1)S(1)}, u32[]{:S(2)}, u32[]{:S(2)}) collective-permute-start(bf16[8,64,128]{2,1,0:T(8,128)(2,1)S(1)} %get-tuple-element.19.s_ref), channel_id=1, source_target_pairs={{0,2},{1,3},{2,4},{3,5},{4,6},{5,7},{8,10},{9,11},{10,12},{11,13},... | collective-permute-start | bytes 393224 | tf_op jit(solution)/shard_map/ppermute | solution.py:319
  42.3 0.5 copy.15
  43.4 3.3 %collective-permute-done.8.s_above_ref = bf16[8,64,128]{2,1,0:T(8,128)(2,1)S(1)} collective-permute-done((bf16[8,64,128]{2,1,0:T(8,128)(2,1)S(1)}, bf16[8,64,128]{2,1,0:T(8,128)(2,1)S(1)}, u32[]{:S(2)}, u32[]{:S(2)}) %collective-permute-start.8) | collective-permute-done | bytes 131104 | tf_op jit(solution)/shard_map/ppermute | solution.py:319
  46.6 14.1 %shard_map.63 = (f32[512,128]{1,0:T(8,128)}, f32[8,64,128]{2,1,0:T(8,128)S(1)}, bf16[8,64,128]{2,1,0:T(8,128)(2,1)S(1)}, f32[4,64,576]{2,1,0:T(8,128)S(1)}) custom-call(f32[512,128]{1,0:T(8,128)S(1)} %bitcast.35, f32[512,128]{1,0:T(8,128)S(1)} %bitcast.37, bf16[8,64,128]{2,1,0:T(8,128)(2,1)S(1)} %get-tuple-element.19.s_ref, ...), custom_call_target="tpu_custom_call" | custom-call | flops 2566914048 | tf_op jit(solution)/shard_map/pallas_call | solution.py:440
  60.9 0.7 collective-permute-start.13
  61.6 0.8 collective-permute-done.16
  62.9 0.7 collective-permute-start.14
  63.5 5.3 %collective-permute-done.17 = bf16[2,64,576]{2,1,0:T(8,128)(2,1)S(1)} collective-permute-done((bf16[2,64,576]{2,1,0:T(8,128)(2,1)S(1)}, bf16[2,64,576]{2,1,0:T(8,128)(2,1)S(1)}, u32[]{:S(2)}, u32[]{:S(2)}) %collective-permute-start.17) | collective-permute-done | bytes 147488 | tf_op jit(solution)/shard_map/ppermute | solution.py:356
  68.9 1.6 %collective-permute-start.18 = (bf16[2,64,576]{2,1,0:T(8,128)(2,1)S(1)}, bf16[2,64,576]{2,1,0:T(8,128)(2,1)S(1)}, u32[]{:S(2)}, u32[]{:S(2)}) collective-permute-start(bf16[2,64,576]{2,1,0:T(8,128)(2,1)S(1)} %add_convert_fusion), channel_id=1, source_target_pairs={{0,1},{1,0},{2,3},{3,2},{4,5},{5,4},{6,7},{7,6},{8,9},{9,8},{10,11... | collective-permute-start | bytes 442376 | tf_op jit(solution)/shard_map/ppermute | solution.py:356
  70.7 1.3 %collective-permute-start.15 = (bf16[8,64,128]{2,1,0:T(8,128)(2,1)S(1)}, bf16[8,64,128]{2,1,0:T(8,128)(2,1)S(1)}, u32[]{:S(2)}, u32[]{:S(2)}) collective-permute-start(bf16[8,64,128]{2,1,0:T(8,128)(2,1)S(1)} %shard_map.65), channel_id=1, source_target_pairs={{8,0},{9,1},{10,2},{11,3},{12,4},{13,5},{14,6},{15,7}} | collective-permute-start | bytes 393224 | tf_op jit(solution)/shard_map/ppermute | solution.py:422
  72.0 2.3 %collective-permute-done.18 = bf16[2,64,576]{2,1,0:T(8,128)(2,1)S(1)} collective-permute-done((bf16[2,64,576]{2,1,0:T(8,128)(2,1)S(1)}, bf16[2,64,576]{2,1,0:T(8,128)(2,1)S(1)}, u32[]{:S(2)}, u32[]{:S(2)}) %collective-permute-start.18) | collective-permute-done | bytes 147488 | tf_op jit(solution)/shard_map/ppermute | solution.py:356
  74.4 14.2 %collective-permute-done.15.refs_3_ = bf16[8,64,128]{2,1,0:T(8,128)(2,1)S(1)} collective-permute-done((bf16[8,64,128]{2,1,0:T(8,128)(2,1)S(1)}, bf16[8,64,128]{2,1,0:T(8,128)(2,1)S(1)}, u32[]{:S(2)}, u32[]{:S(2)}) %collective-permute-start.15) | collective-permute-done | bytes 131104 | tf_op jit(solution)/shard_map/ppermute | solution.py:422
  88.6 0.8 shard_map.66
  89.5 0.9 pad_maximum_fusion
  (51 shorter events, 3.4 us)
Async XLA Ops:
  0.6 1.0 %copy-start = (f32[1,64,8,128]{3,2,1,0:T(8,128)S(1)}, f32[1,64,8,128]{3,2,1,0:T(8,128)}, u32[]{:S(2)}) copy-start(f32[1,64,8,128]{3,2,1,0:T(8,128)} %param.3) | copy-start | bytes 786436
  1.6 0.9 %copy-start.2 = (f32[1,64,8,128]{3,2,1,0:T(8,128)S(1)}, f32[1,64,8,128]{3,2,1,0:T(8,128)}, u32[]{:S(2)}) copy-start(f32[1,64,8,128]{3,2,1,0:T(8,128)} %param.4) | copy-start | bytes 786436
  2.5 12.6 %copy-start.4 = (bf16[4,64,576]{2,1,0:T(8,128)(2,1)S(1)}, bf16[4,64,576]{2,1,0:T(8,128)(2,1)}, u32[]{:S(2)}) copy-start(bf16[4,64,576]{2,1,0:T(8,128)(2,1)} %param.5) | copy-start | bytes 884740
  2.7 13.9 %collective-permute-start.4 = (bf16[2,64,128]{2,1,0:T(8,128)(2,1)S(1)}, bf16[2,64,128]{2,1,0:T(8,128)(2,1)S(1)}, u32[]{:S(2)}, u32[]{:S(2)}) collective-permute-start(bf16[2,64,128]{2,1,0:T(8,128)(2,1)S(1)} %get-tuple-element.16), channel_id=1, source_target_pairs={{2,1},{3,0},{4,3},{5,2},{6,5},{7,4},{10,9},{11,8},{12,11},{13,10},... | collective-permute-start | bytes 98312 | tf_op jit(solution)/shard_map/ppermute | solution.py:330
  5.5 11.0 %collective-permute-start.3 = (bf16[2,64,128]{2,1,0:T(8,128)(2,1)S(1)}, bf16[2,64,128]{2,1,0:T(8,128)(2,1)S(1)}, u32[]{:S(2)}, u32[]{:S(2)}) collective-permute-start(bf16[2,64,128]{2,1,0:T(8,128)(2,1)S(1)} %get-tuple-element.16), channel_id=1, source_target_pairs={{0,1},{1,0},{2,3},{3,2},{4,5},{5,4},{6,7},{7,6},{8,9},{9,8},{10,11... | collective-permute-start | bytes 98312 | tf_op jit(solution)/shard_map/ppermute | solution.py:330
  6.2 10.4 %collective-permute-start.2 = (bf16[2,64,128]{2,1,0:T(8,128)(2,1)S(1)}, bf16[2,64,128]{2,1,0:T(8,128)(2,1)S(1)}, u32[]{:S(2)}, u32[]{:S(2)}) collective-permute-start(bf16[2,64,128]{2,1,0:T(8,128)(2,1)S(1)} %get-tuple-element.16), channel_id=1, source_target_pairs={{0,3},{1,2},{2,5},{3,4},{4,7},{5,6},{8,11},{9,10},{10,13},{11,12},... | collective-permute-start | bytes 98312 | tf_op jit(solution)/shard_map/ppermute | solution.py:330
  9.6 7.1 %collective-permute-start = (bf16[8,64,128]{2,1,0:T(8,128)(2,1)S(1)}, bf16[8,64,128]{2,1,0:T(8,128)(2,1)S(1)}, u32[]{:S(2)}, u32[]{:S(2)}) collective-permute-start(bf16[8,64,128]{2,1,0:T(8,128)(2,1)S(1)} %get-tuple-element.14), channel_id=1, source_target_pairs={{0,2},{1,3},{2,4},{3,5},{4,6},{5,7},{8,10},{9,11},{10,12},{11,13},... | collective-permute-start | bytes 393224 | tf_op jit(solution)/shard_map/ppermute | solution.py:319
  11.5 6.1 %collective-permute-start.1 = (bf16[8,64,128]{2,1,0:T(8,128)(2,1)S(1)}, bf16[8,64,128]{2,1,0:T(8,128)(2,1)S(1)}, u32[]{:S(2)}, u32[]{:S(2)}) collective-permute-start(bf16[8,64,128]{2,1,0:T(8,128)(2,1)S(1)} %get-tuple-element.15), channel_id=1, source_target_pairs={{2,0},{3,1},{4,2},{5,3},{6,4},{7,5},{10,8},{11,9},{12,10},{13,11},... | collective-permute-start | bytes 393224 | tf_op jit(solution)/shard_map/ppermute | solution.py:319
  16.6 1.0 %copy-start.1 = (f32[1,64,8,128]{3,2,1,0:T(8,128)S(1)}, f32[1,64,8,128]{3,2,1,0:T(8,128)}, u32[]{:S(2)}) copy-start(f32[1,64,8,128]{3,2,1,0:T(8,128)} %param.3) | copy-start | bytes 786436
  22.3 6.0 %collective-permute-start.5 = (bf16[8,64,128]{2,1,0:T(8,128)(2,1)S(1)}, bf16[8,64,128]{2,1,0:T(8,128)(2,1)S(1)}, u32[]{:S(2)}, u32[]{:S(2)}) collective-permute-start(bf16[8,64,128]{2,1,0:T(8,128)(2,1)S(1)} %get-tuple-element.17), channel_id=1, source_target_pairs={{0,8},{1,9},{2,10},{3,11},{4,12},{5,13},{6,14},{7,15}} | collective-permute-start | bytes 393224 | tf_op jit(solution)/shard_map/ppermute | solution.py:422
  28.6 0.7 collective-permute-start.6
  29.5 0.7 collective-permute-start.7
  30.4 12.9 %collective-permute-start.12 = (bf16[1,64,128]{2,1,0:T(8,128)(2,1)S(1)}, bf16[1,64,128]{2,1,0:T(8,128)(2,1)S(1)}, u32[]{:S(2)}, u32[]{:S(2)}) collective-permute-start(bf16[1,64,128]{2,1,0:T(8,128)(2,1)S(1)} %get-tuple-element.20), channel_id=1, source_target_pairs={{2,1},{3,0},{4,3},{5,2},{6,5},{7,4},{10,9},{11,8},{12,11},{13,10},... | collective-permute-start | bytes 49160 | tf_op jit(solution)/shard_map/ppermute | solution.py:330
  33.2 10.1 %collective-permute-start.11 = (bf16[1,64,128]{2,1,0:T(8,128)(2,1)S(1)}, bf16[1,64,128]{2,1,0:T(8,128)(2,1)S(1)}, u32[]{:S(2)}, u32[]{:S(2)}) collective-permute-start(bf16[1,64,128]{2,1,0:T(8,128)(2,1)S(1)} %get-tuple-element.20), channel_id=1, source_target_pairs={{0,1},{1,0},{2,3},{3,2},{4,5},{5,4},{6,7},{7,6},{8,9},{9,8},{10,11... | collective-permute-start | bytes 49160 | tf_op jit(solution)/shard_map/ppermute | solution.py:330
  34.8 8.5 %collective-permute-start.10 = (bf16[1,64,128]{2,1,0:T(8,128)(2,1)S(1)}, bf16[1,64,128]{2,1,0:T(8,128)(2,1)S(1)}, u32[]{:S(2)}, u32[]{:S(2)}) collective-permute-start(bf16[1,64,128]{2,1,0:T(8,128)(2,1)S(1)} %get-tuple-element.20), channel_id=1, source_target_pairs={{0,3},{1,2},{2,5},{3,4},{4,7},{5,6},{8,11},{9,10},{10,13},{11,12},... | collective-permute-start | bytes 49160 | tf_op jit(solution)/shard_map/ppermute | solution.py:330
  36.7 6.6 %collective-permute-start.9 = (bf16[8,64,128]{2,1,0:T(8,128)(2,1)S(1)}, bf16[8,64,128]{2,1,0:T(8,128)(2,1)S(1)}, u32[]{:S(2)}, u32[]{:S(2)}) collective-permute-start(bf16[8,64,128]{2,1,0:T(8,128)(2,1)S(1)} %get-tuple-element.19.s_ref), channel_id=1, source_target_pairs={{2,0},{3,1},{4,2},{5,3},{6,4},{7,5},{10,8},{11,9},{12,10},{13,11},... | collective-permute-start | bytes 393224 | tf_op jit(solution)/shard_map/ppermute | solution.py:319
  40.3 6.3 %collective-permute-start.8 = (bf16[8,64,128]{2,1,0:T(8,128)(2,1)S(1)}, bf16[8,64,128]{2,1,0:T(8,128)(2,1)S(1)}, u32[]{:S(2)}, u32[]{:S(2)}) collective-permute-start(bf16[8,64,128]{2,1,0:T(8,128)(2,1)S(1)} %get-tuple-element.19.s_ref), channel_id=1, source_target_pairs={{0,2},{1,3},{2,4},{3,5},{4,6},{5,7},{8,10},{9,11},{10,12},{11,13},... | collective-permute-start | bytes 393224 | tf_op jit(solution)/shard_map/ppermute | solution.py:319
  42.8 3.8 %copy-start.3 = (f32[1,64,8,128]{3,2,1,0:T(8,128)S(1)}, f32[1,64,8,128]{3,2,1,0:T(8,128)}, u32[]{:S(2)}) copy-start(f32[1,64,8,128]{3,2,1,0:T(8,128)} %param.4) | copy-start | bytes 786436
  60.8 1.7 %collective-permute-start.16 = (f32[2,64,576]{2,1,0:T(8,128)S(1)}, f32[2,64,576]{2,1,0:T(8,128)S(1)}, u32[]{:S(2)}, u32[]{:S(2)}) collective-permute-start(f32[2,64,576]{2,1,0:T(8,128)S(1)} %slice_select_fusion), channel_id=1, source_target_pairs={{0,2},{2,0},{4,6},{6,4},{1,3},{3,1},{5,7},{7,5},{8,10},{10,8},{12,... | collective-permute-start | bytes 884744 | tf_op jit(solution)/shard_map/ppermute | solution.py:352
  60.9 1.6 %collective-permute-start.13 = (bf16[8,64,128]{2,1,0:T(8,128)(2,1)S(1)}, bf16[8,64,128]{2,1,0:T(8,128)(2,1)S(1)}, u32[]{:S(2)}, u32[]{:S(2)}) collective-permute-start(bf16[8,64,128]{2,1,0:T(8,128)(2,1)S(1)} %get-tuple-element.22), channel_id=1, source_target_pairs={{24,16},{25,17},{26,18},{27,19},{28,20},{29,21},{30,22},{31,23}} | collective-permute-start | bytes 393224 | tf_op jit(solution)/shard_map/ppermute | solution.py:422
  62.5 6.3 %collective-permute-start.17 = (bf16[2,64,576]{2,1,0:T(8,128)(2,1)S(1)}, bf16[2,64,576]{2,1,0:T(8,128)(2,1)S(1)}, u32[]{:S(2)}, u32[]{:S(2)}) collective-permute-start(bf16[2,64,576]{2,1,0:T(8,128)(2,1)S(1)} %add_convert_fusion.1), channel_id=1, source_target_pairs={{0,4},{2,6},{4,0},{6,2},{1,5},{3,7},{5,1},{7,3},{8,12},{10,14},{12... | collective-permute-start | bytes 442376 | tf_op jit(solution)/shard_map/ppermute | solution.py:356
  62.9 7.6 %collective-permute-start.14 = (bf16[8,64,128]{2,1,0:T(8,128)(2,1)S(1)}, bf16[8,64,128]{2,1,0:T(8,128)(2,1)S(1)}, u32[]{:S(2)}, u32[]{:S(2)}) collective-permute-start(bf16[8,64,128]{2,1,0:T(8,128)(2,1)S(1)} %shard_map.64), channel_id=1, source_target_pairs={{16,8},{17,9},{18,10},{19,11},{20,12},{21,13},{22,14},{23,15}} | collective-permute-start | bytes 393224 | tf_op jit(solution)/shard_map/ppermute | solution.py:422
  68.9 5.5 %collective-permute-start.18 = (bf16[2,64,576]{2,1,0:T(8,128)(2,1)S(1)}, bf16[2,64,576]{2,1,0:T(8,128)(2,1)S(1)}, u32[]{:S(2)}, u32[]{:S(2)}) collective-permute-start(bf16[2,64,576]{2,1,0:T(8,128)(2,1)S(1)} %add_convert_fusion), channel_id=1, source_target_pairs={{0,1},{1,0},{2,3},{3,2},{4,5},{5,4},{6,7},{7,6},{8,9},{9,8},{10,11... | collective-permute-start | bytes 442376 | tf_op jit(solution)/shard_map/ppermute | solution.py:356
  70.7 17.9 %collective-permute-start.15 = (bf16[8,64,128]{2,1,0:T(8,128)(2,1)S(1)}, bf16[8,64,128]{2,1,0:T(8,128)(2,1)S(1)}, u32[]{:S(2)}, u32[]{:S(2)}) collective-permute-start(bf16[8,64,128]{2,1,0:T(8,128)(2,1)S(1)} %shard_map.65), channel_id=1, source_target_pairs={{8,0},{9,1},{10,2},{11,3},{12,4},{13,5},{14,6},{15,7}} | collective-permute-start | bytes 393224 | tf_op jit(solution)/shard_map/ppermute | solution.py:422
  74.4 15.1 %collective-permute-start.19 = (f32[2,64,576]{2,1,0:T(8,128)S(1)}, f32[2,64,576]{2,1,0:T(8,128)S(1)}, u32[]{:S(2)}, u32[]{:S(2)}) collective-permute-start(f32[2,64,576]{2,1,0:T(8,128)S(1)} %convert_add_fusion), channel_id=1, source_target_pairs={{0,2},{2,0},{4,6},{6,4},{1,3},{3,1},{5,7},{7,5},{8,10},{10,8},{12,... | collective-permute-start | bytes 884744 | tf_op jit(solution)/shard_map/ppermute | solution.py:366

commit v3 on v2

--- a/solution.py
+++ b/solution.py
@@ -8,7 +8,6 @@
 from jax.sharding import PartitionSpec as P
 
 step_size = 0.2
-EDGE = 8
 VMEM_BYTES = 40 * 1024 * 1024
 f32 = jnp.float32
 bf16 = jnp.bfloat16
@@ -34,28 +33,37 @@
     return lax.broadcasted_iota(jnp.int32, shape, 1)
 
 
-def fold_edges(rows_list):
-    shape = rows_list[0].shape
-    slot = lanes_of(shape) // (2 * EDGE)
-    total = jnp.zeros(shape, f32)
+def slots(shape, low, width, count):
+    return (lanes_of(shape) - low + width * count) // width - count
+
+
+def fold_edges(rows_list, edge, low, total):
+    doubled = total.shape[1] > rows_list[0].shape[1]
+    cols = rows_list[0].shape[1]
+    slot = slots(total.shape, low, 2 * edge, len(rows_list))
     for place, row in enumerate(rows_list):
-        turned = pltpu.roll(row, (2 * EDGE * place + EDGE) % shape[1], 1)
+        wide = jnp.concatenate([row, row], 1) if doubled else row
+        turned = pltpu.roll(wide, (low + 2 * edge * place + edge - cols) % wide.shape[1], 1)
         total = jnp.where(slot == place, turned, total)
     return total
 
 
-def join_edges(from_left, from_right, has_left, has_right):
+def join_edges(from_left, from_right, left, right, edges):
     lanes = lanes_of(from_left.shape)
-    return jnp.where(
-        lanes % (2 * EDGE) >= EDGE,
-        from_right.astype(f32) * has_right,
-        from_left.astype(f32) * has_left,
-    )
-
-
-def side_lanes(joined, place):
-    cols = joined.shape[1]
-    return pltpu.roll(joined, (cols - (2 * EDGE * place + EDGE)) % cols, 1)
+    far = jnp.zeros(lanes.shape, jnp.bool_)
+    for edge, low, high in edges:
+        inside = (lanes >= low) & (lanes < high)
+        far = far | (inside & ((lanes - low) % (2 * edge) >= edge))
+    return jnp.where(far, from_right.astype(f32) * right, from_left.astype(f32) * left)
+
+
+def side_lanes(joined, edge, low, place):
+    lanes = joined.shape[1]
+    turned = pltpu.roll(joined, (2 * lanes - (low + 2 * edge * place + edge)) % lanes, 1)
+    if lanes == 128:
+        return turned
+    front, back = turned[:, :128], turned[:, lanes - 128 :]
+    return jnp.where(lanes_of(front.shape) < 64, front, back)
 
 
 def convolved(weights, slab):
@@ -85,22 +93,41 @@
     return jnp.where(lanes < cols, 1.0, jnp.where(lanes < cols + cols // 2, right, left))
 
 
-def pack_body(c_ref, q_ref, top_ref, bottom_ref, edge_ref, *, channels, rows, depth):
+def layout(rows, depth):
+    state_edge, adjoint_edge = 3 * depth, depth
+    return (state_edge, 0), (adjoint_edge, 2 * state_edge * rows)
+
+
+def strip_body(c_ref, q_ref, edge_ref, *, channels, rows, depth):
+    total = jnp.zeros(edge_ref.shape, f32)
+    for ref, (edge, low) in zip((c_ref, q_ref), layout(rows, depth)):
+        image = [row_of(ref, row, channels, rows) for row in range(rows)]
+        total = fold_edges(image, edge, low, total)
+    edge_ref[...] = total.astype(bf16)
+
+
+def message_body(
+    c_ref, q_ref, left_ref, right_ref, top_ref, bottom_ref, side_ref, *, channels, rows, depth
+):
+    cols = c_ref.shape[1]
+    _, _, left, right = flags()
+    (c_edge, _), (q_edge, middle) = layout(rows, depth)
+    edges = ((c_edge, 0, middle), (q_edge, middle, 2 * cols))
+    side = join_edges(left_ref[...], right_ref[...], left, right, edges).astype(bf16)
+    side_ref[...] = side
     for which, ref in enumerate((c_ref, q_ref)):
-        image = [row_of(ref, row, channels, rows) for row in range(rows)]
         for row in range(depth):
-            top_ref[which * depth + row] = image[row].astype(bf16)
-            bottom_ref[which * depth + row] = image[rows - depth + row].astype(bf16)
-        edge_ref[which] = fold_edges(image).astype(bf16)
-
-
-def load_halo(dest, first, side_ref, count, halo, joined, offset):
-    for row in range(count):
-        dest(
-            first + row,
-            halo[row].astype(f32),
-            side_lanes(joined, offset + row),
-        )
+            place = which * depth + row
+            top_ref[place] = row_of(ref, row, channels, rows).astype(bf16)
+            bottom_ref[place] = row_of(ref, rows - depth + row, channels, rows).astype(bf16)
+    for half in range(2):
+        part = side[:, half * cols : (half + 1) * cols]
+        top_ref[2 * depth + half] = part
+        bottom_ref[2 * depth + half] = part
+
+
+def strips_of(ref, depth):
+    return jnp.concatenate([ref[2 * depth], ref[2 * depth + 1]], 1).astype(f32)
 
 
 def row_blocks(low, high, body, size=4):
@@ -126,7 +153,7 @@
 
 
 def first_body(
-    c_ref, above_ref, below_ref, left_ref, right_ref, w_ref, f_ref, fb_ref, x_ref, a_ref, a2_ref,
+    c_ref, above_ref, below_ref, side_ref, w_ref, f_ref, fb_ref, strip_ref, x_ref, a_ref, a2_ref,
     *, channels, rows, depth,
 ):
     cols = c_ref.shape[1]
@@ -140,12 +167,19 @@
         a_ref[index, :, :cols] = own.astype(bf16)
         a_ref[index, :, cols:] = beyond.astype(bf16)
 
-    joined = [join_edges(left_ref[j], right_ref[j], left, right) for j in range(3)]
+    (edge, low), _ = layout(rows, depth)
+    own_side = side_ref[...].astype(f32)
+    image = []
     for row in range(rows):
-        put(halo + row, row_of(c_ref, row, channels, rows), side_lanes(joined[1], row))
+        beyond = side_lanes(own_side, edge, low, row)
+        image.append(beyond)
+        put(halo + row, row_of(c_ref, row, channels, rows), beyond)
+    strip_ref[...] = fold_edges(image, 2 * depth, 0, jnp.zeros(strip_ref.shape, f32))
+    above_side, below_side = strips_of(above_ref, depth), strips_of(below_ref, depth)
     for row in range(depth):
-        put(row, above_ref[row].astype(f32), side_lanes(joined[0], rows - depth + row))
-        put(halo + rows + row, below_ref[row].astype(f32), side_lanes(joined[2], row))
+        place = rows - depth + row
+        put(row, above_ref[row].astype(f32), side_lanes(above_side, edge, low, place))
+        put(halo + rows + row, below_ref[row].astype(f32), side_lanes(below_side, edge, low, row))
 
     total = rows + 2 * halo
     for layer in range(depth):
@@ -163,15 +197,20 @@
                     later[first + place] = x.astype(bf16)
 
         row_blocks(layer + 1, total - layer - 1, step)
-    for row in range(rows):
-        value = x_ref[halo + row, :, :cols]
+    image = [x_ref[halo + row, :, cols:] for row in range(rows)]
+    values = [x_ref[halo + row, :, :cols] for row in range(rows)]
+    values.append(fold_edges(image, 2 * depth, 0, jnp.zeros(strip_ref.shape, f32)))
+    for row, value in enumerate(values):
         f_ref[row] = value
         fb_ref[row] = value.astype(bf16)
 
 
-def hop_body(s_ref, c_ref, f_ref, m_ref, out_ref, *, channels, rows):
-    for row in range(rows):
-        e = s_ref[row].astype(f32) - row_of(c_ref, row, channels, rows)
+def hop_body(s_ref, c_ref, *refs, channels, rows):
+    f_ref, m_ref, out_ref = refs[-3:]
+    base = [row_of(c_ref, row, channels, rows) for row in range(rows)]
+    base += [ref[...] for ref in refs[:-3]]
+    for row in range(len(base)):
+        e = s_ref[row].astype(f32) - base[row]
         high = e.astype(bf16)
         low = (e - high.astype(f32)).astype(bf16)
         stacked = jnp.concatenate([high, high, low], 0)
@@ -179,21 +218,17 @@
         out_ref[row] = (f_ref[row] + e + moved).astype(bf16)
 
 
-def settle_body(*refs, channels, rows):
-    c_ref, arrived, s_ref, edge_ref = refs[0], refs[1:-2], refs[-2], refs[-1]
+def settle_body(c_ref, strip_ref, *refs, channels, rows):
+    arrived, s_ref = refs[:-1], refs[-1]
     first = lax.axis_index("layer") == 0
-    image = []
-    for row in range(rows):
+    base = [row_of(c_ref, row, channels, rows) for row in range(rows)] + [strip_ref[...]]
+    for row in range(rows + 1):
         value = sum(ref[row].astype(f32) for ref in arrived)
-        value = jnp.where(first, row_of(c_ref, row, channels, rows), value)
-        s_ref[row] = value.astype(bf16)
-        image.append(value)
-    edge_ref[0] = fold_edges(image).astype(bf16)
+        s_ref[row] = jnp.where(first, base[row], value).astype(bf16)
 
 
 def second_body(
-    c_ref, q_ref, s_ref, s_above_ref, s_below_ref, s_left_ref, s_right_ref,
-    q_above_ref, q_below_ref, q_left_ref, q_right_ref, w_ref, wt_ref,
+    c_ref, q_ref, s_ref, s_above_ref, s_below_ref, above_ref, below_ref, side_ref, w_ref, wt_ref,
     state_ref, g_ref, gb_ref, grad_ref,
     x_ref, a_ref, a2_ref, keep_ref, slope_ref, adj_ref, src_ref,
     *, channels, rows, depth,
@@ -211,25 +246,42 @@
         a_ref[index, :, :cols] = own.astype(bf16)
         a_ref[index, :, cols:] = beyond.astype(bf16)
 
-    joined = [join_edges(s_left_ref[j], s_right_ref[j], left, right) for j in range(3)]
+    edge = 2 * depth
+    own_side, above_side, below_side = (
+        ref[rows].astype(f32) for ref in (s_ref, s_above_ref, s_below_ref)
+    )
     for row in range(rows):
         own = jnp.where(first, row_of(c_ref, row, channels, rows), s_ref[row].astype(f32))
         state_ref[pl.ds(row, channels, stride=rows), :] = own
-        put(halo + row, own, side_lanes(joined[1], row))
+        put(halo + row, own, side_lanes(own_side, edge, 0, row))
     for row in range(halo):
-        put(row, s_above_ref[rows - halo + row].astype(f32), side_lanes(joined[0], rows - halo + row))
-        put(halo + rows + row, s_below_ref[row].astype(f32), side_lanes(joined[2], row))
+        place = rows - halo + row
+        put(row, s_above_ref[place].astype(f32), side_lanes(above_side, edge, 0, place))
+        put(halo + rows + row, s_below_ref[row].astype(f32), side_lanes(below_side, edge, 0, row))
 
     def put_adj(index, own, beyond):
         adj_ref[index, :, :cols] = own
         adj_ref[index, :, cols:] = beyond
 
-    joined = [join_edges(q_left_ref[j], q_right_ref[j], left, right) for j in range(3)]
+    _, (edge, low) = layout(rows, depth)
+    own_side = side_ref[...].astype(f32)
+    above_side, below_side = strips_of(above_ref, depth), strips_of(below_ref, depth)
     for row in range(rows):
-        put_adj(halo + row, row_of(q_ref, row, channels, rows), side_lanes(joined[1], row))
+        put_adj(
+            halo + row, row_of(q_ref, row, channels, rows), side_lanes(own_side, edge, low, row)
+        )
     for row in range(depth):
-        put_adj(halo - depth + row, q_above_ref[row].astype(f32), side_lanes(joined[0], rows - depth + row))
-        put_adj(halo + rows + row, q_below_ref[row].astype(f32), side_lanes(joined[2], row))
+        place = rows - depth + row
+        put_adj(
+            halo - depth + row,
+            above_ref[depth + row].astype(f32),
+            side_lanes(above_side, edge, low, place),
+        )
+        put_adj(
+            halo + rows + row,
+            below_ref[depth + row].astype(f32),
+            side_lanes(below_side, edge, low, row),
+        )
 
     def keep(layer):
         for row in range(rows):
@@ -308,37 +360,17 @@
         out_ref[pl.ds(row, channels, stride=rows), :] = value
 
 
-def shifted(array, row_by, col_by):
-    rows, cols = lax.axis_size("row"), lax.axis_size("col")
-    pairs = [
-        (r * cols + c, (r + row_by) * cols + c + col_by)
-        for r in range(rows)
-        for c in range(cols)
-        if 0 <= r + row_by < rows and 0 <= c + col_by < cols
-    ]
-    return lax.ppermute(array, ("row", "col"), pairs)
-
-
-def swapped(array, row_by):
-    rows = lax.axis_size("row")
-    pairs = [
-        (r * 2 + c, (r + row_by) * 2 + 1 - c)
-        for r in range(rows)
-        for c in range(2)
-        if 0 <= r + row_by < rows
-    ]
-    return lax.ppermute(array, ("row", "col"), pairs)
-
-
-def around(edges):
+def shifted(array, axis, by):
+    count = lax.axis_size(axis)
+    pairs = [(i, i + by) for i in range(count) if 0 <= i + by < count]
+    return lax.ppermute(array, axis, pairs)
+
+
+def from_sides(array):
     if lax.axis_size("col") == 2:
-        parts = [swapped(edges, by) for by in (1, 0, -1)]
-        both = jnp.stack(parts, 0)
-        return both, both
-    return (
-        jnp.stack([shifted(edges, by, 1) for by in (1, 0, -1)], 0),
-        jnp.stack([shifted(edges, by, -1) for by in (1, 0, -1)], 0),
-    )
+        other = lax.ppermute(array, "col", [(0, 1), (1, 0)])
+        return other, other
+    return shifted(array, "col", 1), shifted(array, "col", -1)
 
 
 def total_over_tiles(grads):
@@ -379,17 +411,20 @@
     tile_b = jax.ShapeDtypeStruct((rows, channels, cols), bf16)
     tile_f = jax.ShapeDtypeStruct((rows, channels, cols), f32)
 
-    top, bottom, edges = call(
-        functools.partial(pack_body, depth=depth, **sizes),
-        (
-            jax.ShapeDtypeStruct((2 * depth, channels, cols), bf16),
-            jax.ShapeDtypeStruct((2 * depth, channels, cols), bf16),
-            jax.ShapeDtypeStruct((2, channels, cols), bf16),
-        ),
-    )(c_flat, q_flat)
-    above = shifted(bottom, 1, 0)
-    below = shifted(top, -1, 0)
-    left, right = around(edges)
+    strip_f = jax.ShapeDtypeStruct((channels, cols), f32)
+    wide_b = jax.ShapeDtypeStruct((channels, 2 * cols), bf16)
+    more_f, more_b, message_b = (
+        jax.ShapeDtypeStruct((count, channels, cols), kind)
+        for count, kind in ((rows + 1, f32), (rows + 1, bf16), (2 * depth + 2, bf16))
+    )
+
+    edges = call(functools.partial(strip_body, depth=depth, **sizes), wide_b)(c_flat, q_flat)
+    left, right = from_sides(edges)
+    top, bottom, side = call(
+        functools.partial(message_body, depth=depth, **sizes), (message_b, message_b, wide_b)
+    )(c_flat, q_flat, left, right)
+    above = shifted(bottom, "row", 1)
+    below = shifted(top, "row", -1)
 
     taps = weights.reshape(depth, channels, 3, 3, channels)
     w_fwd = jnp.transpose(taps, (0, 3, 1, 2, 4)).reshape(depth, 3 * channels, 3 * channels)
@@ -405,16 +440,16 @@
     lanes = 2 * cols
     mac = 2 * 9 * channels * channels * lanes
     total = rows + 2 * depth
-    f, sending = call(
+    f, sending, strip = call(
         functools.partial(first_body, depth=depth, **sizes),
-        (tile_f, tile_b),
+        (more_f, more_b, strip_f),
         [
             pltpu.VMEM((total, channels, lanes), f32),
             pltpu.VMEM((total, channels, lanes), bf16),
             pltpu.VMEM((total, channels, lanes), bf16),
         ],
         flops=mac * 44,
-    )(c_flat, above[:depth], below[:depth], left[:, 0], right[:, 0], w_fwd)
+    )(c_flat, above, below, side, w_fwd)
 
     def chain(sending, base, target, matrix, order):
         arrivals = []
@@ -422,19 +457,19 @@
             arrived = lax.ppermute(sending, "layer", [(source, goal)])
             arrivals.append(arrived)
             if place < len(order) - 1:
-                sending = call(functools.partial(hop_body, **sizes), tile_b, flops=10**10)(
-                    arrived, base, target, matrix
-                )
+                sending = call(
+                    functools.partial(hop_body, **sizes),
+                    jax.ShapeDtypeStruct(sending.shape, bf16),
+                    flops=10**10,
+                )(arrived, *base, target, matrix)
         return arrivals
 
-    arrivals = chain(sending, c_flat, f, m_fwd, [(k, k + 1) for k in range(groups - 1)])
-    s, s_edges = call(
-        functools.partial(settle_body, **sizes),
-        (tile_b, jax.ShapeDtypeStruct((1, channels, cols), bf16)),
-    )(c_flat, *arrivals)
-    s_above = shifted(s, 1, 0)
-    s_below = shifted(s, -1, 0)
-    s_left, s_right = around(s_edges)
+    arrivals = chain(
+        sending, (c_flat, strip), f, m_fwd, [(k, k + 1) for k in range(groups - 1)]
+    )
+    s = call(functools.partial(settle_body, **sizes), more_b)(c_flat, strip, *arrivals)
+    s_above = shifted(s, "row", 1)
+    s_below = shifted(s, "row", -1)
 
     total = rows + 4 * depth
     state, g, sending, grads = call(
@@ -456,11 +491,10 @@
         ],
         flops=mac * 136,
     )(
-        c_flat, q_flat, s, s_above, s_below, s_left[:, 0], s_right[:, 0],
-        above[depth:], below[depth:], left[:, 1], right[:, 1], w_fwd, w_back,
+        c_flat, q_flat, s, s_above, s_below, above, below, side, w_fwd, w_back
     )
     returned = chain(
-        sending, q_flat, g, m_back, [(k, k - 1) for k in range(groups - 1, 0, -1)]
+        sending, (q_flat,), g, m_back, [(k, k - 1) for k in range(groups - 1, 0, -1)]
     )
     weight_grads = total_over_tiles(grads)
     adjoint = call(

time: 90.8 us -> 81.4 us (0.90)
  starting transfers between devices: 33.5 us -> 21.3 us
  waiting for transfers between devices: 29.2 us -> 32.5 us
    ppermute x10 -> x5, starting transfers between devices: 24.3 us -> 12 us  [the longest x4 10.4 us: shifted(): return lax.ppermute(array, axis, pairs)]
    ppermute x10 -> x5, waiting for transfers between devices: 4.25 us -> 7.26 us  [the longest x4 4.86 us: shifted(): return lax.ppermute(array, axis, pairs)]
    pallas_call x7 -> x8, Pallas kernels: 5.98 us -> 6.2 us  [the longest x1 4.76 us: local(): call(functools.partial(first_body, depth=depth, **sizes), (more_f, more_b...]
  transfers between devices with their start and end apart: 20 -> 15, of which waited for: 7 -> 8; matrix products, arithmetic and copies ran while one was open for 3% -> 3% of each run, Pallas kernels for 1% -> 2%
where the time goes in v3:
time: 81.4 us; the launch traced here: 81 us
  waiting for transfers between devices  32.5 us (40%)
  starting transfers between devices  21.3 us (26%)
  Pallas kernels  20.6 us (25%)
  local copies, waits for them, and re-layouts  4.34 us (5%)
  other arithmetic  1.25 us (2%)
  between operations  0.97 us (1%)
    ppermute x6, waiting for transfers between devices, chain(): arrived = lax.ppermute(sending, 'layer', [(source, goal)])  16.9 us
    pallas_call x1, Pallas kernels, local(): call(functools.partial(second_body, depth=depth, **sizes), (jax.ShapeDtyp...  13.7 us
    ppermute x4, starting transfers between devices, shifted(): return lax.ppermute(array, axis, pairs)  10.4 us
    ppermute x2, waiting for transfers between devices, add(): return rounded.astype(f32) + lax.ppermute(rounded, axis, pairs).astype(f32)  7.58 us
    ppermute x6, starting transfers between devices, chain(): arrived = lax.ppermute(sending, 'layer', [(source, goal)])  7.44 us
    ppermute x4, waiting for transfers between devices, shifted(): return lax.ppermute(array, axis, pairs)  4.86 us
    pallas_call x1, Pallas kernels, local(): call(functools.partial(first_body, depth=depth, **sizes), (more_f, more_b...  4.76 us
    ppermute x1, waiting for transfers between devices, from_sides(): other = lax.ppermute(array, 'col', [(0, 1), (1, 0)])  2.39 us
  transfers between devices with their start and end apart: 15, of which 8 were waited for; matrix products, arithmetic and copies ran while one was open for 3% of the time, Pallas kernels for 2%

profile of v3, /device:TPU:2, one launch (start us, length us, event | category | flops | bytes accessed | tf_op | source)
XLA Modules:
  0.0 81.0 jit_solution(12485249968043892409)
XLA Ops:
  0.6 0.9 %copy-done = f32[1,64,8,128]{3,2,1,0:T(8,128)S(1)} copy-done((f32[1,64,8,128]{3,2,1,0:T(8,128)S(1)}, f32[1,64,8,128]{3,2,1,0:T(8,128)}, u32[]{:S(2)}) %copy-start) | copy-done | bytes 262168
  1.6 0.9 %copy-done.2 = f32[1,64,8,128]{3,2,1,0:T(8,128)S(1)} copy-done((f32[1,64,8,128]{3,2,1,0:T(8,128)S(1)}, f32[1,64,8,128]{3,2,1,0:T(8,128)}, u32[]{:S(2)}) %copy-start.2) | copy-done | bytes 262168
  2.7 1.6 %collective-permute-start = (bf16[64,256]{1,0:T(8,128)(2,1)S(1)}, bf16[64,256]{1,0:T(8,128)(2,1)S(1)}, u32[]{:S(2)}, u32[]{:S(2)}) collective-permute-start(bf16[64,256]{1,0:T(8,128)(2,1)S(1)} %shard_map.58), channel_id=1, source_target_pairs={{0,1},{1,0},{2,3},{3,2},{4,5},{5,4},{6,7},{7,6},{8,9},{9,8},{10,11... | collective-permute-start | bytes 98312 | tf_op jit(solution)/shard_map/ppermute | solution.py:371
  4.3 2.4 %collective-permute-done.left_ref.right_ref = bf16[64,256]{1,0:T(8,128)(2,1)S(1)} collective-permute-done((bf16[64,256]{1,0:T(8,128)(2,1)S(1)}, bf16[64,256]{1,0:T(8,128)(2,1)S(1)}, u32[]{:S(2)}, u32[]{:S(2)}) %collective-permute-start) | collective-permute-done | bytes 32800 | tf_op jit(solution)/shard_map/ppermute | solution.py:371
  6.8 1.9 %collective-permute-start.1 = (bf16[10,64,128]{2,1,0:T(8,128)(2,1)S(1)}, bf16[10,64,128]{2,1,0:T(8,128)(2,1)S(1)}, u32[]{:S(2)}, u32[]{:S(2)}) collective-permute-start(bf16[10,64,128]{2,1,0:T(8,128)(2,1)S(1)} %get-tuple-element.13), channel_id=1, source_target_pairs={{0,2},{2,4},{4,6},{1,3},{3,5},{5,7},{8,10},{10,12},{12,14},{9,11},... | collective-permute-start | bytes 491528 | tf_op jit(solution)/shard_map/ppermute | solution.py:366
  8.7 3.6 %collective-permute-start.2 = (bf16[10,64,128]{2,1,0:T(8,128)(2,1)S(1)}, bf16[10,64,128]{2,1,0:T(8,128)(2,1)S(1)}, u32[]{:S(2)}, u32[]{:S(2)}) collective-permute-start(bf16[10,64,128]{2,1,0:T(8,128)(2,1)S(1)} %get-tuple-element.14), channel_id=1, source_target_pairs={{2,0},{4,2},{6,4},{3,1},{5,3},{7,5},{10,8},{12,10},{14,12},{11,9},... | collective-permute-start | bytes 491528 | tf_op jit(solution)/shard_map/ppermute | solution.py:366
  12.4 0.3 copy.10
  12.7 0.6 copy.11
  13.3 0.4 reshape.34.w_ref
  13.8 1.4 %collective-permute-done.2.below_ref = bf16[10,64,128]{2,1,0:T(8,128)(2,1)S(1)} collective-permute-done((bf16[10,64,128]{2,1,0:T(8,128)(2,1)S(1)}, bf16[10,64,128]{2,1,0:T(8,128)(2,1)S(1)}, u32[]{:S(2)}, u32[]{:S(2)}) %collective-permute-start.2) | collective-permute-done | bytes 163872 | tf_op jit(solution)/shard_map/ppermute | solution.py:366
  15.2 4.8 %shard_map.60 = (f32[9,64,128]{2,1,0:T(8,128)S(1)}, bf16[9,64,128]{2,1,0:T(8,128)(2,1)S(1)}, f32[64,128]{1,0:T(8,128)S(1)}) custom-call(f32[512,128]{1,0:T(8,128)S(1)} %bitcast.20, bf16[10,64,128]{2,1,0:T(8,128)(2,1)S(1)} %collective-permute-done.1.above_ref, bf16[10,64,128]{2,1,0:T(8,128)(2,1)S(1)} %collective-permute-done.2.below_ref, ...), custom_call_target="tpu_custom_call" | custom-call | flops 830472192 | tf_op jit(solution)/shard_map/pallas_call | solution.py:443
  19.9 3.5 %collective-permute-start.3 = (bf16[9,64,128]{2,1,0:T(8,128)(2,1)S(1)}, bf16[9,64,128]{2,1,0:T(8,128)(2,1)S(1)}, u32[]{:S(2)}, u32[]{:S(2)}) collective-permute-start(bf16[9,64,128]{2,1,0:T(8,128)(2,1)S(1)} %get-tuple-element.17), channel_id=1, source_target_pairs={{0,8},{1,9},{2,10},{3,11},{4,12},{5,13},{6,14},{7,15}} | collective-permute-start | bytes 442376 | tf_op jit(solution)/shard_map/ppermute | solution.py:457
  23.6 2.5 %collective-permute-done.3.s_ref.refs_0_ = bf16[9,64,128]{2,1,0:T(8,128)(2,1)S(1)} collective-permute-done((bf16[9,64,128]{2,1,0:T(8,128)(2,1)S(1)}, bf16[9,64,128]{2,1,0:T(8,128)(2,1)S(1)}, u32[]{:S(2)}, u32[]{:S(2)}) %collective-permute-start.3) | collective-permute-done | bytes 147488 | tf_op jit(solution)/shard_map/ppermute | solution.py:457
  26.4 0.7 collective-permute-start.4
  27.1 0.3 shard_map.62
  27.4 0.7 collective-permute-start.5
  28.1 3.0 %collective-permute-start.7 = (bf16[9,64,128]{2,1,0:T(8,128)(2,1)S(1)}, bf16[9,64,128]{2,1,0:T(8,128)(2,1)S(1)}, u32[]{:S(2)}, u32[]{:S(2)}) collective-permute-start(bf16[9,64,128]{2,1,0:T(8,128)(2,1)S(1)} %shard_map.63.s_ref), channel_id=1, source_target_pairs={{2,0},{4,2},{6,4},{3,1},{5,3},{7,5},{10,8},{12,10},{14,12},{11,9},... | collective-permute-start | bytes 442376 | tf_op jit(solution)/shard_map/ppermute | solution.py:366
  31.1 1.9 %collective-permute-start.6 = (bf16[9,64,128]{2,1,0:T(8,128)(2,1)S(1)}, bf16[9,64,128]{2,1,0:T(8,128)(2,1)S(1)}, u32[]{:S(2)}, u32[]{:S(2)}) collective-permute-start(bf16[9,64,128]{2,1,0:T(8,128)(2,1)S(1)} %shard_map.63.s_ref), channel_id=1, source_target_pairs={{0,2},{2,4},{4,6},{1,3},{3,5},{5,7},{8,10},{10,12},{12,14},{9,11},... | collective-permute-start | bytes 442376 | tf_op jit(solution)/shard_map/ppermute | solution.py:366
  33.1 0.5 copy.15
  33.6 0.4 reshape.35.wt_ref
  34.1 3.5 %collective-permute-done.6.s_above_ref = bf16[9,64,128]{2,1,0:T(8,128)(2,1)S(1)} collective-permute-done((bf16[9,64,128]{2,1,0:T(8,128)(2,1)S(1)}, bf16[9,64,128]{2,1,0:T(8,128)(2,1)S(1)}, u32[]{:S(2)}, u32[]{:S(2)}) %collective-permute-start.6) | collective-permute-done | bytes 147488 | tf_op jit(solution)/shard_map/ppermute | solution.py:366
  37.6 13.7 %shard_map.64 = (f32[512,128]{1,0:T(8,128)}, f32[8,64,128]{2,1,0:T(8,128)S(1)}, bf16[8,64,128]{2,1,0:T(8,128)(2,1)S(1)}, f32[4,64,576]{2,1,0:T(8,128)S(1)}) custom-call(f32[512,128]{1,0:T(8,128)S(1)} %bitcast.24, f32[512,128]{1,0:T(8,128)S(1)} %bitcast.27, bf16[9,64,128]{2,1,0:T(8,128)(2,1)S(1)} %shard_map.63.s_ref, ...), custom_call_target="tpu_custom_call" | custom-call | flops 2566914048 | tf_op jit(solution)/shard_map/pallas_call | solution.py:475
  51.4 0.7 collective-permute-start.8
  52.1 0.8 %collective-permute-done.11 = f32[2,64,576]{2,1,0:T(8,128)S(1)} collective-permute-done((f32[2,64,576]{2,1,0:T(8,128)S(1)}, f32[2,64,576]{2,1,0:T(8,128)S(1)}, u32[]{:S(2)}, u32[]{:S(2)}) %collective-permute-start.11) | collective-permute-done | bytes 294944 | tf_op jit(solution)/shard_map/ppermute | solution.py:384
  53.4 0.7 collective-permute-start.9
  54.0 5.3 %collective-permute-done.12 = bf16[2,64,576]{2,1,0:T(8,128)(2,1)S(1)} collective-permute-done((bf16[2,64,576]{2,1,0:T(8,128)(2,1)S(1)}, bf16[2,64,576]{2,1,0:T(8,128)(2,1)S(1)}, u32[]{:S(2)}, u32[]{:S(2)}) %collective-permute-start.12) | collective-permute-done | bytes 147488 | tf_op jit(solution)/shard_map/ppermute | solution.py:388
  59.3 1.6 %collective-permute-start.13 = (bf16[2,64,576]{2,1,0:T(8,128)(2,1)S(1)}, bf16[2,64,576]{2,1,0:T(8,128)(2,1)S(1)}, u32[]{:S(2)}, u32[]{:S(2)}) collective-permute-start(bf16[2,64,576]{2,1,0:T(8,128)(2,1)S(1)} %add_convert_fusion), channel_id=1, source_target_pairs={{0,1},{1,0},{2,3},{3,2},{4,5},{5,4},{6,7},{7,6},{8,9},{9,8},{10,11... | collective-permute-start | bytes 442376 | tf_op jit(solution)/shard_map/ppermute | solution.py:388
  61.2 1.3 %collective-permute-start.10 = (bf16[8,64,128]{2,1,0:T(8,128)(2,1)S(1)}, bf16[8,64,128]{2,1,0:T(8,128)(2,1)S(1)}, u32[]{:S(2)}, u32[]{:S(2)}) collective-permute-start(bf16[8,64,128]{2,1,0:T(8,128)(2,1)S(1)} %shard_map.66), channel_id=1, source_target_pairs={{8,0},{9,1},{10,2},{11,3},{12,4},{13,5},{14,6},{15,7}} | collective-permute-start | bytes 393224 | tf_op jit(solution)/shard_map/ppermute | solution.py:457
  62.5 2.3 %collective-permute-done.13 = bf16[2,64,576]{2,1,0:T(8,128)(2,1)S(1)} collective-permute-done((bf16[2,64,576]{2,1,0:T(8,128)(2,1)S(1)}, bf16[2,64,576]{2,1,0:T(8,128)(2,1)S(1)}, u32[]{:S(2)}, u32[]{:S(2)}) %collective-permute-start.13) | collective-permute-done | bytes 147488 | tf_op jit(solution)/shard_map/ppermute | solution.py:388
  64.9 14.3 %collective-permute-done.10.refs_3_ = bf16[8,64,128]{2,1,0:T(8,128)(2,1)S(1)} collective-permute-done((bf16[8,64,128]{2,1,0:T(8,128)(2,1)S(1)}, bf16[8,64,128]{2,1,0:T(8,128)(2,1)S(1)}, u32[]{:S(2)}, u32[]{:S(2)}) %collective-permute-start.10) | collective-permute-done | bytes 131104 | tf_op jit(solution)/shard_map/ppermute | solution.py:457
  79.3 0.8 shard_map.67
  80.1 0.9 %pad_maximum_fusion = f32[4,64,576]{2,1,0:T(8,128)} fusion(f32[2,64,576]{2,1,0:T(8,128)S(1)} %get-tuple-element.24, f32[2,64,576]{2,1,0:T(8,128)S(1)} %get-tuple-element.23), kind=kLoop, calls=%fused_computation | loop fusion | flops 147456 | bytes 1179648 | tf_op jit(solution)/shard_map/concatenate | solution.py:401
  (37 shorter events, 1.9 us)
Async XLA Ops:
  0.6 1.0 %copy-start = (f32[1,64,8,128]{3,2,1,0:T(8,128)S(1)}, f32[1,64,8,128]{3,2,1,0:T(8,128)}, u32[]{:S(2)}) copy-start(f32[1,64,8,128]{3,2,1,0:T(8,128)} %param.3) | copy-start | bytes 786436
  1.6 0.9 %copy-start.2 = (f32[1,64,8,128]{3,2,1,0:T(8,128)S(1)}, f32[1,64,8,128]{3,2,1,0:T(8,128)}, u32[]{:S(2)}) copy-start(f32[1,64,8,128]{3,2,1,0:T(8,128)} %param.4) | copy-start | bytes 786436
  2.7 9.7 %copy-start.4 = (bf16[4,64,576]{2,1,0:T(8,128)(2,1)S(1)}, bf16[4,64,576]{2,1,0:T(8,128)(2,1)}, u32[]{:S(2)}) copy-start(bf16[4,64,576]{2,1,0:T(8,128)(2,1)} %param.5) | copy-start | bytes 884740
  2.7 4.0 %collective-permute-start = (bf16[64,256]{1,0:T(8,128)(2,1)S(1)}, bf16[64,256]{1,0:T(8,128)(2,1)S(1)}, u32[]{:S(2)}, u32[]{:S(2)}) collective-permute-start(bf16[64,256]{1,0:T(8,128)(2,1)S(1)} %shard_map.58), channel_id=1, source_target_pairs={{0,1},{1,0},{2,3},{3,2},{4,5},{5,4},{6,7},{7,6},{8,9},{9,8},{10,11... | collective-permute-start | bytes 98312 | tf_op jit(solution)/shard_map/ppermute | solution.py:371
  6.8 7.0 %collective-permute-start.1 = (bf16[10,64,128]{2,1,0:T(8,128)(2,1)S(1)}, bf16[10,64,128]{2,1,0:T(8,128)(2,1)S(1)}, u32[]{:S(2)}, u32[]{:S(2)}) collective-permute-start(bf16[10,64,128]{2,1,0:T(8,128)(2,1)S(1)} %get-tuple-element.13), channel_id=1, source_target_pairs={{0,2},{2,4},{4,6},{1,3},{3,5},{5,7},{8,10},{10,12},{12,14},{9,11},... | collective-permute-start | bytes 491528 | tf_op jit(solution)/shard_map/ppermute | solution.py:366
  8.7 6.5 %collective-permute-start.2 = (bf16[10,64,128]{2,1,0:T(8,128)(2,1)S(1)}, bf16[10,64,128]{2,1,0:T(8,128)(2,1)S(1)}, u32[]{:S(2)}, u32[]{:S(2)}) collective-permute-start(bf16[10,64,128]{2,1,0:T(8,128)(2,1)S(1)} %get-tuple-element.14), channel_id=1, source_target_pairs={{2,0},{4,2},{6,4},{3,1},{5,3},{7,5},{10,8},{12,10},{14,12},{11,9},... | collective-permute-start | bytes 491528 | tf_op jit(solution)/shard_map/ppermute | solution.py:366
  13.3 1.9 %copy-start.1 = (f32[1,64,8,128]{3,2,1,0:T(8,128)S(1)}, f32[1,64,8,128]{3,2,1,0:T(8,128)}, u32[]{:S(2)}) copy-start(f32[1,64,8,128]{3,2,1,0:T(8,128)} %param.3) | copy-start | bytes 786436
  19.9 6.1 %collective-permute-start.3 = (bf16[9,64,128]{2,1,0:T(8,128)(2,1)S(1)}, bf16[9,64,128]{2,1,0:T(8,128)(2,1)S(1)}, u32[]{:S(2)}, u32[]{:S(2)}) collective-permute-start(bf16[9,64,128]{2,1,0:T(8,128)(2,1)S(1)} %get-tuple-element.17), channel_id=1, source_target_pairs={{0,8},{1,9},{2,10},{3,11},{4,12},{5,13},{6,14},{7,15}} | collective-permute-start | bytes 442376 | tf_op jit(solution)/shard_map/ppermute | solution.py:457
  26.4 0.7 collective-permute-start.4
  27.4 0.7 collective-permute-start.5
  28.1 5.9 %collective-permute-start.7 = (bf16[9,64,128]{2,1,0:T(8,128)(2,1)S(1)}, bf16[9,64,128]{2,1,0:T(8,128)(2,1)S(1)}, u32[]{:S(2)}, u32[]{:S(2)}) collective-permute-start(bf16[9,64,128]{2,1,0:T(8,128)(2,1)S(1)} %shard_map.63.s_ref), channel_id=1, source_target_pairs={{2,0},{4,2},{6,4},{3,1},{5,3},{7,5},{10,8},{12,10},{14,12},{11,9},... | collective-permute-start | bytes 442376 | tf_op jit(solution)/shard_map/ppermute | solution.py:366
  31.1 6.5 %collective-permute-start.6 = (bf16[9,64,128]{2,1,0:T(8,128)(2,1)S(1)}, bf16[9,64,128]{2,1,0:T(8,128)(2,1)S(1)}, u32[]{:S(2)}, u32[]{:S(2)}) collective-permute-start(bf16[9,64,128]{2,1,0:T(8,128)(2,1)S(1)} %shard_map.63.s_ref), channel_id=1, source_target_pairs={{0,2},{2,4},{4,6},{1,3},{3,5},{5,7},{8,10},{10,12},{12,14},{9,11},... | collective-permute-start | bytes 442376 | tf_op jit(solution)/shard_map/ppermute | solution.py:366
  33.6 4.0 %copy-start.3 = (f32[1,64,8,128]{3,2,1,0:T(8,128)S(1)}, f32[1,64,8,128]{3,2,1,0:T(8,128)}, u32[]{:S(2)}) copy-start(f32[1,64,8,128]{3,2,1,0:T(8,128)} %param.4) | copy-start | bytes 786436
  51.2 1.7 %collective-permute-start.11 = (f32[2,64,576]{2,1,0:T(8,128)S(1)}, f32[2,64,576]{2,1,0:T(8,128)S(1)}, u32[]{:S(2)}, u32[]{:S(2)}) collective-permute-start(f32[2,64,576]{2,1,0:T(8,128)S(1)} %slice_select_fusion), channel_id=1, source_target_pairs={{0,2},{2,0},{4,6},{6,4},{1,3},{3,1},{5,7},{7,5},{8,10},{10,8},{12,... | collective-permute-start | bytes 884744 | tf_op jit(solution)/shard_map/ppermute | solution.py:384
  51.4 1.6 %collective-permute-start.8 = (bf16[8,64,128]{2,1,0:T(8,128)(2,1)S(1)}, bf16[8,64,128]{2,1,0:T(8,128)(2,1)S(1)}, u32[]{:S(2)}, u32[]{:S(2)}) collective-permute-start(bf16[8,64,128]{2,1,0:T(8,128)(2,1)S(1)} %get-tuple-element.20), channel_id=1, source_target_pairs={{24,16},{25,17},{26,18},{27,19},{28,20},{29,21},{30,22},{31,23}} | collective-permute-start | bytes 393224 | tf_op jit(solution)/shard_map/ppermute | solution.py:457
  53.0 6.3 %collective-permute-start.12 = (bf16[2,64,576]{2,1,0:T(8,128)(2,1)S(1)}, bf16[2,64,576]{2,1,0:T(8,128)(2,1)S(1)}, u32[]{:S(2)}, u32[]{:S(2)}) collective-permute-start(bf16[2,64,576]{2,1,0:T(8,128)(2,1)S(1)} %add_convert_fusion.1), channel_id=1, source_target_pairs={{0,4},{2,6},{4,0},{6,2},{1,5},{3,7},{5,1},{7,3},{8,12},{10,14},{12... | collective-permute-start | bytes 442376 | tf_op jit(solution)/shard_map/ppermute | solution.py:388
  53.4 7.6 %collective-permute-start.9 = (bf16[8,64,128]{2,1,0:T(8,128)(2,1)S(1)}, bf16[8,64,128]{2,1,0:T(8,128)(2,1)S(1)}, u32[]{:S(2)}, u32[]{:S(2)}) collective-permute-start(bf16[8,64,128]{2,1,0:T(8,128)(2,1)S(1)} %shard_map.65), channel_id=1, source_target_pairs={{16,8},{17,9},{18,10},{19,11},{20,12},{21,13},{22,14},{23,15}} | collective-permute-start | bytes 393224 | tf_op jit(solution)/shard_map/ppermute | solution.py:457
  59.3 5.5 %collective-permute-start.13 = (bf16[2,64,576]{2,1,0:T(8,128)(2,1)S(1)}, bf16[2,64,576]{2,1,0:T(8,128)(2,1)S(1)}, u32[]{:S(2)}, u32[]{:S(2)}) collective-permute-start(bf16[2,64,576]{2,1,0:T(8,128)(2,1)S(1)} %add_convert_fusion), channel_id=1, source_target_pairs={{0,1},{1,0},{2,3},{3,2},{4,5},{5,4},{6,7},{7,6},{8,9},{9,8},{10,11... | collective-permute-start | bytes 442376 | tf_op jit(solution)/shard_map/ppermute | solution.py:388
  61.2 18.1 %collective-permute-start.10 = (bf16[8,64,128]{2,1,0:T(8,128)(2,1)S(1)}, bf16[8,64,128]{2,1,0:T(8,128)(2,1)S(1)}, u32[]{:S(2)}, u32[]{:S(2)}) collective-permute-start(bf16[8,64,128]{2,1,0:T(8,128)(2,1)S(1)} %shard_map.66), channel_id=1, source_target_pairs={{8,0},{9,1},{10,2},{11,3},{12,4},{13,5},{14,6},{15,7}} | collective-permute-start | bytes 393224 | tf_op jit(solution)/shard_map/ppermute | solution.py:457
  64.9 15.2 %collective-permute-start.14 = (f32[2,64,576]{2,1,0:T(8,128)S(1)}, f32[2,64,576]{2,1,0:T(8,128)S(1)}, u32[]{:S(2)}, u32[]{:S(2)}) collective-permute-start(f32[2,64,576]{2,1,0:T(8,128)S(1)} %convert_add_fusion), channel_id=1, source_target_pairs={{0,2},{2,0},{4,6},{6,4},{1,3},{3,1},{5,7},{7,5},{8,10},{10,8},{12,... | collective-permute-start | bytes 884744 | tf_op jit(solution)/shard_map/ppermute | solution.py:398

commit v4 on v3

--- a/solution.py
+++ b/solution.py
@@ -23,6 +23,13 @@
         ),
         compiler_params=pltpu.CompilerParams(vmem_limit_bytes=VMEM_BYTES),
     )
+
+
+def piece_of(upper, lower, row, rows):
+    half = rows // 2
+    if row < half:
+        return upper, row
+    return (lower, row - half) if row < rows else (upper, half)
 
 
 def row_of(ref, row, channels, rows):
@@ -153,7 +160,7 @@
 
 
 def first_body(
-    c_ref, above_ref, below_ref, side_ref, w_ref, f_ref, fb_ref, strip_ref, x_ref, a_ref, a2_ref,
+    c_ref, above_ref, below_ref, side_ref, w_ref, f_ref, upper_ref, lower_ref, strip_ref, x_ref, a_ref, a2_ref,
     *, channels, rows, depth,
 ):
     cols = c_ref.shape[1]
@@ -202,35 +209,39 @@
     values.append(fold_edges(image, 2 * depth, 0, jnp.zeros(strip_ref.shape, f32)))
     for row, value in enumerate(values):
         f_ref[row] = value
-        fb_ref[row] = value.astype(bf16)
-
-
-def hop_body(s_ref, c_ref, *refs, channels, rows):
+        ref, place = piece_of(upper_ref, lower_ref, row, rows)
+        ref[place] = value.astype(bf16)
+
+
+def hop_body(s_ref, c_ref, *refs, start, channels, rows):
     f_ref, m_ref, out_ref = refs[-3:]
-    base = [row_of(c_ref, row, channels, rows) for row in range(rows)]
-    base += [ref[...] for ref in refs[:-3]]
-    for row in range(len(base)):
-        e = s_ref[row].astype(f32) - base[row]
+    count = rows // 2
+    work = [(start + row, row_of(c_ref, start + row, channels, rows)) for row in range(count)]
+    work += [(rows, ref[...]) for ref in refs[:-3]]
+    for place, (row, base) in enumerate(work):
+        e = s_ref[place].astype(f32) - base
         high = e.astype(bf16)
         low = (e - high.astype(f32)).astype(bf16)
         stacked = jnp.concatenate([high, high, low], 0)
         moved = jnp.dot(m_ref[...], stacked, preferred_element_type=f32)
-        out_ref[row] = (f_ref[row] + e + moved).astype(bf16)
-
-
-def settle_body(c_ref, strip_ref, *refs, channels, rows):
-    arrived, s_ref = refs[:-1], refs[-1]
+        out_ref[place] = (f_ref[row] + e + moved).astype(bf16)
+
+
+def settle_body(c_ref, *refs, start, strips, channels, rows):
+    arrived, s_ref = refs[strips:-1], refs[-1]
     first = lax.axis_index("layer") == 0
-    base = [row_of(c_ref, row, channels, rows) for row in range(rows)] + [strip_ref[...]]
-    for row in range(rows + 1):
-        value = sum(ref[row].astype(f32) for ref in arrived)
-        s_ref[row] = jnp.where(first, base[row], value).astype(bf16)
+    base = [row_of(c_ref, start + row, channels, rows) for row in range(rows // 2)]
+    base += [ref[...] for ref in refs[:strips]]
+    for place in range(len(base)):
+        value = sum(ref[place].astype(f32) for ref in arrived)
+        s_ref[place] = jnp.where(first, base[place], value).astype(bf16)
 
 
 def second_body(
-    c_ref, q_ref, s_ref, s_above_ref, s_below_ref, above_ref, below_ref, side_ref, w_ref, wt_ref,
-    state_ref, g_ref, gb_ref, grad_ref,
-    x_ref, a_ref, a2_ref, keep_ref, slope_ref, adj_ref, src_ref,
+    c_ref, q_ref, s_up_ref, s_lo_ref, above_up_ref, above_lo_ref, below_up_ref, below_lo_ref,
+    above_ref, below_ref, side_ref, w_ref, wt_ref,
+    state_ref, g_ref, g_up_ref, g_lo_ref, kept_ref, sent_ref,
+    x_ref, a_ref, a2_ref, slope_ref, adj_ref, src_ref,
     *, channels, rows, depth,
 ):
     cols = c_ref.shape[1]
@@ -247,17 +258,32 @@
         a_ref[index, :, cols:] = beyond.astype(bf16)
 
     edge = 2 * depth
-    own_side, above_side, below_side = (
-        ref[rows].astype(f32) for ref in (s_ref, s_above_ref, s_below_ref)
-    )
+
+    def piece(upper, lower, row):
+        ref, place = piece_of(upper, lower, row, rows)
+        return ref[place].astype(f32)
+
+    own_side = piece(s_up_ref, s_lo_ref, rows)
+    above_side = piece(above_up_ref, above_lo_ref, rows)
+    below_side = piece(below_up_ref, below_lo_ref, rows)
     for row in range(rows):
-        own = jnp.where(first, row_of(c_ref, row, channels, rows), s_ref[row].astype(f32))
+        own = jnp.where(
+            first, row_of(c_ref, row, channels, rows), piece(s_up_ref, s_lo_ref, row)
+        )
         state_ref[pl.ds(row, channels, stride=rows), :] = own
         put(halo + row, own, side_lanes(own_side, edge, 0, row))
     for row in range(halo):
         place = rows - halo + row
-        put(row, s_above_ref[place].astype(f32), side_lanes(above_side, edge, 0, place))
-        put(halo + rows + row, s_below_ref[row].astype(f32), side_lanes(below_side, edge, 0, row))
+        put(
+            row,
+            piece(above_up_ref, above_lo_ref, place),
+            side_lanes(above_side, edge, 0, place),
+        )
+        put(
+            halo + rows + row,
+            piece(below_up_ref, below_lo_ref, row),
+            side_lanes(below_side, edge, 0, row),
+        )
 
     def put_adj(index, own, beyond):
         adj_ref[index, :, :cols] = own
@@ -283,22 +309,9 @@
             side_lanes(below_side, edge, low, row),
         )
 
-    def keep(layer):
-        for row in range(rows):
-            x = x_ref[halo + row]
-            lanes = 2 * cols
-            keep_ref[layer, :, pl.ds(row * cols, cols)] = jnp.concatenate(
-                [
-                    pltpu.roll(x, 1, 1)[:, :cols],
-                    x[:, :cols],
-                    pltpu.roll(x, lanes - 1, 1)[:, :cols],
-                ],
-                0,
-            ).astype(bf16)
-
     for layer in range(depth):
         now, later = (a_ref, a2_ref) if layer % 2 == 0 else (a2_ref, a_ref)
-        keep(layer)
+        kept_ref[layer] = now[pl.ds(halo, rows)]
 
         def step(first, count, layer=layer, now=now, later=later):
             states = x_ref[pl.ds(first, count)]
@@ -331,31 +344,54 @@
                 adj_ref[first + place] = adjoints[place] + moved[place]
 
         row_blocks(halo - layer, halo + rows + layer, back)
-        stacked = jnp.concatenate(
-            [
-                src_ref[pl.ds(halo + row - 1, 3)].reshape(3 * channels, 2 * cols)[:, :cols]
-                for row in range(rows)
-            ],
-            1,
-        )
+        sent_ref[layer] = src_ref[pl.ds(halo - 1, rows + 2), :, :cols]
+    for row in range(rows):
+        value = adj_ref[halo + row, :, :cols]
+        g_ref[row] = value
+        ref, place = piece_of(g_up_ref, g_lo_ref, row, rows)
+        ref[place] = value.astype(bf16)
+
+
+def grad_body(kept_ref, sent_ref, grad_ref, *, channels, rows, depth):
+    lanes = kept_ref.shape[3]
+    cols = lanes // 2
+    for layer in range(depth):
+        columns = []
+        for row in range(rows):
+            a = kept_ref[layer, row].astype(f32)
+            columns.append(
+                jnp.concatenate(
+                    [
+                        pltpu.roll(a, 1, 1)[:, :cols],
+                        a[:, :cols],
+                        pltpu.roll(a, lanes - 1, 1)[:, :cols],
+                    ],
+                    0,
+                ).astype(bf16)
+            )
+        sources = [
+            sent_ref[layer, pl.ds(row, 3)].reshape(3 * channels, cols) for row in range(rows)
+        ]
         grad = lax.dot_general(
-            stacked, keep_ref[layer], (((1,), (1,)), ((), ())), preferred_element_type=f32
+            jnp.concatenate(sources, 1),
+            jnp.concatenate(columns, 1),
+            (((1,), (1,)), ((), ())),
+            preferred_element_type=f32,
         )
         for tap in range(3):
             grad_ref[layer, :, pl.ds(tap * 3 * channels, 3 * channels)] = grad[
                 (2 - tap) * channels : (3 - tap) * channels
             ]
+
+
+def last_body(q_ref, *refs, channels, rows):
+    out_ref = refs[-1]
+    uppers, lowers = refs[: len(refs) // 2], refs[len(refs) // 2 : -1]
+    last = lax.axis_index("layer") == lax.axis_size("layer") - 1
+    half = rows // 2
     for row in range(rows):
-        value = adj_ref[halo + row, :, :cols]
-        g_ref[row] = value
-        gb_ref[row] = value.astype(bf16)
-
-
-def last_body(*refs, channels, rows):
-    q_ref, arrived, out_ref = refs[0], refs[1:-1], refs[-1]
-    last = lax.axis_index("layer") == lax.axis_size("layer") - 1
-    for row in range(rows):
-        value = sum(ref[row].astype(f32) for ref in arrived)
+        arrived, place = (uppers, row) if row < half else (lowers, row - half)
+        value = sum(ref[place].astype(f32) for ref in arrived)
         value = jnp.where(last, row_of(q_ref, row, channels, rows), value)
         out_ref[pl.ds(row, channels, stride=rows), :] = value
 
@@ -383,18 +419,18 @@
     pair = [(r, r ^ 1) for r in range(rows)]
     value = own + lax.ppermute(sent, "row", pair)
 
-    def add(value, axis, pairs):
+    flips = [(1 << bit, 0) for bit in range(1, rows.bit_length() - 1)]
+    flips += [(0, 1 << bit) for bit in range(cols.bit_length() - 1)]
+    for even, uneven in zip(flips, flips[::-1]):
+        pairs = []
+        for r in range(rows):
+            row_by, col_by = uneven if r % 2 else even
+            pairs += [
+                (r * cols + c, (r ^ row_by) * cols + (c ^ col_by)) for c in range(cols)
+            ]
         rounded = value.astype(bf16)
-        return rounded.astype(f32) + lax.ppermute(rounded, axis, pairs).astype(f32)
-
-    bit = 2
-    while bit < rows:
-        value = add(value, "row", [(r, r ^ bit) for r in range(rows)])
-        bit *= 2
-    bit = 1
-    while bit < cols:
-        value = add(value, "col", [(c, c ^ bit) for c in range(cols)])
-        bit *= 2
+        arrived = lax.ppermute(rounded, ("row", "col"), pairs)
+        value = rounded.astype(f32) + arrived.astype(f32)
     other = lax.ppermute(value, "row", pair)
     first = jnp.where(odd, other, value)
     second = jnp.where(odd, value, other)
@@ -408,14 +444,16 @@
     flat = (channels * rows, cols)
     c_flat, q_flat = c_states.reshape(flat), c_adjoints.reshape(flat)
     sizes = dict(channels=channels, rows=rows)
-    tile_b = jax.ShapeDtypeStruct((rows, channels, cols), bf16)
     tile_f = jax.ShapeDtypeStruct((rows, channels, cols), f32)
 
     strip_f = jax.ShapeDtypeStruct((channels, cols), f32)
     wide_b = jax.ShapeDtypeStruct((channels, 2 * cols), bf16)
-    more_f, more_b, message_b = (
+    half = rows // 2
+    more_f, upper_b, lower_b, message_b = (
         jax.ShapeDtypeStruct((count, channels, cols), kind)
-        for count, kind in ((rows + 1, f32), (rows + 1, bf16), (2 * depth + 2, bf16))
+        for count, kind in (
+            (rows + 1, f32), (half + 1, bf16), (half, bf16), (2 * depth + 2, bf16)
+        )
     )
 
     edges = call(functools.partial(strip_body, depth=depth, **sizes), wide_b)(c_flat, q_flat)
@@ -428,9 +466,11 @@
 
     taps = weights.reshape(depth, channels, 3, 3, channels)
     w_fwd = jnp.transpose(taps, (0, 3, 1, 2, 4)).reshape(depth, 3 * channels, 3 * channels)
-    w_back = jnp.transpose(taps[:, :, ::-1, ::-1, :], (0, 3, 4, 2, 1)).reshape(
+    later_taps, _ = lax.optimization_barrier((taps, top))
+    w_back = jnp.transpose(later_taps[:, :, ::-1, ::-1, :], (0, 3, 4, 2, 1)).reshape(
         depth, 3 * channels, 3 * channels
     )
+    w_fwd, w_back = lax.optimization_barrier((w_fwd, w_back))
     coarse = step_size * jnp.sum(weights[0].astype(f32).reshape(channels, 9, channels), axis=1)
     high = coarse.astype(bf16)
     low = (coarse - high.astype(f32)).astype(bf16)
@@ -440,9 +480,9 @@
     lanes = 2 * cols
     mac = 2 * 9 * channels * channels * lanes
     total = rows + 2 * depth
-    f, sending, strip = call(
+    f, f_upper, f_lower, strip = call(
         functools.partial(first_body, depth=depth, **sizes),
-        (more_f, more_b, strip_f),
+        (more_f, upper_b, lower_b, strip_f),
         [
             pltpu.VMEM((total, channels, lanes), f32),
             pltpu.VMEM((total, channels, lanes), bf16),
@@ -451,55 +491,76 @@
         flops=mac * 44,
     )(c_flat, above, below, side, w_fwd)
 
-    def chain(sending, base, target, matrix, order):
+    def chain(pieces, target, matrix, order):
+        sendings = [piece[0] for piece in pieces]
         arrivals = []
-        for place, (source, goal) in enumerate(order):
-            arrived = lax.ppermute(sending, "layer", [(source, goal)])
+        for turn, hop in enumerate(order):
+            arrived = [lax.ppermute(sending, "layer", [hop]) for sending in sendings]
             arrivals.append(arrived)
-            if place < len(order) - 1:
-                sending = call(
-                    functools.partial(hop_body, **sizes),
-                    jax.ShapeDtypeStruct(sending.shape, bf16),
-                    flops=10**10,
-                )(arrived, *base, target, matrix)
-        return arrivals
-
-    arrivals = chain(
-        sending, (c_flat, strip), f, m_fwd, [(k, k + 1) for k in range(groups - 1)]
-    )
-    s = call(functools.partial(settle_body, **sizes), more_b)(c_flat, strip, *arrivals)
-    s_above = shifted(s, "row", 1)
-    s_below = shifted(s, "row", -1)
+            if turn < len(order) - 1:
+                sendings = [
+                    call(
+                        functools.partial(hop_body, start=start, **sizes),
+                        jax.ShapeDtypeStruct(value.shape, bf16),
+                        flops=10**10,
+                    )(value, *base, target, matrix)
+                    for value, (_, start, base) in zip(arrived, pieces)
+                ]
+        return [list(piece) for piece in zip(*arrivals)]
+
+    uppers, lowers = chain(
+        ((f_upper, 0, (c_flat, strip)), (f_lower, half, (c_flat,))),
+        f,
+        m_fwd,
+        [(k, k + 1) for k in range(groups - 1)],
+    )
+    tiles = []
+    for start, kind, strips, arrived in (
+        (0, upper_b, (strip,), uppers),
+        (half, lower_b, (), lowers),
+    ):
+        s = call(
+            functools.partial(settle_body, start=start, strips=len(strips), **sizes), kind
+        )(c_flat, *strips, *arrived)
+        tiles.append((s, shifted(s, "row", 1), shifted(s, "row", -1)))
+    pieces = [part for parts in zip(*tiles) for part in parts]
 
     total = rows + 4 * depth
-    state, g, sending, grads = call(
+    state, g, g_upper, g_lower, kept, sources = call(
         functools.partial(second_body, depth=depth, **sizes),
         (
             jax.ShapeDtypeStruct(flat, f32),
             tile_f,
-            tile_b,
-            jax.ShapeDtypeStruct((depth, channels, 9 * channels), f32),
+            lower_b,
+            lower_b,
+            jax.ShapeDtypeStruct((depth, rows, channels, lanes), bf16),
+            jax.ShapeDtypeStruct((depth, rows + 2, channels, cols), bf16),
         ),
         [
             pltpu.VMEM((total, channels, lanes), f32),
             pltpu.VMEM((total, channels, lanes), bf16),
             pltpu.VMEM((total, channels, lanes), bf16),
-            pltpu.VMEM((depth, 3 * channels, rows * cols), bf16),
             pltpu.VMEM((depth, total, channels, lanes), f32),
             pltpu.VMEM((total, channels, lanes), f32),
             pltpu.VMEM((total, channels, lanes), bf16),
         ],
-        flops=mac * 136,
-    )(
-        c_flat, q_flat, s, s_above, s_below, above, below, side, w_fwd, w_back
-    )
-    returned = chain(
-        sending, (q_flat,), g, m_back, [(k, k - 1) for k in range(groups - 1, 0, -1)]
-    )
+        flops=mac * 120,
+    )(c_flat, q_flat, *pieces, above, below, side, w_fwd, w_back)
+    uppers, lowers = chain(
+        ((g_upper, 0, (q_flat,)), (g_lower, half, (q_flat,))),
+        g,
+        m_back,
+        [(k, k - 1) for k in range(groups - 1, 0, -1)],
+    )
+    grads = call(
+        functools.partial(grad_body, depth=depth, **sizes),
+        jax.ShapeDtypeStruct((depth, channels, 9 * channels), f32),
+        flops=10**9,
+    )(kept, sources)
     weight_grads = total_over_tiles(grads)
     adjoint = call(
         functools.partial(last_body, **sizes), jax.ShapeDtypeStruct(flat, f32), flops=10**10
-    )(q_flat, *returned)
+    )(q_flat, *uppers, *lowers)
     return state.reshape(c_states.shape), adjoint.reshape(c_states.shape), weight_grads
 
 

time: 81.4 us -> 83.9 us (1.031)
  the two profiles are of different devices: /device:TPU:2 before, /device:TPU:19 now
where the time goes in v4:
time: 83.9 us; the launch traced here: 83.4 us
  starting transfers between devices  42.6 us (51%)
  Pallas kernels  21.5 us (26%)
  waiting for transfers between devices  12.7 us (15%)
  local copies, waits for them, and re-layouts  4.32 us (5%)
  other arithmetic  1.25 us (1%)
  between operations  1.09 us (1%)
    ppermute x6, starting transfers between devices, shifted(): return lax.ppermute(array, axis, pairs)  17.7 us
    ppermute x12, starting transfers between devices, chain(): arrived = [lax.ppermute(sending, 'layer', [hop]) for sending in sendings]  13 us
    pallas_call x1, Pallas kernels, local(): call(functools.partial(second_body, depth=depth, **sizes), (jax.ShapeDtyp...  12.9 us
    pallas_call x1, Pallas kernels, local(): call(functools.partial(first_body, depth=depth, **sizes), (more_f, upper_...  4.76 us
    ppermute x1, starting transfers between devices, total_over_tiles(): other = lax.ppermute(value, 'row', pair)  4.64 us
    ppermute x2, waiting for transfers between devices, total_over_tiles(): arrived = lax.ppermute(rounded, ('row', 'col'), pairs)  4.22 us
    ppermute x12, waiting for transfers between devices, chain(): arrived = [lax.ppermute(sending, 'layer', [hop]) for sending in sendings]  4.11 us
    ppermute x1, starting transfers between devices, total_over_tiles(): value = own + lax.ppermute(sent, 'row', pair)  3.16 us
  transfers between devices with their start and end apart: 23, of which 7 were waited for; matrix products, arithmetic and copies ran while one was open for 3% of the time, Pallas kernels for 4%

profile of v4, /device:TPU:19, one launch (start us, length us, event | category | flops | bytes accessed | tf_op | source)
XLA Modules:
  0.0 83.4 jit_solution(6756406134064226475)
XLA Ops:
  0.6 0.9 %copy-done = f32[1,64,8,128]{3,2,1,0:T(8,128)S(1)} copy-done((f32[1,64,8,128]{3,2,1,0:T(8,128)S(1)}, f32[1,64,8,128]{3,2,1,0:T(8,128)}, u32[]{:S(2)}) %copy-start) | copy-done | bytes 262168
  1.6 0.9 %copy-done.2 = f32[1,64,8,128]{3,2,1,0:T(8,128)S(1)} copy-done((f32[1,64,8,128]{3,2,1,0:T(8,128)S(1)}, f32[1,64,8,128]{3,2,1,0:T(8,128)}, u32[]{:S(2)}) %copy-start.2) | copy-done | bytes 262168
  2.7 1.3 %collective-permute-start = (bf16[64,256]{1,0:T(8,128)(2,1)S(1)}, bf16[64,256]{1,0:T(8,128)(2,1)S(1)}, u32[]{:S(2)}, u32[]{:S(2)}) collective-permute-start(bf16[64,256]{1,0:T(8,128)(2,1)S(1)} %shard_map.58), channel_id=1, source_target_pairs={{0,1},{1,0},{2,3},{3,2},{4,5},{5,4},{6,7},{7,6},{8,9},{9,8},{10,11... | collective-permute-start | bytes 98312 | tf_op jit(solution)/shard_map/ppermute | solution.py:407
  4.4 1.1 %collective-permute-done.left_ref.right_ref = bf16[64,256]{1,0:T(8,128)(2,1)S(1)} collective-permute-done((bf16[64,256]{1,0:T(8,128)(2,1)S(1)}, bf16[64,256]{1,0:T(8,128)(2,1)S(1)}, u32[]{:S(2)}, u32[]{:S(2)}) %collective-permute-start) | collective-permute-done | bytes 32800 | tf_op jit(solution)/shard_map/ppermute | solution.py:407
  5.6 1.3 %collective-permute-start.1 = (bf16[10,64,128]{2,1,0:T(8,128)(2,1)S(1)}, bf16[10,64,128]{2,1,0:T(8,128)(2,1)S(1)}, u32[]{:S(2)}, u32[]{:S(2)}) collective-permute-start(bf16[10,64,128]{2,1,0:T(8,128)(2,1)S(1)} %get-tuple-element.19), channel_id=1, source_target_pairs={{0,2},{2,4},{4,6},{1,3},{3,5},{5,7},{8,10},{10,12},{12,14},{9,11},... | collective-permute-start | bytes 491528 | tf_op jit(solution)/shard_map/ppermute | solution.py:402
  6.9 4.4 %collective-permute-start.2 = (bf16[10,64,128]{2,1,0:T(8,128)(2,1)S(1)}, bf16[10,64,128]{2,1,0:T(8,128)(2,1)S(1)}, u32[]{:S(2)}, u32[]{:S(2)}) collective-permute-start(bf16[10,64,128]{2,1,0:T(8,128)(2,1)S(1)} %get-tuple-element.20), channel_id=1, source_target_pairs={{2,0},{4,2},{6,4},{3,1},{5,3},{7,5},{10,8},{12,10},{14,12},{11,9},... | collective-permute-start | bytes 491528 | tf_op jit(solution)/shard_map/ppermute | solution.py:402
  13.4 4.8 %shard_map.60 = (f32[9,64,128]{2,1,0:T(8,128)S(1)}, bf16[5,64,128]{2,1,0:T(8,128)(2,1)S(1)}, bf16[4,64,128]{2,1,0:T(8,128)(2,1)S(1)}, f32[64,128]{1,0:T(8,128)S(1)}) custom-call(f32[512,128]{1,0:T(8,128)S(1)} %bitcast.20, bf16[10,64,128]{2,1,0:T(8,128)(2,1)S(1)} %collective-permute-done.1.above_ref, ...), custom_call_target="tpu_custom_call" | custom-call | flops 830472192 | tf_op jit(solution)/shard_map/pallas_call | solution.py:483
  18.9 0.7 collective-permute-start.3
  19.8 1.3 %collective-permute-start.7 = (bf16[4,64,128]{2,1,0:T(8,128)(2,1)S(1)}, bf16[4,64,128]{2,1,0:T(8,128)(2,1)S(1)}, u32[]{:S(2)}, u32[]{:S(2)}) collective-permute-start(bf16[4,64,128]{2,1,0:T(8,128)(2,1)S(1)} %shard_map.64), channel_id=1, source_target_pairs={{8,16},{9,17},{10,18},{11,19},{12,20},{13,21},{14,22},{15,23}} | collective-permute-start | bytes 196616 | tf_op jit(solution)/shard_map/ppermute | solution.py:498
  21.4 1.3 %collective-permute-start.4 = (bf16[5,64,128]{2,1,0:T(8,128)(2,1)S(1)}, bf16[5,64,128]{2,1,0:T(8,128)(2,1)S(1)}, u32[]{:S(2)}, u32[]{:S(2)}) collective-permute-start(bf16[5,64,128]{2,1,0:T(8,128)(2,1)S(1)} %shard_map.61), channel_id=1, source_target_pairs={{8,16},{9,17},{10,18},{11,19},{12,20},{13,21},{14,22},{15,23}} | collective-permute-start | bytes 245768 | tf_op jit(solution)/shard_map/ppermute | solution.py:498
  22.7 3.8 %collective-permute-done.7.s_ref.refs_1_ = bf16[4,64,128]{2,1,0:T(8,128)(2,1)S(1)} collective-permute-done((bf16[4,64,128]{2,1,0:T(8,128)(2,1)S(1)}, bf16[4,64,128]{2,1,0:T(8,128)(2,1)S(1)}, u32[]{:S(2)}, u32[]{:S(2)}) %collective-permute-start.7) | collective-permute-done | bytes 65568 | tf_op jit(solution)/shard_map/ppermute | solution.py:498
  26.7 1.3 %collective-permute-start.8 = (bf16[4,64,128]{2,1,0:T(8,128)(2,1)S(1)}, bf16[4,64,128]{2,1,0:T(8,128)(2,1)S(1)}, u32[]{:S(2)}, u32[]{:S(2)}) collective-permute-start(bf16[4,64,128]{2,1,0:T(8,128)(2,1)S(1)} %shard_map.65), channel_id=1, source_target_pairs={{16,24},{17,25},{18,26},{19,27},{20,28},{21,29},{22,30},{23,31}} | collective-permute-start | bytes 196616 | tf_op jit(solution)/shard_map/ppermute | solution.py:498
  28.5 1.3 %collective-permute-start.5 = (bf16[5,64,128]{2,1,0:T(8,128)(2,1)S(1)}, bf16[5,64,128]{2,1,0:T(8,128)(2,1)S(1)}, u32[]{:S(2)}, u32[]{:S(2)}) collective-permute-start(bf16[5,64,128]{2,1,0:T(8,128)(2,1)S(1)} %shard_map.62), channel_id=1, source_target_pairs={{16,24},{17,25},{18,26},{19,27},{20,28},{21,29},{22,30},{23,31}} | collective-permute-start | bytes 245768 | tf_op jit(solution)/shard_map/ppermute | solution.py:498
  29.9 6.4 %collective-permute-start.12 = (bf16[4,64,128]{2,1,0:T(8,128)(2,1)S(1)}, bf16[4,64,128]{2,1,0:T(8,128)(2,1)S(1)}, u32[]{:S(2)}, u32[]{:S(2)}) collective-permute-start(bf16[4,64,128]{2,1,0:T(8,128)(2,1)S(1)} %shard_map.66.s_lo_ref), channel_id=1, source_target_pairs={{2,0},{4,2},{6,4},{3,1},{5,3},{7,5},{10,8},{12,10},{14,12},{11,9},... | collective-permute-start | bytes 196616 | tf_op jit(solution)/shard_map/ppermute | solution.py:402
  36.3 1.3 %collective-permute-start.10 = (bf16[4,64,128]{2,1,0:T(8,128)(2,1)S(1)}, bf16[4,64,128]{2,1,0:T(8,128)(2,1)S(1)}, u32[]{:S(2)}, u32[]{:S(2)}) collective-permute-start(bf16[4,64,128]{2,1,0:T(8,128)(2,1)S(1)} %shard_map.66.s_lo_ref), channel_id=1, source_target_pairs={{0,2},{2,4},{4,6},{1,3},{3,5},{5,7},{8,10},{10,12},{12,14},{9,11},... | collective-permute-start | bytes 196616 | tf_op jit(solution)/shard_map/ppermute | solution.py:402
  37.7 3.0 %collective-permute-start.11 = (bf16[5,64,128]{2,1,0:T(8,128)(2,1)S(1)}, bf16[5,64,128]{2,1,0:T(8,128)(2,1)S(1)}, u32[]{:S(2)}, u32[]{:S(2)}) collective-permute-start(bf16[5,64,128]{2,1,0:T(8,128)(2,1)S(1)} %shard_map.63.s_up_ref), channel_id=1, source_target_pairs={{2,0},{4,2},{6,4},{3,1},{5,3},{7,5},{10,8},{12,10},{14,12},{11,9},... | collective-permute-start | bytes 245768 | tf_op jit(solution)/shard_map/ppermute | solution.py:402
  40.7 1.3 %collective-permute-start.9 = (bf16[5,64,128]{2,1,0:T(8,128)(2,1)S(1)}, bf16[5,64,128]{2,1,0:T(8,128)(2,1)S(1)}, u32[]{:S(2)}, u32[]{:S(2)}) collective-permute-start(bf16[5,64,128]{2,1,0:T(8,128)(2,1)S(1)} %shard_map.63.s_up_ref), channel_id=1, source_target_pairs={{0,2},{2,4},{4,6},{1,3},{3,5},{5,7},{8,10},{10,12},{12,14},{9,11},... | collective-permute-start | bytes 245768 | tf_op jit(solution)/shard_map/ppermute | solution.py:402
  42.1 2.7 %collective-permute-done.9.above_up_ref = bf16[5,64,128]{2,1,0:T(8,128)(2,1)S(1)} collective-permute-done((bf16[5,64,128]{2,1,0:T(8,128)(2,1)S(1)}, bf16[5,64,128]{2,1,0:T(8,128)(2,1)S(1)}, u32[]{:S(2)}, u32[]{:S(2)}) %collective-permute-start.9) | collective-permute-done | bytes 81952 | tf_op jit(solution)/shard_map/ppermute | solution.py:402
  44.8 12.9 %shard_map.67 = (f32[512,128]{1,0:T(8,128)}, f32[8,64,128]{2,1,0:T(8,128)S(1)}, bf16[4,64,128]{2,1,0:T(8,128)(2,1)S(1)}, bf16[4,64,128]{2,1,0:T(8,128)(2,1)S(1)}...) custom-call(f32[512,128]{1,0:T(8,128)S(1)} %bitcast.27, f32[512,128]{1,0:T(8,128)S(1)} %bitcast.30, ...), custom_call_target="tpu_custom_call" | custom-call | flops 2264924160 | tf_op jit(solution)/shard_map/pallas_call | solution.py:529
  57.7 1.3 %collective-permute-start.13 = (bf16[4,64,128]{2,1,0:T(8,128)(2,1)S(1)}, bf16[4,64,128]{2,1,0:T(8,128)(2,1)S(1)}, u32[]{:S(2)}, u32[]{:S(2)}) collective-permute-start(bf16[4,64,128]{2,1,0:T(8,128)(2,1)S(1)} %get-tuple-element.30), channel_id=1, source_target_pairs={{24,16},{25,17},{26,18},{27,19},{28,20},{29,21},{30,22},{31,23}} | collective-permute-start | bytes 196616 | tf_op jit(solution)/shard_map/ppermute | solution.py:498
  59.0 1.3 %collective-permute-start.16 = (bf16[4,64,128]{2,1,0:T(8,128)(2,1)S(1)}, bf16[4,64,128]{2,1,0:T(8,128)(2,1)S(1)}, u32[]{:S(2)}, u32[]{:S(2)}) collective-permute-start(bf16[4,64,128]{2,1,0:T(8,128)(2,1)S(1)} %get-tuple-element.32), channel_id=1, source_target_pairs={{24,16},{25,17},{26,18},{27,19},{28,20},{29,21},{30,22},{31,23}} | collective-permute-start | bytes 196616 | tf_op jit(solution)/shard_map/ppermute | solution.py:498
  60.3 1.1 %shard_map.73 = f32[4,64,576]{2,1,0:T(8,128)S(1)} custom-call(bf16[4,8,64,256]{3,2,1,0:T(8,128)(2,1)S(1)} %get-tuple-element.33.kept_ref, bf16[4,10,64,128]{3,2,1,0:T(8,128)(2,1)S(1)} %get-tuple-element.34.sent_ref), custom_call_target="tpu_custom_call" | custom-call | flops 1000000000 | tf_op jit(solution)/shard_map/pallas_call | solution.py:555
  61.5 3.2 %collective-permute-start.19 = (f32[2,64,576]{2,1,0:T(8,128)S(1)}, f32[2,64,576]{2,1,0:T(8,128)S(1)}, u32[]{:S(2)}, u32[]{:S(2)}) collective-permute-start(f32[2,64,576]{2,1,0:T(8,128)S(1)} %slice_select_fusion), channel_id=1, source_target_pairs={{0,2},{2,0},{4,6},{6,4},{1,3},{3,1},{5,7},{7,5},{8,10},{10,8},{12,... | collective-permute-start | bytes 884744 | tf_op jit(solution)/shard_map/ppermute | solution.py:420
  64.8 1.3 %collective-permute-start.14 = (bf16[4,64,128]{2,1,0:T(8,128)(2,1)S(1)}, bf16[4,64,128]{2,1,0:T(8,128)(2,1)S(1)}, u32[]{:S(2)}, u32[]{:S(2)}) collective-permute-start(bf16[4,64,128]{2,1,0:T(8,128)(2,1)S(1)} %shard_map.68), channel_id=1, source_target_pairs={{16,8},{17,9},{18,10},{19,11},{20,12},{21,13},{22,14},{23,15}} | collective-permute-start | bytes 196616 | tf_op jit(solution)/shard_map/ppermute | solution.py:498
  66.3 1.3 %collective-permute-start.17 = (bf16[4,64,128]{2,1,0:T(8,128)(2,1)S(1)}, bf16[4,64,128]{2,1,0:T(8,128)(2,1)S(1)}, u32[]{:S(2)}, u32[]{:S(2)}) collective-permute-start(bf16[4,64,128]{2,1,0:T(8,128)(2,1)S(1)} %shard_map.70), channel_id=1, source_target_pairs={{16,8},{17,9},{18,10},{19,11},{20,12},{21,13},{22,14},{23,15}} | collective-permute-start | bytes 196616 | tf_op jit(solution)/shard_map/ppermute | solution.py:498
  67.7 1.3 %collective-permute-start.20 = (bf16[2,64,576]{2,1,0:T(8,128)(2,1)S(1)}, bf16[2,64,576]{2,1,0:T(8,128)(2,1)S(1)}, u32[]{:S(2)}, u32[]{:S(2)}) collective-permute-start(bf16[2,64,576]{2,1,0:T(8,128)(2,1)S(1)} %add_convert_fusion.1), channel_id=1, source_target_pairs={{0,4},{1,5},{2,3},{3,2},{4,0},{5,1},{6,7},{7,6},{8,12},{9,13},{10,... | collective-permute-start | bytes 442376 | tf_op jit(solution)/shard_map/ppermute | solution.py:432
  69.9 2.1 %collective-permute-done.20 = bf16[2,64,576]{2,1,0:T(8,128)(2,1)S(1)} collective-permute-done((bf16[2,64,576]{2,1,0:T(8,128)(2,1)S(1)}, bf16[2,64,576]{2,1,0:T(8,128)(2,1)S(1)}, u32[]{:S(2)}, u32[]{:S(2)}) %collective-permute-start.20) | collective-permute-done | bytes 147488 | tf_op jit(solution)/shard_map/ppermute | solution.py:432
  72.0 1.5 %collective-permute-start.21 = (bf16[2,64,576]{2,1,0:T(8,128)(2,1)S(1)}, bf16[2,64,576]{2,1,0:T(8,128)(2,1)S(1)}, u32[]{:S(2)}, u32[]{:S(2)}) collective-permute-start(bf16[2,64,576]{2,1,0:T(8,128)(2,1)S(1)} %add_convert_fusion), channel_id=1, source_target_pairs={{0,1},{1,0},{2,6},{3,7},{4,5},{5,4},{6,2},{7,3},{8,9},{9,8},{10,14... | collective-permute-start | bytes 442376 | tf_op jit(solution)/shard_map/ppermute | solution.py:432
  74.3 2.2 %collective-permute-done.21 = bf16[2,64,576]{2,1,0:T(8,128)(2,1)S(1)} collective-permute-done((bf16[2,64,576]{2,1,0:T(8,128)(2,1)S(1)}, bf16[2,64,576]{2,1,0:T(8,128)(2,1)S(1)}, u32[]{:S(2)}, u32[]{:S(2)}) %collective-permute-start.21) | collective-permute-done | bytes 147488 | tf_op jit(solution)/shard_map/ppermute | solution.py:432
  76.5 4.6 %collective-permute-start.22 = (f32[2,64,576]{2,1,0:T(8,128)S(1)}, f32[2,64,576]{2,1,0:T(8,128)S(1)}, u32[]{:S(2)}, u32[]{:S(2)}) collective-permute-start(f32[2,64,576]{2,1,0:T(8,128)S(1)} %convert_add_fusion), channel_id=1, source_target_pairs={{0,2},{2,0},{4,6},{6,4},{1,3},{3,1},{5,7},{7,5},{8,10},{10,8},{12,... | collective-permute-start | bytes 884744 | tf_op jit(solution)/shard_map/ppermute | solution.py:434
  81.2 0.8 shard_map.72
  82.5 0.9 %pad_maximum_fusion = f32[4,64,576]{2,1,0:T(8,128)} fusion(f32[2,64,576]{2,1,0:T(8,128)S(1)} %get-tuple-element.36, f32[2,64,576]{2,1,0:T(8,128)S(1)} %get-tuple-element.35), kind=kLoop, calls=%fused_computation | loop fusion | flops 147456 | bytes 1179648 | tf_op jit(solution)/shard_map/concatenate | solution.py:437
  (59 shorter events, 7.5 us)
Async XLA Ops:
  0.6 1.0 %copy-start = (f32[1,64,8,128]{3,2,1,0:T(8,128)S(1)}, f32[1,64,8,128]{3,2,1,0:T(8,128)}, u32[]{:S(2)}) copy-start(f32[1,64,8,128]{3,2,1,0:T(8,128)} %param.3) | copy-start | bytes 786436
  1.6 0.9 %copy-start.2 = (f32[1,64,8,128]{3,2,1,0:T(8,128)S(1)}, f32[1,64,8,128]{3,2,1,0:T(8,128)}, u32[]{:S(2)}) copy-start(f32[1,64,8,128]{3,2,1,0:T(8,128)} %param.4) | copy-start | bytes 786436
  2.5 1.5 %copy-start.4 = (bf16[4,64,576]{2,1,0:T(8,128)(2,1)S(1)}, bf16[4,64,576]{2,1,0:T(8,128)(2,1)}, u32[]{:S(2)}) copy-start(bf16[4,64,576]{2,1,0:T(8,128)(2,1)} %param.5) | copy-start | bytes 884740
  2.7 2.8 %collective-permute-start = (bf16[64,256]{1,0:T(8,128)(2,1)S(1)}, bf16[64,256]{1,0:T(8,128)(2,1)S(1)}, u32[]{:S(2)}, u32[]{:S(2)}) collective-permute-start(bf16[64,256]{1,0:T(8,128)(2,1)S(1)} %shard_map.58), channel_id=1, source_target_pairs={{0,1},{1,0},{2,3},{3,2},{4,5},{5,4},{6,7},{7,6},{8,9},{9,8},{10,11... | collective-permute-start | bytes 98312 | tf_op jit(solution)/shard_map/ppermute | solution.py:407
  4.0 1.5 %copy-start.3 = (f32[1,64,8,128]{3,2,1,0:T(8,128)S(1)}, f32[1,64,8,128]{3,2,1,0:T(8,128)}, u32[]{:S(2)}) copy-start(f32[1,64,8,128]{3,2,1,0:T(8,128)} %param.4) | copy-start | bytes 786436
  4.3 1.2 %copy-start.1 = (f32[1,64,8,128]{3,2,1,0:T(8,128)S(1)}, f32[1,64,8,128]{3,2,1,0:T(8,128)}, u32[]{:S(2)}) copy-start(f32[1,64,8,128]{3,2,1,0:T(8,128)} %param.3) | copy-start | bytes 786436
  5.6 7.7 %collective-permute-start.1 = (bf16[10,64,128]{2,1,0:T(8,128)(2,1)S(1)}, bf16[10,64,128]{2,1,0:T(8,128)(2,1)S(1)}, u32[]{:S(2)}, u32[]{:S(2)}) collective-permute-start(bf16[10,64,128]{2,1,0:T(8,128)(2,1)S(1)} %get-tuple-element.19), channel_id=1, source_target_pairs={{0,2},{2,4},{4,6},{1,3},{3,5},{5,7},{8,10},{10,12},{12,14},{9,11},... | collective-permute-start | bytes 491528 | tf_op jit(solution)/shard_map/ppermute | solution.py:402
  6.9 6.5 %collective-permute-start.2 = (bf16[10,64,128]{2,1,0:T(8,128)(2,1)S(1)}, bf16[10,64,128]{2,1,0:T(8,128)(2,1)S(1)}, u32[]{:S(2)}, u32[]{:S(2)}) collective-permute-start(bf16[10,64,128]{2,1,0:T(8,128)(2,1)S(1)} %get-tuple-element.20), channel_id=1, source_target_pairs={{2,0},{4,2},{6,4},{3,1},{5,3},{7,5},{10,8},{12,10},{14,12},{11,9},... | collective-permute-start | bytes 491528 | tf_op jit(solution)/shard_map/ppermute | solution.py:402
  18.1 1.5 %collective-permute-start.6 = (bf16[4,64,128]{2,1,0:T(8,128)(2,1)S(1)}, bf16[4,64,128]{2,1,0:T(8,128)(2,1)S(1)}, u32[]{:S(2)}, u32[]{:S(2)}) collective-permute-start(bf16[4,64,128]{2,1,0:T(8,128)(2,1)S(1)} %get-tuple-element.27), channel_id=1, source_target_pairs={{0,8},{1,9},{2,10},{3,11},{4,12},{5,13},{6,14},{7,15}} | collective-permute-start | bytes 196616 | tf_op jit(solution)/shard_map/ppermute | solution.py:498
  18.9 2.2 %collective-permute-start.3 = (bf16[5,64,128]{2,1,0:T(8,128)(2,1)S(1)}, bf16[5,64,128]{2,1,0:T(8,128)(2,1)S(1)}, u32[]{:S(2)}, u32[]{:S(2)}) collective-permute-start(bf16[5,64,128]{2,1,0:T(8,128)(2,1)S(1)} %get-tuple-element.25), channel_id=1, source_target_pairs={{0,8},{1,9},{2,10},{3,11},{4,12},{5,13},{6,14},{7,15}} | collective-permute-start | bytes 245768 | tf_op jit(solution)/shard_map/ppermute | solution.py:498
  19.8 6.6 %collective-permute-start.7 = (bf16[4,64,128]{2,1,0:T(8,128)(2,1)S(1)}, bf16[4,64,128]{2,1,0:T(8,128)(2,1)S(1)}, u32[]{:S(2)}, u32[]{:S(2)}) collective-permute-start(bf16[4,64,128]{2,1,0:T(8,128)(2,1)S(1)} %shard_map.64), channel_id=1, source_target_pairs={{8,16},{9,17},{10,18},{11,19},{12,20},{13,21},{14,22},{15,23}} | collective-permute-start | bytes 196616 | tf_op jit(solution)/shard_map/ppermute | solution.py:498
  21.4 6.9 %collective-permute-start.4 = (bf16[5,64,128]{2,1,0:T(8,128)(2,1)S(1)}, bf16[5,64,128]{2,1,0:T(8,128)(2,1)S(1)}, u32[]{:S(2)}, u32[]{:S(2)}) collective-permute-start(bf16[5,64,128]{2,1,0:T(8,128)(2,1)S(1)} %shard_map.61), channel_id=1, source_target_pairs={{8,16},{9,17},{10,18},{11,19},{12,20},{13,21},{14,22},{15,23}} | collective-permute-start | bytes 245768 | tf_op jit(solution)/shard_map/ppermute | solution.py:498
  26.7 3.1 %collective-permute-start.8 = (bf16[4,64,128]{2,1,0:T(8,128)(2,1)S(1)}, bf16[4,64,128]{2,1,0:T(8,128)(2,1)S(1)}, u32[]{:S(2)}, u32[]{:S(2)}) collective-permute-start(bf16[4,64,128]{2,1,0:T(8,128)(2,1)S(1)} %shard_map.65), channel_id=1, source_target_pairs={{16,24},{17,25},{18,26},{19,27},{20,28},{21,29},{22,30},{23,31}} | collective-permute-start | bytes 196616 | tf_op jit(solution)/shard_map/ppermute | solution.py:498
  28.5 9.1 %collective-permute-start.5 = (bf16[5,64,128]{2,1,0:T(8,128)(2,1)S(1)}, bf16[5,64,128]{2,1,0:T(8,128)(2,1)S(1)}, u32[]{:S(2)}, u32[]{:S(2)}) collective-permute-start(bf16[5,64,128]{2,1,0:T(8,128)(2,1)S(1)} %shard_map.62), channel_id=1, source_target_pairs={{16,24},{17,25},{18,26},{19,27},{20,28},{21,29},{22,30},{23,31}} | collective-permute-start | bytes 245768 | tf_op jit(solution)/shard_map/ppermute | solution.py:498
  29.9 12.2 %collective-permute-start.12 = (bf16[4,64,128]{2,1,0:T(8,128)(2,1)S(1)}, bf16[4,64,128]{2,1,0:T(8,128)(2,1)S(1)}, u32[]{:S(2)}, u32[]{:S(2)}) collective-permute-start(bf16[4,64,128]{2,1,0:T(8,128)(2,1)S(1)} %shard_map.66.s_lo_ref), channel_id=1, source_target_pairs={{2,0},{4,2},{6,4},{3,1},{5,3},{7,5},{10,8},{12,10},{14,12},{11,9},... | collective-permute-start | bytes 196616 | tf_op jit(solution)/shard_map/ppermute | solution.py:402
  36.3 5.8 %collective-permute-start.10 = (bf16[4,64,128]{2,1,0:T(8,128)(2,1)S(1)}, bf16[4,64,128]{2,1,0:T(8,128)(2,1)S(1)}, u32[]{:S(2)}, u32[]{:S(2)}) collective-permute-start(bf16[4,64,128]{2,1,0:T(8,128)(2,1)S(1)} %shard_map.66.s_lo_ref), channel_id=1, source_target_pairs={{0,2},{2,4},{4,6},{1,3},{3,5},{5,7},{8,10},{10,12},{12,14},{9,11},... | collective-permute-start | bytes 196616 | tf_op jit(solution)/shard_map/ppermute | solution.py:402
  37.7 4.4 %collective-permute-start.11 = (bf16[5,64,128]{2,1,0:T(8,128)(2,1)S(1)}, bf16[5,64,128]{2,1,0:T(8,128)(2,1)S(1)}, u32[]{:S(2)}, u32[]{:S(2)}) collective-permute-start(bf16[5,64,128]{2,1,0:T(8,128)(2,1)S(1)} %shard_map.63.s_up_ref), channel_id=1, source_target_pairs={{2,0},{4,2},{6,4},{3,1},{5,3},{7,5},{10,8},{12,10},{14,12},{11,9},... | collective-permute-start | bytes 245768 | tf_op jit(solution)/shard_map/ppermute | solution.py:402
  40.7 4.1 %collective-permute-start.9 = (bf16[5,64,128]{2,1,0:T(8,128)(2,1)S(1)}, bf16[5,64,128]{2,1,0:T(8,128)(2,1)S(1)}, u32[]{:S(2)}, u32[]{:S(2)}) collective-permute-start(bf16[5,64,128]{2,1,0:T(8,128)(2,1)S(1)} %shard_map.63.s_up_ref), channel_id=1, source_target_pairs={{0,2},{2,4},{4,6},{1,3},{3,5},{5,7},{8,10},{10,12},{12,14},{9,11},... | collective-permute-start | bytes 245768 | tf_op jit(solution)/shard_map/ppermute | solution.py:402
  57.7 6.9 %collective-permute-start.13 = (bf16[4,64,128]{2,1,0:T(8,128)(2,1)S(1)}, bf16[4,64,128]{2,1,0:T(8,128)(2,1)S(1)}, u32[]{:S(2)}, u32[]{:S(2)}) collective-permute-start(bf16[4,64,128]{2,1,0:T(8,128)(2,1)S(1)} %get-tuple-element.30), channel_id=1, source_target_pairs={{24,16},{25,17},{26,18},{27,19},{28,20},{29,21},{30,22},{31,23}} | collective-permute-start | bytes 196616 | tf_op jit(solution)/shard_map/ppermute | solution.py:498
  59.0 7.1 %collective-permute-start.16 = (bf16[4,64,128]{2,1,0:T(8,128)(2,1)S(1)}, bf16[4,64,128]{2,1,0:T(8,128)(2,1)S(1)}, u32[]{:S(2)}, u32[]{:S(2)}) collective-permute-start(bf16[4,64,128]{2,1,0:T(8,128)(2,1)S(1)} %get-tuple-element.32), channel_id=1, source_target_pairs={{24,16},{25,17},{26,18},{27,19},{28,20},{29,21},{30,22},{31,23}} | collective-permute-start | bytes 196616 | tf_op jit(solution)/shard_map/ppermute | solution.py:498
  61.5 6.2 %collective-permute-start.19 = (f32[2,64,576]{2,1,0:T(8,128)S(1)}, f32[2,64,576]{2,1,0:T(8,128)S(1)}, u32[]{:S(2)}, u32[]{:S(2)}) collective-permute-start(f32[2,64,576]{2,1,0:T(8,128)S(1)} %slice_select_fusion), channel_id=1, source_target_pairs={{0,2},{2,0},{4,6},{6,4},{1,3},{3,1},{5,7},{7,5},{8,10},{10,8},{12,... | collective-permute-start | bytes 884744 | tf_op jit(solution)/shard_map/ppermute | solution.py:420
  64.8 4.2 %collective-permute-start.14 = (bf16[4,64,128]{2,1,0:T(8,128)(2,1)S(1)}, bf16[4,64,128]{2,1,0:T(8,128)(2,1)S(1)}, u32[]{:S(2)}, u32[]{:S(2)}) collective-permute-start(bf16[4,64,128]{2,1,0:T(8,128)(2,1)S(1)} %shard_map.68), channel_id=1, source_target_pairs={{16,8},{17,9},{18,10},{19,11},{20,12},{21,13},{22,14},{23,15}} | collective-permute-start | bytes 196616 | tf_op jit(solution)/shard_map/ppermute | solution.py:498
  66.3 7.1 %collective-permute-start.17 = (bf16[4,64,128]{2,1,0:T(8,128)(2,1)S(1)}, bf16[4,64,128]{2,1,0:T(8,128)(2,1)S(1)}, u32[]{:S(2)}, u32[]{:S(2)}) collective-permute-start(bf16[4,64,128]{2,1,0:T(8,128)(2,1)S(1)} %shard_map.70), channel_id=1, source_target_pairs={{16,8},{17,9},{18,10},{19,11},{20,12},{21,13},{22,14},{23,15}} | collective-permute-start | bytes 196616 | tf_op jit(solution)/shard_map/ppermute | solution.py:498
  67.7 4.2 %collective-permute-start.20 = (bf16[2,64,576]{2,1,0:T(8,128)(2,1)S(1)}, bf16[2,64,576]{2,1,0:T(8,128)(2,1)S(1)}, u32[]{:S(2)}, u32[]{:S(2)}) collective-permute-start(bf16[2,64,576]{2,1,0:T(8,128)(2,1)S(1)} %add_convert_fusion.1), channel_id=1, source_target_pairs={{0,4},{1,5},{2,3},{3,2},{4,0},{5,1},{6,7},{7,6},{8,12},{9,13},{10,... | collective-permute-start | bytes 442376 | tf_op jit(solution)/shard_map/ppermute | solution.py:432
  69.2 12.0 %collective-permute-start.15 = (bf16[4,64,128]{2,1,0:T(8,128)(2,1)S(1)}, bf16[4,64,128]{2,1,0:T(8,128)(2,1)S(1)}, u32[]{:S(2)}, u32[]{:S(2)}) collective-permute-start(bf16[4,64,128]{2,1,0:T(8,128)(2,1)S(1)} %shard_map.69), channel_id=1, source_target_pairs={{8,0},{9,1},{10,2},{11,3},{12,4},{13,5},{14,6},{15,7}} | collective-permute-start | bytes 196616 | tf_op jit(solution)/shard_map/ppermute | solution.py:498
  72.0 4.5 %collective-permute-start.21 = (bf16[2,64,576]{2,1,0:T(8,128)(2,1)S(1)}, bf16[2,64,576]{2,1,0:T(8,128)(2,1)S(1)}, u32[]{:S(2)}, u32[]{:S(2)}) collective-permute-start(bf16[2,64,576]{2,1,0:T(8,128)(2,1)S(1)} %add_convert_fusion), channel_id=1, source_target_pairs={{0,1},{1,0},{2,6},{3,7},{4,5},{5,4},{6,2},{7,3},{8,9},{9,8},{10,14... | collective-permute-start | bytes 442376 | tf_op jit(solution)/shard_map/ppermute | solution.py:432
  73.7 7.5 %collective-permute-start.18 = (bf16[4,64,128]{2,1,0:T(8,128)(2,1)S(1)}, bf16[4,64,128]{2,1,0:T(8,128)(2,1)S(1)}, u32[]{:S(2)}, u32[]{:S(2)}) collective-permute-start(bf16[4,64,128]{2,1,0:T(8,128)(2,1)S(1)} %shard_map.71), channel_id=1, source_target_pairs={{8,0},{9,1},{10,2},{11,3},{12,4},{13,5},{14,6},{15,7}} | collective-permute-start | bytes 196616 | tf_op jit(solution)/shard_map/ppermute | solution.py:498
  76.5 5.9 %collective-permute-start.22 = (f32[2,64,576]{2,1,0:T(8,128)S(1)}, f32[2,64,576]{2,1,0:T(8,128)S(1)}, u32[]{:S(2)}, u32[]{:S(2)}) collective-permute-start(f32[2,64,576]{2,1,0:T(8,128)S(1)} %convert_add_fusion), channel_id=1, source_target_pairs={{0,2},{2,0},{4,6},{6,4},{1,3},{3,1},{5,7},{7,5},{8,10},{10,8},{12,... | collective-permute-start | bytes 884744 | tf_op jit(solution)/shard_map/ppermute | solution.py:434

commit v5 on v4

--- a/solution.py
+++ b/solution.py
@@ -13,7 +13,7 @@
 bf16 = jnp.bfloat16
 
 
-def call(body, out_shape, scratch=(), flops=0, moved=0):
+def call(body, out_shape, scratch=(), flops=0, moved=0, **more):
     return pl.pallas_call(
         body,
         out_shape=out_shape,
@@ -22,6 +22,7 @@
             flops=int(flops), bytes_accessed=int(moved), transcendentals=0
         ),
         compiler_params=pltpu.CompilerParams(vmem_limit_bytes=VMEM_BYTES),
+        **more,
     )
 
 
@@ -95,6 +96,10 @@
     return up, down, left, right
 
 
+def even_row():
+    return lax.axis_index("row") % 2 == 0
+
+
 def lane_mask(cols, left, right):
     lanes = lax.broadcasted_iota(jnp.int32, (1, 2 * cols), 1)
     return jnp.where(lanes < cols, 1.0, jnp.where(lanes < cols + cols // 2, right, left))
@@ -105,7 +110,17 @@
     return (state_edge, 0), (adjoint_edge, 2 * state_edge * rows)
 
 
-def strip_body(c_ref, q_ref, edge_ref, *, channels, rows, depth):
+def strip_body(
+    c_hbm, q_hbm, edge_ref, c_ref, q_ref, arrived, *, channels, rows, depth
+):
+    copies = [
+        pltpu.make_async_copy(source, target, arrived.at[place])
+        for place, (source, target) in enumerate(((c_hbm, c_ref), (q_hbm, q_ref)))
+    ]
+    for copy in copies:
+        copy.start()
+    for copy in copies:
+        copy.wait()
     total = jnp.zeros(edge_ref.shape, f32)
     for ref, (edge, low) in zip((c_ref, q_ref), layout(rows, depth)):
         image = [row_of(ref, row, channels, rows) for row in range(rows)]
@@ -114,7 +129,7 @@
 
 
 def message_body(
-    c_ref, q_ref, left_ref, right_ref, top_ref, bottom_ref, side_ref, *, channels, rows, depth
+    c_ref, q_ref, left_ref, right_ref, pair_ref, cross_ref, side_ref, *, channels, rows, depth
 ):
     cols = c_ref.shape[1]
     _, _, left, right = flags()
@@ -122,22 +137,40 @@
     edges = ((c_edge, 0, middle), (q_edge, middle, 2 * cols))
     side = join_edges(left_ref[...], right_ref[...], left, right, edges).astype(bf16)
     side_ref[...] = side
+    even = even_row()
     for which, ref in enumerate((c_ref, q_ref)):
         for row in range(depth):
             place = which * depth + row
-            top_ref[place] = row_of(ref, row, channels, rows).astype(bf16)
-            bottom_ref[place] = row_of(ref, rows - depth + row, channels, rows).astype(bf16)
+            top = row_of(ref, row, channels, rows)
+            bottom = row_of(ref, rows - depth + row, channels, rows)
+            pair_ref[place] = jnp.where(even, bottom, top).astype(bf16)
+            cross_ref[place] = jnp.where(even, top, bottom).astype(bf16)
     for half in range(2):
         part = side[:, half * cols : (half + 1) * cols]
-        top_ref[2 * depth + half] = part
-        bottom_ref[2 * depth + half] = part
-
-
-def strips_of(ref, depth):
-    return jnp.concatenate([ref[2 * depth], ref[2 * depth + 1]], 1).astype(f32)
-
-
-def row_blocks(low, high, body, size=4):
+        pair_ref[2 * depth + half] = part
+        cross_ref[2 * depth + half] = part
+
+
+class Beside:
+    def __init__(self, pair_ref, cross_ref):
+        self.pair, self.cross, self.even = pair_ref, cross_ref, even_row()
+
+    def above(self, place):
+        return jnp.where(
+            self.even, self.cross[place].astype(f32), self.pair[place].astype(f32)
+        )
+
+    def below(self, place):
+        return jnp.where(
+            self.even, self.pair[place].astype(f32), self.cross[place].astype(f32)
+        )
+
+
+def strips_of(get, depth):
+    return jnp.concatenate([get(2 * depth), get(2 * depth + 1)], 1)
+
+
+def row_blocks(low, high, body, size=6):
     turns, rest = divmod(high - low, size)
 
     def turn(number, carry):
@@ -160,7 +193,7 @@
 
 
 def first_body(
-    c_ref, above_ref, below_ref, side_ref, w_ref, f_ref, upper_ref, lower_ref, strip_ref, x_ref, a_ref, a2_ref,
+    c_ref, pair_ref, cross_ref, side_ref, w_ref, f_ref, upper_ref, lower_ref, strip_ref, x_ref, a_ref, a2_ref,
     *, channels, rows, depth,
 ):
     cols = c_ref.shape[1]
@@ -182,11 +215,12 @@
         image.append(beyond)
         put(halo + row, row_of(c_ref, row, channels, rows), beyond)
     strip_ref[...] = fold_edges(image, 2 * depth, 0, jnp.zeros(strip_ref.shape, f32))
-    above_side, below_side = strips_of(above_ref, depth), strips_of(below_ref, depth)
+    beside = Beside(pair_ref, cross_ref)
+    above_side, below_side = strips_of(beside.above, depth), strips_of(beside.below, depth)
     for row in range(depth):
         place = rows - depth + row
-        put(row, above_ref[row].astype(f32), side_lanes(above_side, edge, low, place))
-        put(halo + rows + row, below_ref[row].astype(f32), side_lanes(below_side, edge, low, row))
+        put(row, beside.above(row), side_lanes(above_side, edge, low, place))
+        put(halo + rows + row, beside.below(row), side_lanes(below_side, edge, low, row))
 
     total = rows + 2 * halo
     for layer in range(depth):
@@ -227,19 +261,21 @@
         out_ref[place] = (f_ref[row] + e + moved).astype(bf16)
 
 
-def settle_body(c_ref, *refs, start, strips, channels, rows):
-    arrived, s_ref = refs[strips:-1], refs[-1]
+def settle_body(c_ref, strip_ref, *refs, channels, rows):
+    s_ref = refs[-1]
+    uppers, lowers = refs[: len(refs) // 2], refs[len(refs) // 2 : -1]
     first = lax.axis_index("layer") == 0
-    base = [row_of(c_ref, start + row, channels, rows) for row in range(rows // 2)]
-    base += [ref[...] for ref in refs[:strips]]
-    for place in range(len(base)):
-        value = sum(ref[place].astype(f32) for ref in arrived)
-        s_ref[place] = jnp.where(first, base[place], value).astype(bf16)
+    base = [row_of(c_ref, row, channels, rows) for row in range(rows)] + [strip_ref[...]]
+    for row in range(rows + 1):
+        value = 0.0
+        for upper, lower in zip(uppers, lowers):
+            ref, place = piece_of(upper, lower, row, rows)
+            value = value + ref[place].astype(f32)
+        s_ref[row] = jnp.where(first, base[row], value).astype(bf16)
 
 
 def second_body(
-    c_ref, q_ref, s_up_ref, s_lo_ref, above_up_ref, above_lo_ref, below_up_ref, below_lo_ref,
-    above_ref, below_ref, side_ref, w_ref, wt_ref,
+    c_ref, q_ref, s_ref, s_pair_ref, s_cross_ref, pair_ref, cross_ref, side_ref, w_ref, wt_ref,
     state_ref, g_ref, g_up_ref, g_lo_ref, kept_ref, sent_ref,
     x_ref, a_ref, a2_ref, slope_ref, adj_ref, src_ref,
     *, channels, rows, depth,
@@ -259,29 +295,23 @@
 
     edge = 2 * depth
 
-    def piece(upper, lower, row):
-        ref, place = piece_of(upper, lower, row, rows)
-        return ref[place].astype(f32)
-
-    own_side = piece(s_up_ref, s_lo_ref, rows)
-    above_side = piece(above_up_ref, above_lo_ref, rows)
-    below_side = piece(below_up_ref, below_lo_ref, rows)
+    beside = Beside(s_pair_ref, s_cross_ref)
+    own_side = s_ref[rows].astype(f32)
+    above_side, below_side = beside.above(rows), beside.below(rows)
     for row in range(rows):
-        own = jnp.where(
-            first, row_of(c_ref, row, channels, rows), piece(s_up_ref, s_lo_ref, row)
-        )
+        own = jnp.where(first, row_of(c_ref, row, channels, rows), s_ref[row].astype(f32))
         state_ref[pl.ds(row, channels, stride=rows), :] = own
         put(halo + row, own, side_lanes(own_side, edge, 0, row))
     for row in range(halo):
         place = rows - halo + row
         put(
             row,
-            piece(above_up_ref, above_lo_ref, place),
+            beside.above(place),
             side_lanes(above_side, edge, 0, place),
         )
         put(
             halo + rows + row,
-            piece(below_up_ref, below_lo_ref, row),
+            beside.below(row),
             side_lanes(below_side, edge, 0, row),
         )
 
@@ -291,7 +321,8 @@
 
     _, (edge, low) = layout(rows, depth)
     own_side = side_ref[...].astype(f32)
-    above_side, below_side = strips_of(above_ref, depth), strips_of(below_ref, depth)
+    beside = Beside(pair_ref, cross_ref)
+    above_side, below_side = strips_of(beside.above, depth), strips_of(beside.below, depth)
     for row in range(rows):
         put_adj(
             halo + row, row_of(q_ref, row, channels, rows), side_lanes(own_side, edge, low, row)
@@ -300,12 +331,12 @@
         place = rows - depth + row
         put_adj(
             halo - depth + row,
-            above_ref[depth + row].astype(f32),
+            beside.above(depth + row),
             side_lanes(above_side, edge, low, place),
         )
         put_adj(
             halo + rows + row,
-            below_ref[depth + row].astype(f32),
+            beside.below(depth + row),
             side_lanes(below_side, edge, low, row),
         )
 
@@ -402,6 +433,13 @@
     return lax.ppermute(array, axis, pairs)
 
 
+def exchanged(to_pair, to_cross):
+    rows = lax.axis_size("row")
+    pairs = [(r, r ^ 1) for r in range(rows)]
+    crossing = [(r, r + 1 if r % 2 else r - 1) for r in range(1, rows - 1)]
+    return lax.ppermute(to_pair, "row", pairs), lax.ppermute(to_cross, "row", crossing)
+
+
 def from_sides(array):
     if lax.axis_size("col") == 2:
         other = lax.ppermute(array, "col", [(0, 1), (1, 0)])
@@ -449,24 +487,29 @@
     strip_f = jax.ShapeDtypeStruct((channels, cols), f32)
     wide_b = jax.ShapeDtypeStruct((channels, 2 * cols), bf16)
     half = rows // 2
-    more_f, upper_b, lower_b, message_b = (
+    more_f, more_b, upper_b, lower_b, message_b = (
         jax.ShapeDtypeStruct((count, channels, cols), kind)
         for count, kind in (
-            (rows + 1, f32), (half + 1, bf16), (half, bf16), (2 * depth + 2, bf16)
-        )
-    )
-
-    edges = call(functools.partial(strip_body, depth=depth, **sizes), wide_b)(c_flat, q_flat)
+            (rows + 1, f32), (rows + 1, bf16), (half + 1, bf16), (half, bf16),
+            (2 * depth + 2, bf16),
+        )
+    )
+
+    edges = call(
+        functools.partial(strip_body, depth=depth, **sizes),
+        wide_b,
+        [pltpu.VMEM(flat, f32), pltpu.VMEM(flat, f32), pltpu.SemaphoreType.DMA((2,))],
+        in_specs=[pl.BlockSpec(memory_space=pltpu.HBM)] * 2,
+    )(c_flat, q_flat)
     left, right = from_sides(edges)
-    top, bottom, side = call(
+    to_pair, to_cross, side = call(
         functools.partial(message_body, depth=depth, **sizes), (message_b, message_b, wide_b)
     )(c_flat, q_flat, left, right)
-    above = shifted(bottom, "row", 1)
-    below = shifted(top, "row", -1)
+    pair, cross = exchanged(to_pair, to_cross)
 
     taps = weights.reshape(depth, channels, 3, 3, channels)
     w_fwd = jnp.transpose(taps, (0, 3, 1, 2, 4)).reshape(depth, 3 * channels, 3 * channels)
-    later_taps, _ = lax.optimization_barrier((taps, top))
+    later_taps, _ = lax.optimization_barrier((taps, to_pair))
     w_back = jnp.transpose(later_taps[:, :, ::-1, ::-1, :], (0, 3, 4, 2, 1)).reshape(
         depth, 3 * channels, 3 * channels
     )
@@ -489,7 +532,7 @@
             pltpu.VMEM((total, channels, lanes), bf16),
         ],
         flops=mac * 44,
-    )(c_flat, above, below, side, w_fwd)
+    )(c_flat, pair, cross, side, w_fwd)
 
     def chain(pieces, target, matrix, order):
         sendings = [piece[0] for piece in pieces]
@@ -514,16 +557,10 @@
         m_fwd,
         [(k, k + 1) for k in range(groups - 1)],
     )
-    tiles = []
-    for start, kind, strips, arrived in (
-        (0, upper_b, (strip,), uppers),
-        (half, lower_b, (), lowers),
-    ):
-        s = call(
-            functools.partial(settle_body, start=start, strips=len(strips), **sizes), kind
-        )(c_flat, *strips, *arrived)
-        tiles.append((s, shifted(s, "row", 1), shifted(s, "row", -1)))
-    pieces = [part for parts in zip(*tiles) for part in parts]
+    s = call(functools.partial(settle_body, **sizes), more_b)(
+        c_flat, strip, *uppers, *lowers
+    )
+    s_pair, s_cross = exchanged(s, s)
 
     total = rows + 4 * depth
     state, g, g_upper, g_lower, kept, sources = call(
@@ -545,7 +582,7 @@
             pltpu.VMEM((total, channels, lanes), bf16),
         ],
         flops=mac * 120,
-    )(c_flat, q_flat, *pieces, above, below, side, w_fwd, w_back)
+    )(c_flat, q_flat, s, s_pair, s_cross, pair, cross, side, w_fwd, w_back)
     uppers, lowers = chain(
         ((g_upper, 0, (q_flat,)), (g_lower, half, (q_flat,))),
         g,

time: 83.9 us -> 72.7 us (0.87)
  starting transfers between devices: 42.6 us -> 36.2 us
  Pallas kernels: 21.5 us -> 17.5 us
    ppermute x6 -> x4, starting transfers between devices: 17.7 us -> 10.9 us  [the longest x2 9.6 us: exchanged(): lax.ppermute(to_pair, 'row', pairs)]
    pallas_call x1, Pallas kernels: 12.9 us -> 10.2 us  [local(): call(functools.partial(second_body, depth=depth, **sizes), (jax.ShapeDtyp...]
    ppermute x6 -> x4, waiting for transfers between devices: 2.73 us -> 0.9 us  [the longest x2 0.89 us: exchanged(): lax.ppermute(to_pair, 'row', pairs)]
    ppermute x12, waiting for transfers between devices: 4.11 us -> 5.51 us  [chain(): arrived = [lax.ppermute(sending, 'layer', [hop]) for sending in sendings]]
    pallas_call x1, Pallas kernels: 4.76 us -> 3.39 us  [local(): call(functools.partial(first_body, depth=depth, **sizes), (more_f, upper_...]
  transfers between devices with their start and end apart: 23 -> 21, of which waited for: 7 -> 7; matrix products, arithmetic and copies ran while one was open for 3% -> 4% of each run, Pallas kernels for 4% -> 5%
where the time goes in v5:
time: 72.7 us; the launch traced here: 72.3 us
  starting transfers between devices  36.2 us (50%)
  Pallas kernels  17.5 us (24%)
  waiting for transfers between devices  12 us (17%)
  local copies, waits for them, and re-layouts  4.33 us (6%)
  other arithmetic  1.25 us (2%)
  between operations  1.02 us (1%)
    ppermute x12, starting transfers between devices, chain(): arrived = [lax.ppermute(sending, 'layer', [hop]) for sending in sendings]  13 us
    pallas_call x1, Pallas kernels, local(): call(functools.partial(second_body, depth=depth, **sizes), (jax.ShapeDtyp...  10.2 us
    ppermute x2, starting transfers between devices, exchanged(): lax.ppermute(to_pair, 'row', pairs)  9.6 us
    ppermute x12, waiting for transfers between devices, chain(): arrived = [lax.ppermute(sending, 'layer', [hop]) for sending in sendings]  5.51 us
    ppermute x1, starting transfers between devices, total_over_tiles(): other = lax.ppermute(value, 'row', pair)  4.46 us
    ppermute x2, waiting for transfers between devices, total_over_tiles(): arrived = lax.ppermute(rounded, ('row', 'col'), pairs)  3.98 us
    ppermute x1, starting transfers between devices, total_over_tiles(): value = own + lax.ppermute(sent, 'row', pair)  3.53 us
    pallas_call x1, Pallas kernels, local(): call(functools.partial(first_body, depth=depth, **sizes), (more_f, upper_...  3.39 us
  transfers between devices with their start and end apart: 21, of which 7 were waited for; matrix products, arithmetic and copies ran while one was open for 4% of the time, Pallas kernels for 5%

profile of v5, /device:TPU:19, one launch (start us, length us, event | category | flops | bytes accessed | tf_op | source)
XLA Modules:
  0.0 72.3 jit_solution(5099343801871150675)
XLA Ops:
  0.6 0.9 %copy-done = f32[1,64,8,128]{3,2,1,0:T(8,128)S(1)} copy-done((f32[1,64,8,128]{3,2,1,0:T(8,128)S(1)}, f32[1,64,8,128]{3,2,1,0:T(8,128)}, u32[]{:S(2)}) %copy-start) | copy-done | bytes 262168
  1.6 0.9 %copy-done.2 = f32[1,64,8,128]{3,2,1,0:T(8,128)S(1)} copy-done((f32[1,64,8,128]{3,2,1,0:T(8,128)S(1)}, f32[1,64,8,128]{3,2,1,0:T(8,128)}, u32[]{:S(2)}) %copy-start.2) | copy-done | bytes 262168
  2.7 1.3 %collective-permute-start = (bf16[64,256]{1,0:T(8,128)(2,1)S(1)}, bf16[64,256]{1,0:T(8,128)(2,1)S(1)}, u32[]{:S(2)}, u32[]{:S(2)}) collective-permute-start(bf16[64,256]{1,0:T(8,128)(2,1)S(1)} %shard_map.58), channel_id=1, source_target_pairs={{0,1},{1,0},{2,3},{3,2},{4,5},{5,4},{6,7},{7,6},{8,9},{9,8},{10,11... | collective-permute-start | bytes 98312 | tf_op jit(solution)/shard_map/ppermute | solution.py:445
  4.4 1.1 %collective-permute-done.left_ref.right_ref = bf16[64,256]{1,0:T(8,128)(2,1)S(1)} collective-permute-done((bf16[64,256]{1,0:T(8,128)(2,1)S(1)}, bf16[64,256]{1,0:T(8,128)(2,1)S(1)}, u32[]{:S(2)}, u32[]{:S(2)}) %collective-permute-start) | collective-permute-done | bytes 32800 | tf_op jit(solution)/shard_map/ppermute | solution.py:445
  5.7 0.7 collective-permute-start.2
  6.4 3.1 %collective-permute-start.1 = (bf16[10,64,128]{2,1,0:T(8,128)(2,1)S(1)}, bf16[10,64,128]{2,1,0:T(8,128)(2,1)S(1)}, u32[]{:S(2)}, u32[]{:S(2)}) collective-permute-start(bf16[10,64,128]{2,1,0:T(8,128)(2,1)S(1)} %get-tuple-element.19), channel_id=1, source_target_pairs={{0,2},{2,0},{4,6},{6,4},{1,3},{3,1},{5,7},{7,5},{8,10},{10,8},{12,... | collective-permute-start | bytes 491528 | tf_op jit(solution)/shard_map/ppermute | solution.py:440
  11.6 3.4 %shard_map.60 = (f32[9,64,128]{2,1,0:T(8,128)S(1)}, bf16[5,64,128]{2,1,0:T(8,128)(2,1)S(1)}, bf16[4,64,128]{2,1,0:T(8,128)(2,1)S(1)}, f32[64,128]{1,0:T(8,128)S(1)}) custom-call(f32[512,128]{1,0:T(8,128)S(1)} %bitcast.20, bf16[10,64,128]{2,1,0:T(8,128)(2,1)S(1)} %collective-permute-done.1.pair_ref, ...), custom_call_target="tpu_custom_call" | custom-call | flops 830472192 | tf_op jit(solution)/shard_map/pallas_call | solution.py:526
  15.0 0.7 collective-permute-start.3
  15.8 0.7 collective-permute-start.6
  16.7 1.3 %collective-permute-start.4 = (bf16[5,64,128]{2,1,0:T(8,128)(2,1)S(1)}, bf16[5,64,128]{2,1,0:T(8,128)(2,1)S(1)}, u32[]{:S(2)}, u32[]{:S(2)}) collective-permute-start(bf16[5,64,128]{2,1,0:T(8,128)(2,1)S(1)} %shard_map.61), channel_id=1, source_target_pairs={{8,16},{9,17},{10,18},{11,19},{12,20},{13,21},{14,22},{15,23}} | collective-permute-start | bytes 245768 | tf_op jit(solution)/shard_map/ppermute | solution.py:541
  18.2 1.3 %collective-permute-start.7 = (bf16[4,64,128]{2,1,0:T(8,128)(2,1)S(1)}, bf16[4,64,128]{2,1,0:T(8,128)(2,1)S(1)}, u32[]{:S(2)}, u32[]{:S(2)}) collective-permute-start(bf16[4,64,128]{2,1,0:T(8,128)(2,1)S(1)} %shard_map.63), channel_id=1, source_target_pairs={{8,16},{9,17},{10,18},{11,19},{12,20},{13,21},{14,22},{15,23}} | collective-permute-start | bytes 196616 | tf_op jit(solution)/shard_map/ppermute | solution.py:541
  19.5 4.2 %collective-permute-done.4.s_ref.refs_1_ = bf16[5,64,128]{2,1,0:T(8,128)(2,1)S(1)} collective-permute-done((bf16[5,64,128]{2,1,0:T(8,128)(2,1)S(1)}, bf16[5,64,128]{2,1,0:T(8,128)(2,1)S(1)}, u32[]{:S(2)}, u32[]{:S(2)}) %collective-permute-start.4) | collective-permute-done | bytes 81952 | tf_op jit(solution)/shard_map/ppermute | solution.py:541
  23.9 1.3 %collective-permute-start.5 = (bf16[5,64,128]{2,1,0:T(8,128)(2,1)S(1)}, bf16[5,64,128]{2,1,0:T(8,128)(2,1)S(1)}, u32[]{:S(2)}, u32[]{:S(2)}) collective-permute-start(bf16[5,64,128]{2,1,0:T(8,128)(2,1)S(1)} %shard_map.62), channel_id=1, source_target_pairs={{16,24},{17,25},{18,26},{19,27},{20,28},{21,29},{22,30},{23,31}} | collective-permute-start | bytes 245768 | tf_op jit(solution)/shard_map/ppermute | solution.py:541
  25.4 1.3 %collective-permute-start.8 = (bf16[4,64,128]{2,1,0:T(8,128)(2,1)S(1)}, bf16[4,64,128]{2,1,0:T(8,128)(2,1)S(1)}, u32[]{:S(2)}, u32[]{:S(2)}) collective-permute-start(bf16[4,64,128]{2,1,0:T(8,128)(2,1)S(1)} %shard_map.64), channel_id=1, source_target_pairs={{16,24},{17,25},{18,26},{19,27},{20,28},{21,29},{22,30},{23,31}} | collective-permute-start | bytes 196616 | tf_op jit(solution)/shard_map/ppermute | solution.py:541
  26.7 1.3 %collective-permute-done.8.refs_5_ = bf16[4,64,128]{2,1,0:T(8,128)(2,1)S(1)} collective-permute-done((bf16[4,64,128]{2,1,0:T(8,128)(2,1)S(1)}, bf16[4,64,128]{2,1,0:T(8,128)(2,1)S(1)}, u32[]{:S(2)}, u32[]{:S(2)}) %collective-permute-start.8) | collective-permute-done | bytes 65568 | tf_op jit(solution)/shard_map/ppermute | solution.py:541
  28.1 0.7 collective-permute-start.10
  28.8 6.5 %collective-permute-start.9 = (bf16[9,64,128]{2,1,0:T(8,128)(2,1)S(1)}, bf16[9,64,128]{2,1,0:T(8,128)(2,1)S(1)}, u32[]{:S(2)}, u32[]{:S(2)}) collective-permute-start(bf16[9,64,128]{2,1,0:T(8,128)(2,1)S(1)} %shard_map.65.s_ref), channel_id=1, source_target_pairs={{0,2},{2,0},{4,6},{6,4},{1,3},{3,1},{5,7},{7,5},{8,10},{10,8},{12,... | collective-permute-start | bytes 442376 | tf_op jit(solution)/shard_map/ppermute | solution.py:440
  35.3 0.9 %collective-permute-done.9.s_pair_ref = bf16[9,64,128]{2,1,0:T(8,128)(2,1)S(1)} collective-permute-done((bf16[9,64,128]{2,1,0:T(8,128)(2,1)S(1)}, bf16[9,64,128]{2,1,0:T(8,128)(2,1)S(1)}, u32[]{:S(2)}, u32[]{:S(2)}) %collective-permute-start.9) | collective-permute-done | bytes 147488 | tf_op jit(solution)/shard_map/ppermute | solution.py:440
  36.2 10.2 %shard_map.66 = (f32[512,128]{1,0:T(8,128)}, f32[8,64,128]{2,1,0:T(8,128)S(1)}, bf16[4,64,128]{2,1,0:T(8,128)(2,1)S(1)}, bf16[4,64,128]{2,1,0:T(8,128)(2,1)S(1)}...) custom-call(f32[512,128]{1,0:T(8,128)S(1)} %bitcast.26, f32[512,128]{1,0:T(8,128)S(1)} %bitcast.29, ...), custom_call_target="tpu_custom_call" | custom-call | flops 2264924160 | tf_op jit(solution)/shard_map/pallas_call | solution.py:566
  46.5 1.3 %collective-permute-start.11 = (bf16[4,64,128]{2,1,0:T(8,128)(2,1)S(1)}, bf16[4,64,128]{2,1,0:T(8,128)(2,1)S(1)}, u32[]{:S(2)}, u32[]{:S(2)}) collective-permute-start(bf16[4,64,128]{2,1,0:T(8,128)(2,1)S(1)} %get-tuple-element.30), channel_id=1, source_target_pairs={{24,16},{25,17},{26,18},{27,19},{28,20},{29,21},{30,22},{31,23}} | collective-permute-start | bytes 196616 | tf_op jit(solution)/shard_map/ppermute | solution.py:541
  47.8 1.3 %collective-permute-start.14 = (bf16[4,64,128]{2,1,0:T(8,128)(2,1)S(1)}, bf16[4,64,128]{2,1,0:T(8,128)(2,1)S(1)}, u32[]{:S(2)}, u32[]{:S(2)}) collective-permute-start(bf16[4,64,128]{2,1,0:T(8,128)(2,1)S(1)} %get-tuple-element.32), channel_id=1, source_target_pairs={{24,16},{25,17},{26,18},{27,19},{28,20},{29,21},{30,22},{31,23}} | collective-permute-start | bytes 196616 | tf_op jit(solution)/shard_map/ppermute | solution.py:541
  49.1 1.1 %shard_map.72 = f32[4,64,576]{2,1,0:T(8,128)S(1)} custom-call(bf16[4,8,64,256]{3,2,1,0:T(8,128)(2,1)S(1)} %get-tuple-element.33.kept_ref, bf16[4,10,64,128]{3,2,1,0:T(8,128)(2,1)S(1)} %get-tuple-element.34.sent_ref), custom_call_target="tpu_custom_call" | custom-call | flops 1000000000 | tf_op jit(solution)/shard_map/pallas_call | solution.py:592
  50.2 3.5 %collective-permute-start.17 = (f32[2,64,576]{2,1,0:T(8,128)S(1)}, f32[2,64,576]{2,1,0:T(8,128)S(1)}, u32[]{:S(2)}, u32[]{:S(2)}) collective-permute-start(f32[2,64,576]{2,1,0:T(8,128)S(1)} %slice_select_fusion), channel_id=1, source_target_pairs={{0,2},{2,0},{4,6},{6,4},{1,3},{3,1},{5,7},{7,5},{8,10},{10,8},{12,... | collective-permute-start | bytes 884744 | tf_op jit(solution)/shard_map/ppermute | solution.py:458
  54.0 1.3 %collective-permute-start.12 = (bf16[4,64,128]{2,1,0:T(8,128)(2,1)S(1)}, bf16[4,64,128]{2,1,0:T(8,128)(2,1)S(1)}, u32[]{:S(2)}, u32[]{:S(2)}) collective-permute-start(bf16[4,64,128]{2,1,0:T(8,128)(2,1)S(1)} %shard_map.67), channel_id=1, source_target_pairs={{16,8},{17,9},{18,10},{19,11},{20,12},{21,13},{22,14},{23,15}} | collective-permute-start | bytes 196616 | tf_op jit(solution)/shard_map/ppermute | solution.py:541
  55.5 1.3 %collective-permute-start.15 = (bf16[4,64,128]{2,1,0:T(8,128)(2,1)S(1)}, bf16[4,64,128]{2,1,0:T(8,128)(2,1)S(1)}, u32[]{:S(2)}, u32[]{:S(2)}) collective-permute-start(bf16[4,64,128]{2,1,0:T(8,128)(2,1)S(1)} %shard_map.69), channel_id=1, source_target_pairs={{16,8},{17,9},{18,10},{19,11},{20,12},{21,13},{22,14},{23,15}} | collective-permute-start | bytes 196616 | tf_op jit(solution)/shard_map/ppermute | solution.py:541
  56.8 1.3 %collective-permute-start.18 = (bf16[2,64,576]{2,1,0:T(8,128)(2,1)S(1)}, bf16[2,64,576]{2,1,0:T(8,128)(2,1)S(1)}, u32[]{:S(2)}, u32[]{:S(2)}) collective-permute-start(bf16[2,64,576]{2,1,0:T(8,128)(2,1)S(1)} %add_convert_fusion.1), channel_id=1, source_target_pairs={{0,4},{1,5},{2,3},{3,2},{4,0},{5,1},{6,7},{7,6},{8,12},{9,13},{10,... | collective-permute-start | bytes 442376 | tf_op jit(solution)/shard_map/ppermute | solution.py:470
  59.0 2.1 %collective-permute-done.18 = bf16[2,64,576]{2,1,0:T(8,128)(2,1)S(1)} collective-permute-done((bf16[2,64,576]{2,1,0:T(8,128)(2,1)S(1)}, bf16[2,64,576]{2,1,0:T(8,128)(2,1)S(1)}, u32[]{:S(2)}, u32[]{:S(2)}) %collective-permute-start.18) | collective-permute-done | bytes 147488 | tf_op jit(solution)/shard_map/ppermute | solution.py:470
  61.1 1.7 %collective-permute-start.19 = (bf16[2,64,576]{2,1,0:T(8,128)(2,1)S(1)}, bf16[2,64,576]{2,1,0:T(8,128)(2,1)S(1)}, u32[]{:S(2)}, u32[]{:S(2)}) collective-permute-start(bf16[2,64,576]{2,1,0:T(8,128)(2,1)S(1)} %add_convert_fusion), channel_id=1, source_target_pairs={{0,1},{1,0},{2,6},{3,7},{4,5},{5,4},{6,2},{7,3},{8,9},{9,8},{10,14... | collective-permute-start | bytes 442376 | tf_op jit(solution)/shard_map/ppermute | solution.py:470
  63.7 1.9 %collective-permute-done.19 = bf16[2,64,576]{2,1,0:T(8,128)(2,1)S(1)} collective-permute-done((bf16[2,64,576]{2,1,0:T(8,128)(2,1)S(1)}, bf16[2,64,576]{2,1,0:T(8,128)(2,1)S(1)}, u32[]{:S(2)}, u32[]{:S(2)}) %collective-permute-start.19) | collective-permute-done | bytes 147488 | tf_op jit(solution)/shard_map/ppermute | solution.py:470
  65.7 4.5 %collective-permute-start.20 = (f32[2,64,576]{2,1,0:T(8,128)S(1)}, f32[2,64,576]{2,1,0:T(8,128)S(1)}, u32[]{:S(2)}, u32[]{:S(2)}) collective-permute-start(f32[2,64,576]{2,1,0:T(8,128)S(1)} %convert_add_fusion), channel_id=1, source_target_pairs={{0,2},{2,0},{4,6},{6,4},{1,3},{3,1},{5,7},{7,5},{8,10},{10,8},{12,... | collective-permute-start | bytes 884744 | tf_op jit(solution)/shard_map/ppermute | solution.py:472
  70.1 0.8 %shard_map.71 = f32[512,128]{1,0:T(8,128)} custom-call(f32[512,128]{1,0:T(8,128)S(1)} %bitcast.34, bf16[4,64,128]{2,1,0:T(8,128)(2,1)S(1)} %collective-permute-done.11.s_ref.refs_0_, bf16[4,64,128]{2,1,0:T(8,128)(2,1)S(1)} %collective-permute-done.12.s_ref.refs_1_, bf16[4,64,128]{2,1,0:T(8,128)(2,1)S(1)} %collective-permute-done.13.refs_2_, ...), custom_call_target="tpu_custom_call" | custom-call | flops 10000000000 | tf_op jit(solution)/shard_map/pallas_call | solution.py:598
  71.5 0.9 %pad_maximum_fusion = f32[4,64,576]{2,1,0:T(8,128)} fusion(f32[2,64,576]{2,1,0:T(8,128)S(1)} %get-tuple-element.36, f32[2,64,576]{2,1,0:T(8,128)S(1)} %get-tuple-element.35), kind=kLoop, calls=%fused_computation | loop fusion | flops 147456 | bytes 1179648 | tf_op jit(solution)/shard_map/concatenate | solution.py:475
  (54 shorter events, 6.6 us)
Async XLA Ops:
  0.6 1.0 %copy-start = (f32[1,64,8,128]{3,2,1,0:T(8,128)S(1)}, f32[1,64,8,128]{3,2,1,0:T(8,128)}, u32[]{:S(2)}) copy-start(f32[1,64,8,128]{3,2,1,0:T(8,128)} %param.3) | copy-start | bytes 786436
  1.6 0.9 %copy-start.2 = (f32[1,64,8,128]{3,2,1,0:T(8,128)S(1)}, f32[1,64,8,128]{3,2,1,0:T(8,128)}, u32[]{:S(2)}) copy-start(f32[1,64,8,128]{3,2,1,0:T(8,128)} %param.4) | copy-start | bytes 786436
  2.5 1.5 %copy-start.4 = (bf16[4,64,576]{2,1,0:T(8,128)(2,1)S(1)}, bf16[4,64,576]{2,1,0:T(8,128)(2,1)}, u32[]{:S(2)}) copy-start(bf16[4,64,576]{2,1,0:T(8,128)(2,1)} %param.5) | copy-start | bytes 884740
  2.7 2.8 %collective-permute-start = (bf16[64,256]{1,0:T(8,128)(2,1)S(1)}, bf16[64,256]{1,0:T(8,128)(2,1)S(1)}, u32[]{:S(2)}, u32[]{:S(2)}) collective-permute-start(bf16[64,256]{1,0:T(8,128)(2,1)S(1)} %shard_map.58), channel_id=1, source_target_pairs={{0,1},{1,0},{2,3},{3,2},{4,5},{5,4},{6,7},{7,6},{8,9},{9,8},{10,11... | collective-permute-start | bytes 98312 | tf_op jit(solution)/shard_map/ppermute | solution.py:445
  4.1 1.5 %copy-start.3 = (f32[1,64,8,128]{3,2,1,0:T(8,128)S(1)}, f32[1,64,8,128]{3,2,1,0:T(8,128)}, u32[]{:S(2)}) copy-start(f32[1,64,8,128]{3,2,1,0:T(8,128)} %param.4) | copy-start | bytes 786436
  4.4 1.2 %copy-start.1 = (f32[1,64,8,128]{3,2,1,0:T(8,128)S(1)}, f32[1,64,8,128]{3,2,1,0:T(8,128)}, u32[]{:S(2)}) copy-start(f32[1,64,8,128]{3,2,1,0:T(8,128)} %param.3) | copy-start | bytes 786436
  5.7 5.9 %collective-permute-start.2 = (bf16[10,64,128]{2,1,0:T(8,128)(2,1)S(1)}, bf16[10,64,128]{2,1,0:T(8,128)(2,1)S(1)}, u32[]{:S(2)}, u32[]{:S(2)}) collective-permute-start(bf16[10,64,128]{2,1,0:T(8,128)(2,1)S(1)} %get-tuple-element.20), channel_id=1, source_target_pairs={{2,4},{4,2},{3,5},{5,3},{10,12},{12,10},{11,13},{13,11},{18,20},{2... | collective-permute-start | bytes 491528 | tf_op jit(solution)/shard_map/ppermute | solution.py:440
  6.4 5.2 %collective-permute-start.1 = (bf16[10,64,128]{2,1,0:T(8,128)(2,1)S(1)}, bf16[10,64,128]{2,1,0:T(8,128)(2,1)S(1)}, u32[]{:S(2)}, u32[]{:S(2)}) collective-permute-start(bf16[10,64,128]{2,1,0:T(8,128)(2,1)S(1)} %get-tuple-element.19), channel_id=1, source_target_pairs={{0,2},{2,0},{4,6},{6,4},{1,3},{3,1},{5,7},{7,5},{8,10},{10,8},{12,... | collective-permute-start | bytes 491528 | tf_op jit(solution)/shard_map/ppermute | solution.py:440
  15.0 1.5 %collective-permute-start.3 = (bf16[5,64,128]{2,1,0:T(8,128)(2,1)S(1)}, bf16[5,64,128]{2,1,0:T(8,128)(2,1)S(1)}, u32[]{:S(2)}, u32[]{:S(2)}) collective-permute-start(bf16[5,64,128]{2,1,0:T(8,128)(2,1)S(1)} %get-tuple-element.25), channel_id=1, source_target_pairs={{0,8},{1,9},{2,10},{3,11},{4,12},{5,13},{6,14},{7,15}} | collective-permute-start | bytes 245768 | tf_op jit(solution)/shard_map/ppermute | solution.py:541
  15.8 2.2 %collective-permute-start.6 = (bf16[4,64,128]{2,1,0:T(8,128)(2,1)S(1)}, bf16[4,64,128]{2,1,0:T(8,128)(2,1)S(1)}, u32[]{:S(2)}, u32[]{:S(2)}) collective-permute-start(bf16[4,64,128]{2,1,0:T(8,128)(2,1)S(1)} %get-tuple-element.27), channel_id=1, source_target_pairs={{0,8},{1,9},{2,10},{3,11},{4,12},{5,13},{6,14},{7,15}} | collective-permute-start | bytes 196616 | tf_op jit(solution)/shard_map/ppermute | solution.py:541
  16.7 7.0 %collective-permute-start.4 = (bf16[5,64,128]{2,1,0:T(8,128)(2,1)S(1)}, bf16[5,64,128]{2,1,0:T(8,128)(2,1)S(1)}, u32[]{:S(2)}, u32[]{:S(2)}) collective-permute-start(bf16[5,64,128]{2,1,0:T(8,128)(2,1)S(1)} %shard_map.61), channel_id=1, source_target_pairs={{8,16},{9,17},{10,18},{11,19},{12,20},{13,21},{14,22},{15,23}} | collective-permute-start | bytes 245768 | tf_op jit(solution)/shard_map/ppermute | solution.py:541
  18.2 7.0 %collective-permute-start.7 = (bf16[4,64,128]{2,1,0:T(8,128)(2,1)S(1)}, bf16[4,64,128]{2,1,0:T(8,128)(2,1)S(1)}, u32[]{:S(2)}, u32[]{:S(2)}) collective-permute-start(bf16[4,64,128]{2,1,0:T(8,128)(2,1)S(1)} %shard_map.63), channel_id=1, source_target_pairs={{8,16},{9,17},{10,18},{11,19},{12,20},{13,21},{14,22},{15,23}} | collective-permute-start | bytes 196616 | tf_op jit(solution)/shard_map/ppermute | solution.py:541
  23.9 4.1 %collective-permute-start.5 = (bf16[5,64,128]{2,1,0:T(8,128)(2,1)S(1)}, bf16[5,64,128]{2,1,0:T(8,128)(2,1)S(1)}, u32[]{:S(2)}, u32[]{:S(2)}) collective-permute-start(bf16[5,64,128]{2,1,0:T(8,128)(2,1)S(1)} %shard_map.62), channel_id=1, source_target_pairs={{16,24},{17,25},{18,26},{19,27},{20,28},{21,29},{22,30},{23,31}} | collective-permute-start | bytes 245768 | tf_op jit(solution)/shard_map/ppermute | solution.py:541
  25.4 2.6 %collective-permute-start.8 = (bf16[4,64,128]{2,1,0:T(8,128)(2,1)S(1)}, bf16[4,64,128]{2,1,0:T(8,128)(2,1)S(1)}, u32[]{:S(2)}, u32[]{:S(2)}) collective-permute-start(bf16[4,64,128]{2,1,0:T(8,128)(2,1)S(1)} %shard_map.64), channel_id=1, source_target_pairs={{16,24},{17,25},{18,26},{19,27},{20,28},{21,29},{22,30},{23,31}} | collective-permute-start | bytes 196616 | tf_op jit(solution)/shard_map/ppermute | solution.py:541
  28.1 7.2 %collective-permute-start.10 = (bf16[9,64,128]{2,1,0:T(8,128)(2,1)S(1)}, bf16[9,64,128]{2,1,0:T(8,128)(2,1)S(1)}, u32[]{:S(2)}, u32[]{:S(2)}) collective-permute-start(bf16[9,64,128]{2,1,0:T(8,128)(2,1)S(1)} %shard_map.65.s_ref), channel_id=1, source_target_pairs={{2,4},{4,2},{3,5},{5,3},{10,12},{12,10},{11,13},{13,11},{18,20},{2... | collective-permute-start | bytes 442376 | tf_op jit(solution)/shard_map/ppermute | solution.py:440
  28.8 7.5 %collective-permute-start.9 = (bf16[9,64,128]{2,1,0:T(8,128)(2,1)S(1)}, bf16[9,64,128]{2,1,0:T(8,128)(2,1)S(1)}, u32[]{:S(2)}, u32[]{:S(2)}) collective-permute-start(bf16[9,64,128]{2,1,0:T(8,128)(2,1)S(1)} %shard_map.65.s_ref), channel_id=1, source_target_pairs={{0,2},{2,0},{4,6},{6,4},{1,3},{3,1},{5,7},{7,5},{8,10},{10,8},{12,... | collective-permute-start | bytes 442376 | tf_op jit(solution)/shard_map/ppermute | solution.py:440
  46.5 7.3 %collective-permute-start.11 = (bf16[4,64,128]{2,1,0:T(8,128)(2,1)S(1)}, bf16[4,64,128]{2,1,0:T(8,128)(2,1)S(1)}, u32[]{:S(2)}, u32[]{:S(2)}) collective-permute-start(bf16[4,64,128]{2,1,0:T(8,128)(2,1)S(1)} %get-tuple-element.30), channel_id=1, source_target_pairs={{24,16},{25,17},{26,18},{27,19},{28,20},{29,21},{30,22},{31,23}} | collective-permute-start | bytes 196616 | tf_op jit(solution)/shard_map/ppermute | solution.py:541
  47.8 7.5 %collective-permute-start.14 = (bf16[4,64,128]{2,1,0:T(8,128)(2,1)S(1)}, bf16[4,64,128]{2,1,0:T(8,128)(2,1)S(1)}, u32[]{:S(2)}, u32[]{:S(2)}) collective-permute-start(bf16[4,64,128]{2,1,0:T(8,128)(2,1)S(1)} %get-tuple-element.32), channel_id=1, source_target_pairs={{24,16},{25,17},{26,18},{27,19},{28,20},{29,21},{30,22},{31,23}} | collective-permute-start | bytes 196616 | tf_op jit(solution)/shard_map/ppermute | solution.py:541
  50.2 6.6 %collective-permute-start.17 = (f32[2,64,576]{2,1,0:T(8,128)S(1)}, f32[2,64,576]{2,1,0:T(8,128)S(1)}, u32[]{:S(2)}, u32[]{:S(2)}) collective-permute-start(f32[2,64,576]{2,1,0:T(8,128)S(1)} %slice_select_fusion), channel_id=1, source_target_pairs={{0,2},{2,0},{4,6},{6,4},{1,3},{3,1},{5,7},{7,5},{8,10},{10,8},{12,... | collective-permute-start | bytes 884744 | tf_op jit(solution)/shard_map/ppermute | solution.py:458
  54.0 4.2 %collective-permute-start.12 = (bf16[4,64,128]{2,1,0:T(8,128)(2,1)S(1)}, bf16[4,64,128]{2,1,0:T(8,128)(2,1)S(1)}, u32[]{:S(2)}, u32[]{:S(2)}) collective-permute-start(bf16[4,64,128]{2,1,0:T(8,128)(2,1)S(1)} %shard_map.67), channel_id=1, source_target_pairs={{16,8},{17,9},{18,10},{19,11},{20,12},{21,13},{22,14},{23,15}} | collective-permute-start | bytes 196616 | tf_op jit(solution)/shard_map/ppermute | solution.py:541
  55.5 7.4 %collective-permute-start.15 = (bf16[4,64,128]{2,1,0:T(8,128)(2,1)S(1)}, bf16[4,64,128]{2,1,0:T(8,128)(2,1)S(1)}, u32[]{:S(2)}, u32[]{:S(2)}) collective-permute-start(bf16[4,64,128]{2,1,0:T(8,128)(2,1)S(1)} %shard_map.69), channel_id=1, source_target_pairs={{16,8},{17,9},{18,10},{19,11},{20,12},{21,13},{22,14},{23,15}} | collective-permute-start | bytes 196616 | tf_op jit(solution)/shard_map/ppermute | solution.py:541
  56.8 4.2 %collective-permute-start.18 = (bf16[2,64,576]{2,1,0:T(8,128)(2,1)S(1)}, bf16[2,64,576]{2,1,0:T(8,128)(2,1)S(1)}, u32[]{:S(2)}, u32[]{:S(2)}) collective-permute-start(bf16[2,64,576]{2,1,0:T(8,128)(2,1)S(1)} %add_convert_fusion.1), channel_id=1, source_target_pairs={{0,4},{1,5},{2,3},{3,2},{4,0},{5,1},{6,7},{7,6},{8,12},{9,13},{10,... | collective-permute-start | bytes 442376 | tf_op jit(solution)/shard_map/ppermute | solution.py:470
  58.3 11.8 %collective-permute-start.13 = (bf16[4,64,128]{2,1,0:T(8,128)(2,1)S(1)}, bf16[4,64,128]{2,1,0:T(8,128)(2,1)S(1)}, u32[]{:S(2)}, u32[]{:S(2)}) collective-permute-start(bf16[4,64,128]{2,1,0:T(8,128)(2,1)S(1)} %shard_map.68), channel_id=1, source_target_pairs={{8,0},{9,1},{10,2},{11,3},{12,4},{13,5},{14,6},{15,7}} | collective-permute-start | bytes 196616 | tf_op jit(solution)/shard_map/ppermute | solution.py:541
  61.1 4.5 %collective-permute-start.19 = (bf16[2,64,576]{2,1,0:T(8,128)(2,1)S(1)}, bf16[2,64,576]{2,1,0:T(8,128)(2,1)S(1)}, u32[]{:S(2)}, u32[]{:S(2)}) collective-permute-start(bf16[2,64,576]{2,1,0:T(8,128)(2,1)S(1)} %add_convert_fusion), channel_id=1, source_target_pairs={{0,1},{1,0},{2,6},{3,7},{4,5},{5,4},{6,2},{7,3},{8,9},{9,8},{10,14... | collective-permute-start | bytes 442376 | tf_op jit(solution)/shard_map/ppermute | solution.py:470
  63.0 7.1 %collective-permute-start.16 = (bf16[4,64,128]{2,1,0:T(8,128)(2,1)S(1)}, bf16[4,64,128]{2,1,0:T(8,128)(2,1)S(1)}, u32[]{:S(2)}, u32[]{:S(2)}) collective-permute-start(bf16[4,64,128]{2,1,0:T(8,128)(2,1)S(1)} %shard_map.70), channel_id=1, source_target_pairs={{8,0},{9,1},{10,2},{11,3},{12,4},{13,5},{14,6},{15,7}} | collective-permute-start | bytes 196616 | tf_op jit(solution)/shard_map/ppermute | solution.py:541
  65.7 5.7 %collective-permute-start.20 = (f32[2,64,576]{2,1,0:T(8,128)S(1)}, f32[2,64,576]{2,1,0:T(8,128)S(1)}, u32[]{:S(2)}, u32[]{:S(2)}) collective-permute-start(f32[2,64,576]{2,1,0:T(8,128)S(1)} %convert_add_fusion), channel_id=1, source_target_pairs={{0,2},{2,0},{4,6},{6,4},{1,3},{3,1},{5,7},{7,5},{8,10},{10,8},{12,... | collective-permute-start | bytes 884744 | tf_op jit(solution)/shard_map/ppermute | solution.py:472

commit v6 on v5

--- a/solution.py
+++ b/solution.py
@@ -13,7 +13,7 @@
 bf16 = jnp.bfloat16
 
 
-def call(body, out_shape, scratch=(), flops=0, moved=0, **more):
+def call(body, out_shape, scratch=(), flops=0, moved=0):
     return pl.pallas_call(
         body,
         out_shape=out_shape,
@@ -22,15 +22,7 @@
             flops=int(flops), bytes_accessed=int(moved), transcendentals=0
         ),
         compiler_params=pltpu.CompilerParams(vmem_limit_bytes=VMEM_BYTES),
-        **more,
-    )
-
-
-def piece_of(upper, lower, row, rows):
-    half = rows // 2
-    if row < half:
-        return upper, row
-    return (lower, row - half) if row < rows else (upper, half)
+    )
 
 
 def row_of(ref, row, channels, rows):
@@ -110,17 +102,7 @@
     return (state_edge, 0), (adjoint_edge, 2 * state_edge * rows)
 
 
-def strip_body(
-    c_hbm, q_hbm, edge_ref, c_ref, q_ref, arrived, *, channels, rows, depth
-):
-    copies = [
-        pltpu.make_async_copy(source, target, arrived.at[place])
-        for place, (source, target) in enumerate(((c_hbm, c_ref), (q_hbm, q_ref)))
-    ]
-    for copy in copies:
-        copy.start()
-    for copy in copies:
-        copy.wait()
+def strip_body(c_ref, q_ref, edge_ref, *, channels, rows, depth):
     total = jnp.zeros(edge_ref.shape, f32)
     for ref, (edge, low) in zip((c_ref, q_ref), layout(rows, depth)):
         image = [row_of(ref, row, channels, rows) for row in range(rows)]
@@ -129,7 +111,8 @@
 
 
 def message_body(
-    c_ref, q_ref, left_ref, right_ref, pair_ref, cross_ref, side_ref, *, channels, rows, depth
+    c_ref, q_ref, left_ref, right_ref, pair_ref, cross_ref, side_ref, strip_ref,
+    *, channels, rows, depth,
 ):
     cols = c_ref.shape[1]
     _, _, left, right = flags()
@@ -137,6 +120,9 @@
     edges = ((c_edge, 0, middle), (q_edge, middle, 2 * cols))
     side = join_edges(left_ref[...], right_ref[...], left, right, edges).astype(bf16)
     side_ref[...] = side
+    wide = side.astype(f32)
+    image = [side_lanes(wide, c_edge, 0, row) for row in range(rows)]
+    strip_ref[...] = fold_edges(image, 2 * depth, 0, jnp.zeros(strip_ref.shape, f32))
     even = even_row()
     for which, ref in enumerate((c_ref, q_ref)):
         for row in range(depth):
@@ -170,14 +156,14 @@
     return jnp.concatenate([get(2 * depth), get(2 * depth + 1)], 1)
 
 
-def row_blocks(low, high, body, size=6):
-    turns, rest = divmod(high - low, size)
+def row_blocks(low, high, body, turns=2):
+    size, rest = divmod(high - low, turns)
 
     def turn(number, carry):
         body(low + size * number, size)
         return carry
 
-    if turns > 0:
+    if size > 0:
         lax.fori_loop(0, turns, turn, 0)
     if rest > 0:
         body(low + size * turns, rest)
@@ -193,8 +179,26 @@
 
 
 def first_body(
-    c_ref, pair_ref, cross_ref, side_ref, w_ref, f_ref, upper_ref, lower_ref, strip_ref, x_ref, a_ref, a2_ref,
-    *, channels, rows, depth,
+    c_ref, pair_ref, cross_ref, side_ref, w_ref, out_ref, x_ref, a_ref, a2_ref,
+    *, channels, rows, depth, sender,
+):
+    active = (lax.axis_index("layer") == 0) == sender
+
+    @pl.when(jnp.logical_not(active))
+    def nothing():
+        out_ref[...] = jnp.zeros(out_ref.shape, out_ref.dtype)
+
+    @pl.when(active)
+    def run():
+        first_pass(
+            c_ref, pair_ref, cross_ref, side_ref, w_ref, out_ref, x_ref, a_ref, a2_ref,
+            channels, rows, depth,
+        )
+
+
+def first_pass(
+    c_ref, pair_ref, cross_ref, side_ref, w_ref, out_ref, x_ref, a_ref, a2_ref,
+    channels, rows, depth,
 ):
     cols = c_ref.shape[1]
     up, down, left, right = flags()
@@ -209,12 +213,9 @@
 
     (edge, low), _ = layout(rows, depth)
     own_side = side_ref[...].astype(f32)
-    image = []
     for row in range(rows):
-        beyond = side_lanes(own_side, edge, low, row)
-        image.append(beyond)
-        put(halo + row, row_of(c_ref, row, channels, rows), beyond)
-    strip_ref[...] = fold_edges(image, 2 * depth, 0, jnp.zeros(strip_ref.shape, f32))
+        own = row_of(c_ref, row, channels, rows)
+        put(halo + row, own, side_lanes(own_side, edge, low, row))
     beside = Beside(pair_ref, cross_ref)
     above_side, below_side = strips_of(beside.above, depth), strips_of(beside.below, depth)
     for row in range(depth):
@@ -240,43 +241,36 @@
         row_blocks(layer + 1, total - layer - 1, step)
     image = [x_ref[halo + row, :, cols:] for row in range(rows)]
     values = [x_ref[halo + row, :, :cols] for row in range(rows)]
-    values.append(fold_edges(image, 2 * depth, 0, jnp.zeros(strip_ref.shape, f32)))
+    values.append(fold_edges(image, 2 * depth, 0, jnp.zeros((channels, cols), f32)))
     for row, value in enumerate(values):
-        f_ref[row] = value
-        ref, place = piece_of(upper_ref, lower_ref, row, rows)
-        ref[place] = value.astype(bf16)
-
-
-def hop_body(s_ref, c_ref, *refs, start, channels, rows):
+        out_ref[row] = value.astype(out_ref.dtype)
+
+
+def hop_body(s_ref, c_ref, *refs, channels, rows):
     f_ref, m_ref, out_ref = refs[-3:]
-    count = rows // 2
-    work = [(start + row, row_of(c_ref, start + row, channels, rows)) for row in range(count)]
-    work += [(rows, ref[...]) for ref in refs[:-3]]
-    for place, (row, base) in enumerate(work):
-        e = s_ref[place].astype(f32) - base
+    base = [row_of(c_ref, row, channels, rows) for row in range(rows)]
+    base += [ref[...] for ref in refs[:-3]]
+    for row in range(len(base)):
+        e = s_ref[row].astype(f32) - base[row]
         high = e.astype(bf16)
         low = (e - high.astype(f32)).astype(bf16)
         stacked = jnp.concatenate([high, high, low], 0)
         moved = jnp.dot(m_ref[...], stacked, preferred_element_type=f32)
-        out_ref[place] = (f_ref[row] + e + moved).astype(bf16)
+        out_ref[row] = (f_ref[row] + e + moved).astype(bf16)
 
 
 def settle_body(c_ref, strip_ref, *refs, channels, rows):
-    s_ref = refs[-1]
-    uppers, lowers = refs[: len(refs) // 2], refs[len(refs) // 2 : -1]
+    arrived, s_ref = refs[:-1], refs[-1]
     first = lax.axis_index("layer") == 0
     base = [row_of(c_ref, row, channels, rows) for row in range(rows)] + [strip_ref[...]]
     for row in range(rows + 1):
-        value = 0.0
-        for upper, lower in zip(uppers, lowers):
-            ref, place = piece_of(upper, lower, row, rows)
-            value = value + ref[place].astype(f32)
+        value = sum(ref[row].astype(f32) for ref in arrived)
         s_ref[row] = jnp.where(first, base[row], value).astype(bf16)
 
 
 def second_body(
     c_ref, q_ref, s_ref, s_pair_ref, s_cross_ref, pair_ref, cross_ref, side_ref, w_ref, wt_ref,
-    state_ref, g_ref, g_up_ref, g_lo_ref, kept_ref, sent_ref,
+    state_ref, g_ref, sending_ref, kept_ref, sent_ref,
     x_ref, a_ref, a2_ref, slope_ref, adj_ref, src_ref,
     *, channels, rows, depth,
 ):
@@ -366,7 +360,7 @@
             part = pl.ds(first, count)
             src_ref[part] = (adj_ref[part] * slope_ref[layer, part]).astype(bf16)
 
-        row_blocks(halo - reach, halo + rows + reach, source, 2)
+        row_blocks(halo - reach, halo + rows + reach, source)
 
         def back(first, count, layer=layer):
             adjoints = adj_ref[pl.ds(first, count)]
@@ -379,8 +373,7 @@
     for row in range(rows):
         value = adj_ref[halo + row, :, :cols]
         g_ref[row] = value
-        ref, place = piece_of(g_up_ref, g_lo_ref, row, rows)
-        ref[place] = value.astype(bf16)
+        sending_ref[row] = value.astype(bf16)
 
 
 def grad_body(kept_ref, sent_ref, grad_ref, *, channels, rows, depth):
@@ -416,13 +409,10 @@
 
 
 def last_body(q_ref, *refs, channels, rows):
-    out_ref = refs[-1]
-    uppers, lowers = refs[: len(refs) // 2], refs[len(refs) // 2 : -1]
+    arrived, out_ref = refs[:-1], refs[-1]
     last = lax.axis_index("layer") == lax.axis_size("layer") - 1
-    half = rows // 2
     for row in range(rows):
-        arrived, place = (uppers, row) if row < half else (lowers, row - half)
-        value = sum(ref[place].astype(f32) for ref in arrived)
+        value = sum(ref[row].astype(f32) for ref in arrived)
         value = jnp.where(last, row_of(q_ref, row, channels, rows), value)
         out_ref[pl.ds(row, channels, stride=rows), :] = value
 
@@ -486,24 +476,16 @@
 
     strip_f = jax.ShapeDtypeStruct((channels, cols), f32)
     wide_b = jax.ShapeDtypeStruct((channels, 2 * cols), bf16)
-    half = rows // 2
-    more_f, more_b, upper_b, lower_b, message_b = (
+    more_f, more_b, message_b = (
         jax.ShapeDtypeStruct((count, channels, cols), kind)
-        for count, kind in (
-            (rows + 1, f32), (rows + 1, bf16), (half + 1, bf16), (half, bf16),
-            (2 * depth + 2, bf16),
-        )
-    )
-
-    edges = call(
-        functools.partial(strip_body, depth=depth, **sizes),
-        wide_b,
-        [pltpu.VMEM(flat, f32), pltpu.VMEM(flat, f32), pltpu.SemaphoreType.DMA((2,))],
-        in_specs=[pl.BlockSpec(memory_space=pltpu.HBM)] * 2,
-    )(c_flat, q_flat)
+        for count, kind in ((rows + 1, f32), (rows + 1, bf16), (2 * depth + 2, bf16))
+    )
+    flat_f = jax.ShapeDtypeStruct(flat, f32)
+    edges = call(functools.partial(strip_body, depth=depth, **sizes), wide_b)(c_flat, q_flat)
     left, right = from_sides(edges)
-    to_pair, to_cross, side = call(
-        functools.partial(message_body, depth=depth, **sizes), (message_b, message_b, wide_b)
+    to_pair, to_cross, side, strip = call(
+        functools.partial(message_body, depth=depth, **sizes),
+        (message_b, message_b, wide_b, strip_f),
     )(c_flat, q_flat, left, right)
     pair, cross = exchanged(to_pair, to_cross)
 
@@ -523,53 +505,45 @@
     lanes = 2 * cols
     mac = 2 * 9 * channels * channels * lanes
     total = rows + 2 * depth
-    f, f_upper, f_lower, strip = call(
-        functools.partial(first_body, depth=depth, **sizes),
-        (more_f, upper_b, lower_b, strip_f),
-        [
-            pltpu.VMEM((total, channels, lanes), f32),
-            pltpu.VMEM((total, channels, lanes), bf16),
-            pltpu.VMEM((total, channels, lanes), bf16),
-        ],
-        flops=mac * 44,
-    )(c_flat, pair, cross, side, w_fwd)
-
-    def chain(pieces, target, matrix, order):
-        sendings = [piece[0] for piece in pieces]
-        arrivals = []
-        for turn, hop in enumerate(order):
-            arrived = [lax.ppermute(sending, "layer", [hop]) for sending in sendings]
-            arrivals.append(arrived)
-            if turn < len(order) - 1:
-                sendings = [
-                    call(
-                        functools.partial(hop_body, start=start, **sizes),
-                        jax.ShapeDtypeStruct(value.shape, bf16),
-                        flops=10**10,
-                    )(value, *base, target, matrix)
-                    for value, (_, start, base) in zip(arrived, pieces)
-                ]
-        return [list(piece) for piece in zip(*arrivals)]
-
-    uppers, lowers = chain(
-        ((f_upper, 0, (c_flat, strip)), (f_lower, half, (c_flat,))),
-        f,
-        m_fwd,
-        [(k, k + 1) for k in range(groups - 1)],
-    )
-    s = call(functools.partial(settle_body, **sizes), more_b)(
-        c_flat, strip, *uppers, *lowers
-    )
+
+    def first(kind, sender, *inputs):
+        return call(
+            functools.partial(first_body, depth=depth, sender=sender, **sizes),
+            kind,
+            [
+                pltpu.VMEM((total, channels, lanes), f32),
+                pltpu.VMEM((total, channels, lanes), bf16),
+                pltpu.VMEM((total, channels, lanes), bf16),
+            ],
+            flops=mac * 44,
+        )(*inputs)
+
+    def hop(arrived, base, target, matrix):
+        return call(
+            functools.partial(hop_body, **sizes),
+            jax.ShapeDtypeStruct(arrived.shape, bf16),
+            flops=10**10,
+        )(arrived, *base, target, matrix)
+
+    inputs = (c_flat, pair, cross, side, w_fwd)
+    sending = first(more_b, True, *inputs)
+    inputs = lax.optimization_barrier((inputs, sending))[0]
+    f = first(more_f, False, *inputs)
+    arrivals = []
+    for k in range(groups - 1):
+        arrivals.append(lax.ppermute(sending, "layer", [(k, k + 1)]))
+        if k < groups - 2:
+            sending = hop(arrivals[-1], (c_flat, strip), f, m_fwd)
+    s = call(functools.partial(settle_body, **sizes), more_b)(c_flat, strip, *arrivals)
     s_pair, s_cross = exchanged(s, s)
 
     total = rows + 4 * depth
-    state, g, g_upper, g_lower, kept, sources = call(
+    state, g, sending, kept, sources = call(
         functools.partial(second_body, depth=depth, **sizes),
         (
-            jax.ShapeDtypeStruct(flat, f32),
+            flat_f,
             tile_f,
-            lower_b,
-            lower_b,
+            jax.ShapeDtypeStruct(tile_f.shape, bf16),
             jax.ShapeDtypeStruct((depth, rows, channels, lanes), bf16),
             jax.ShapeDtypeStruct((depth, rows + 2, channels, cols), bf16),
         ),
@@ -583,12 +557,11 @@
         ],
         flops=mac * 120,
     )(c_flat, q_flat, s, s_pair, s_cross, pair, cross, side, w_fwd, w_back)
-    uppers, lowers = chain(
-        ((g_upper, 0, (q_flat,)), (g_lower, half, (q_flat,))),
-        g,
-        m_back,
-        [(k, k - 1) for k in range(groups - 1, 0, -1)],
-    )
+    returned = []
+    for k in range(groups - 1, 0, -1):
+        returned.append(lax.ppermute(sending, "layer", [(k, k - 1)]))
+        if k > 1:
+            sending = hop(returned[-1], (q_flat,), g, m_back)
     grads = call(
         functools.partial(grad_body, depth=depth, **sizes),
         jax.ShapeDtypeStruct((depth, channels, 9 * channels), f32),
@@ -597,7 +570,7 @@
     weight_grads = total_over_tiles(grads)
     adjoint = call(
         functools.partial(last_body, **sizes), jax.ShapeDtypeStruct(flat, f32), flops=10**10
-    )(q_flat, *uppers, *lowers)
+    )(q_flat, *returned)
     return state.reshape(c_states.shape), adjoint.reshape(c_states.shape), weight_grads
 
 

time: 72.7 us -> 73.1 us (level)
  the two profiles are of different devices: /device:TPU:19 before, /device:TPU:0 now
where the time goes in v6:
time: 73.1 us; the launch traced here: 72.7 us
  waiting for transfers between devices  28 us (38%)
  starting transfers between devices  20.7 us (28%)
  Pallas kernels  16.8 us (23%)
  local copies, waits for them, and re-layouts  4.35 us (6%)
  other arithmetic  1.86 us (3%)
  between operations  0.96 us (1%)
    ppermute x3, waiting for transfers between devices, local(): returned.append(lax.ppermute(sending, 'layer', [(k, k - 1)]))  16.3 us
    pallas_call x1, Pallas kernels, local(): call(functools.partial(second_body, depth=depth, **sizes), (flat_f, tile_...  9.48 us
    ppermute x2, starting transfers between devices, exchanged(): lax.ppermute(to_pair, 'row', pairs)  5.57 us
    ppermute x2, waiting for transfers between devices, total_over_tiles(): arrived = lax.ppermute(rounded, ('row', 'col'), pairs)  5.19 us
    pallas_call x2, Pallas kernels, first(): call(functools.partial(first_body, depth=depth, sender=sender, **sizes),...  3.83 us
    ppermute x3, waiting for transfers between devices, local(): arrivals.append(lax.ppermute(sending, 'layer', [(k, k + 1)]))  3.57 us
    ppermute x2, starting transfers between devices, total_over_tiles(): arrived = lax.ppermute(rounded, ('row', 'col'), pairs)  3.05 us
    ppermute x1, starting transfers between devices, from_sides(): other = lax.ppermute(array, 'col', [(0, 1), (1, 0)])  3.03 us
  transfers between devices with their start and end apart: 15, of which 7 were waited for; matrix products, arithmetic and copies ran while one was open for 5% of the time, Pallas kernels for 2%

profile of v6, /device:TPU:0, one launch (start us, length us, event | category | flops | bytes accessed | tf_op | source)
XLA Modules:
  0.0 72.7 jit_solution(11771669043894894530)
XLA Ops:
  0.6 0.9 %copy-done = f32[1,64,8,128]{3,2,1,0:T(8,128)S(1)} copy-done((f32[1,64,8,128]{3,2,1,0:T(8,128)S(1)}, f32[1,64,8,128]{3,2,1,0:T(8,128)}, u32[]{:S(2)}) %copy-start) | copy-done | bytes 262168
  1.6 0.9 %copy-done.2 = f32[1,64,8,128]{3,2,1,0:T(8,128)S(1)} copy-done((f32[1,64,8,128]{3,2,1,0:T(8,128)S(1)}, f32[1,64,8,128]{3,2,1,0:T(8,128)}, u32[]{:S(2)}) %copy-start.2) | copy-done | bytes 262168
  2.7 3.0 %collective-permute-start = (bf16[64,256]{1,0:T(8,128)(2,1)S(1)}, bf16[64,256]{1,0:T(8,128)(2,1)S(1)}, u32[]{:S(2)}, u32[]{:S(2)}) collective-permute-start(bf16[64,256]{1,0:T(8,128)(2,1)S(1)} %shard_map.58), channel_id=1, source_target_pairs={{0,1},{1,0},{2,3},{3,2},{4,5},{5,4},{6,7},{7,6},{8,9},{9,8},{10,11... | collective-permute-start | bytes 98312 | tf_op jit(solution)/shard_map/ppermute | solution.py:435
  6.1 1.5 %collective-permute-done.left_ref.right_ref = bf16[64,256]{1,0:T(8,128)(2,1)S(1)} collective-permute-done((bf16[64,256]{1,0:T(8,128)(2,1)S(1)}, bf16[64,256]{1,0:T(8,128)(2,1)S(1)}, u32[]{:S(2)}, u32[]{:S(2)}) %collective-permute-start) | collective-permute-done | bytes 32800 | tf_op jit(solution)/shard_map/ppermute | solution.py:435
  7.9 0.7 collective-permute-start.2
  8.5 3.4 %collective-permute-start.1 = (bf16[10,64,128]{2,1,0:T(8,128)(2,1)S(1)}, bf16[10,64,128]{2,1,0:T(8,128)(2,1)S(1)}, u32[]{:S(2)}, u32[]{:S(2)}) collective-permute-start(bf16[10,64,128]{2,1,0:T(8,128)(2,1)S(1)} %get-tuple-element.21), channel_id=1, source_target_pairs={{0,2},{2,0},{4,6},{6,4},{1,3},{3,1},{5,7},{7,5},{8,10},{10,8},{12,... | collective-permute-start | bytes 491528 | tf_op jit(solution)/shard_map/ppermute | solution.py:430
  12.0 0.6 bitcast_convert_fusion
  12.6 0.6 copy.11
  13.2 0.4 reshape.34.w_ref
  13.7 0.5 copy.12
  14.7 3.8 %shard_map.60 = bf16[9,64,128]{2,1,0:T(8,128)(2,1)S(1)} custom-call(f32[512,128]{1,0:T(8,128)S(1)} %bitcast.20, bf16[10,64,128]{2,1,0:T(8,128)(2,1)S(1)} %collective-permute-done.1.pair_ref, bf16[10,64,128]{2,1,0:T(8,128)(2,1)S(1)} %collective-permute-done.2.cross_ref, bf16[64,256]{1,0:T(8,128)(2,1)S(1)} %get-tuple-element.29.side_ref, ...), custom_call_target="tpu_custom_call" | custom-call | flops 830472192 | tf_op jit(solution)/shard_map/pallas_call | solution.py:510
  18.5 1.3 %collective-permute-start.3 = (bf16[9,64,128]{2,1,0:T(8,128)(2,1)S(1)}, bf16[9,64,128]{2,1,0:T(8,128)(2,1)S(1)}, u32[]{:S(2)}, u32[]{:S(2)}) collective-permute-start(bf16[9,64,128]{2,1,0:T(8,128)(2,1)S(1)} %shard_map.60), channel_id=1, source_target_pairs={{0,8},{1,9},{2,10},{3,11},{4,12},{5,13},{6,14},{7,15}} | collective-permute-start | bytes 442376 | tf_op jit(solution)/shard_map/ppermute | solution.py:534
  19.9 3.6 %collective-permute-done.3.s_ref.refs_0_ = bf16[9,64,128]{2,1,0:T(8,128)(2,1)S(1)} collective-permute-done((bf16[9,64,128]{2,1,0:T(8,128)(2,1)S(1)}, bf16[9,64,128]{2,1,0:T(8,128)(2,1)S(1)}, u32[]{:S(2)}, u32[]{:S(2)}) %collective-permute-start.3) | collective-permute-done | bytes 147488 | tf_op jit(solution)/shard_map/ppermute | solution.py:534
  23.8 0.7 collective-permute-start.4
  24.8 0.7 collective-permute-start.5
  25.5 0.9 %collective-permute-start.7 = (bf16[9,64,128]{2,1,0:T(8,128)(2,1)S(1)}, bf16[9,64,128]{2,1,0:T(8,128)(2,1)S(1)}, u32[]{:S(2)}, u32[]{:S(2)}) collective-permute-start(bf16[9,64,128]{2,1,0:T(8,128)(2,1)S(1)} %shard_map.64.s_ref), channel_id=1, source_target_pairs={{2,4},{4,2},{3,5},{5,3},{10,12},{12,10},{11,13},{13,11},{18,20},{2... | collective-permute-start | bytes 442376 | tf_op jit(solution)/shard_map/ppermute | solution.py:430
  26.4 2.2 %collective-permute-start.6 = (bf16[9,64,128]{2,1,0:T(8,128)(2,1)S(1)}, bf16[9,64,128]{2,1,0:T(8,128)(2,1)S(1)}, u32[]{:S(2)}, u32[]{:S(2)}) collective-permute-start(bf16[9,64,128]{2,1,0:T(8,128)(2,1)S(1)} %shard_map.64.s_ref), channel_id=1, source_target_pairs={{0,2},{2,0},{4,6},{6,4},{1,3},{3,1},{5,7},{7,5},{8,10},{10,8},{12,... | collective-permute-start | bytes 442376 | tf_op jit(solution)/shard_map/ppermute | solution.py:430
  28.6 1.0 %collective-permute-done.6.s_pair_ref = bf16[9,64,128]{2,1,0:T(8,128)(2,1)S(1)} collective-permute-done((bf16[9,64,128]{2,1,0:T(8,128)(2,1)S(1)}, bf16[9,64,128]{2,1,0:T(8,128)(2,1)S(1)}, u32[]{:S(2)}, u32[]{:S(2)}) %collective-permute-start.6) | collective-permute-done | bytes 147488 | tf_op jit(solution)/shard_map/ppermute | solution.py:430
  29.6 9.5 %shard_map.65 = (f32[512,128]{1,0:T(8,128)}, f32[8,64,128]{2,1,0:T(8,128)S(1)}, bf16[8,64,128]{2,1,0:T(8,128)(2,1)S(1)}, bf16[4,8,64,256]{3,2,1,0:T(8,128)(2,1)S(1)}, bf16[4,10,64,128]{3,2,1,0:T(8,128)(2,1)S(1)}) custom-call(f32[512,128]{1,0:T(8,128)S(1)} %bitcast.25, f32[512,128]{1,0:T(8,128)S(1)} %bitcast.28, bf16[9,64,128]{2,1,0:T(8,128)(2,1)S(1)} %shard_map.64.s_ref, ...), custom_call_target="tpu_custom_call" | custom-call | flops 2264924160 | tf_op jit(solution)/shard_map/pallas_call | solution.py:541
  39.0 1.1 %shard_map.69 = f32[4,64,576]{2,1,0:T(8,128)S(1)} custom-call(bf16[4,8,64,256]{3,2,1,0:T(8,128)(2,1)S(1)} %get-tuple-element.35.kept_ref, bf16[4,10,64,128]{3,2,1,0:T(8,128)(2,1)S(1)} %get-tuple-element.36.sent_ref), custom_call_target="tpu_custom_call" | custom-call | flops 1000000000 | tf_op jit(solution)/shard_map/pallas_call | solution.py:565
  40.2 2.2 %collective-permute-start.11 = (f32[2,64,576]{2,1,0:T(8,128)S(1)}, f32[2,64,576]{2,1,0:T(8,128)S(1)}, u32[]{:S(2)}, u32[]{:S(2)}) collective-permute-start(f32[2,64,576]{2,1,0:T(8,128)S(1)} %slice_select_fusion), channel_id=1, source_target_pairs={{0,2},{2,0},{4,6},{6,4},{1,3},{3,1},{5,7},{7,5},{8,10},{10,8},{12,... | collective-permute-start | bytes 884744 | tf_op jit(solution)/shard_map/ppermute | solution.py:448
  42.5 0.7 collective-permute-start.8
  43.2 0.5 collective-permute-done.11
  43.7 1.5 %collective-permute-start.12 = (bf16[2,64,576]{2,1,0:T(8,128)(2,1)S(1)}, bf16[2,64,576]{2,1,0:T(8,128)(2,1)S(1)}, u32[]{:S(2)}, u32[]{:S(2)}) collective-permute-start(bf16[2,64,576]{2,1,0:T(8,128)(2,1)S(1)} %add_convert_fusion.1), channel_id=1, source_target_pairs={{0,4},{1,5},{2,3},{3,2},{4,0},{5,1},{6,7},{7,6},{8,12},{9,13},{10,... | collective-permute-start | bytes 442376 | tf_op jit(solution)/shard_map/ppermute | solution.py:460
  45.5 0.7 collective-permute-start.9
  46.2 3.0 %collective-permute-done.12 = bf16[2,64,576]{2,1,0:T(8,128)(2,1)S(1)} collective-permute-done((bf16[2,64,576]{2,1,0:T(8,128)(2,1)S(1)}, bf16[2,64,576]{2,1,0:T(8,128)(2,1)S(1)}, u32[]{:S(2)}, u32[]{:S(2)}) %collective-permute-start.12) | collective-permute-done | bytes 147488 | tf_op jit(solution)/shard_map/ppermute | solution.py:460
  49.2 1.6 %collective-permute-start.13 = (bf16[2,64,576]{2,1,0:T(8,128)(2,1)S(1)}, bf16[2,64,576]{2,1,0:T(8,128)(2,1)S(1)}, u32[]{:S(2)}, u32[]{:S(2)}) collective-permute-start(bf16[2,64,576]{2,1,0:T(8,128)(2,1)S(1)} %add_convert_fusion), channel_id=1, source_target_pairs={{0,1},{1,0},{2,6},{3,7},{4,5},{5,4},{6,2},{7,3},{8,9},{9,8},{10,14... | collective-permute-start | bytes 442376 | tf_op jit(solution)/shard_map/ppermute | solution.py:460
  51.0 1.3 %collective-permute-start.10 = (bf16[8,64,128]{2,1,0:T(8,128)(2,1)S(1)}, bf16[8,64,128]{2,1,0:T(8,128)(2,1)S(1)}, u32[]{:S(2)}, u32[]{:S(2)}) collective-permute-start(bf16[8,64,128]{2,1,0:T(8,128)(2,1)S(1)} %shard_map.67), channel_id=1, source_target_pairs={{8,0},{9,1},{10,2},{11,3},{12,4},{13,5},{14,6},{15,7}} | collective-permute-start | bytes 393224 | tf_op jit(solution)/shard_map/ppermute | solution.py:562
  52.3 2.2 %collective-permute-done.13 = bf16[2,64,576]{2,1,0:T(8,128)(2,1)S(1)} collective-permute-done((bf16[2,64,576]{2,1,0:T(8,128)(2,1)S(1)}, bf16[2,64,576]{2,1,0:T(8,128)(2,1)S(1)}, u32[]{:S(2)}, u32[]{:S(2)}) %collective-permute-start.13) | collective-permute-done | bytes 147488 | tf_op jit(solution)/shard_map/ppermute | solution.py:460
  54.7 16.3 %collective-permute-done.10.refs_2_ = bf16[8,64,128]{2,1,0:T(8,128)(2,1)S(1)} collective-permute-done((bf16[8,64,128]{2,1,0:T(8,128)(2,1)S(1)}, bf16[8,64,128]{2,1,0:T(8,128)(2,1)S(1)}, u32[]{:S(2)}, u32[]{:S(2)}) %collective-permute-start.10) | collective-permute-done | bytes 131104 | tf_op jit(solution)/shard_map/ppermute | solution.py:562
  71.0 0.8 %shard_map.68 = f32[512,128]{1,0:T(8,128)} custom-call(f32[512,128]{1,0:T(8,128)S(1)} %bitcast.31, bf16[8,64,128]{2,1,0:T(8,128)(2,1)S(1)} %collective-permute-done.8.s_ref.refs_0_, bf16[8,64,128]{2,1,0:T(8,128)(2,1)S(1)} %collective-permute-done.9.s_ref.refs_1_, bf16[8,64,128]{2,1,0:T(8,128)(2,1)S(1)} %collective-permute-done.10.refs_2_), custom_call_target="tpu_custom_call" | custom-call | flops 10000000000 | tf_op jit(solution)/shard_map/pallas_call | solution.py:571
  71.8 0.9 %pad_maximum_fusion = f32[4,64,576]{2,1,0:T(8,128)} fusion(f32[2,64,576]{2,1,0:T(8,128)S(1)} %get-tuple-element.38, f32[2,64,576]{2,1,0:T(8,128)S(1)} %get-tuple-element.37), kind=kLoop, calls=%fused_computation | loop fusion | flops 147456 | bytes 1179648 | tf_op jit(solution)/shard_map/concatenate | solution.py:465
  (47 shorter events, 3.0 us)
Async XLA Ops:
  0.6 1.0 %copy-start = (f32[1,64,8,128]{3,2,1,0:T(8,128)S(1)}, f32[1,64,8,128]{3,2,1,0:T(8,128)}, u32[]{:S(2)}) copy-start(f32[1,64,8,128]{3,2,1,0:T(8,128)} %param.3) | copy-start | bytes 786436
  1.6 0.9 %copy-start.2 = (f32[1,64,8,128]{3,2,1,0:T(8,128)S(1)}, f32[1,64,8,128]{3,2,1,0:T(8,128)}, u32[]{:S(2)}) copy-start(f32[1,64,8,128]{3,2,1,0:T(8,128)} %param.4) | copy-start | bytes 786436
  2.5 3.2 %copy-start.4 = (bf16[4,64,576]{2,1,0:T(8,128)(2,1)S(1)}, bf16[4,64,576]{2,1,0:T(8,128)(2,1)}, u32[]{:S(2)}) copy-start(bf16[4,64,576]{2,1,0:T(8,128)(2,1)} %param.5) | copy-start | bytes 884740
  2.7 4.9 %collective-permute-start = (bf16[64,256]{1,0:T(8,128)(2,1)S(1)}, bf16[64,256]{1,0:T(8,128)(2,1)S(1)}, u32[]{:S(2)}, u32[]{:S(2)}) collective-permute-start(bf16[64,256]{1,0:T(8,128)(2,1)S(1)} %shard_map.58), channel_id=1, source_target_pairs={{0,1},{1,0},{2,3},{3,2},{4,5},{5,4},{6,7},{7,6},{8,9},{9,8},{10,11... | collective-permute-start | bytes 98312 | tf_op jit(solution)/shard_map/ppermute | solution.py:435
  5.7 1.9 %copy-start.3 = (f32[1,64,8,128]{3,2,1,0:T(8,128)S(1)}, f32[1,64,8,128]{3,2,1,0:T(8,128)}, u32[]{:S(2)}) copy-start(f32[1,64,8,128]{3,2,1,0:T(8,128)} %param.4) | copy-start | bytes 786436
  6.0 1.6 %copy-start.1 = (f32[1,64,8,128]{3,2,1,0:T(8,128)S(1)}, f32[1,64,8,128]{3,2,1,0:T(8,128)}, u32[]{:S(2)}) copy-start(f32[1,64,8,128]{3,2,1,0:T(8,128)} %param.3) | copy-start | bytes 786436
  6.1 5.9 %copy-start.5 = (f32[64,64]{0,1:T(8,128)}, f32[64,64]{0,1:T(8,128)S(1)}, u32[]{:S(2)}) copy-start(f32[64,64]{0,1:T(8,128)S(1)} %convert_reduce_fusion) | copy-start | bytes 49156
  7.9 6.8 %collective-permute-start.2 = (bf16[10,64,128]{2,1,0:T(8,128)(2,1)S(1)}, bf16[10,64,128]{2,1,0:T(8,128)(2,1)S(1)}, u32[]{:S(2)}, u32[]{:S(2)}) collective-permute-start(bf16[10,64,128]{2,1,0:T(8,128)(2,1)S(1)} %get-tuple-element.22), channel_id=1, source_target_pairs={{2,4},{4,2},{3,5},{5,3},{10,12},{12,10},{11,13},{13,11},{18,20},{2... | collective-permute-start | bytes 491528 | tf_op jit(solution)/shard_map/ppermute | solution.py:430
  8.5 6.1 %collective-permute-start.1 = (bf16[10,64,128]{2,1,0:T(8,128)(2,1)S(1)}, bf16[10,64,128]{2,1,0:T(8,128)(2,1)S(1)}, u32[]{:S(2)}, u32[]{:S(2)}) collective-permute-start(bf16[10,64,128]{2,1,0:T(8,128)(2,1)S(1)} %get-tuple-element.21), channel_id=1, source_target_pairs={{0,2},{2,0},{4,6},{6,4},{1,3},{3,1},{5,7},{7,5},{8,10},{10,8},{12,... | collective-permute-start | bytes 491528 | tf_op jit(solution)/shard_map/ppermute | solution.py:430
  14.6 5.1 %copy-start.7 = (bf16[64,64]{0,1:T(8,128)(2,1)S(1)}, bf16[64,64]{0,1:T(8,128)(2,1)}, u32[]{:S(2)}) copy-start(bf16[64,64]{0,1:T(8,128)(2,1)} %get-tuple-element.41) | copy-start | bytes 24580
  18.5 5.0 %collective-permute-start.3 = (bf16[9,64,128]{2,1,0:T(8,128)(2,1)S(1)}, bf16[9,64,128]{2,1,0:T(8,128)(2,1)S(1)}, u32[]{:S(2)}, u32[]{:S(2)}) collective-permute-start(bf16[9,64,128]{2,1,0:T(8,128)(2,1)S(1)} %shard_map.60), channel_id=1, source_target_pairs={{0,8},{1,9},{2,10},{3,11},{4,12},{5,13},{6,14},{7,15}} | collective-permute-start | bytes 442376 | tf_op jit(solution)/shard_map/ppermute | solution.py:534
  23.8 0.7 collective-permute-start.4
  24.8 0.7 collective-permute-start.5
  25.5 3.0 %collective-permute-start.7 = (bf16[9,64,128]{2,1,0:T(8,128)(2,1)S(1)}, bf16[9,64,128]{2,1,0:T(8,128)(2,1)S(1)}, u32[]{:S(2)}, u32[]{:S(2)}) collective-permute-start(bf16[9,64,128]{2,1,0:T(8,128)(2,1)S(1)} %shard_map.64.s_ref), channel_id=1, source_target_pairs={{2,4},{4,2},{3,5},{5,3},{10,12},{12,10},{11,13},{13,11},{18,20},{2... | collective-permute-start | bytes 442376 | tf_op jit(solution)/shard_map/ppermute | solution.py:430
  26.4 3.2 %collective-permute-start.6 = (bf16[9,64,128]{2,1,0:T(8,128)(2,1)S(1)}, bf16[9,64,128]{2,1,0:T(8,128)(2,1)S(1)}, u32[]{:S(2)}, u32[]{:S(2)}) collective-permute-start(bf16[9,64,128]{2,1,0:T(8,128)(2,1)S(1)} %shard_map.64.s_ref), channel_id=1, source_target_pairs={{0,2},{2,0},{4,6},{6,4},{1,3},{3,1},{5,7},{7,5},{8,10},{10,8},{12,... | collective-permute-start | bytes 442376 | tf_op jit(solution)/shard_map/ppermute | solution.py:430
  40.1 2.3 %copy-start.6 = (f32[64,64]{0,1:T(8,128)S(1)}, f32[64,64]{0,1:T(8,128)}, u32[]{:S(2)}) copy-start(f32[64,64]{0,1:T(8,128)} %copy-done.5) | copy-start | bytes 49156
  40.2 2.2 %copy-start.8 = (bf16[64,64]{1,0:T(8,128)(2,1)S(1)}, bf16[64,64]{1,0:T(8,128)(2,1)}, u32[]{:S(2)}) copy-start(bf16[64,64]{1,0:T(8,128)(2,1)} %get-tuple-element.39) | copy-start | bytes 24580
  40.2 3.5 %collective-permute-start.11 = (f32[2,64,576]{2,1,0:T(8,128)S(1)}, f32[2,64,576]{2,1,0:T(8,128)S(1)}, u32[]{:S(2)}, u32[]{:S(2)}) collective-permute-start(f32[2,64,576]{2,1,0:T(8,128)S(1)} %slice_select_fusion), channel_id=1, source_target_pairs={{0,2},{2,0},{4,6},{6,4},{1,3},{3,1},{5,7},{7,5},{8,10},{10,8},{12,... | collective-permute-start | bytes 884744 | tf_op jit(solution)/shard_map/ppermute | solution.py:448
  42.5 2.7 %collective-permute-start.8 = (bf16[8,64,128]{2,1,0:T(8,128)(2,1)S(1)}, bf16[8,64,128]{2,1,0:T(8,128)(2,1)S(1)}, u32[]{:S(2)}, u32[]{:S(2)}) collective-permute-start(bf16[8,64,128]{2,1,0:T(8,128)(2,1)S(1)} %get-tuple-element.33), channel_id=1, source_target_pairs={{24,16},{25,17},{26,18},{27,19},{28,20},{29,21},{30,22},{31,23}} | collective-permute-start | bytes 393224 | tf_op jit(solution)/shard_map/ppermute | solution.py:562
  43.7 5.4 %collective-permute-start.12 = (bf16[2,64,576]{2,1,0:T(8,128)(2,1)S(1)}, bf16[2,64,576]{2,1,0:T(8,128)(2,1)S(1)}, u32[]{:S(2)}, u32[]{:S(2)}) collective-permute-start(bf16[2,64,576]{2,1,0:T(8,128)(2,1)S(1)} %add_convert_fusion.1), channel_id=1, source_target_pairs={{0,4},{1,5},{2,3},{3,2},{4,0},{5,1},{6,7},{7,6},{8,12},{9,13},{10,... | collective-permute-start | bytes 442376 | tf_op jit(solution)/shard_map/ppermute | solution.py:460
  45.5 5.3 %collective-permute-start.9 = (bf16[8,64,128]{2,1,0:T(8,128)(2,1)S(1)}, bf16[8,64,128]{2,1,0:T(8,128)(2,1)S(1)}, u32[]{:S(2)}, u32[]{:S(2)}) collective-permute-start(bf16[8,64,128]{2,1,0:T(8,128)(2,1)S(1)} %shard_map.66), channel_id=1, source_target_pairs={{16,8},{17,9},{18,10},{19,11},{20,12},{21,13},{22,14},{23,15}} | collective-permute-start | bytes 393224 | tf_op jit(solution)/shard_map/ppermute | solution.py:562
  49.2 5.4 %collective-permute-start.13 = (bf16[2,64,576]{2,1,0:T(8,128)(2,1)S(1)}, bf16[2,64,576]{2,1,0:T(8,128)(2,1)S(1)}, u32[]{:S(2)}, u32[]{:S(2)}) collective-permute-start(bf16[2,64,576]{2,1,0:T(8,128)(2,1)S(1)} %add_convert_fusion), channel_id=1, source_target_pairs={{0,1},{1,0},{2,6},{3,7},{4,5},{5,4},{6,2},{7,3},{8,9},{9,8},{10,14... | collective-permute-start | bytes 442376 | tf_op jit(solution)/shard_map/ppermute | solution.py:460
  51.0 19.9 %collective-permute-start.10 = (bf16[8,64,128]{2,1,0:T(8,128)(2,1)S(1)}, bf16[8,64,128]{2,1,0:T(8,128)(2,1)S(1)}, u32[]{:S(2)}, u32[]{:S(2)}) collective-permute-start(bf16[8,64,128]{2,1,0:T(8,128)(2,1)S(1)} %shard_map.67), channel_id=1, source_target_pairs={{8,0},{9,1},{10,2},{11,3},{12,4},{13,5},{14,6},{15,7}} | collective-permute-start | bytes 393224 | tf_op jit(solution)/shard_map/ppermute | solution.py:562
  54.6 17.2 %collective-permute-start.14 = (f32[2,64,576]{2,1,0:T(8,128)S(1)}, f32[2,64,576]{2,1,0:T(8,128)S(1)}, u32[]{:S(2)}, u32[]{:S(2)}) collective-permute-start(f32[2,64,576]{2,1,0:T(8,128)S(1)} %convert_add_fusion), channel_id=1, source_target_pairs={{0,2},{2,0},{4,6},{6,4},{1,3},{3,1},{5,7},{7,5},{8,10},{10,8},{12,... | collective-permute-start | bytes 884744 | tf_op jit(solution)/shard_map/ppermute | solution.py:462

commit v7 on v6

--- a/solution.py
+++ b/solution.py
@@ -156,7 +156,8 @@
     return jnp.concatenate([get(2 * depth), get(2 * depth + 1)], 1)
 
 
-def row_blocks(low, high, body, turns=2):
+def row_blocks(low, high, body):
+    turns = 1 if high - low <= 10 else 2
     size, rest = divmod(high - low, turns)
 
     def turn(number, carry):
@@ -557,17 +558,20 @@
         ],
         flops=mac * 120,
     )(c_flat, q_flat, s, s_pair, s_cross, pair, cross, side, w_fwd, w_back)
-    returned = []
-    for k in range(groups - 1, 0, -1):
-        returned.append(lax.ppermute(sending, "layer", [(k, k - 1)]))
-        if k > 1:
-            sending = hop(returned[-1], (q_flat,), g, m_back)
+    returned = [lax.ppermute(sending, "layer", [(groups - 1, groups - 2)])]
     grads = call(
         functools.partial(grad_body, depth=depth, **sizes),
         jax.ShapeDtypeStruct((depth, channels, 9 * channels), f32),
         flops=10**9,
     )(kept, sources)
+    sending = hop(returned[0], (q_flat,), g, m_back)
+    grads, sending = lax.optimization_barrier((grads, sending))
+    for k in range(groups - 2, 0, -1):
+        returned.append(lax.ppermute(sending, "layer", [(k, k - 1)]))
+        if k > 1:
+            sending = hop(returned[-1], (q_flat,), g, m_back)
     weight_grads = total_over_tiles(grads)
+    returned[-1], weight_grads = lax.optimization_barrier((returned[-1], weight_grads))
     adjoint = call(
         functools.partial(last_body, **sizes), jax.ShapeDtypeStruct(flat, f32), flops=10**10
     )(q_flat, *returned)

time: 73.1 us -> 77.2 us (1.056)
  waiting for transfers between devices: 28 us -> 32 us
  local copies, waits for them, and re-layouts: 4.35 us -> 6.25 us
  Pallas kernels: 16.8 us -> 15.4 us
    ppermute x2, waiting for transfers between devices: 5.19 us -> 7.41 us  [total_over_tiles(): arrived = lax.ppermute(rounded, ('row', 'col'), pairs)]
    unnamed x19 -> x15, local copies, waits for them, and re-layouts: 2.23 us -> 4.13 us
    ppermute x1, waiting for transfers between devices: 0.47 us -> 1.26 us  [total_over_tiles(): value = own + lax.ppermute(sent, 'row', pair)]
    ppermute x3 -> x2, starting transfers between devices: 2.62 us -> 1.95 us  [local(): returned.append(lax.ppermute(sending, 'layer', [(k, k - 1)]))]
    ppermute x3 -> x2, waiting for transfers between devices: 16.3 us -> 16.8 us  [local(): returned.append(lax.ppermute(sending, 'layer', [(k, k - 1)]))]
where the time goes in v7:
time: 77.2 us; the launch traced here: 76.8 us
  waiting for transfers between devices  32 us (41%)
  starting transfers between devices  21 us (27%)
  Pallas kernels  15.4 us (20%)
  local copies, waits for them, and re-layouts  6.25 us (8%)
  other arithmetic  1.25 us (2%)
  between operations  0.94 us (1%)
    ppermute x2, waiting for transfers between devices, local(): returned.append(lax.ppermute(sending, 'layer', [(k, k - 1)]))  16.8 us
    pallas_call x1, Pallas kernels, local(): call(functools.partial(second_body, depth=depth, **sizes), (flat_f, tile_...  8.82 us
    ppermute x2, waiting for transfers between devices, total_over_tiles(): arrived = lax.ppermute(rounded, ('row', 'col'), pairs)  7.41 us
    ppermute x2, starting transfers between devices, exchanged(): lax.ppermute(to_pair, 'row', pairs)  5.83 us
    unnamed x15, local copies, waits for them, and re-layouts  4.13 us
    ppermute x3, waiting for transfers between devices, local(): arrivals.append(lax.ppermute(sending, 'layer', [(k, k + 1)]))  3.93 us
    pallas_call x2, Pallas kernels, first(): call(functools.partial(first_body, depth=depth, sender=sender, **sizes),...  3.14 us
    ppermute x1, starting transfers between devices, from_sides(): other = lax.ppermute(array, 'col', [(0, 1), (1, 0)])  3.03 us
  transfers between devices with their start and end apart: 15, of which 7 were waited for; matrix products, arithmetic and copies ran while one was open for 5% of the time, Pallas kernels for 2%

profile of v7, /device:TPU:0, one launch (start us, length us, event | category | flops | bytes accessed | tf_op | source)
XLA Modules:
  0.0 76.8 jit_solution(3742651173035945481)
XLA Ops:
  0.6 0.9 %copy-done = f32[1,64,8,128]{3,2,1,0:T(8,128)S(1)} copy-done((f32[1,64,8,128]{3,2,1,0:T(8,128)S(1)}, f32[1,64,8,128]{3,2,1,0:T(8,128)}, u32[]{:S(2)}) %copy-start) | copy-done | bytes 262168
  1.6 0.9 %copy-done.2 = f32[1,64,8,128]{3,2,1,0:T(8,128)S(1)} copy-done((f32[1,64,8,128]{3,2,1,0:T(8,128)S(1)}, f32[1,64,8,128]{3,2,1,0:T(8,128)}, u32[]{:S(2)}) %copy-start.2) | copy-done | bytes 262168
  2.7 3.0 %collective-permute-start = (bf16[64,256]{1,0:T(8,128)(2,1)S(1)}, bf16[64,256]{1,0:T(8,128)(2,1)S(1)}, u32[]{:S(2)}, u32[]{:S(2)}) collective-permute-start(bf16[64,256]{1,0:T(8,128)(2,1)S(1)} %shard_map.58), channel_id=1, source_target_pairs={{0,1},{1,0},{2,3},{3,2},{4,5},{5,4},{6,7},{7,6},{8,9},{9,8},{10,11... | collective-permute-start | bytes 98312 | tf_op jit(solution)/shard_map/ppermute | solution.py:436
  6.1 1.5 %collective-permute-done.left_ref.right_ref = bf16[64,256]{1,0:T(8,128)(2,1)S(1)} collective-permute-done((bf16[64,256]{1,0:T(8,128)(2,1)S(1)}, bf16[64,256]{1,0:T(8,128)(2,1)S(1)}, u32[]{:S(2)}, u32[]{:S(2)}) %collective-permute-start) | collective-permute-done | bytes 32800 | tf_op jit(solution)/shard_map/ppermute | solution.py:436
  7.9 0.7 collective-permute-start.2
  8.5 3.4 %collective-permute-start.1 = (bf16[10,64,128]{2,1,0:T(8,128)(2,1)S(1)}, bf16[10,64,128]{2,1,0:T(8,128)(2,1)S(1)}, u32[]{:S(2)}, u32[]{:S(2)}) collective-permute-start(bf16[10,64,128]{2,1,0:T(8,128)(2,1)S(1)} %get-tuple-element.25), channel_id=1, source_target_pairs={{0,2},{2,0},{4,6},{6,4},{1,3},{3,1},{5,7},{7,5},{8,10},{10,8},{12,... | collective-permute-start | bytes 491528 | tf_op jit(solution)/shard_map/ppermute | solution.py:431
  12.0 0.6 copy.11
  13.1 0.5 copy.12
  14.0 3.1 %shard_map.60 = bf16[9,64,128]{2,1,0:T(8,128)(2,1)S(1)} custom-call(f32[512,128]{1,0:T(8,128)S(1)} %bitcast.20, bf16[10,64,128]{2,1,0:T(8,128)(2,1)S(1)} %collective-permute-done.1.pair_ref, bf16[10,64,128]{2,1,0:T(8,128)(2,1)S(1)} %collective-permute-done.2.cross_ref, bf16[64,256]{1,0:T(8,128)(2,1)S(1)} %get-tuple-element.33.side_ref, ...), custom_call_target="tpu_custom_call" | custom-call | flops 830472192 | tf_op jit(solution)/shard_map/pallas_call | solution.py:511
  17.2 1.3 %collective-permute-start.3 = (bf16[9,64,128]{2,1,0:T(8,128)(2,1)S(1)}, bf16[9,64,128]{2,1,0:T(8,128)(2,1)S(1)}, u32[]{:S(2)}, u32[]{:S(2)}) collective-permute-start(bf16[9,64,128]{2,1,0:T(8,128)(2,1)S(1)} %shard_map.60), channel_id=1, source_target_pairs={{0,8},{1,9},{2,10},{3,11},{4,12},{5,13},{6,14},{7,15}} | collective-permute-start | bytes 442376 | tf_op jit(solution)/shard_map/ppermute | solution.py:535
  18.6 3.9 %collective-permute-done.3.s_ref.refs_0_ = bf16[9,64,128]{2,1,0:T(8,128)(2,1)S(1)} collective-permute-done((bf16[9,64,128]{2,1,0:T(8,128)(2,1)S(1)}, bf16[9,64,128]{2,1,0:T(8,128)(2,1)S(1)}, u32[]{:S(2)}, u32[]{:S(2)}) %collective-permute-start.3) | collective-permute-done | bytes 147488 | tf_op jit(solution)/shard_map/ppermute | solution.py:535
  22.8 0.7 collective-permute-start.4
  23.8 0.7 collective-permute-start.5
  24.6 0.7 collective-permute-start.7
  25.3 2.4 %collective-permute-start.6 = (bf16[9,64,128]{2,1,0:T(8,128)(2,1)S(1)}, bf16[9,64,128]{2,1,0:T(8,128)(2,1)S(1)}, u32[]{:S(2)}, u32[]{:S(2)}) collective-permute-start(bf16[9,64,128]{2,1,0:T(8,128)(2,1)S(1)} %shard_map.64.s_ref), channel_id=1, source_target_pairs={{0,2},{2,0},{4,6},{6,4},{1,3},{3,1},{5,7},{7,5},{8,10},{10,8},{12,... | collective-permute-start | bytes 442376 | tf_op jit(solution)/shard_map/ppermute | solution.py:431
  27.7 1.0 %collective-permute-done.6.s_pair_ref = bf16[9,64,128]{2,1,0:T(8,128)(2,1)S(1)} collective-permute-done((bf16[9,64,128]{2,1,0:T(8,128)(2,1)S(1)}, bf16[9,64,128]{2,1,0:T(8,128)(2,1)S(1)}, u32[]{:S(2)}, u32[]{:S(2)}) %collective-permute-start.6) | collective-permute-done | bytes 147488 | tf_op jit(solution)/shard_map/ppermute | solution.py:431
  28.7 8.8 %shard_map.65 = (f32[512,128]{1,0:T(8,128)}, f32[8,64,128]{2,1,0:T(8,128)S(1)}, bf16[8,64,128]{2,1,0:T(8,128)(2,1)S(1)}, bf16[4,8,64,256]{3,2,1,0:T(8,128)(2,1)S(1)}, bf16[4,10,64,128]{3,2,1,0:T(8,128)(2,1)S(1)}) custom-call(f32[512,128]{1,0:T(8,128)S(1)} %bitcast.25, f32[512,128]{1,0:T(8,128)S(1)} %bitcast.28, bf16[9,64,128]{2,1,0:T(8,128)(2,1)S(1)} %shard_map.64.s_ref, ...), custom_call_target="tpu_custom_call" | custom-call | flops 2264924160 | tf_op jit(solution)/shard_map/pallas_call | solution.py:542
  37.5 0.8 %copy-done.4 = bf16[4,10,64,128]{3,2,1,0:T(8,128)(2,1)} copy-done((bf16[4,10,64,128]{3,2,1,0:T(8,128)(2,1)}, bf16[4,10,64,128]{3,2,1,0:T(8,128)(2,1)S(1)}, u32[]{:S(2)}) %copy-start.4) | copy-done | bytes 655384
  38.4 0.7 collective-permute-start.8
  39.1 1.1 %copy-done.5 = bf16[4,10,64,128]{3,2,1,0:T(8,128)(2,1)S(1)} copy-done((bf16[4,10,64,128]{3,2,1,0:T(8,128)(2,1)S(1)}, bf16[4,10,64,128]{3,2,1,0:T(8,128)(2,1)}, u32[]{:S(2)}) %copy-start.5) | copy-done | bytes 655384
  40.2 1.1 %shard_map.66 = f32[4,64,576]{2,1,0:T(8,128)S(1)} custom-call(bf16[4,8,64,256]{3,2,1,0:T(8,128)(2,1)S(1)} %get-tuple-element.38.kept_ref, bf16[4,10,64,128]{3,2,1,0:T(8,128)(2,1)S(1)} %copy-done.5), custom_call_target="tpu_custom_call" | custom-call | flops 1000000000 | tf_op jit(solution)/shard_map/pallas_call | solution.py:562
  41.6 2.8 %collective-permute-start.11 = (f32[2,64,576]{2,1,0:T(8,128)S(1)}, f32[2,64,576]{2,1,0:T(8,128)S(1)}, u32[]{:S(2)}, u32[]{:S(2)}) collective-permute-start(f32[2,64,576]{2,1,0:T(8,128)S(1)} %slice_select_fusion), channel_id=1, source_target_pairs={{0,2},{2,0},{4,6},{6,4},{1,3},{3,1},{5,7},{7,5},{8,10},{10,8},{12,... | collective-permute-start | bytes 884744 | tf_op jit(solution)/shard_map/ppermute | solution.py:449
  44.4 1.3 %collective-permute-done.11 = f32[2,64,576]{2,1,0:T(8,128)S(1)} collective-permute-done((f32[2,64,576]{2,1,0:T(8,128)S(1)}, f32[2,64,576]{2,1,0:T(8,128)S(1)}, u32[]{:S(2)}, u32[]{:S(2)}) %collective-permute-start.11) | collective-permute-done | bytes 294944 | tf_op jit(solution)/shard_map/ppermute | solution.py:449
  45.7 1.1 %collective-permute-start.12 = (bf16[2,64,576]{2,1,0:T(8,128)(2,1)S(1)}, bf16[2,64,576]{2,1,0:T(8,128)(2,1)S(1)}, u32[]{:S(2)}, u32[]{:S(2)}) collective-permute-start(bf16[2,64,576]{2,1,0:T(8,128)(2,1)S(1)} %add_convert_fusion.1), channel_id=1, source_target_pairs={{0,4},{1,5},{2,3},{3,2},{4,0},{5,1},{6,7},{7,6},{8,12},{9,13},{10,... | collective-permute-start | bytes 442376 | tf_op jit(solution)/shard_map/ppermute | solution.py:461
  46.8 4.3 %collective-permute-done.12 = bf16[2,64,576]{2,1,0:T(8,128)(2,1)S(1)} collective-permute-done((bf16[2,64,576]{2,1,0:T(8,128)(2,1)S(1)}, bf16[2,64,576]{2,1,0:T(8,128)(2,1)S(1)}, u32[]{:S(2)}, u32[]{:S(2)}) %collective-permute-start.12) | collective-permute-done | bytes 147488 | tf_op jit(solution)/shard_map/ppermute | solution.py:461
  51.1 1.6 %collective-permute-start.13 = (bf16[2,64,576]{2,1,0:T(8,128)(2,1)S(1)}, bf16[2,64,576]{2,1,0:T(8,128)(2,1)S(1)}, u32[]{:S(2)}, u32[]{:S(2)}) collective-permute-start(bf16[2,64,576]{2,1,0:T(8,128)(2,1)S(1)} %add_convert_fusion), channel_id=1, source_target_pairs={{0,1},{1,0},{2,6},{3,7},{4,5},{5,4},{6,2},{7,3},{8,9},{9,8},{10,14... | collective-permute-start | bytes 442376 | tf_op jit(solution)/shard_map/ppermute | solution.py:461
  52.7 0.7 collective-permute-start.9
  53.4 3.1 %collective-permute-done.13 = bf16[2,64,576]{2,1,0:T(8,128)(2,1)S(1)} collective-permute-done((bf16[2,64,576]{2,1,0:T(8,128)(2,1)S(1)}, bf16[2,64,576]{2,1,0:T(8,128)(2,1)S(1)}, u32[]{:S(2)}, u32[]{:S(2)}) %collective-permute-start.13) | collective-permute-done | bytes 147488 | tf_op jit(solution)/shard_map/ppermute | solution.py:461
  56.9 1.3 %collective-permute-start.10 = (bf16[8,64,128]{2,1,0:T(8,128)(2,1)S(1)}, bf16[8,64,128]{2,1,0:T(8,128)(2,1)S(1)}, u32[]{:S(2)}, u32[]{:S(2)}) collective-permute-start(bf16[8,64,128]{2,1,0:T(8,128)(2,1)S(1)} %shard_map.68), channel_id=1, source_target_pairs={{8,0},{9,1},{10,2},{11,3},{12,4},{13,5},{14,6},{15,7}} | collective-permute-start | bytes 393224 | tf_op jit(solution)/shard_map/ppermute | solution.py:570
  58.3 0.9 %pad_maximum_fusion = f32[4,64,576]{2,1,0:T(8,128)} fusion(f32[2,64,576]{2,1,0:T(8,128)S(1)} %get-tuple-element.46, f32[2,64,576]{2,1,0:T(8,128)S(1)} %get-tuple-element.45), kind=kLoop, calls=%fused_computation | loop fusion | flops 147456 | bytes 1179648 | tf_op jit(solution)/shard_map/concatenate | solution.py:466
  59.2 16.8 %collective-permute-done.10.refs_2_ = bf16[8,64,128]{2,1,0:T(8,128)(2,1)S(1)} collective-permute-done((bf16[8,64,128]{2,1,0:T(8,128)(2,1)S(1)}, bf16[8,64,128]{2,1,0:T(8,128)(2,1)S(1)}, u32[]{:S(2)}, u32[]{:S(2)}) %collective-permute-start.10) | collective-permute-done | bytes 131104 | tf_op jit(solution)/shard_map/ppermute | solution.py:570
  76.0 0.8 %shard_map.69 = f32[512,128]{1,0:T(8,128)} custom-call(f32[512,128]{1,0:T(8,128)S(1)} %bitcast.31, bf16[8,64,128]{2,1,0:T(8,128)(2,1)S(1)} %collective-permute-done.8.s_ref.refs_0_, bf16[8,64,128]{2,1,0:T(8,128)(2,1)S(1)} %collective-permute-done.9.s_ref.refs_1_, bf16[8,64,128]{2,1,0:T(8,128)(2,1)S(1)} %collective-permute-done.10.refs_2_), custom_call_target="tpu_custom_call" | custom-call | flops 10000000000 | tf_op jit(solution)/shard_map/pallas_call | solution.py:575
  (43 shorter events, 3.5 us)
Async XLA Ops:
  0.6 1.0 %copy-start = (f32[1,64,8,128]{3,2,1,0:T(8,128)S(1)}, f32[1,64,8,128]{3,2,1,0:T(8,128)}, u32[]{:S(2)}) copy-start(f32[1,64,8,128]{3,2,1,0:T(8,128)} %param.3) | copy-start | bytes 786436
  1.6 0.9 %copy-start.2 = (f32[1,64,8,128]{3,2,1,0:T(8,128)S(1)}, f32[1,64,8,128]{3,2,1,0:T(8,128)}, u32[]{:S(2)}) copy-start(f32[1,64,8,128]{3,2,1,0:T(8,128)} %param.4) | copy-start | bytes 786436
  2.5 3.2 %copy-start.6 = (bf16[4,64,576]{2,1,0:T(8,128)(2,1)S(1)}, bf16[4,64,576]{2,1,0:T(8,128)(2,1)}, u32[]{:S(2)}) copy-start(bf16[4,64,576]{2,1,0:T(8,128)(2,1)} %param.5) | copy-start | bytes 884740
  2.7 4.9 %collective-permute-start = (bf16[64,256]{1,0:T(8,128)(2,1)S(1)}, bf16[64,256]{1,0:T(8,128)(2,1)S(1)}, u32[]{:S(2)}, u32[]{:S(2)}) collective-permute-start(bf16[64,256]{1,0:T(8,128)(2,1)S(1)} %shard_map.58), channel_id=1, source_target_pairs={{0,1},{1,0},{2,3},{3,2},{4,5},{5,4},{6,7},{7,6},{8,9},{9,8},{10,11... | collective-permute-start | bytes 98312 | tf_op jit(solution)/shard_map/ppermute | solution.py:436
  5.7 1.9 %copy-start.3 = (f32[1,64,8,128]{3,2,1,0:T(8,128)S(1)}, f32[1,64,8,128]{3,2,1,0:T(8,128)}, u32[]{:S(2)}) copy-start(f32[1,64,8,128]{3,2,1,0:T(8,128)} %param.4) | copy-start | bytes 786436
  6.0 1.6 %copy-start.1 = (f32[1,64,8,128]{3,2,1,0:T(8,128)S(1)}, f32[1,64,8,128]{3,2,1,0:T(8,128)}, u32[]{:S(2)}) copy-start(f32[1,64,8,128]{3,2,1,0:T(8,128)} %param.3) | copy-start | bytes 786436
  7.9 6.2 %collective-permute-start.2 = (bf16[10,64,128]{2,1,0:T(8,128)(2,1)S(1)}, bf16[10,64,128]{2,1,0:T(8,128)(2,1)S(1)}, u32[]{:S(2)}, u32[]{:S(2)}) collective-permute-start(bf16[10,64,128]{2,1,0:T(8,128)(2,1)S(1)} %get-tuple-element.26), channel_id=1, source_target_pairs={{2,4},{4,2},{3,5},{5,3},{10,12},{12,10},{11,13},{13,11},{18,20},{2... | collective-permute-start | bytes 491528 | tf_op jit(solution)/shard_map/ppermute | solution.py:431
  8.5 5.5 %collective-permute-start.1 = (bf16[10,64,128]{2,1,0:T(8,128)(2,1)S(1)}, bf16[10,64,128]{2,1,0:T(8,128)(2,1)S(1)}, u32[]{:S(2)}, u32[]{:S(2)}) collective-permute-start(bf16[10,64,128]{2,1,0:T(8,128)(2,1)S(1)} %get-tuple-element.25), channel_id=1, source_target_pairs={{0,2},{2,0},{4,6},{6,4},{1,3},{3,1},{5,7},{7,5},{8,10},{10,8},{12,... | collective-permute-start | bytes 491528 | tf_op jit(solution)/shard_map/ppermute | solution.py:431
  17.2 5.4 %collective-permute-start.3 = (bf16[9,64,128]{2,1,0:T(8,128)(2,1)S(1)}, bf16[9,64,128]{2,1,0:T(8,128)(2,1)S(1)}, u32[]{:S(2)}, u32[]{:S(2)}) collective-permute-start(bf16[9,64,128]{2,1,0:T(8,128)(2,1)S(1)} %shard_map.60), channel_id=1, source_target_pairs={{0,8},{1,9},{2,10},{3,11},{4,12},{5,13},{6,14},{7,15}} | collective-permute-start | bytes 442376 | tf_op jit(solution)/shard_map/ppermute | solution.py:535
  22.8 0.7 collective-permute-start.4
  23.8 0.7 collective-permute-start.5
  24.6 3.1 %collective-permute-start.7 = (bf16[9,64,128]{2,1,0:T(8,128)(2,1)S(1)}, bf16[9,64,128]{2,1,0:T(8,128)(2,1)S(1)}, u32[]{:S(2)}, u32[]{:S(2)}) collective-permute-start(bf16[9,64,128]{2,1,0:T(8,128)(2,1)S(1)} %shard_map.64.s_ref), channel_id=1, source_target_pairs={{2,4},{4,2},{3,5},{5,3},{10,12},{12,10},{11,13},{13,11},{18,20},{2... | collective-permute-start | bytes 442376 | tf_op jit(solution)/shard_map/ppermute | solution.py:431
  25.3 3.4 %collective-permute-start.6 = (bf16[9,64,128]{2,1,0:T(8,128)(2,1)S(1)}, bf16[9,64,128]{2,1,0:T(8,128)(2,1)S(1)}, u32[]{:S(2)}, u32[]{:S(2)}) collective-permute-start(bf16[9,64,128]{2,1,0:T(8,128)(2,1)S(1)} %shard_map.64.s_ref), channel_id=1, source_target_pairs={{0,2},{2,0},{4,6},{6,4},{1,3},{3,1},{5,7},{7,5},{8,10},{10,8},{12,... | collective-permute-start | bytes 442376 | tf_op jit(solution)/shard_map/ppermute | solution.py:431
  37.5 0.8 %copy-start.4 = (bf16[4,10,64,128]{3,2,1,0:T(8,128)(2,1)}, bf16[4,10,64,128]{3,2,1,0:T(8,128)(2,1)S(1)}, u32[]{:S(2)}) copy-start(bf16[4,10,64,128]{3,2,1,0:T(8,128)(2,1)S(1)} %get-tuple-element.39.sent_ref) | copy-start | bytes 1966084
  38.4 2.9 %collective-permute-start.8 = (bf16[8,64,128]{2,1,0:T(8,128)(2,1)S(1)}, bf16[8,64,128]{2,1,0:T(8,128)(2,1)S(1)}, u32[]{:S(2)}, u32[]{:S(2)}) collective-permute-start(bf16[8,64,128]{2,1,0:T(8,128)(2,1)S(1)} %get-tuple-element.37), channel_id=1, source_target_pairs={{24,16},{25,17},{26,18},{27,19},{28,20},{29,21},{30,22},{31,23}} | collective-permute-start | bytes 393224 | tf_op jit(solution)/shard_map/ppermute | solution.py:561
  39.1 1.1 %copy-start.5 = (bf16[4,10,64,128]{3,2,1,0:T(8,128)(2,1)S(1)}, bf16[4,10,64,128]{3,2,1,0:T(8,128)(2,1)}, u32[]{:S(2)}) copy-start(bf16[4,10,64,128]{3,2,1,0:T(8,128)(2,1)} %copy-done.4) | copy-start | bytes 1966084
  41.6 4.0 %collective-permute-start.11 = (f32[2,64,576]{2,1,0:T(8,128)S(1)}, f32[2,64,576]{2,1,0:T(8,128)S(1)}, u32[]{:S(2)}, u32[]{:S(2)}) collective-permute-start(f32[2,64,576]{2,1,0:T(8,128)S(1)} %slice_select_fusion), channel_id=1, source_target_pairs={{0,2},{2,0},{4,6},{6,4},{1,3},{3,1},{5,7},{7,5},{8,10},{10,8},{12,... | collective-permute-start | bytes 884744 | tf_op jit(solution)/shard_map/ppermute | solution.py:449
  45.7 5.4 %collective-permute-start.12 = (bf16[2,64,576]{2,1,0:T(8,128)(2,1)S(1)}, bf16[2,64,576]{2,1,0:T(8,128)(2,1)S(1)}, u32[]{:S(2)}, u32[]{:S(2)}) collective-permute-start(bf16[2,64,576]{2,1,0:T(8,128)(2,1)S(1)} %add_convert_fusion.1), channel_id=1, source_target_pairs={{0,4},{1,5},{2,3},{3,2},{4,0},{5,1},{6,7},{7,6},{8,12},{9,13},{10,... | collective-permute-start | bytes 442376 | tf_op jit(solution)/shard_map/ppermute | solution.py:461
  51.1 5.4 %collective-permute-start.13 = (bf16[2,64,576]{2,1,0:T(8,128)(2,1)S(1)}, bf16[2,64,576]{2,1,0:T(8,128)(2,1)S(1)}, u32[]{:S(2)}, u32[]{:S(2)}) collective-permute-start(bf16[2,64,576]{2,1,0:T(8,128)(2,1)S(1)} %add_convert_fusion), channel_id=1, source_target_pairs={{0,1},{1,0},{2,6},{3,7},{4,5},{5,4},{6,2},{7,3},{8,9},{9,8},{10,14... | collective-permute-start | bytes 442376 | tf_op jit(solution)/shard_map/ppermute | solution.py:461
  52.7 3.9 %collective-permute-start.9 = (bf16[8,64,128]{2,1,0:T(8,128)(2,1)S(1)}, bf16[8,64,128]{2,1,0:T(8,128)(2,1)S(1)}, u32[]{:S(2)}, u32[]{:S(2)}) collective-permute-start(bf16[8,64,128]{2,1,0:T(8,128)(2,1)S(1)} %shard_map.67), channel_id=1, source_target_pairs={{16,8},{17,9},{18,10},{19,11},{20,12},{21,13},{22,14},{23,15}} | collective-permute-start | bytes 393224 | tf_op jit(solution)/shard_map/ppermute | solution.py:570
  56.5 1.7 %collective-permute-start.14 = (f32[2,64,576]{2,1,0:T(8,128)S(1)}, f32[2,64,576]{2,1,0:T(8,128)S(1)}, u32[]{:S(2)}, u32[]{:S(2)}) collective-permute-start(f32[2,64,576]{2,1,0:T(8,128)S(1)} %convert_add_fusion), channel_id=1, source_target_pairs={{0,2},{2,0},{4,6},{6,4},{1,3},{3,1},{5,7},{7,5},{8,10},{10,8},{12,... | collective-permute-start | bytes 884744 | tf_op jit(solution)/shard_map/ppermute | solution.py:463
  56.9 19.1 %collective-permute-start.10 = (bf16[8,64,128]{2,1,0:T(8,128)(2,1)S(1)}, bf16[8,64,128]{2,1,0:T(8,128)(2,1)S(1)}, u32[]{:S(2)}, u32[]{:S(2)}) collective-permute-start(bf16[8,64,128]{2,1,0:T(8,128)(2,1)S(1)} %shard_map.68), channel_id=1, source_target_pairs={{8,0},{9,1},{10,2},{11,3},{12,4},{13,5},{14,6},{15,7}} | collective-permute-start | bytes 393224 | tf_op jit(solution)/shard_map/ppermute | solution.py:570

commit v8 on v7

--- a/solution.py
+++ b/solution.py
@@ -23,6 +23,13 @@
         ),
         compiler_params=pltpu.CompilerParams(vmem_limit_bytes=VMEM_BYTES),
     )
+
+
+def piece_of(parts, row, rows):
+    half = rows // 2
+    if len(parts) == 1 or row < half:
+        return parts[0], row
+    return (parts[1], row - half) if row < rows else (parts[0], half)
 
 
 def row_of(ref, row, channels, rows):
@@ -180,25 +187,26 @@
 
 
 def first_body(
-    c_ref, pair_ref, cross_ref, side_ref, w_ref, out_ref, x_ref, a_ref, a2_ref,
-    *, channels, rows, depth, sender,
+    c_ref, pair_ref, cross_ref, side_ref, w_ref, *refs, channels, rows, depth, sender
 ):
+    outs = refs[:-3]
     active = (lax.axis_index("layer") == 0) == sender
 
     @pl.when(jnp.logical_not(active))
     def nothing():
-        out_ref[...] = jnp.zeros(out_ref.shape, out_ref.dtype)
+        for out_ref in outs:
+            out_ref[...] = jnp.zeros(out_ref.shape, out_ref.dtype)
 
     @pl.when(active)
     def run():
         first_pass(
-            c_ref, pair_ref, cross_ref, side_ref, w_ref, out_ref, x_ref, a_ref, a2_ref,
+            c_ref, pair_ref, cross_ref, side_ref, w_ref, outs, *refs[-3:],
             channels, rows, depth,
         )
 
 
 def first_pass(
-    c_ref, pair_ref, cross_ref, side_ref, w_ref, out_ref, x_ref, a_ref, a2_ref,
+    c_ref, pair_ref, cross_ref, side_ref, w_ref, outs, x_ref, a_ref, a2_ref,
     channels, rows, depth,
 ):
     cols = c_ref.shape[1]
@@ -244,20 +252,31 @@
     values = [x_ref[halo + row, :, :cols] for row in range(rows)]
     values.append(fold_edges(image, 2 * depth, 0, jnp.zeros((channels, cols), f32)))
     for row, value in enumerate(values):
-        out_ref[row] = value.astype(out_ref.dtype)
-
-
-def hop_body(s_ref, c_ref, *refs, channels, rows):
+        out_ref, place = piece_of(outs, row, rows)
+        out_ref[place] = value.astype(out_ref.dtype)
+
+
+def hop_body(s_ref, c_ref, *refs, start, channels, rows):
     f_ref, m_ref, out_ref = refs[-3:]
-    base = [row_of(c_ref, row, channels, rows) for row in range(rows)]
-    base += [ref[...] for ref in refs[:-3]]
-    for row in range(len(base)):
-        e = s_ref[row].astype(f32) - base[row]
+    work = [
+        (row, row_of(c_ref, row, channels, rows)) for row in range(start, start + rows // 2)
+    ]
+    work += [(rows, ref[...]) for ref in refs[:-3]]
+    for place, (row, base) in enumerate(work):
+        e = s_ref[place].astype(f32) - base
         high = e.astype(bf16)
         low = (e - high.astype(f32)).astype(bf16)
         stacked = jnp.concatenate([high, high, low], 0)
         moved = jnp.dot(m_ref[...], stacked, preferred_element_type=f32)
-        out_ref[row] = (f_ref[row] + e + moved).astype(bf16)
+        out_ref[place] = (f_ref[row] + e + moved).astype(bf16)
+
+
+def arrived_row(refs, row, rows):
+    value = 0.0
+    for pieces in zip(refs[::2], refs[1::2]):
+        ref, place = piece_of(pieces, row, rows)
+        value = value + ref[place].astype(f32)
+    return value
 
 
 def settle_body(c_ref, strip_ref, *refs, channels, rows):
@@ -265,13 +284,13 @@
     first = lax.axis_index("layer") == 0
     base = [row_of(c_ref, row, channels, rows) for row in range(rows)] + [strip_ref[...]]
     for row in range(rows + 1):
-        value = sum(ref[row].astype(f32) for ref in arrived)
+        value = arrived_row(arrived, row, rows)
         s_ref[row] = jnp.where(first, base[row], value).astype(bf16)
 
 
 def second_body(
     c_ref, q_ref, s_ref, s_pair_ref, s_cross_ref, pair_ref, cross_ref, side_ref, w_ref, wt_ref,
-    state_ref, g_ref, sending_ref, kept_ref, sent_ref,
+    state_ref, g_ref, g_upper_ref, g_lower_ref, kept_ref, sent_ref,
     x_ref, a_ref, a2_ref, slope_ref, adj_ref, src_ref,
     *, channels, rows, depth,
 ):
@@ -374,7 +393,8 @@
     for row in range(rows):
         value = adj_ref[halo + row, :, :cols]
         g_ref[row] = value
-        sending_ref[row] = value.astype(bf16)
+        ref, place = piece_of((g_upper_ref, g_lower_ref), row, rows)
+        ref[place] = value.astype(bf16)
 
 
 def grad_body(kept_ref, sent_ref, grad_ref, *, channels, rows, depth):
@@ -413,7 +433,7 @@
     arrived, out_ref = refs[:-1], refs[-1]
     last = lax.axis_index("layer") == lax.axis_size("layer") - 1
     for row in range(rows):
-        value = sum(ref[row].astype(f32) for ref in arrived)
+        value = arrived_row(arrived, row, rows)
         value = jnp.where(last, row_of(q_ref, row, channels, rows), value)
         out_ref[pl.ds(row, channels, stride=rows), :] = value
 
@@ -477,9 +497,13 @@
 
     strip_f = jax.ShapeDtypeStruct((channels, cols), f32)
     wide_b = jax.ShapeDtypeStruct((channels, 2 * cols), bf16)
-    more_f, more_b, message_b = (
+    half = rows // 2
+    more_f, more_b, upper_b, lower_b, message_b = (
         jax.ShapeDtypeStruct((count, channels, cols), kind)
-        for count, kind in ((rows + 1, f32), (rows + 1, bf16), (2 * depth + 2, bf16))
+        for count, kind in (
+            (rows + 1, f32), (rows + 1, bf16), (half + 1, bf16), (half, bf16),
+            (2 * depth + 2, bf16),
+        )
     )
     flat_f = jax.ShapeDtypeStruct(flat, f32)
     edges = call(functools.partial(strip_body, depth=depth, **sizes), wide_b)(c_flat, q_flat)
@@ -519,32 +543,44 @@
             flops=mac * 44,
         )(*inputs)
 
-    def hop(arrived, base, target, matrix):
-        return call(
-            functools.partial(hop_body, **sizes),
-            jax.ShapeDtypeStruct(arrived.shape, bf16),
-            flops=10**10,
-        )(arrived, *base, target, matrix)
+    def chain(pieces, target, matrix, order):
+        sendings = [piece[0] for piece in pieces]
+        arrivals = []
+        for turn, step in enumerate(order):
+            arrived = [lax.ppermute(sending, "layer", [step]) for sending in sendings]
+            arrivals += arrived
+            if turn < len(order) - 1:
+                sendings = [
+                    call(
+                        functools.partial(hop_body, start=start, **sizes),
+                        jax.ShapeDtypeStruct(value.shape, bf16),
+                        flops=10**10,
+                    )(value, *base, target, matrix)
+                    for value, (_, start, base) in zip(arrived, pieces)
+                ]
+        return arrivals
 
     inputs = (c_flat, pair, cross, side, w_fwd)
-    sending = first(more_b, True, *inputs)
-    inputs = lax.optimization_barrier((inputs, sending))[0]
-    f = first(more_f, False, *inputs)
-    arrivals = []
-    for k in range(groups - 1):
-        arrivals.append(lax.ppermute(sending, "layer", [(k, k + 1)]))
-        if k < groups - 2:
-            sending = hop(arrivals[-1], (c_flat, strip), f, m_fwd)
+    upper, lower = first((upper_b, lower_b), True, *inputs)
+    inputs = lax.optimization_barrier((inputs, upper))[0]
+    (f,) = first((more_f,), False, *inputs)
+    arrivals = chain(
+        ((upper, 0, (c_flat, strip)), (lower, half, (c_flat,))),
+        f,
+        m_fwd,
+        [(k, k + 1) for k in range(groups - 1)],
+    )
     s = call(functools.partial(settle_body, **sizes), more_b)(c_flat, strip, *arrivals)
     s_pair, s_cross = exchanged(s, s)
 
     total = rows + 4 * depth
-    state, g, sending, kept, sources = call(
+    state, g, upper, lower, kept, sources = call(
         functools.partial(second_body, depth=depth, **sizes),
         (
             flat_f,
             tile_f,
-            jax.ShapeDtypeStruct(tile_f.shape, bf16),
+            lower_b,
+            lower_b,
             jax.ShapeDtypeStruct((depth, rows, channels, lanes), bf16),
             jax.ShapeDtypeStruct((depth, rows + 2, channels, cols), bf16),
         ),
@@ -558,20 +594,18 @@
         ],
         flops=mac * 120,
     )(c_flat, q_flat, s, s_pair, s_cross, pair, cross, side, w_fwd, w_back)
-    returned = [lax.ppermute(sending, "layer", [(groups - 1, groups - 2)])]
+    returned = chain(
+        ((upper, 0, (q_flat,)), (lower, half, (q_flat,))),
+        g,
+        m_back,
+        [(k, k - 1) for k in range(groups - 1, 0, -1)],
+    )
     grads = call(
         functools.partial(grad_body, depth=depth, **sizes),
         jax.ShapeDtypeStruct((depth, channels, 9 * channels), f32),
         flops=10**9,
     )(kept, sources)
-    sending = hop(returned[0], (q_flat,), g, m_back)
-    grads, sending = lax.optimization_barrier((grads, sending))
-    for k in range(groups - 2, 0, -1):
-        returned.append(lax.ppermute(sending, "layer", [(k, k - 1)]))
-        if k > 1:
-            sending = hop(returned[-1], (q_flat,), g, m_back)
     weight_grads = total_over_tiles(grads)
-    returned[-1], weight_grads = lax.optimization_barrier((returned[-1], weight_grads))
     adjoint = call(
         functools.partial(last_body, **sizes), jax.ShapeDtypeStruct(flat, f32), flops=10**10
     )(q_flat, *returned)

time: 77.2 us -> 68.9 us (0.89)
  the two profiles are of different devices: /device:TPU:0 before, /device:TPU:19 now
where the time goes in v8:
time: 68.9 us; the launch traced here: 68.5 us
  starting transfers between devices  35.8 us (52%)
  Pallas kernels  16 us (23%)
  waiting for transfers between devices  10.1 us (15%)
  local copies, waits for them, and re-layouts  4.33 us (6%)
  other arithmetic  1.25 us (2%)
  between operations  1.02 us (1%)
    ppermute x12, starting transfers between devices, chain(): arrived = [lax.ppermute(sending, 'layer', [step]) for sending in sendings]  13 us
    ppermute x2, starting transfers between devices, exchanged(): lax.ppermute(to_pair, 'row', pairs)  9.26 us
    pallas_call x1, Pallas kernels, local(): call(functools.partial(second_body, depth=depth, **sizes), (flat_f, tile_...  8.83 us
    ppermute x1, starting transfers between devices, total_over_tiles(): other = lax.ppermute(value, 'row', pair)  4.29 us
    ppermute x2, waiting for transfers between devices, total_over_tiles(): arrived = lax.ppermute(rounded, ('row', 'col'), pairs)  3.88 us
    ppermute x12, waiting for transfers between devices, chain(): arrived = [lax.ppermute(sending, 'layer', [step]) for sending in sendings]  3.71 us
    ppermute x2, starting transfers between devices, total_over_tiles(): arrived = lax.ppermute(rounded, ('row', 'col'), pairs)  3.25 us
    ppermute x1, starting transfers between devices, total_over_tiles(): value = own + lax.ppermute(sent, 'row', pair)  3.22 us
  transfers between devices with their start and end apart: 21, of which 7 were waited for; matrix products, arithmetic and copies ran while one was open for 4% of the time, Pallas kernels for 10%

profile of v8, /device:TPU:19, one launch (start us, length us, event | category | flops | bytes accessed | tf_op | source)
XLA Modules:
  0.0 68.5 jit_solution(8569047306098531786)
XLA Ops:
  0.6 0.9 %copy-done = f32[1,64,8,128]{3,2,1,0:T(8,128)S(1)} copy-done((f32[1,64,8,128]{3,2,1,0:T(8,128)S(1)}, f32[1,64,8,128]{3,2,1,0:T(8,128)}, u32[]{:S(2)}) %copy-start) | copy-done | bytes 262168
  1.6 0.9 %copy-done.2 = f32[1,64,8,128]{3,2,1,0:T(8,128)S(1)} copy-done((f32[1,64,8,128]{3,2,1,0:T(8,128)S(1)}, f32[1,64,8,128]{3,2,1,0:T(8,128)}, u32[]{:S(2)}) %copy-start.2) | copy-done | bytes 262168
  2.7 1.3 %collective-permute-start = (bf16[64,256]{1,0:T(8,128)(2,1)S(1)}, bf16[64,256]{1,0:T(8,128)(2,1)S(1)}, u32[]{:S(2)}, u32[]{:S(2)}) collective-permute-start(bf16[64,256]{1,0:T(8,128)(2,1)S(1)} %shard_map.58), channel_id=1, source_target_pairs={{0,1},{1,0},{2,3},{3,2},{4,5},{5,4},{6,7},{7,6},{8,9},{9,8},{10,11... | collective-permute-start | bytes 98312 | tf_op jit(solution)/shard_map/ppermute | solution.py:456
  4.4 1.1 %collective-permute-done.left_ref.right_ref = bf16[64,256]{1,0:T(8,128)(2,1)S(1)} collective-permute-done((bf16[64,256]{1,0:T(8,128)(2,1)S(1)}, bf16[64,256]{1,0:T(8,128)(2,1)S(1)}, u32[]{:S(2)}, u32[]{:S(2)}) %collective-permute-start) | collective-permute-done | bytes 32800 | tf_op jit(solution)/shard_map/ppermute | solution.py:456
  5.8 0.7 collective-permute-start.2
  6.4 3.1 %collective-permute-start.1 = (bf16[10,64,128]{2,1,0:T(8,128)(2,1)S(1)}, bf16[10,64,128]{2,1,0:T(8,128)(2,1)S(1)}, u32[]{:S(2)}, u32[]{:S(2)}) collective-permute-start(bf16[10,64,128]{2,1,0:T(8,128)(2,1)S(1)} %get-tuple-element.24), channel_id=1, source_target_pairs={{0,2},{2,0},{4,6},{6,4},{1,3},{3,1},{5,7},{7,5},{8,10},{10,8},{12,... | collective-permute-start | bytes 491528 | tf_op jit(solution)/shard_map/ppermute | solution.py:451
  11.7 0.7 collective-permute-start.3
  13.2 3.1 %shard_map.61.refs_1_.refs_0_ = f32[9,64,128]{2,1,0:T(8,128)S(1)} custom-call(f32[512,128]{1,0:T(8,128)S(1)} %bitcast.21, bf16[10,64,128]{2,1,0:T(8,128)(2,1)S(1)} %collective-permute-done.1.pair_ref, bf16[10,64,128]{2,1,0:T(8,128)(2,1)S(1)} %collective-permute-done.2.cross_ref, bf16[64,256]{1,0:T(8,128)(2,1)S(1)} %get-tuple-element.34.side_ref, ...), custom_call_target="tpu_custom_call" | custom-call | flops 830472192 | tf_op jit(solution)/shard_map/pallas_call | solution.py:535
  16.5 1.3 %collective-permute-start.5 = (bf16[5,64,128]{2,1,0:T(8,128)(2,1)S(1)}, bf16[5,64,128]{2,1,0:T(8,128)(2,1)S(1)}, u32[]{:S(2)}, u32[]{:S(2)}) collective-permute-start(bf16[5,64,128]{2,1,0:T(8,128)(2,1)S(1)} %shard_map.62), channel_id=1, source_target_pairs={{8,16},{9,17},{10,18},{11,19},{12,20},{13,21},{14,22},{15,23}} | collective-permute-start | bytes 245768 | tf_op jit(solution)/shard_map/ppermute | solution.py:550
  18.1 1.3 %collective-permute-start.6 = (bf16[4,64,128]{2,1,0:T(8,128)(2,1)S(1)}, bf16[4,64,128]{2,1,0:T(8,128)(2,1)S(1)}, u32[]{:S(2)}, u32[]{:S(2)}) collective-permute-start(bf16[4,64,128]{2,1,0:T(8,128)(2,1)S(1)} %shard_map.63), channel_id=1, source_target_pairs={{8,16},{9,17},{10,18},{11,19},{12,20},{13,21},{14,22},{15,23}} | collective-permute-start | bytes 196616 | tf_op jit(solution)/shard_map/ppermute | solution.py:550
  19.4 2.4 %collective-permute-done.5.s_ref.refs_2_ = bf16[5,64,128]{2,1,0:T(8,128)(2,1)S(1)} collective-permute-done((bf16[5,64,128]{2,1,0:T(8,128)(2,1)S(1)}, bf16[5,64,128]{2,1,0:T(8,128)(2,1)S(1)}, u32[]{:S(2)}, u32[]{:S(2)}) %collective-permute-start.5) | collective-permute-done | bytes 81952 | tf_op jit(solution)/shard_map/ppermute | solution.py:550
  21.9 1.3 %collective-permute-start.7 = (bf16[5,64,128]{2,1,0:T(8,128)(2,1)S(1)}, bf16[5,64,128]{2,1,0:T(8,128)(2,1)S(1)}, u32[]{:S(2)}, u32[]{:S(2)}) collective-permute-start(bf16[5,64,128]{2,1,0:T(8,128)(2,1)S(1)} %shard_map.64), channel_id=1, source_target_pairs={{16,24},{17,25},{18,26},{19,27},{20,28},{21,29},{22,30},{23,31}} | collective-permute-start | bytes 245768 | tf_op jit(solution)/shard_map/ppermute | solution.py:550
  23.5 1.3 %collective-permute-start.8 = (bf16[4,64,128]{2,1,0:T(8,128)(2,1)S(1)}, bf16[4,64,128]{2,1,0:T(8,128)(2,1)S(1)}, u32[]{:S(2)}, u32[]{:S(2)}) collective-permute-start(bf16[4,64,128]{2,1,0:T(8,128)(2,1)S(1)} %shard_map.65), channel_id=1, source_target_pairs={{16,24},{17,25},{18,26},{19,27},{20,28},{21,29},{22,30},{23,31}} | collective-permute-start | bytes 196616 | tf_op jit(solution)/shard_map/ppermute | solution.py:550
  24.8 1.3 %collective-permute-done.8.refs_5_ = bf16[4,64,128]{2,1,0:T(8,128)(2,1)S(1)} collective-permute-done((bf16[4,64,128]{2,1,0:T(8,128)(2,1)S(1)}, bf16[4,64,128]{2,1,0:T(8,128)(2,1)S(1)}, u32[]{:S(2)}, u32[]{:S(2)}) %collective-permute-start.8) | collective-permute-done | bytes 65568 | tf_op jit(solution)/shard_map/ppermute | solution.py:550
  26.2 0.9 %collective-permute-start.10 = (bf16[9,64,128]{2,1,0:T(8,128)(2,1)S(1)}, bf16[9,64,128]{2,1,0:T(8,128)(2,1)S(1)}, u32[]{:S(2)}, u32[]{:S(2)}) collective-permute-start(bf16[9,64,128]{2,1,0:T(8,128)(2,1)S(1)} %shard_map.66.s_ref), channel_id=1, source_target_pairs={{2,4},{4,2},{3,5},{5,3},{10,12},{12,10},{11,13},{13,11},{18,20},{2... | collective-permute-start | bytes 442376 | tf_op jit(solution)/shard_map/ppermute | solution.py:451
  27.0 6.1 %collective-permute-start.9 = (bf16[9,64,128]{2,1,0:T(8,128)(2,1)S(1)}, bf16[9,64,128]{2,1,0:T(8,128)(2,1)S(1)}, u32[]{:S(2)}, u32[]{:S(2)}) collective-permute-start(bf16[9,64,128]{2,1,0:T(8,128)(2,1)S(1)} %shard_map.66.s_ref), channel_id=1, source_target_pairs={{0,2},{2,0},{4,6},{6,4},{1,3},{3,1},{5,7},{7,5},{8,10},{10,8},{12,... | collective-permute-start | bytes 442376 | tf_op jit(solution)/shard_map/ppermute | solution.py:451
  33.2 0.9 %collective-permute-done.9.s_pair_ref = bf16[9,64,128]{2,1,0:T(8,128)(2,1)S(1)} collective-permute-done((bf16[9,64,128]{2,1,0:T(8,128)(2,1)S(1)}, bf16[9,64,128]{2,1,0:T(8,128)(2,1)S(1)}, u32[]{:S(2)}, u32[]{:S(2)}) %collective-permute-start.9) | collective-permute-done | bytes 147488 | tf_op jit(solution)/shard_map/ppermute | solution.py:451
  34.1 8.8 %shard_map.67 = (f32[512,128]{1,0:T(8,128)}, f32[8,64,128]{2,1,0:T(8,128)S(1)}, bf16[4,64,128]{2,1,0:T(8,128)(2,1)S(1)}, bf16[4,64,128]{2,1,0:T(8,128)(2,1)S(1)}...) custom-call(f32[512,128]{1,0:T(8,128)S(1)} %bitcast.27, f32[512,128]{1,0:T(8,128)S(1)} %bitcast.30, ...), custom_call_target="tpu_custom_call" | custom-call | flops 2264924160 | tf_op jit(solution)/shard_map/pallas_call | solution.py:577
  43.0 1.3 %collective-permute-start.11 = (bf16[4,64,128]{2,1,0:T(8,128)(2,1)S(1)}, bf16[4,64,128]{2,1,0:T(8,128)(2,1)S(1)}, u32[]{:S(2)}, u32[]{:S(2)}) collective-permute-start(bf16[4,64,128]{2,1,0:T(8,128)(2,1)S(1)} %get-tuple-element.38), channel_id=1, source_target_pairs={{24,16},{25,17},{26,18},{27,19},{28,20},{29,21},{30,22},{31,23}} | collective-permute-start | bytes 196616 | tf_op jit(solution)/shard_map/ppermute | solution.py:550
  44.3 1.3 %collective-permute-start.12 = (bf16[4,64,128]{2,1,0:T(8,128)(2,1)S(1)}, bf16[4,64,128]{2,1,0:T(8,128)(2,1)S(1)}, u32[]{:S(2)}, u32[]{:S(2)}) collective-permute-start(bf16[4,64,128]{2,1,0:T(8,128)(2,1)S(1)} %get-tuple-element.39), channel_id=1, source_target_pairs={{24,16},{25,17},{26,18},{27,19},{28,20},{29,21},{30,22},{31,23}} | collective-permute-start | bytes 196616 | tf_op jit(solution)/shard_map/ppermute | solution.py:550
  45.6 1.1 %shard_map.73 = f32[4,64,576]{2,1,0:T(8,128)S(1)} custom-call(bf16[4,8,64,256]{3,2,1,0:T(8,128)(2,1)S(1)} %get-tuple-element.41.kept_ref, bf16[4,10,64,128]{3,2,1,0:T(8,128)(2,1)S(1)} %get-tuple-element.42.sent_ref), custom_call_target="tpu_custom_call" | custom-call | flops 1000000000 | tf_op jit(solution)/shard_map/pallas_call | solution.py:603
  46.7 3.2 %collective-permute-start.17 = (f32[2,64,576]{2,1,0:T(8,128)S(1)}, f32[2,64,576]{2,1,0:T(8,128)S(1)}, u32[]{:S(2)}, u32[]{:S(2)}) collective-permute-start(f32[2,64,576]{2,1,0:T(8,128)S(1)} %slice_select_fusion), channel_id=1, source_target_pairs={{0,2},{2,0},{4,6},{6,4},{1,3},{3,1},{5,7},{7,5},{8,10},{10,8},{12,... | collective-permute-start | bytes 884744 | tf_op jit(solution)/shard_map/ppermute | solution.py:469
  50.1 1.3 %collective-permute-start.13 = (bf16[4,64,128]{2,1,0:T(8,128)(2,1)S(1)}, bf16[4,64,128]{2,1,0:T(8,128)(2,1)S(1)}, u32[]{:S(2)}, u32[]{:S(2)}) collective-permute-start(bf16[4,64,128]{2,1,0:T(8,128)(2,1)S(1)} %shard_map.68), channel_id=1, source_target_pairs={{16,8},{17,9},{18,10},{19,11},{20,12},{21,13},{22,14},{23,15}} | collective-permute-start | bytes 196616 | tf_op jit(solution)/shard_map/ppermute | solution.py:550
  51.7 1.3 %collective-permute-start.14 = (bf16[4,64,128]{2,1,0:T(8,128)(2,1)S(1)}, bf16[4,64,128]{2,1,0:T(8,128)(2,1)S(1)}, u32[]{:S(2)}, u32[]{:S(2)}) collective-permute-start(bf16[4,64,128]{2,1,0:T(8,128)(2,1)S(1)} %shard_map.69), channel_id=1, source_target_pairs={{16,8},{17,9},{18,10},{19,11},{20,12},{21,13},{22,14},{23,15}} | collective-permute-start | bytes 196616 | tf_op jit(solution)/shard_map/ppermute | solution.py:550
  53.0 1.3 %collective-permute-start.18 = (bf16[2,64,576]{2,1,0:T(8,128)(2,1)S(1)}, bf16[2,64,576]{2,1,0:T(8,128)(2,1)S(1)}, u32[]{:S(2)}, u32[]{:S(2)}) collective-permute-start(bf16[2,64,576]{2,1,0:T(8,128)(2,1)S(1)} %add_convert_fusion.1), channel_id=1, source_target_pairs={{0,4},{1,5},{2,3},{3,2},{4,0},{5,1},{6,7},{7,6},{8,12},{9,13},{10,... | collective-permute-start | bytes 442376 | tf_op jit(solution)/shard_map/ppermute | solution.py:481
  54.5 0.7 collective-permute-start.15
  55.2 2.1 %collective-permute-done.18 = bf16[2,64,576]{2,1,0:T(8,128)(2,1)S(1)} collective-permute-done((bf16[2,64,576]{2,1,0:T(8,128)(2,1)S(1)}, bf16[2,64,576]{2,1,0:T(8,128)(2,1)S(1)}, u32[]{:S(2)}, u32[]{:S(2)}) %collective-permute-start.18) | collective-permute-done | bytes 147488 | tf_op jit(solution)/shard_map/ppermute | solution.py:481
  57.3 2.0 %collective-permute-start.19 = (bf16[2,64,576]{2,1,0:T(8,128)(2,1)S(1)}, bf16[2,64,576]{2,1,0:T(8,128)(2,1)S(1)}, u32[]{:S(2)}, u32[]{:S(2)}) collective-permute-start(bf16[2,64,576]{2,1,0:T(8,128)(2,1)S(1)} %add_convert_fusion), channel_id=1, source_target_pairs={{0,1},{1,0},{2,6},{3,7},{4,5},{5,4},{6,2},{7,3},{8,9},{9,8},{10,14... | collective-permute-start | bytes 442376 | tf_op jit(solution)/shard_map/ppermute | solution.py:481
  60.1 1.8 %collective-permute-done.19 = bf16[2,64,576]{2,1,0:T(8,128)(2,1)S(1)} collective-permute-done((bf16[2,64,576]{2,1,0:T(8,128)(2,1)S(1)}, bf16[2,64,576]{2,1,0:T(8,128)(2,1)S(1)}, u32[]{:S(2)}, u32[]{:S(2)}) %collective-permute-start.19) | collective-permute-done | bytes 147488 | tf_op jit(solution)/shard_map/ppermute | solution.py:481
  62.0 4.3 %collective-permute-start.20 = (f32[2,64,576]{2,1,0:T(8,128)S(1)}, f32[2,64,576]{2,1,0:T(8,128)S(1)}, u32[]{:S(2)}, u32[]{:S(2)}) collective-permute-start(f32[2,64,576]{2,1,0:T(8,128)S(1)} %convert_add_fusion), channel_id=1, source_target_pairs={{0,2},{2,0},{4,6},{6,4},{1,3},{3,1},{5,7},{7,5},{8,10},{10,8},{12,... | collective-permute-start | bytes 884744 | tf_op jit(solution)/shard_map/ppermute | solution.py:483
  66.3 0.8 %shard_map.72 = f32[512,128]{1,0:T(8,128)} custom-call(f32[512,128]{1,0:T(8,128)S(1)} %bitcast.35, bf16[4,64,128]{2,1,0:T(8,128)(2,1)S(1)} %collective-permute-done.11.s_ref.refs_0_, bf16[4,64,128]{2,1,0:T(8,128)(2,1)S(1)} %collective-permute-done.12.s_ref.refs_1_, bf16[4,64,128]{2,1,0:T(8,128)(2,1)S(1)} %collective-permute-done.13.s_ref.refs_2_, ...), custom_call_target="tpu_custom_call" | custom-call | flops 10000000000 | tf_op jit(solution)/shard_map/pallas_call | solution.py:609
  67.6 0.9 %pad_maximum_fusion = f32[4,64,576]{2,1,0:T(8,128)} fusion(f32[2,64,576]{2,1,0:T(8,128)S(1)} %get-tuple-element.44, f32[2,64,576]{2,1,0:T(8,128)S(1)} %get-tuple-element.43), kind=kLoop, calls=%fused_computation | loop fusion | flops 147456 | bytes 1179648 | tf_op jit(solution)/shard_map/concatenate | solution.py:486
  (55 shorter events, 6.8 us)
Async XLA Ops:
  0.6 1.0 %copy-start = (f32[1,64,8,128]{3,2,1,0:T(8,128)S(1)}, f32[1,64,8,128]{3,2,1,0:T(8,128)}, u32[]{:S(2)}) copy-start(f32[1,64,8,128]{3,2,1,0:T(8,128)} %param.3) | copy-start | bytes 786436
  1.6 0.9 %copy-start.2 = (f32[1,64,8,128]{3,2,1,0:T(8,128)S(1)}, f32[1,64,8,128]{3,2,1,0:T(8,128)}, u32[]{:S(2)}) copy-start(f32[1,64,8,128]{3,2,1,0:T(8,128)} %param.4) | copy-start | bytes 786436
  2.5 1.5 %copy-start.4 = (bf16[4,64,576]{2,1,0:T(8,128)(2,1)S(1)}, bf16[4,64,576]{2,1,0:T(8,128)(2,1)}, u32[]{:S(2)}) copy-start(bf16[4,64,576]{2,1,0:T(8,128)(2,1)} %param.5) | copy-start | bytes 884740
  2.7 2.8 %collective-permute-start = (bf16[64,256]{1,0:T(8,128)(2,1)S(1)}, bf16[64,256]{1,0:T(8,128)(2,1)S(1)}, u32[]{:S(2)}, u32[]{:S(2)}) collective-permute-start(bf16[64,256]{1,0:T(8,128)(2,1)S(1)} %shard_map.58), channel_id=1, source_target_pairs={{0,1},{1,0},{2,3},{3,2},{4,5},{5,4},{6,7},{7,6},{8,9},{9,8},{10,11... | collective-permute-start | bytes 98312 | tf_op jit(solution)/shard_map/ppermute | solution.py:456
  4.0 1.5 %copy-start.3 = (f32[1,64,8,128]{3,2,1,0:T(8,128)S(1)}, f32[1,64,8,128]{3,2,1,0:T(8,128)}, u32[]{:S(2)}) copy-start(f32[1,64,8,128]{3,2,1,0:T(8,128)} %param.4) | copy-start | bytes 786436
  4.3 1.2 %copy-start.1 = (f32[1,64,8,128]{3,2,1,0:T(8,128)S(1)}, f32[1,64,8,128]{3,2,1,0:T(8,128)}, u32[]{:S(2)}) copy-start(f32[1,64,8,128]{3,2,1,0:T(8,128)} %param.3) | copy-start | bytes 786436
  5.8 5.9 %collective-permute-start.2 = (bf16[10,64,128]{2,1,0:T(8,128)(2,1)S(1)}, bf16[10,64,128]{2,1,0:T(8,128)(2,1)S(1)}, u32[]{:S(2)}, u32[]{:S(2)}) collective-permute-start(bf16[10,64,128]{2,1,0:T(8,128)(2,1)S(1)} %get-tuple-element.25), channel_id=1, source_target_pairs={{2,4},{4,2},{3,5},{5,3},{10,12},{12,10},{11,13},{13,11},{18,20},{2... | collective-permute-start | bytes 491528 | tf_op jit(solution)/shard_map/ppermute | solution.py:451
  6.4 5.2 %collective-permute-start.1 = (bf16[10,64,128]{2,1,0:T(8,128)(2,1)S(1)}, bf16[10,64,128]{2,1,0:T(8,128)(2,1)S(1)}, u32[]{:S(2)}, u32[]{:S(2)}) collective-permute-start(bf16[10,64,128]{2,1,0:T(8,128)(2,1)S(1)} %get-tuple-element.24), channel_id=1, source_target_pairs={{0,2},{2,0},{4,6},{6,4},{1,3},{3,1},{5,7},{7,5},{8,10},{10,8},{12,... | collective-permute-start | bytes 491528 | tf_op jit(solution)/shard_map/ppermute | solution.py:451
  11.7 4.6 %collective-permute-start.3 = (bf16[5,64,128]{2,1,0:T(8,128)(2,1)S(1)}, bf16[5,64,128]{2,1,0:T(8,128)(2,1)S(1)}, u32[]{:S(2)}, u32[]{:S(2)}) collective-permute-start(bf16[5,64,128]{2,1,0:T(8,128)(2,1)S(1)} %get-tuple-element.29), channel_id=1, source_target_pairs={{0,8},{1,9},{2,10},{3,11},{4,12},{5,13},{6,14},{7,15}} | collective-permute-start | bytes 245768 | tf_op jit(solution)/shard_map/ppermute | solution.py:550
  12.5 5.3 %collective-permute-start.4 = (bf16[4,64,128]{2,1,0:T(8,128)(2,1)S(1)}, bf16[4,64,128]{2,1,0:T(8,128)(2,1)S(1)}, u32[]{:S(2)}, u32[]{:S(2)}) collective-permute-start(bf16[4,64,128]{2,1,0:T(8,128)(2,1)S(1)} %get-tuple-element.30), channel_id=1, source_target_pairs={{0,8},{1,9},{2,10},{3,11},{4,12},{5,13},{6,14},{7,15}} | collective-permute-start | bytes 196616 | tf_op jit(solution)/shard_map/ppermute | solution.py:550
  16.5 5.2 %collective-permute-start.5 = (bf16[5,64,128]{2,1,0:T(8,128)(2,1)S(1)}, bf16[5,64,128]{2,1,0:T(8,128)(2,1)S(1)}, u32[]{:S(2)}, u32[]{:S(2)}) collective-permute-start(bf16[5,64,128]{2,1,0:T(8,128)(2,1)S(1)} %shard_map.62), channel_id=1, source_target_pairs={{8,16},{9,17},{10,18},{11,19},{12,20},{13,21},{14,22},{15,23}} | collective-permute-start | bytes 245768 | tf_op jit(solution)/shard_map/ppermute | solution.py:550
  18.1 5.2 %collective-permute-start.6 = (bf16[4,64,128]{2,1,0:T(8,128)(2,1)S(1)}, bf16[4,64,128]{2,1,0:T(8,128)(2,1)S(1)}, u32[]{:S(2)}, u32[]{:S(2)}) collective-permute-start(bf16[4,64,128]{2,1,0:T(8,128)(2,1)S(1)} %shard_map.63), channel_id=1, source_target_pairs={{8,16},{9,17},{10,18},{11,19},{12,20},{13,21},{14,22},{15,23}} | collective-permute-start | bytes 196616 | tf_op jit(solution)/shard_map/ppermute | solution.py:550
  21.9 4.1 %collective-permute-start.7 = (bf16[5,64,128]{2,1,0:T(8,128)(2,1)S(1)}, bf16[5,64,128]{2,1,0:T(8,128)(2,1)S(1)}, u32[]{:S(2)}, u32[]{:S(2)}) collective-permute-start(bf16[5,64,128]{2,1,0:T(8,128)(2,1)S(1)} %shard_map.64), channel_id=1, source_target_pairs={{16,24},{17,25},{18,26},{19,27},{20,28},{21,29},{22,30},{23,31}} | collective-permute-start | bytes 245768 | tf_op jit(solution)/shard_map/ppermute | solution.py:550
  23.5 2.6 %collective-permute-start.8 = (bf16[4,64,128]{2,1,0:T(8,128)(2,1)S(1)}, bf16[4,64,128]{2,1,0:T(8,128)(2,1)S(1)}, u32[]{:S(2)}, u32[]{:S(2)}) collective-permute-start(bf16[4,64,128]{2,1,0:T(8,128)(2,1)S(1)} %shard_map.65), channel_id=1, source_target_pairs={{16,24},{17,25},{18,26},{19,27},{20,28},{21,29},{22,30},{23,31}} | collective-permute-start | bytes 196616 | tf_op jit(solution)/shard_map/ppermute | solution.py:550
  26.2 7.1 %collective-permute-start.10 = (bf16[9,64,128]{2,1,0:T(8,128)(2,1)S(1)}, bf16[9,64,128]{2,1,0:T(8,128)(2,1)S(1)}, u32[]{:S(2)}, u32[]{:S(2)}) collective-permute-start(bf16[9,64,128]{2,1,0:T(8,128)(2,1)S(1)} %shard_map.66.s_ref), channel_id=1, source_target_pairs={{2,4},{4,2},{3,5},{5,3},{10,12},{12,10},{11,13},{13,11},{18,20},{2... | collective-permute-start | bytes 442376 | tf_op jit(solution)/shard_map/ppermute | solution.py:451
  27.0 7.1 %collective-permute-start.9 = (bf16[9,64,128]{2,1,0:T(8,128)(2,1)S(1)}, bf16[9,64,128]{2,1,0:T(8,128)(2,1)S(1)}, u32[]{:S(2)}, u32[]{:S(2)}) collective-permute-start(bf16[9,64,128]{2,1,0:T(8,128)(2,1)S(1)} %shard_map.66.s_ref), channel_id=1, source_target_pairs={{0,2},{2,0},{4,6},{6,4},{1,3},{3,1},{5,7},{7,5},{8,10},{10,8},{12,... | collective-permute-start | bytes 442376 | tf_op jit(solution)/shard_map/ppermute | solution.py:451
  43.0 7.0 %collective-permute-start.11 = (bf16[4,64,128]{2,1,0:T(8,128)(2,1)S(1)}, bf16[4,64,128]{2,1,0:T(8,128)(2,1)S(1)}, u32[]{:S(2)}, u32[]{:S(2)}) collective-permute-start(bf16[4,64,128]{2,1,0:T(8,128)(2,1)S(1)} %get-tuple-element.38), channel_id=1, source_target_pairs={{24,16},{25,17},{26,18},{27,19},{28,20},{29,21},{30,22},{31,23}} | collective-permute-start | bytes 196616 | tf_op jit(solution)/shard_map/ppermute | solution.py:550
  44.3 7.2 %collective-permute-start.12 = (bf16[4,64,128]{2,1,0:T(8,128)(2,1)S(1)}, bf16[4,64,128]{2,1,0:T(8,128)(2,1)S(1)}, u32[]{:S(2)}, u32[]{:S(2)}) collective-permute-start(bf16[4,64,128]{2,1,0:T(8,128)(2,1)S(1)} %get-tuple-element.39), channel_id=1, source_target_pairs={{24,16},{25,17},{26,18},{27,19},{28,20},{29,21},{30,22},{31,23}} | collective-permute-start | bytes 196616 | tf_op jit(solution)/shard_map/ppermute | solution.py:550
  46.7 6.3 %collective-permute-start.17 = (f32[2,64,576]{2,1,0:T(8,128)S(1)}, f32[2,64,576]{2,1,0:T(8,128)S(1)}, u32[]{:S(2)}, u32[]{:S(2)}) collective-permute-start(f32[2,64,576]{2,1,0:T(8,128)S(1)} %slice_select_fusion), channel_id=1, source_target_pairs={{0,2},{2,0},{4,6},{6,4},{1,3},{3,1},{5,7},{7,5},{8,10},{10,8},{12,... | collective-permute-start | bytes 884744 | tf_op jit(solution)/shard_map/ppermute | solution.py:469
  50.1 4.2 %collective-permute-start.13 = (bf16[4,64,128]{2,1,0:T(8,128)(2,1)S(1)}, bf16[4,64,128]{2,1,0:T(8,128)(2,1)S(1)}, u32[]{:S(2)}, u32[]{:S(2)}) collective-permute-start(bf16[4,64,128]{2,1,0:T(8,128)(2,1)S(1)} %shard_map.68), channel_id=1, source_target_pairs={{16,8},{17,9},{18,10},{19,11},{20,12},{21,13},{22,14},{23,15}} | collective-permute-start | bytes 196616 | tf_op jit(solution)/shard_map/ppermute | solution.py:550
  51.7 7.6 %collective-permute-start.14 = (bf16[4,64,128]{2,1,0:T(8,128)(2,1)S(1)}, bf16[4,64,128]{2,1,0:T(8,128)(2,1)S(1)}, u32[]{:S(2)}, u32[]{:S(2)}) collective-permute-start(bf16[4,64,128]{2,1,0:T(8,128)(2,1)S(1)} %shard_map.69), channel_id=1, source_target_pairs={{16,8},{17,9},{18,10},{19,11},{20,12},{21,13},{22,14},{23,15}} | collective-permute-start | bytes 196616 | tf_op jit(solution)/shard_map/ppermute | solution.py:550
  53.0 4.2 %collective-permute-start.18 = (bf16[2,64,576]{2,1,0:T(8,128)(2,1)S(1)}, bf16[2,64,576]{2,1,0:T(8,128)(2,1)S(1)}, u32[]{:S(2)}, u32[]{:S(2)}) collective-permute-start(bf16[2,64,576]{2,1,0:T(8,128)(2,1)S(1)} %add_convert_fusion.1), channel_id=1, source_target_pairs={{0,4},{1,5},{2,3},{3,2},{4,0},{5,1},{6,7},{7,6},{8,12},{9,13},{10,... | collective-permute-start | bytes 442376 | tf_op jit(solution)/shard_map/ppermute | solution.py:481
  54.5 11.8 %collective-permute-start.15 = (bf16[4,64,128]{2,1,0:T(8,128)(2,1)S(1)}, bf16[4,64,128]{2,1,0:T(8,128)(2,1)S(1)}, u32[]{:S(2)}, u32[]{:S(2)}) collective-permute-start(bf16[4,64,128]{2,1,0:T(8,128)(2,1)S(1)} %shard_map.70), channel_id=1, source_target_pairs={{8,0},{9,1},{10,2},{11,3},{12,4},{13,5},{14,6},{15,7}} | collective-permute-start | bytes 196616 | tf_op jit(solution)/shard_map/ppermute | solution.py:550
  57.3 4.7 %collective-permute-start.19 = (bf16[2,64,576]{2,1,0:T(8,128)(2,1)S(1)}, bf16[2,64,576]{2,1,0:T(8,128)(2,1)S(1)}, u32[]{:S(2)}, u32[]{:S(2)}) collective-permute-start(bf16[2,64,576]{2,1,0:T(8,128)(2,1)S(1)} %add_convert_fusion), channel_id=1, source_target_pairs={{0,1},{1,0},{2,6},{3,7},{4,5},{5,4},{6,2},{7,3},{8,9},{9,8},{10,14... | collective-permute-start | bytes 442376 | tf_op jit(solution)/shard_map/ppermute | solution.py:481
  59.5 6.8 %collective-permute-start.16 = (bf16[4,64,128]{2,1,0:T(8,128)(2,1)S(1)}, bf16[4,64,128]{2,1,0:T(8,128)(2,1)S(1)}, u32[]{:S(2)}, u32[]{:S(2)}) collective-permute-start(bf16[4,64,128]{2,1,0:T(8,128)(2,1)S(1)} %shard_map.71), channel_id=1, source_target_pairs={{8,0},{9,1},{10,2},{11,3},{12,4},{13,5},{14,6},{15,7}} | collective-permute-start | bytes 196616 | tf_op jit(solution)/shard_map/ppermute | solution.py:550
  62.0 5.5 %collective-permute-start.20 = (f32[2,64,576]{2,1,0:T(8,128)S(1)}, f32[2,64,576]{2,1,0:T(8,128)S(1)}, u32[]{:S(2)}, u32[]{:S(2)}) collective-permute-start(f32[2,64,576]{2,1,0:T(8,128)S(1)} %convert_add_fusion), channel_id=1, source_target_pairs={{0,2},{2,0},{4,6},{6,4},{1,3},{3,1},{5,7},{7,5},{8,10},{10,8},{12,... | collective-permute-start | bytes 884744 | tf_op jit(solution)/shard_map/ppermute | solution.py:483

commit v9 on v8

--- a/solution.py
+++ b/solution.py
@@ -9,19 +9,20 @@
 
 step_size = 0.2
 VMEM_BYTES = 40 * 1024 * 1024
+STRIP_VMEM_BYTES = 63 * 1024 * 1024
 f32 = jnp.float32
 bf16 = jnp.bfloat16
 
 
-def call(body, out_shape, scratch=(), flops=0, moved=0):
+def call(body, out_shape, scratch=(), flops=0, vmem=VMEM_BYTES):
     return pl.pallas_call(
         body,
         out_shape=out_shape,
         scratch_shapes=list(scratch),
         cost_estimate=pl.CostEstimate(
-            flops=int(flops), bytes_accessed=int(moved), transcendentals=0
+            flops=int(flops), bytes_accessed=0, transcendentals=0
         ),
-        compiler_params=pltpu.CompilerParams(vmem_limit_bytes=VMEM_BYTES),
+        compiler_params=pltpu.CompilerParams(vmem_limit_bytes=vmem),
     )
 
 
@@ -364,7 +365,8 @@
             for place, z in enumerate(convolved_rows(w_ref[layer], now, first, count)):
                 gain = mask * (step_size * row_flag(first + place, halo, rows, up, down))
                 t = jnp.tanh(z)
-                done.append((gain * (1.0 - t * t), states[place] + gain * t))
+                moved = gain * t
+                done.append((gain - moved * t, states[place] + moved))
             for place, (slope, x) in enumerate(done):
                 slope_ref[layer, first + place] = slope
                 if layer < depth - 1:
@@ -429,8 +431,12 @@
             ]
 
 
-def last_body(q_ref, *refs, channels, rows):
-    arrived, out_ref = refs[:-1], refs[-1]
+def last_body(q_ref, half_ref, other_ref, *refs, channels, rows):
+    arrived, out_ref, grad_ref = refs[:-2], refs[-2], refs[-1]
+    half = half_ref.shape[0]
+    odd = jnp.logical_not(even_row()).astype(jnp.int32)
+    grad_ref[pl.ds(odd * half, half)] = half_ref[...]
+    grad_ref[pl.ds((1 - odd) * half, half)] = other_ref[...]
     last = lax.axis_index("layer") == lax.axis_size("layer") - 1
     for row in range(rows):
         value = arrived_row(arrived, row, rows)
@@ -480,10 +486,7 @@
         rounded = value.astype(bf16)
         arrived = lax.ppermute(rounded, ("row", "col"), pairs)
         value = rounded.astype(f32) + arrived.astype(f32)
-    other = lax.ppermute(value, "row", pair)
-    first = jnp.where(odd, other, value)
-    second = jnp.where(odd, value, other)
-    return jnp.concatenate([first, second], 0)
+    return value, lax.ppermute(value, "row", pair)
 
 
 def local(c_states, c_adjoints, weights):
@@ -506,7 +509,9 @@
         )
     )
     flat_f = jax.ShapeDtypeStruct(flat, f32)
-    edges = call(functools.partial(strip_body, depth=depth, **sizes), wide_b)(c_flat, q_flat)
+    edges = call(
+        functools.partial(strip_body, depth=depth, **sizes), wide_b, vmem=STRIP_VMEM_BYTES
+    )(c_flat, q_flat)
     left, right = from_sides(edges)
     to_pair, to_cross, side, strip = call(
         functools.partial(message_body, depth=depth, **sizes),
@@ -605,10 +610,12 @@
         jax.ShapeDtypeStruct((depth, channels, 9 * channels), f32),
         flops=10**9,
     )(kept, sources)
-    weight_grads = total_over_tiles(grads)
-    adjoint = call(
-        functools.partial(last_body, **sizes), jax.ShapeDtypeStruct(flat, f32), flops=10**10
-    )(q_flat, *returned)
+    own_half, other_half = total_over_tiles(grads)
+    adjoint, weight_grads = call(
+        functools.partial(last_body, **sizes),
+        (flat_f, jax.ShapeDtypeStruct((depth, channels, 9 * channels), f32)),
+        flops=10**10,
+    )(q_flat, own_half, other_half, *returned)
     return state.reshape(c_states.shape), adjoint.reshape(c_states.shape), weight_grads
 
 

time: 68.9 us -> 68.1 us (0.988)
  local copies, waits for them, and re-layouts: 4.33 us -> 2.43 us
  Pallas kernels: 16 us -> 17.9 us
  other arithmetic: 1.25 us -> 0.31 us
    pallas_call x2, Pallas kernels: 0.94 us -> 2.88 us  [the longest x1 1.84 us: local(): call(functools.partial(strip_body, depth=depth, **sizes), wide_b, vmem=ST...]
    unnamed x11 -> x7, local copies, waits for them, and re-layouts: 2.21 us -> 0.31 us
    concatenate x1 -> x0, other arithmetic: 0.88 us -> none  [total_over_tiles(): return jnp.concatenate([first, second], 0)]
  transfers between devices with their start and end apart: 21 -> 21, of which waited for: 7 -> 7; matrix products, arithmetic and copies ran while one was open for 4% -> 4% of each run, Pallas kernels for 10% -> 9%
where the time goes in v9:
time: 68.1 us; the launch traced here: 67 us
  starting transfers between devices  35.8 us (53%)
  Pallas kernels  17.9 us (26%)
  waiting for transfers between devices  9.57 us (14%)
  local copies, waits for them, and re-layouts  2.43 us (4%)
  between operations  1.01 us (1%)
    ppermute x12, starting transfers between devices, chain(): arrived = [lax.ppermute(sending, 'layer', [step]) for sending in sendings]  13 us
    ppermute x2, starting transfers between devices, exchanged(): lax.ppermute(to_pair, 'row', pairs)  9.2 us
    pallas_call x1, Pallas kernels, local(): call(functools.partial(second_body, depth=depth, **sizes), (flat_f, tile_...  8.83 us
    ppermute x1, starting transfers between devices, total_over_tiles(): return (value, lax.ppermute(value, 'row', pair))  4.27 us
    ppermute x12, waiting for transfers between devices, chain(): arrived = [lax.ppermute(sending, 'layer', [step]) for sending in sendings]  3.71 us
    ppermute x1, starting transfers between devices, total_over_tiles(): value = own + lax.ppermute(sent, 'row', pair)  3.31 us
    ppermute x2, starting transfers between devices, total_over_tiles(): arrived = lax.ppermute(rounded, ('row', 'col'), pairs)  3.27 us
    ppermute x2, waiting for transfers between devices, total_over_tiles(): arrived = lax.ppermute(rounded, ('row', 'col'), pairs)  3.25 us
  transfers between devices with their start and end apart: 21, of which 7 were waited for; matrix products, arithmetic and copies ran while one was open for 4% of the time, Pallas kernels for 9%

profile of v9, /device:TPU:19, one launch (start us, length us, event | category | flops | bytes accessed | tf_op | source)
XLA Modules:
  0.0 67.0 jit_solution(2123182956824247801)
XLA Ops:
  0.6 1.8 %shard_map.58 = bf16[64,256]{1,0:T(8,128)(2,1)} custom-call(f32[512,128]{1,0:T(8,128)} %bitcast.18, f32[512,128]{1,0:T(8,128)} %bitcast.28), custom_call_target="tpu_custom_call" | custom-call | tf_op jit(solution)/shard_map/pallas_call | solution.py:512
  2.5 1.2 %collective-permute-start = (bf16[64,256]{1,0:T(8,128)(2,1)}, bf16[64,256]{1,0:T(8,128)(2,1)S(1)}, u32[]{:S(2)}, u32[]{:S(2)}) collective-permute-start(bf16[64,256]{1,0:T(8,128)(2,1)} %shard_map.58), channel_id=1, source_target_pairs={{0,1},{1,0},{2,3},{3,2},{4,5},{5,4},{6,7},{7,6},{8,9},{9,8},{10,11... | collective-permute-start | bytes 98312 | tf_op jit(solution)/shard_map/ppermute | solution.py:462
  4.1 1.4 %collective-permute-done.left_ref.right_ref = bf16[64,256]{1,0:T(8,128)(2,1)S(1)} collective-permute-done((bf16[64,256]{1,0:T(8,128)(2,1)}, bf16[64,256]{1,0:T(8,128)(2,1)S(1)}, u32[]{:S(2)}, u32[]{:S(2)}) %collective-permute-start) | collective-permute-done | bytes 32800 | tf_op jit(solution)/shard_map/ppermute | solution.py:462
  5.7 0.7 %collective-permute-start.2 = (bf16[10,64,128]{2,1,0:T(8,128)(2,1)S(1)}, bf16[10,64,128]{2,1,0:T(8,128)(2,1)S(1)}, u32[]{:S(2)}, u32[]{:S(2)}) collective-permute-start(bf16[10,64,128]{2,1,0:T(8,128)(2,1)S(1)} %get-tuple-element.27), channel_id=1, source_target_pairs={{2,4},{4,2},{3,5},{5,3},{10,12},{12,10},{11,13},{13,11},{18,20},{2... | collective-permute-start | bytes 491528 | tf_op jit(solution)/shard_map/ppermute | solution.py:457
  6.4 3.1 %collective-permute-start.1 = (bf16[10,64,128]{2,1,0:T(8,128)(2,1)S(1)}, bf16[10,64,128]{2,1,0:T(8,128)(2,1)S(1)}, u32[]{:S(2)}, u32[]{:S(2)}) collective-permute-start(bf16[10,64,128]{2,1,0:T(8,128)(2,1)S(1)} %get-tuple-element.26), channel_id=1, source_target_pairs={{0,2},{2,0},{4,6},{6,4},{1,3},{3,1},{5,7},{7,5},{8,10},{10,8},{12,... | collective-permute-start | bytes 491528 | tf_op jit(solution)/shard_map/ppermute | solution.py:457
  11.6 0.7 collective-permute-start.3
  12.4 0.7 collective-permute-start.4
  13.1 3.1 %shard_map.61.refs_1_.refs_0_ = f32[9,64,128]{2,1,0:T(8,128)S(1)} custom-call(f32[512,128]{1,0:T(8,128)S(1)} %bitcast.21, bf16[10,64,128]{2,1,0:T(8,128)(2,1)S(1)} %collective-permute-done.1.pair_ref, bf16[10,64,128]{2,1,0:T(8,128)(2,1)S(1)} %collective-permute-done.2.cross_ref, bf16[64,256]{1,0:T(8,128)(2,1)S(1)} %get-tuple-element.36.side_ref, ...), custom_call_target="tpu_custom_call" | custom-call | flops 830472192 | tf_op jit(solution)/shard_map/pallas_call | solution.py:540
  16.5 1.3 %collective-permute-start.5 = (bf16[5,64,128]{2,1,0:T(8,128)(2,1)S(1)}, bf16[5,64,128]{2,1,0:T(8,128)(2,1)S(1)}, u32[]{:S(2)}, u32[]{:S(2)}) collective-permute-start(bf16[5,64,128]{2,1,0:T(8,128)(2,1)S(1)} %shard_map.62), channel_id=1, source_target_pairs={{8,16},{9,17},{10,18},{11,19},{12,20},{13,21},{14,22},{15,23}} | collective-permute-start | bytes 245768 | tf_op jit(solution)/shard_map/ppermute | solution.py:555
  18.0 1.3 %collective-permute-start.6 = (bf16[4,64,128]{2,1,0:T(8,128)(2,1)S(1)}, bf16[4,64,128]{2,1,0:T(8,128)(2,1)S(1)}, u32[]{:S(2)}, u32[]{:S(2)}) collective-permute-start(bf16[4,64,128]{2,1,0:T(8,128)(2,1)S(1)} %shard_map.63), channel_id=1, source_target_pairs={{8,16},{9,17},{10,18},{11,19},{12,20},{13,21},{14,22},{15,23}} | collective-permute-start | bytes 196616 | tf_op jit(solution)/shard_map/ppermute | solution.py:555
  19.3 2.4 %collective-permute-done.5.s_ref.refs_2_ = bf16[5,64,128]{2,1,0:T(8,128)(2,1)S(1)} collective-permute-done((bf16[5,64,128]{2,1,0:T(8,128)(2,1)S(1)}, bf16[5,64,128]{2,1,0:T(8,128)(2,1)S(1)}, u32[]{:S(2)}, u32[]{:S(2)}) %collective-permute-start.5) | collective-permute-done | bytes 81952 | tf_op jit(solution)/shard_map/ppermute | solution.py:555
  21.9 1.3 %collective-permute-start.7 = (bf16[5,64,128]{2,1,0:T(8,128)(2,1)S(1)}, bf16[5,64,128]{2,1,0:T(8,128)(2,1)S(1)}, u32[]{:S(2)}, u32[]{:S(2)}) collective-permute-start(bf16[5,64,128]{2,1,0:T(8,128)(2,1)S(1)} %shard_map.64), channel_id=1, source_target_pairs={{16,24},{17,25},{18,26},{19,27},{20,28},{21,29},{22,30},{23,31}} | collective-permute-start | bytes 245768 | tf_op jit(solution)/shard_map/ppermute | solution.py:555
  23.4 1.3 %collective-permute-start.8 = (bf16[4,64,128]{2,1,0:T(8,128)(2,1)S(1)}, bf16[4,64,128]{2,1,0:T(8,128)(2,1)S(1)}, u32[]{:S(2)}, u32[]{:S(2)}) collective-permute-start(bf16[4,64,128]{2,1,0:T(8,128)(2,1)S(1)} %shard_map.65), channel_id=1, source_target_pairs={{16,24},{17,25},{18,26},{19,27},{20,28},{21,29},{22,30},{23,31}} | collective-permute-start | bytes 196616 | tf_op jit(solution)/shard_map/ppermute | solution.py:555
  24.7 1.3 %collective-permute-done.8.refs_5_ = bf16[4,64,128]{2,1,0:T(8,128)(2,1)S(1)} collective-permute-done((bf16[4,64,128]{2,1,0:T(8,128)(2,1)S(1)}, bf16[4,64,128]{2,1,0:T(8,128)(2,1)S(1)}, u32[]{:S(2)}, u32[]{:S(2)}) %collective-permute-start.8) | collective-permute-done | bytes 65568 | tf_op jit(solution)/shard_map/ppermute | solution.py:555
  26.1 0.9 %collective-permute-start.10 = (bf16[9,64,128]{2,1,0:T(8,128)(2,1)S(1)}, bf16[9,64,128]{2,1,0:T(8,128)(2,1)S(1)}, u32[]{:S(2)}, u32[]{:S(2)}) collective-permute-start(bf16[9,64,128]{2,1,0:T(8,128)(2,1)S(1)} %shard_map.66.s_ref), channel_id=1, source_target_pairs={{2,4},{4,2},{3,5},{5,3},{10,12},{12,10},{11,13},{13,11},{18,20},{2... | collective-permute-start | bytes 442376 | tf_op jit(solution)/shard_map/ppermute | solution.py:457
  26.9 6.1 %collective-permute-start.9 = (bf16[9,64,128]{2,1,0:T(8,128)(2,1)S(1)}, bf16[9,64,128]{2,1,0:T(8,128)(2,1)S(1)}, u32[]{:S(2)}, u32[]{:S(2)}) collective-permute-start(bf16[9,64,128]{2,1,0:T(8,128)(2,1)S(1)} %shard_map.66.s_ref), channel_id=1, source_target_pairs={{0,2},{2,0},{4,6},{6,4},{1,3},{3,1},{5,7},{7,5},{8,10},{10,8},{12,... | collective-permute-start | bytes 442376 | tf_op jit(solution)/shard_map/ppermute | solution.py:457
  33.1 0.9 %collective-permute-done.9.s_pair_ref = bf16[9,64,128]{2,1,0:T(8,128)(2,1)S(1)} collective-permute-done((bf16[9,64,128]{2,1,0:T(8,128)(2,1)S(1)}, bf16[9,64,128]{2,1,0:T(8,128)(2,1)S(1)}, u32[]{:S(2)}, u32[]{:S(2)}) %collective-permute-start.9) | collective-permute-done | bytes 147488 | tf_op jit(solution)/shard_map/ppermute | solution.py:457
  34.0 8.8 %shard_map.67 = (f32[512,128]{1,0:T(8,128)}, f32[8,64,128]{2,1,0:T(8,128)S(1)}, bf16[4,64,128]{2,1,0:T(8,128)(2,1)S(1)}, bf16[4,64,128]{2,1,0:T(8,128)(2,1)S(1)}...) custom-call(f32[512,128]{1,0:T(8,128)S(1)} %bitcast.27, f32[512,128]{1,0:T(8,128)S(1)} %bitcast.30, ...), custom_call_target="tpu_custom_call" | custom-call | flops 2264924160 | tf_op jit(solution)/shard_map/pallas_call | solution.py:582
  42.8 1.3 %collective-permute-start.15 = (bf16[4,64,128]{2,1,0:T(8,128)(2,1)S(1)}, bf16[4,64,128]{2,1,0:T(8,128)(2,1)S(1)}, u32[]{:S(2)}, u32[]{:S(2)}) collective-permute-start(bf16[4,64,128]{2,1,0:T(8,128)(2,1)S(1)} %get-tuple-element.42), channel_id=1, source_target_pairs={{24,16},{25,17},{26,18},{27,19},{28,20},{29,21},{30,22},{31,23}} | collective-permute-start | bytes 196616 | tf_op jit(solution)/shard_map/ppermute | solution.py:555
  44.1 1.3 %collective-permute-start.16 = (bf16[4,64,128]{2,1,0:T(8,128)(2,1)S(1)}, bf16[4,64,128]{2,1,0:T(8,128)(2,1)S(1)}, u32[]{:S(2)}, u32[]{:S(2)}) collective-permute-start(bf16[4,64,128]{2,1,0:T(8,128)(2,1)S(1)} %get-tuple-element.43), channel_id=1, source_target_pairs={{24,16},{25,17},{26,18},{27,19},{28,20},{29,21},{30,22},{31,23}} | collective-permute-start | bytes 196616 | tf_op jit(solution)/shard_map/ppermute | solution.py:555
  45.4 1.1 %shard_map.68 = f32[4,64,576]{2,1,0:T(8,128)S(1)} custom-call(bf16[4,8,64,256]{3,2,1,0:T(8,128)(2,1)S(1)} %get-tuple-element.40.kept_ref, bf16[4,10,64,128]{3,2,1,0:T(8,128)(2,1)S(1)} %get-tuple-element.41.sent_ref), custom_call_target="tpu_custom_call" | custom-call | flops 1000000000 | tf_op jit(solution)/shard_map/pallas_call | solution.py:608
  46.6 3.3 %collective-permute-start.11 = (f32[2,64,576]{2,1,0:T(8,128)S(1)}, f32[2,64,576]{2,1,0:T(8,128)S(1)}, u32[]{:S(2)}, u32[]{:S(2)}) collective-permute-start(f32[2,64,576]{2,1,0:T(8,128)S(1)} %slice_select_fusion), channel_id=1, source_target_pairs={{0,2},{2,0},{4,6},{6,4},{1,3},{3,1},{5,7},{7,5},{8,10},{10,8},{12,... | collective-permute-start | bytes 884744 | tf_op jit(solution)/shard_map/ppermute | solution.py:475
  50.1 1.3 %collective-permute-start.17 = (bf16[4,64,128]{2,1,0:T(8,128)(2,1)S(1)}, bf16[4,64,128]{2,1,0:T(8,128)(2,1)S(1)}, u32[]{:S(2)}, u32[]{:S(2)}) collective-permute-start(bf16[4,64,128]{2,1,0:T(8,128)(2,1)S(1)} %shard_map.69), channel_id=1, source_target_pairs={{16,8},{17,9},{18,10},{19,11},{20,12},{21,13},{22,14},{23,15}} | collective-permute-start | bytes 196616 | tf_op jit(solution)/shard_map/ppermute | solution.py:555
  51.5 1.3 %collective-permute-start.12 = (bf16[2,64,576]{2,1,0:T(8,128)(2,1)S(1)}, bf16[2,64,576]{2,1,0:T(8,128)(2,1)S(1)}, u32[]{:S(2)}, u32[]{:S(2)}) collective-permute-start(bf16[2,64,576]{2,1,0:T(8,128)(2,1)S(1)} %add_convert_fusion.1), channel_id=1, source_target_pairs={{0,4},{1,5},{2,3},{3,2},{4,0},{5,1},{6,7},{7,6},{8,12},{9,13},{10,... | collective-permute-start | bytes 442376 | tf_op jit(solution)/shard_map/ppermute | solution.py:487
  53.0 1.3 %collective-permute-start.18 = (bf16[4,64,128]{2,1,0:T(8,128)(2,1)S(1)}, bf16[4,64,128]{2,1,0:T(8,128)(2,1)S(1)}, u32[]{:S(2)}, u32[]{:S(2)}) collective-permute-start(bf16[4,64,128]{2,1,0:T(8,128)(2,1)S(1)} %shard_map.70), channel_id=1, source_target_pairs={{16,8},{17,9},{18,10},{19,11},{20,12},{21,13},{22,14},{23,15}} | collective-permute-start | bytes 196616 | tf_op jit(solution)/shard_map/ppermute | solution.py:555
  54.3 1.4 %collective-permute-done.12 = bf16[2,64,576]{2,1,0:T(8,128)(2,1)S(1)} collective-permute-done((bf16[2,64,576]{2,1,0:T(8,128)(2,1)S(1)}, bf16[2,64,576]{2,1,0:T(8,128)(2,1)S(1)}, u32[]{:S(2)}, u32[]{:S(2)}) %collective-permute-start.12) | collective-permute-done | bytes 147488 | tf_op jit(solution)/shard_map/ppermute | solution.py:487
  55.7 2.0 %collective-permute-start.13 = (bf16[2,64,576]{2,1,0:T(8,128)(2,1)S(1)}, bf16[2,64,576]{2,1,0:T(8,128)(2,1)S(1)}, u32[]{:S(2)}, u32[]{:S(2)}) collective-permute-start(bf16[2,64,576]{2,1,0:T(8,128)(2,1)S(1)} %add_convert_fusion), channel_id=1, source_target_pairs={{0,1},{1,0},{2,6},{3,7},{4,5},{5,4},{6,2},{7,3},{8,9},{9,8},{10,14... | collective-permute-start | bytes 442376 | tf_op jit(solution)/shard_map/ppermute | solution.py:487
  57.9 0.7 collective-permute-start.19
  58.6 1.8 %collective-permute-done.13 = bf16[2,64,576]{2,1,0:T(8,128)(2,1)S(1)} collective-permute-done((bf16[2,64,576]{2,1,0:T(8,128)(2,1)S(1)}, bf16[2,64,576]{2,1,0:T(8,128)(2,1)S(1)}, u32[]{:S(2)}, u32[]{:S(2)}) %collective-permute-start.13) | collective-permute-done | bytes 147488 | tf_op jit(solution)/shard_map/ppermute | solution.py:487
  60.4 4.3 %collective-permute-start.14 = (f32[2,64,576]{2,1,0:T(8,128)S(1)}, f32[2,64,576]{2,1,0:T(8,128)S(1)}, u32[]{:S(2)}, u32[]{:S(2)}) collective-permute-start(f32[2,64,576]{2,1,0:T(8,128)S(1)} %convert_add_fusion.half_ref), channel_id=1, source_target_pairs={{0,2},{2,0},{4,6},{6,4},{1,3},{3,1},{5,7},{7,5},{8,10},{10,8},{12,... | collective-permute-start | bytes 884744 | tf_op jit(solution)/shard_map/ppermute | solution.py:489
  64.9 0.7 collective-permute-start.20
  66.0 1.0 %shard_map.73 = (f32[512,128]{1,0:T(8,128)}, f32[4,64,576]{2,1,0:T(8,128)}) custom-call(f32[512,128]{1,0:T(8,128)S(1)} %bitcast.35, f32[2,64,576]{2,1,0:T(8,128)S(1)} %convert_add_fusion.half_ref, f32[2,64,576]{2,1,0:T(8,128)S(1)} %collective-permute-done.14.other_ref, bf16[4,64,128]{2,1,0:T(8,128)(2,1)S(1)} %collective-permute-done.15.s_ref.refs_0_, ...), custom_call_target="tpu_custom_call" | custom-call | flops 10000000000 | tf_op jit(solution)/shard_map/pallas_call | solution.py:614
  (49 shorter events, 5.1 us)
Async XLA Ops:
  0.6 3.1 %copy-start.2 = (bf16[4,64,576]{2,1,0:T(8,128)(2,1)S(1)}, bf16[4,64,576]{2,1,0:T(8,128)(2,1)}, u32[]{:S(2)}) copy-start(bf16[4,64,576]{2,1,0:T(8,128)(2,1)} %param.5) | copy-start | bytes 884740
  2.5 3.0 %collective-permute-start = (bf16[64,256]{1,0:T(8,128)(2,1)}, bf16[64,256]{1,0:T(8,128)(2,1)S(1)}, u32[]{:S(2)}, u32[]{:S(2)}) collective-permute-start(bf16[64,256]{1,0:T(8,128)(2,1)} %shard_map.58), channel_id=1, source_target_pairs={{0,1},{1,0},{2,3},{3,2},{4,5},{5,4},{6,7},{7,6},{8,9},{9,8},{10,11... | collective-permute-start | bytes 98312 | tf_op jit(solution)/shard_map/ppermute | solution.py:462
  3.7 1.7 %copy-start.1 = (f32[1,64,8,128]{3,2,1,0:T(8,128)S(1)}, f32[1,64,8,128]{3,2,1,0:T(8,128)}, u32[]{:S(2)}) copy-start(f32[1,64,8,128]{3,2,1,0:T(8,128)} %param.4) | copy-start | bytes 786436
  4.0 1.4 %copy-start = (f32[1,64,8,128]{3,2,1,0:T(8,128)S(1)}, f32[1,64,8,128]{3,2,1,0:T(8,128)}, u32[]{:S(2)}) copy-start(f32[1,64,8,128]{3,2,1,0:T(8,128)} %param.3) | copy-start | bytes 786436
  5.7 5.9 %collective-permute-start.2 = (bf16[10,64,128]{2,1,0:T(8,128)(2,1)S(1)}, bf16[10,64,128]{2,1,0:T(8,128)(2,1)S(1)}, u32[]{:S(2)}, u32[]{:S(2)}) collective-permute-start(bf16[10,64,128]{2,1,0:T(8,128)(2,1)S(1)} %get-tuple-element.27), channel_id=1, source_target_pairs={{2,4},{4,2},{3,5},{5,3},{10,12},{12,10},{11,13},{13,11},{18,20},{2... | collective-permute-start | bytes 491528 | tf_op jit(solution)/shard_map/ppermute | solution.py:457
  6.4 5.2 %collective-permute-start.1 = (bf16[10,64,128]{2,1,0:T(8,128)(2,1)S(1)}, bf16[10,64,128]{2,1,0:T(8,128)(2,1)S(1)}, u32[]{:S(2)}, u32[]{:S(2)}) collective-permute-start(bf16[10,64,128]{2,1,0:T(8,128)(2,1)S(1)} %get-tuple-element.26), channel_id=1, source_target_pairs={{0,2},{2,0},{4,6},{6,4},{1,3},{3,1},{5,7},{7,5},{8,10},{10,8},{12,... | collective-permute-start | bytes 491528 | tf_op jit(solution)/shard_map/ppermute | solution.py:457
  11.6 4.6 %collective-permute-start.3 = (bf16[5,64,128]{2,1,0:T(8,128)(2,1)S(1)}, bf16[5,64,128]{2,1,0:T(8,128)(2,1)S(1)}, u32[]{:S(2)}, u32[]{:S(2)}) collective-permute-start(bf16[5,64,128]{2,1,0:T(8,128)(2,1)S(1)} %get-tuple-element.31), channel_id=1, source_target_pairs={{0,8},{1,9},{2,10},{3,11},{4,12},{5,13},{6,14},{7,15}} | collective-permute-start | bytes 245768 | tf_op jit(solution)/shard_map/ppermute | solution.py:555
  12.4 5.3 %collective-permute-start.4 = (bf16[4,64,128]{2,1,0:T(8,128)(2,1)S(1)}, bf16[4,64,128]{2,1,0:T(8,128)(2,1)S(1)}, u32[]{:S(2)}, u32[]{:S(2)}) collective-permute-start(bf16[4,64,128]{2,1,0:T(8,128)(2,1)S(1)} %get-tuple-element.32), channel_id=1, source_target_pairs={{0,8},{1,9},{2,10},{3,11},{4,12},{5,13},{6,14},{7,15}} | collective-permute-start | bytes 196616 | tf_op jit(solution)/shard_map/ppermute | solution.py:555
  16.5 5.2 %collective-permute-start.5 = (bf16[5,64,128]{2,1,0:T(8,128)(2,1)S(1)}, bf16[5,64,128]{2,1,0:T(8,128)(2,1)S(1)}, u32[]{:S(2)}, u32[]{:S(2)}) collective-permute-start(bf16[5,64,128]{2,1,0:T(8,128)(2,1)S(1)} %shard_map.62), channel_id=1, source_target_pairs={{8,16},{9,17},{10,18},{11,19},{12,20},{13,21},{14,22},{15,23}} | collective-permute-start | bytes 245768 | tf_op jit(solution)/shard_map/ppermute | solution.py:555
  18.0 5.2 %collective-permute-start.6 = (bf16[4,64,128]{2,1,0:T(8,128)(2,1)S(1)}, bf16[4,64,128]{2,1,0:T(8,128)(2,1)S(1)}, u32[]{:S(2)}, u32[]{:S(2)}) collective-permute-start(bf16[4,64,128]{2,1,0:T(8,128)(2,1)S(1)} %shard_map.63), channel_id=1, source_target_pairs={{8,16},{9,17},{10,18},{11,19},{12,20},{13,21},{14,22},{15,23}} | collective-permute-start | bytes 196616 | tf_op jit(solution)/shard_map/ppermute | solution.py:555
  21.9 4.1 %collective-permute-start.7 = (bf16[5,64,128]{2,1,0:T(8,128)(2,1)S(1)}, bf16[5,64,128]{2,1,0:T(8,128)(2,1)S(1)}, u32[]{:S(2)}, u32[]{:S(2)}) collective-permute-start(bf16[5,64,128]{2,1,0:T(8,128)(2,1)S(1)} %shard_map.64), channel_id=1, source_target_pairs={{16,24},{17,25},{18,26},{19,27},{20,28},{21,29},{22,30},{23,31}} | collective-permute-start | bytes 245768 | tf_op jit(solution)/shard_map/ppermute | solution.py:555
  23.4 2.6 %collective-permute-start.8 = (bf16[4,64,128]{2,1,0:T(8,128)(2,1)S(1)}, bf16[4,64,128]{2,1,0:T(8,128)(2,1)S(1)}, u32[]{:S(2)}, u32[]{:S(2)}) collective-permute-start(bf16[4,64,128]{2,1,0:T(8,128)(2,1)S(1)} %shard_map.65), channel_id=1, source_target_pairs={{16,24},{17,25},{18,26},{19,27},{20,28},{21,29},{22,30},{23,31}} | collective-permute-start | bytes 196616 | tf_op jit(solution)/shard_map/ppermute | solution.py:555
  26.1 7.0 %collective-permute-start.10 = (bf16[9,64,128]{2,1,0:T(8,128)(2,1)S(1)}, bf16[9,64,128]{2,1,0:T(8,128)(2,1)S(1)}, u32[]{:S(2)}, u32[]{:S(2)}) collective-permute-start(bf16[9,64,128]{2,1,0:T(8,128)(2,1)S(1)} %shard_map.66.s_ref), channel_id=1, source_target_pairs={{2,4},{4,2},{3,5},{5,3},{10,12},{12,10},{11,13},{13,11},{18,20},{2... | collective-permute-start | bytes 442376 | tf_op jit(solution)/shard_map/ppermute | solution.py:457
  26.9 7.1 %collective-permute-start.9 = (bf16[9,64,128]{2,1,0:T(8,128)(2,1)S(1)}, bf16[9,64,128]{2,1,0:T(8,128)(2,1)S(1)}, u32[]{:S(2)}, u32[]{:S(2)}) collective-permute-start(bf16[9,64,128]{2,1,0:T(8,128)(2,1)S(1)} %shard_map.66.s_ref), channel_id=1, source_target_pairs={{0,2},{2,0},{4,6},{6,4},{1,3},{3,1},{5,7},{7,5},{8,10},{10,8},{12,... | collective-permute-start | bytes 442376 | tf_op jit(solution)/shard_map/ppermute | solution.py:457
  42.8 7.0 %collective-permute-start.15 = (bf16[4,64,128]{2,1,0:T(8,128)(2,1)S(1)}, bf16[4,64,128]{2,1,0:T(8,128)(2,1)S(1)}, u32[]{:S(2)}, u32[]{:S(2)}) collective-permute-start(bf16[4,64,128]{2,1,0:T(8,128)(2,1)S(1)} %get-tuple-element.42), channel_id=1, source_target_pairs={{24,16},{25,17},{26,18},{27,19},{28,20},{29,21},{30,22},{31,23}} | collective-permute-start | bytes 196616 | tf_op jit(solution)/shard_map/ppermute | solution.py:555
  44.1 8.6 %collective-permute-start.16 = (bf16[4,64,128]{2,1,0:T(8,128)(2,1)S(1)}, bf16[4,64,128]{2,1,0:T(8,128)(2,1)S(1)}, u32[]{:S(2)}, u32[]{:S(2)}) collective-permute-start(bf16[4,64,128]{2,1,0:T(8,128)(2,1)S(1)} %get-tuple-element.43), channel_id=1, source_target_pairs={{24,16},{25,17},{26,18},{27,19},{28,20},{29,21},{30,22},{31,23}} | collective-permute-start | bytes 196616 | tf_op jit(solution)/shard_map/ppermute | solution.py:555
  46.6 4.8 %collective-permute-start.11 = (f32[2,64,576]{2,1,0:T(8,128)S(1)}, f32[2,64,576]{2,1,0:T(8,128)S(1)}, u32[]{:S(2)}, u32[]{:S(2)}) collective-permute-start(f32[2,64,576]{2,1,0:T(8,128)S(1)} %slice_select_fusion), channel_id=1, source_target_pairs={{0,2},{2,0},{4,6},{6,4},{1,3},{3,1},{5,7},{7,5},{8,10},{10,8},{12,... | collective-permute-start | bytes 884744 | tf_op jit(solution)/shard_map/ppermute | solution.py:475
  50.1 7.6 %collective-permute-start.17 = (bf16[4,64,128]{2,1,0:T(8,128)(2,1)S(1)}, bf16[4,64,128]{2,1,0:T(8,128)(2,1)S(1)}, u32[]{:S(2)}, u32[]{:S(2)}) collective-permute-start(bf16[4,64,128]{2,1,0:T(8,128)(2,1)S(1)} %shard_map.69), channel_id=1, source_target_pairs={{16,8},{17,9},{18,10},{19,11},{20,12},{21,13},{22,14},{23,15}} | collective-permute-start | bytes 196616 | tf_op jit(solution)/shard_map/ppermute | solution.py:555
  51.5 4.2 %collective-permute-start.12 = (bf16[2,64,576]{2,1,0:T(8,128)(2,1)S(1)}, bf16[2,64,576]{2,1,0:T(8,128)(2,1)S(1)}, u32[]{:S(2)}, u32[]{:S(2)}) collective-permute-start(bf16[2,64,576]{2,1,0:T(8,128)(2,1)S(1)} %add_convert_fusion.1), channel_id=1, source_target_pairs={{0,4},{1,5},{2,3},{3,2},{4,0},{5,1},{6,7},{7,6},{8,12},{9,13},{10,... | collective-permute-start | bytes 442376 | tf_op jit(solution)/shard_map/ppermute | solution.py:487
  53.0 11.8 %collective-permute-start.18 = (bf16[4,64,128]{2,1,0:T(8,128)(2,1)S(1)}, bf16[4,64,128]{2,1,0:T(8,128)(2,1)S(1)}, u32[]{:S(2)}, u32[]{:S(2)}) collective-permute-start(bf16[4,64,128]{2,1,0:T(8,128)(2,1)S(1)} %shard_map.70), channel_id=1, source_target_pairs={{16,8},{17,9},{18,10},{19,11},{20,12},{21,13},{22,14},{23,15}} | collective-permute-start | bytes 196616 | tf_op jit(solution)/shard_map/ppermute | solution.py:555
  55.7 4.7 %collective-permute-start.13 = (bf16[2,64,576]{2,1,0:T(8,128)(2,1)S(1)}, bf16[2,64,576]{2,1,0:T(8,128)(2,1)S(1)}, u32[]{:S(2)}, u32[]{:S(2)}) collective-permute-start(bf16[2,64,576]{2,1,0:T(8,128)(2,1)S(1)} %add_convert_fusion), channel_id=1, source_target_pairs={{0,1},{1,0},{2,6},{3,7},{4,5},{5,4},{6,2},{7,3},{8,9},{9,8},{10,14... | collective-permute-start | bytes 442376 | tf_op jit(solution)/shard_map/ppermute | solution.py:487
  57.9 7.7 %collective-permute-start.19 = (bf16[4,64,128]{2,1,0:T(8,128)(2,1)S(1)}, bf16[4,64,128]{2,1,0:T(8,128)(2,1)S(1)}, u32[]{:S(2)}, u32[]{:S(2)}) collective-permute-start(bf16[4,64,128]{2,1,0:T(8,128)(2,1)S(1)} %shard_map.71), channel_id=1, source_target_pairs={{8,0},{9,1},{10,2},{11,3},{12,4},{13,5},{14,6},{15,7}} | collective-permute-start | bytes 196616 | tf_op jit(solution)/shard_map/ppermute | solution.py:555
  60.4 5.5 %collective-permute-start.14 = (f32[2,64,576]{2,1,0:T(8,128)S(1)}, f32[2,64,576]{2,1,0:T(8,128)S(1)}, u32[]{:S(2)}, u32[]{:S(2)}) collective-permute-start(f32[2,64,576]{2,1,0:T(8,128)S(1)} %convert_add_fusion.half_ref), channel_id=1, source_target_pairs={{0,2},{2,0},{4,6},{6,4},{1,3},{3,1},{5,7},{7,5},{8,10},{10,8},{12,... | collective-permute-start | bytes 884744 | tf_op jit(solution)/shard_map/ppermute | solution.py:489
  64.9 0.7 %collective-permute-start.20 = (bf16[4,64,128]{2,1,0:T(8,128)(2,1)S(1)}, bf16[4,64,128]{2,1,0:T(8,128)(2,1)S(1)}, u32[]{:S(2)}, u32[]{:S(2)}) collective-permute-start(bf16[4,64,128]{2,1,0:T(8,128)(2,1)S(1)} %shard_map.72), channel_id=1, source_target_pairs={{8,0},{9,1},{10,2},{11,3},{12,4},{13,5},{14,6},{15,7}} | collective-permute-start | bytes 196616 | tf_op jit(solution)/shard_map/ppermute | solution.py:555

commit v10 on v9

--- a/solution.py
+++ b/solution.py
@@ -10,11 +10,14 @@
 step_size = 0.2
 VMEM_BYTES = 40 * 1024 * 1024
 STRIP_VMEM_BYTES = 63 * 1024 * 1024
+PARTS = 4
 f32 = jnp.float32
 bf16 = jnp.bfloat16
-
-
-def call(body, out_shape, scratch=(), flops=0, vmem=VMEM_BYTES):
+HERE = pl.BlockSpec(memory_space=pltpu.VMEM)
+AWAY = pl.BlockSpec(memory_space=pltpu.HBM)
+
+
+def call(body, out_shape, scratch=(), flops=0, vmem=VMEM_BYTES, **more):
     return pl.pallas_call(
         body,
         out_shape=out_shape,
@@ -23,7 +26,20 @@
             flops=int(flops), bytes_accessed=0, transcendentals=0
         ),
         compiler_params=pltpu.CompilerParams(vmem_limit_bytes=vmem),
-    )
+        **more,
+    )
+
+
+def in_parts(source, target, arrived, first):
+    size = source.shape[0] // PARTS
+    return [
+        pltpu.make_async_copy(
+            source.at[pl.ds(part * size, size)],
+            target.at[pl.ds(part * size, size)],
+            arrived.at[first + part],
+        )
+        for part in range(PARTS)
+    ]
 
 
 def piece_of(parts, row, rows):
@@ -110,7 +126,12 @@
     return (state_edge, 0), (adjoint_edge, 2 * state_edge * rows)
 
 
-def strip_body(c_ref, q_ref, edge_ref, *, channels, rows, depth):
+def strip_body(c_hbm, q_hbm, edge_ref, c_ref, q_ref, arrived, *, channels, rows, depth):
+    copies = in_parts(c_hbm, c_ref, arrived, 0) + in_parts(q_hbm, q_ref, arrived, PARTS)
+    for copy in copies:
+        copy.start()
+    for copy in copies:
+        copy.wait()
     total = jnp.zeros(edge_ref.shape, f32)
     for ref, (edge, low) in zip((c_ref, q_ref), layout(rows, depth)):
         image = [row_of(ref, row, channels, rows) for row in range(rows)]
@@ -291,8 +312,8 @@
 
 def second_body(
     c_ref, q_ref, s_ref, s_pair_ref, s_cross_ref, pair_ref, cross_ref, side_ref, w_ref, wt_ref,
-    state_ref, g_ref, g_upper_ref, g_lower_ref, kept_ref, sent_ref,
-    x_ref, a_ref, a2_ref, slope_ref, adj_ref, src_ref,
+    state_hbm, g_ref, g_upper_ref, g_lower_ref, kept_ref, sent_ref,
+    x_ref, a_ref, a2_ref, slope_ref, adj_ref, src_ref, state_ref, left_here,
     *, channels, rows, depth,
 ):
     cols = c_ref.shape[1]
@@ -317,6 +338,9 @@
         own = jnp.where(first, row_of(c_ref, row, channels, rows), s_ref[row].astype(f32))
         state_ref[pl.ds(row, channels, stride=rows), :] = own
         put(halo + row, own, side_lanes(own_side, edge, 0, row))
+    leaving = in_parts(state_ref, state_hbm, left_here, 0)
+    for copy in leaving:
+        copy.start()
     for row in range(halo):
         place = rows - halo + row
         put(
@@ -397,6 +421,8 @@
         g_ref[row] = value
         ref, place = piece_of((g_upper_ref, g_lower_ref), row, rows)
         ref[place] = value.astype(bf16)
+    for copy in leaving:
+        copy.wait()
 
 
 def grad_body(kept_ref, sent_ref, grad_ref, *, channels, rows, depth):
@@ -432,16 +458,30 @@
 
 
 def last_body(q_ref, half_ref, other_ref, *refs, channels, rows):
-    arrived, out_ref, grad_ref = refs[:-2], refs[-2], refs[-1]
+    arrived, (out_hbm, grad_hbm, out_ref, left_here) = refs[:-4], refs[-4:]
     half = half_ref.shape[0]
     odd = jnp.logical_not(even_row()).astype(jnp.int32)
-    grad_ref[pl.ds(odd * half, half)] = half_ref[...]
-    grad_ref[pl.ds((1 - odd) * half, half)] = other_ref[...]
+    leaving = []
+    for which, ref in enumerate((half_ref, other_ref)):
+        low = half * (odd if which == 0 else 1 - odd)
+        for layer in range(half):
+            leaving.append(
+                pltpu.make_async_copy(
+                    ref.at[layer], grad_hbm.at[low + layer], left_here.at[len(leaving)]
+                )
+            )
+    for copy in leaving:
+        copy.start()
     last = lax.axis_index("layer") == lax.axis_size("layer") - 1
     for row in range(rows):
         value = arrived_row(arrived, row, rows)
         value = jnp.where(last, row_of(q_ref, row, channels, rows), value)
         out_ref[pl.ds(row, channels, stride=rows), :] = value
+    parts = in_parts(out_ref, out_hbm, left_here, 2 * half)
+    for copy in parts:
+        copy.start()
+    for copy in leaving + parts:
+        copy.wait()
 
 
 def shifted(array, axis, by):
@@ -510,7 +550,16 @@
     )
     flat_f = jax.ShapeDtypeStruct(flat, f32)
     edges = call(
-        functools.partial(strip_body, depth=depth, **sizes), wide_b, vmem=STRIP_VMEM_BYTES
+        functools.partial(strip_body, depth=depth, **sizes),
+        wide_b,
+        [
+            pltpu.VMEM(flat, f32),
+            pltpu.VMEM(flat, f32),
+            pltpu.SemaphoreType.DMA((2 * PARTS,)),
+        ],
+        vmem=STRIP_VMEM_BYTES,
+        in_specs=[AWAY, AWAY],
+        out_specs=HERE,
     )(c_flat, q_flat)
     left, right = from_sides(edges)
     to_pair, to_cross, side, strip = call(
@@ -596,8 +645,11 @@
             pltpu.VMEM((depth, total, channels, lanes), f32),
             pltpu.VMEM((total, channels, lanes), f32),
             pltpu.VMEM((total, channels, lanes), bf16),
+            pltpu.VMEM(flat, f32),
+            pltpu.SemaphoreType.DMA((PARTS,)),
         ],
         flops=mac * 120,
+        out_specs=(AWAY, HERE, HERE, HERE, HERE, HERE),
     )(c_flat, q_flat, s, s_pair, s_cross, pair, cross, side, w_fwd, w_back)
     returned = chain(
         ((upper, 0, (q_flat,)), (lower, half, (q_flat,))),
@@ -614,7 +666,9 @@
     adjoint, weight_grads = call(
         functools.partial(last_body, **sizes),
         (flat_f, jax.ShapeDtypeStruct((depth, channels, 9 * channels), f32)),
+        [pltpu.VMEM(flat, f32), pltpu.SemaphoreType.DMA((depth + PARTS,))],
         flops=10**10,
+        out_specs=(AWAY, AWAY),
     )(q_flat, own_half, other_half, *returned)
     return state.reshape(c_states.shape), adjoint.reshape(c_states.shape), weight_grads
 

time: 68.1 us -> 67.8 us (level)
  no operation moved by 1% of the time
where the time goes in v10:
time: 67.8 us; the launch traced here: 66.7 us
  starting transfers between devices  35.9 us (53%)
  Pallas kernels  17.4 us (26%)
  waiting for transfers between devices  9.57 us (14%)
  local copies, waits for them, and re-layouts  2.43 us (4%)
  between operations  1.19 us (2%)
    ppermute x12, starting transfers between devices, chain(): arrived = [lax.ppermute(sending, 'layer', [step]) for sending in sendings]  13 us
    ppermute x2, starting transfers between devices, exchanged(): lax.ppermute(to_pair, 'row', pairs)  9.2 us
    pallas_call x1, Pallas kernels, local(): call(functools.partial(second_body, depth=depth, **sizes), (flat_f, tile_...  8.23 us
    ppermute x1, starting transfers between devices, total_over_tiles(): return (value, lax.ppermute(value, 'row', pair))  4.27 us
    ppermute x12, waiting for transfers between devices, chain(): arrived = [lax.ppermute(sending, 'layer', [step]) for sending in sendings]  3.71 us
    ppermute x1, starting transfers between devices, total_over_tiles(): value = own + lax.ppermute(sent, 'row', pair)  3.3 us
    ppermute x2, starting transfers between devices, total_over_tiles(): arrived = lax.ppermute(rounded, ('row', 'col'), pairs)  3.27 us
    ppermute x2, waiting for transfers between devices, total_over_tiles(): arrived = lax.ppermute(rounded, ('row', 'col'), pairs)  3.25 us
  transfers between devices with their start and end apart: 21, of which 7 were waited for; matrix products, arithmetic and copies ran while one was open for 4% of the time, Pallas kernels for 9%

profile of v10, /device:TPU:19, one launch (start us, length us, event | category | flops | bytes accessed | tf_op | source)
XLA Modules:
  0.0 66.7 jit_solution(462379985656504145)
XLA Ops:
  0.6 1.9 %shard_map.58 = bf16[64,256]{1,0:T(8,128)(2,1)} custom-call(f32[512,128]{1,0:T(8,128)} %bitcast.18, f32[512,128]{1,0:T(8,128)} %bitcast.28), custom_call_target="tpu_custom_call" | custom-call | tf_op jit(solution)/shard_map/pallas_call | solution.py:552
  2.6 1.3 %collective-permute-start = (bf16[64,256]{1,0:T(8,128)(2,1)}, bf16[64,256]{1,0:T(8,128)(2,1)S(1)}, u32[]{:S(2)}, u32[]{:S(2)}) collective-permute-start(bf16[64,256]{1,0:T(8,128)(2,1)} %shard_map.58), channel_id=1, source_target_pairs={{0,1},{1,0},{2,3},{3,2},{4,5},{5,4},{6,7},{7,6},{8,9},{9,8},{10,11... | collective-permute-start | bytes 98312 | tf_op jit(solution)/shard_map/ppermute | solution.py:502
  4.3 1.4 %collective-permute-done.left_ref.right_ref = bf16[64,256]{1,0:T(8,128)(2,1)S(1)} collective-permute-done((bf16[64,256]{1,0:T(8,128)(2,1)}, bf16[64,256]{1,0:T(8,128)(2,1)S(1)}, u32[]{:S(2)}, u32[]{:S(2)}) %collective-permute-start) | collective-permute-done | bytes 32800 | tf_op jit(solution)/shard_map/ppermute | solution.py:502
  5.9 0.7 %collective-permute-start.2 = (bf16[10,64,128]{2,1,0:T(8,128)(2,1)S(1)}, bf16[10,64,128]{2,1,0:T(8,128)(2,1)S(1)}, u32[]{:S(2)}, u32[]{:S(2)}) collective-permute-start(bf16[10,64,128]{2,1,0:T(8,128)(2,1)S(1)} %get-tuple-element.27), channel_id=1, source_target_pairs={{2,4},{4,2},{3,5},{5,3},{10,12},{12,10},{11,13},{13,11},{18,20},{2... | collective-permute-start | bytes 491528 | tf_op jit(solution)/shard_map/ppermute | solution.py:497
  6.6 3.1 %collective-permute-start.1 = (bf16[10,64,128]{2,1,0:T(8,128)(2,1)S(1)}, bf16[10,64,128]{2,1,0:T(8,128)(2,1)S(1)}, u32[]{:S(2)}, u32[]{:S(2)}) collective-permute-start(bf16[10,64,128]{2,1,0:T(8,128)(2,1)S(1)} %get-tuple-element.26), channel_id=1, source_target_pairs={{0,2},{2,0},{4,6},{6,4},{1,3},{3,1},{5,7},{7,5},{8,10},{10,8},{12,... | collective-permute-start | bytes 491528 | tf_op jit(solution)/shard_map/ppermute | solution.py:497
  11.8 0.7 collective-permute-start.3
  12.6 0.7 collective-permute-start.4
  13.3 3.1 %shard_map.61.refs_1_.refs_0_ = f32[9,64,128]{2,1,0:T(8,128)S(1)} custom-call(f32[512,128]{1,0:T(8,128)S(1)} %bitcast.21, bf16[10,64,128]{2,1,0:T(8,128)(2,1)S(1)} %collective-permute-done.1.pair_ref, bf16[10,64,128]{2,1,0:T(8,128)(2,1)S(1)} %collective-permute-done.2.cross_ref, bf16[64,256]{1,0:T(8,128)(2,1)S(1)} %get-tuple-element.36.side_ref, ...), custom_call_target="tpu_custom_call" | custom-call | flops 830472192 | tf_op jit(solution)/shard_map/pallas_call | solution.py:589
  16.6 1.3 %collective-permute-start.5 = (bf16[5,64,128]{2,1,0:T(8,128)(2,1)S(1)}, bf16[5,64,128]{2,1,0:T(8,128)(2,1)S(1)}, u32[]{:S(2)}, u32[]{:S(2)}) collective-permute-start(bf16[5,64,128]{2,1,0:T(8,128)(2,1)S(1)} %shard_map.62), channel_id=1, source_target_pairs={{8,16},{9,17},{10,18},{11,19},{12,20},{13,21},{14,22},{15,23}} | collective-permute-start | bytes 245768 | tf_op jit(solution)/shard_map/ppermute | solution.py:604
  18.1 1.3 %collective-permute-start.6 = (bf16[4,64,128]{2,1,0:T(8,128)(2,1)S(1)}, bf16[4,64,128]{2,1,0:T(8,128)(2,1)S(1)}, u32[]{:S(2)}, u32[]{:S(2)}) collective-permute-start(bf16[4,64,128]{2,1,0:T(8,128)(2,1)S(1)} %shard_map.63), channel_id=1, source_target_pairs={{8,16},{9,17},{10,18},{11,19},{12,20},{13,21},{14,22},{15,23}} | collective-permute-start | bytes 196616 | tf_op jit(solution)/shard_map/ppermute | solution.py:604
  19.4 2.4 %collective-permute-done.5.s_ref.refs_2_ = bf16[5,64,128]{2,1,0:T(8,128)(2,1)S(1)} collective-permute-done((bf16[5,64,128]{2,1,0:T(8,128)(2,1)S(1)}, bf16[5,64,128]{2,1,0:T(8,128)(2,1)S(1)}, u32[]{:S(2)}, u32[]{:S(2)}) %collective-permute-start.5) | collective-permute-done | bytes 81952 | tf_op jit(solution)/shard_map/ppermute | solution.py:604
  22.0 1.3 %collective-permute-start.7 = (bf16[5,64,128]{2,1,0:T(8,128)(2,1)S(1)}, bf16[5,64,128]{2,1,0:T(8,128)(2,1)S(1)}, u32[]{:S(2)}, u32[]{:S(2)}) collective-permute-start(bf16[5,64,128]{2,1,0:T(8,128)(2,1)S(1)} %shard_map.64), channel_id=1, source_target_pairs={{16,24},{17,25},{18,26},{19,27},{20,28},{21,29},{22,30},{23,31}} | collective-permute-start | bytes 245768 | tf_op jit(solution)/shard_map/ppermute | solution.py:604
  23.6 1.3 %collective-permute-start.8 = (bf16[4,64,128]{2,1,0:T(8,128)(2,1)S(1)}, bf16[4,64,128]{2,1,0:T(8,128)(2,1)S(1)}, u32[]{:S(2)}, u32[]{:S(2)}) collective-permute-start(bf16[4,64,128]{2,1,0:T(8,128)(2,1)S(1)} %shard_map.65), channel_id=1, source_target_pairs={{16,24},{17,25},{18,26},{19,27},{20,28},{21,29},{22,30},{23,31}} | collective-permute-start | bytes 196616 | tf_op jit(solution)/shard_map/ppermute | solution.py:604
  24.9 1.3 %collective-permute-done.8.refs_5_ = bf16[4,64,128]{2,1,0:T(8,128)(2,1)S(1)} collective-permute-done((bf16[4,64,128]{2,1,0:T(8,128)(2,1)S(1)}, bf16[4,64,128]{2,1,0:T(8,128)(2,1)S(1)}, u32[]{:S(2)}, u32[]{:S(2)}) %collective-permute-start.8) | collective-permute-done | bytes 65568 | tf_op jit(solution)/shard_map/ppermute | solution.py:604
  26.3 0.9 %collective-permute-start.10 = (bf16[9,64,128]{2,1,0:T(8,128)(2,1)S(1)}, bf16[9,64,128]{2,1,0:T(8,128)(2,1)S(1)}, u32[]{:S(2)}, u32[]{:S(2)}) collective-permute-start(bf16[9,64,128]{2,1,0:T(8,128)(2,1)S(1)} %shard_map.66.s_ref), channel_id=1, source_target_pairs={{2,4},{4,2},{3,5},{5,3},{10,12},{12,10},{11,13},{13,11},{18,20},{2... | collective-permute-start | bytes 442376 | tf_op jit(solution)/shard_map/ppermute | solution.py:497
  27.1 6.1 %collective-permute-start.9 = (bf16[9,64,128]{2,1,0:T(8,128)(2,1)S(1)}, bf16[9,64,128]{2,1,0:T(8,128)(2,1)S(1)}, u32[]{:S(2)}, u32[]{:S(2)}) collective-permute-start(bf16[9,64,128]{2,1,0:T(8,128)(2,1)S(1)} %shard_map.66.s_ref), channel_id=1, source_target_pairs={{0,2},{2,0},{4,6},{6,4},{1,3},{3,1},{5,7},{7,5},{8,10},{10,8},{12,... | collective-permute-start | bytes 442376 | tf_op jit(solution)/shard_map/ppermute | solution.py:497
  33.3 0.9 %collective-permute-done.9.s_pair_ref = bf16[9,64,128]{2,1,0:T(8,128)(2,1)S(1)} collective-permute-done((bf16[9,64,128]{2,1,0:T(8,128)(2,1)S(1)}, bf16[9,64,128]{2,1,0:T(8,128)(2,1)S(1)}, u32[]{:S(2)}, u32[]{:S(2)}) %collective-permute-start.9) | collective-permute-done | bytes 147488 | tf_op jit(solution)/shard_map/ppermute | solution.py:497
  34.2 8.2 %shard_map.67 = (f32[512,128]{1,0:T(8,128)}, f32[8,64,128]{2,1,0:T(8,128)S(1)}, bf16[4,64,128]{2,1,0:T(8,128)(2,1)S(1)}, bf16[4,64,128]{2,1,0:T(8,128)(2,1)S(1)}...) custom-call(f32[512,128]{1,0:T(8,128)S(1)} %bitcast.27, f32[512,128]{1,0:T(8,128)S(1)} %bitcast.30, ...), custom_call_target="tpu_custom_call" | custom-call | flops 2264924160 | tf_op jit(solution)/shard_map/pallas_call | solution.py:631
  42.4 1.3 %collective-permute-start.15 = (bf16[4,64,128]{2,1,0:T(8,128)(2,1)S(1)}, bf16[4,64,128]{2,1,0:T(8,128)(2,1)S(1)}, u32[]{:S(2)}, u32[]{:S(2)}) collective-permute-start(bf16[4,64,128]{2,1,0:T(8,128)(2,1)S(1)} %get-tuple-element.42), channel_id=1, source_target_pairs={{24,16},{25,17},{26,18},{27,19},{28,20},{29,21},{30,22},{31,23}} | collective-permute-start | bytes 196616 | tf_op jit(solution)/shard_map/ppermute | solution.py:604
  43.7 1.3 %collective-permute-start.16 = (bf16[4,64,128]{2,1,0:T(8,128)(2,1)S(1)}, bf16[4,64,128]{2,1,0:T(8,128)(2,1)S(1)}, u32[]{:S(2)}, u32[]{:S(2)}) collective-permute-start(bf16[4,64,128]{2,1,0:T(8,128)(2,1)S(1)} %get-tuple-element.43), channel_id=1, source_target_pairs={{24,16},{25,17},{26,18},{27,19},{28,20},{29,21},{30,22},{31,23}} | collective-permute-start | bytes 196616 | tf_op jit(solution)/shard_map/ppermute | solution.py:604
  45.0 1.1 %shard_map.68 = f32[4,64,576]{2,1,0:T(8,128)S(1)} custom-call(bf16[4,8,64,256]{3,2,1,0:T(8,128)(2,1)S(1)} %get-tuple-element.40.kept_ref, bf16[4,10,64,128]{3,2,1,0:T(8,128)(2,1)S(1)} %get-tuple-element.41.sent_ref), custom_call_target="tpu_custom_call" | custom-call | flops 1000000000 | tf_op jit(solution)/shard_map/pallas_call | solution.py:660
  46.2 3.3 %collective-permute-start.11 = (f32[2,64,576]{2,1,0:T(8,128)S(1)}, f32[2,64,576]{2,1,0:T(8,128)S(1)}, u32[]{:S(2)}, u32[]{:S(2)}) collective-permute-start(f32[2,64,576]{2,1,0:T(8,128)S(1)} %slice_select_fusion), channel_id=1, source_target_pairs={{0,2},{2,0},{4,6},{6,4},{1,3},{3,1},{5,7},{7,5},{8,10},{10,8},{12,... | collective-permute-start | bytes 884744 | tf_op jit(solution)/shard_map/ppermute | solution.py:515
  49.7 1.3 %collective-permute-start.17 = (bf16[4,64,128]{2,1,0:T(8,128)(2,1)S(1)}, bf16[4,64,128]{2,1,0:T(8,128)(2,1)S(1)}, u32[]{:S(2)}, u32[]{:S(2)}) collective-permute-start(bf16[4,64,128]{2,1,0:T(8,128)(2,1)S(1)} %shard_map.69), channel_id=1, source_target_pairs={{16,8},{17,9},{18,10},{19,11},{20,12},{21,13},{22,14},{23,15}} | collective-permute-start | bytes 196616 | tf_op jit(solution)/shard_map/ppermute | solution.py:604
  51.0 1.3 %collective-permute-start.12 = (bf16[2,64,576]{2,1,0:T(8,128)(2,1)S(1)}, bf16[2,64,576]{2,1,0:T(8,128)(2,1)S(1)}, u32[]{:S(2)}, u32[]{:S(2)}) collective-permute-start(bf16[2,64,576]{2,1,0:T(8,128)(2,1)S(1)} %add_convert_fusion.1), channel_id=1, source_target_pairs={{0,4},{1,5},{2,3},{3,2},{4,0},{5,1},{6,7},{7,6},{8,12},{9,13},{10,... | collective-permute-start | bytes 442376 | tf_op jit(solution)/shard_map/ppermute | solution.py:527
  52.5 1.3 %collective-permute-start.18 = (bf16[4,64,128]{2,1,0:T(8,128)(2,1)S(1)}, bf16[4,64,128]{2,1,0:T(8,128)(2,1)S(1)}, u32[]{:S(2)}, u32[]{:S(2)}) collective-permute-start(bf16[4,64,128]{2,1,0:T(8,128)(2,1)S(1)} %shard_map.70), channel_id=1, source_target_pairs={{16,8},{17,9},{18,10},{19,11},{20,12},{21,13},{22,14},{23,15}} | collective-permute-start | bytes 196616 | tf_op jit(solution)/shard_map/ppermute | solution.py:604
  53.8 1.4 %collective-permute-done.12 = bf16[2,64,576]{2,1,0:T(8,128)(2,1)S(1)} collective-permute-done((bf16[2,64,576]{2,1,0:T(8,128)(2,1)S(1)}, bf16[2,64,576]{2,1,0:T(8,128)(2,1)S(1)}, u32[]{:S(2)}, u32[]{:S(2)}) %collective-permute-start.12) | collective-permute-done | bytes 147488 | tf_op jit(solution)/shard_map/ppermute | solution.py:527
  55.3 2.0 %collective-permute-start.13 = (bf16[2,64,576]{2,1,0:T(8,128)(2,1)S(1)}, bf16[2,64,576]{2,1,0:T(8,128)(2,1)S(1)}, u32[]{:S(2)}, u32[]{:S(2)}) collective-permute-start(bf16[2,64,576]{2,1,0:T(8,128)(2,1)S(1)} %add_convert_fusion), channel_id=1, source_target_pairs={{0,1},{1,0},{2,6},{3,7},{4,5},{5,4},{6,2},{7,3},{8,9},{9,8},{10,14... | collective-permute-start | bytes 442376 | tf_op jit(solution)/shard_map/ppermute | solution.py:527
  57.5 0.7 collective-permute-start.19
  58.2 1.8 %collective-permute-done.13 = bf16[2,64,576]{2,1,0:T(8,128)(2,1)S(1)} collective-permute-done((bf16[2,64,576]{2,1,0:T(8,128)(2,1)S(1)}, bf16[2,64,576]{2,1,0:T(8,128)(2,1)S(1)}, u32[]{:S(2)}, u32[]{:S(2)}) %collective-permute-start.13) | collective-permute-done | bytes 147488 | tf_op jit(solution)/shard_map/ppermute | solution.py:527
  60.0 4.3 %collective-permute-start.14 = (f32[2,64,576]{2,1,0:T(8,128)S(1)}, f32[2,64,576]{2,1,0:T(8,128)S(1)}, u32[]{:S(2)}, u32[]{:S(2)}) collective-permute-start(f32[2,64,576]{2,1,0:T(8,128)S(1)} %convert_add_fusion.half_ref), channel_id=1, source_target_pairs={{0,2},{2,0},{4,6},{6,4},{1,3},{3,1},{5,7},{7,5},{8,10},{10,8},{12,... | collective-permute-start | bytes 884744 | tf_op jit(solution)/shard_map/ppermute | solution.py:529
  64.5 0.7 collective-permute-start.20
  65.6 1.0 %shard_map.73 = (f32[512,128]{1,0:T(8,128)}, f32[4,64,576]{2,1,0:T(8,128)}) custom-call(f32[512,128]{1,0:T(8,128)S(1)} %bitcast.35, f32[2,64,576]{2,1,0:T(8,128)S(1)} %convert_add_fusion.half_ref, f32[2,64,576]{2,1,0:T(8,128)S(1)} %collective-permute-done.14.other_ref, bf16[4,64,128]{2,1,0:T(8,128)(2,1)S(1)} %collective-permute-done.15.s_ref.refs_0_, ...), custom_call_target="tpu_custom_call" | custom-call | flops 10000000000 | tf_op jit(solution)/shard_map/pallas_call | solution.py:666
  (49 shorter events, 5.1 us)
Async XLA Ops:
  0.6 3.3 %copy-start.2 = (bf16[4,64,576]{2,1,0:T(8,128)(2,1)S(1)}, bf16[4,64,576]{2,1,0:T(8,128)(2,1)}, u32[]{:S(2)}) copy-start(bf16[4,64,576]{2,1,0:T(8,128)(2,1)} %param.5) | copy-start | bytes 884740
  2.6 3.0 %collective-permute-start = (bf16[64,256]{1,0:T(8,128)(2,1)}, bf16[64,256]{1,0:T(8,128)(2,1)S(1)}, u32[]{:S(2)}, u32[]{:S(2)}) collective-permute-start(bf16[64,256]{1,0:T(8,128)(2,1)} %shard_map.58), channel_id=1, source_target_pairs={{0,1},{1,0},{2,3},{3,2},{4,5},{5,4},{6,7},{7,6},{8,9},{9,8},{10,11... | collective-permute-start | bytes 98312 | tf_op jit(solution)/shard_map/ppermute | solution.py:502
  3.9 1.7 %copy-start.1 = (f32[1,64,8,128]{3,2,1,0:T(8,128)S(1)}, f32[1,64,8,128]{3,2,1,0:T(8,128)}, u32[]{:S(2)}) copy-start(f32[1,64,8,128]{3,2,1,0:T(8,128)} %param.4) | copy-start | bytes 786436
  4.2 1.4 %copy-start = (f32[1,64,8,128]{3,2,1,0:T(8,128)S(1)}, f32[1,64,8,128]{3,2,1,0:T(8,128)}, u32[]{:S(2)}) copy-start(f32[1,64,8,128]{3,2,1,0:T(8,128)} %param.3) | copy-start | bytes 786436
  5.9 5.9 %collective-permute-start.2 = (bf16[10,64,128]{2,1,0:T(8,128)(2,1)S(1)}, bf16[10,64,128]{2,1,0:T(8,128)(2,1)S(1)}, u32[]{:S(2)}, u32[]{:S(2)}) collective-permute-start(bf16[10,64,128]{2,1,0:T(8,128)(2,1)S(1)} %get-tuple-element.27), channel_id=1, source_target_pairs={{2,4},{4,2},{3,5},{5,3},{10,12},{12,10},{11,13},{13,11},{18,20},{2... | collective-permute-start | bytes 491528 | tf_op jit(solution)/shard_map/ppermute | solution.py:497
  6.6 5.2 %collective-permute-start.1 = (bf16[10,64,128]{2,1,0:T(8,128)(2,1)S(1)}, bf16[10,64,128]{2,1,0:T(8,128)(2,1)S(1)}, u32[]{:S(2)}, u32[]{:S(2)}) collective-permute-start(bf16[10,64,128]{2,1,0:T(8,128)(2,1)S(1)} %get-tuple-element.26), channel_id=1, source_target_pairs={{0,2},{2,0},{4,6},{6,4},{1,3},{3,1},{5,7},{7,5},{8,10},{10,8},{12,... | collective-permute-start | bytes 491528 | tf_op jit(solution)/shard_map/ppermute | solution.py:497
  11.8 4.6 %collective-permute-start.3 = (bf16[5,64,128]{2,1,0:T(8,128)(2,1)S(1)}, bf16[5,64,128]{2,1,0:T(8,128)(2,1)S(1)}, u32[]{:S(2)}, u32[]{:S(2)}) collective-permute-start(bf16[5,64,128]{2,1,0:T(8,128)(2,1)S(1)} %get-tuple-element.31), channel_id=1, source_target_pairs={{0,8},{1,9},{2,10},{3,11},{4,12},{5,13},{6,14},{7,15}} | collective-permute-start | bytes 245768 | tf_op jit(solution)/shard_map/ppermute | solution.py:604
  12.6 5.3 %collective-permute-start.4 = (bf16[4,64,128]{2,1,0:T(8,128)(2,1)S(1)}, bf16[4,64,128]{2,1,0:T(8,128)(2,1)S(1)}, u32[]{:S(2)}, u32[]{:S(2)}) collective-permute-start(bf16[4,64,128]{2,1,0:T(8,128)(2,1)S(1)} %get-tuple-element.32), channel_id=1, source_target_pairs={{0,8},{1,9},{2,10},{3,11},{4,12},{5,13},{6,14},{7,15}} | collective-permute-start | bytes 196616 | tf_op jit(solution)/shard_map/ppermute | solution.py:604
  16.6 5.2 %collective-permute-start.5 = (bf16[5,64,128]{2,1,0:T(8,128)(2,1)S(1)}, bf16[5,64,128]{2,1,0:T(8,128)(2,1)S(1)}, u32[]{:S(2)}, u32[]{:S(2)}) collective-permute-start(bf16[5,64,128]{2,1,0:T(8,128)(2,1)S(1)} %shard_map.62), channel_id=1, source_target_pairs={{8,16},{9,17},{10,18},{11,19},{12,20},{13,21},{14,22},{15,23}} | collective-permute-start | bytes 245768 | tf_op jit(solution)/shard_map/ppermute | solution.py:604
  18.1 5.2 %collective-permute-start.6 = (bf16[4,64,128]{2,1,0:T(8,128)(2,1)S(1)}, bf16[4,64,128]{2,1,0:T(8,128)(2,1)S(1)}, u32[]{:S(2)}, u32[]{:S(2)}) collective-permute-start(bf16[4,64,128]{2,1,0:T(8,128)(2,1)S(1)} %shard_map.63), channel_id=1, source_target_pairs={{8,16},{9,17},{10,18},{11,19},{12,20},{13,21},{14,22},{15,23}} | collective-permute-start | bytes 196616 | tf_op jit(solution)/shard_map/ppermute | solution.py:604
  22.0 4.1 %collective-permute-start.7 = (bf16[5,64,128]{2,1,0:T(8,128)(2,1)S(1)}, bf16[5,64,128]{2,1,0:T(8,128)(2,1)S(1)}, u32[]{:S(2)}, u32[]{:S(2)}) collective-permute-start(bf16[5,64,128]{2,1,0:T(8,128)(2,1)S(1)} %shard_map.64), channel_id=1, source_target_pairs={{16,24},{17,25},{18,26},{19,27},{20,28},{21,29},{22,30},{23,31}} | collective-permute-start | bytes 245768 | tf_op jit(solution)/shard_map/ppermute | solution.py:604
  23.6 2.6 %collective-permute-start.8 = (bf16[4,64,128]{2,1,0:T(8,128)(2,1)S(1)}, bf16[4,64,128]{2,1,0:T(8,128)(2,1)S(1)}, u32[]{:S(2)}, u32[]{:S(2)}) collective-permute-start(bf16[4,64,128]{2,1,0:T(8,128)(2,1)S(1)} %shard_map.65), channel_id=1, source_target_pairs={{16,24},{17,25},{18,26},{19,27},{20,28},{21,29},{22,30},{23,31}} | collective-permute-start | bytes 196616 | tf_op jit(solution)/shard_map/ppermute | solution.py:604
  26.3 7.0 %collective-permute-start.10 = (bf16[9,64,128]{2,1,0:T(8,128)(2,1)S(1)}, bf16[9,64,128]{2,1,0:T(8,128)(2,1)S(1)}, u32[]{:S(2)}, u32[]{:S(2)}) collective-permute-start(bf16[9,64,128]{2,1,0:T(8,128)(2,1)S(1)} %shard_map.66.s_ref), channel_id=1, source_target_pairs={{2,4},{4,2},{3,5},{5,3},{10,12},{12,10},{11,13},{13,11},{18,20},{2... | collective-permute-start | bytes 442376 | tf_op jit(solution)/shard_map/ppermute | solution.py:497
  27.1 7.1 %collective-permute-start.9 = (bf16[9,64,128]{2,1,0:T(8,128)(2,1)S(1)}, bf16[9,64,128]{2,1,0:T(8,128)(2,1)S(1)}, u32[]{:S(2)}, u32[]{:S(2)}) collective-permute-start(bf16[9,64,128]{2,1,0:T(8,128)(2,1)S(1)} %shard_map.66.s_ref), channel_id=1, source_target_pairs={{0,2},{2,0},{4,6},{6,4},{1,3},{3,1},{5,7},{7,5},{8,10},{10,8},{12,... | collective-permute-start | bytes 442376 | tf_op jit(solution)/shard_map/ppermute | solution.py:497
  42.4 7.0 %collective-permute-start.15 = (bf16[4,64,128]{2,1,0:T(8,128)(2,1)S(1)}, bf16[4,64,128]{2,1,0:T(8,128)(2,1)S(1)}, u32[]{:S(2)}, u32[]{:S(2)}) collective-permute-start(bf16[4,64,128]{2,1,0:T(8,128)(2,1)S(1)} %get-tuple-element.42), channel_id=1, source_target_pairs={{24,16},{25,17},{26,18},{27,19},{28,20},{29,21},{30,22},{31,23}} | collective-permute-start | bytes 196616 | tf_op jit(solution)/shard_map/ppermute | solution.py:604
  43.7 8.6 %collective-permute-start.16 = (bf16[4,64,128]{2,1,0:T(8,128)(2,1)S(1)}, bf16[4,64,128]{2,1,0:T(8,128)(2,1)S(1)}, u32[]{:S(2)}, u32[]{:S(2)}) collective-permute-start(bf16[4,64,128]{2,1,0:T(8,128)(2,1)S(1)} %get-tuple-element.43), channel_id=1, source_target_pairs={{24,16},{25,17},{26,18},{27,19},{28,20},{29,21},{30,22},{31,23}} | collective-permute-start | bytes 196616 | tf_op jit(solution)/shard_map/ppermute | solution.py:604
  46.2 4.8 %collective-permute-start.11 = (f32[2,64,576]{2,1,0:T(8,128)S(1)}, f32[2,64,576]{2,1,0:T(8,128)S(1)}, u32[]{:S(2)}, u32[]{:S(2)}) collective-permute-start(f32[2,64,576]{2,1,0:T(8,128)S(1)} %slice_select_fusion), channel_id=1, source_target_pairs={{0,2},{2,0},{4,6},{6,4},{1,3},{3,1},{5,7},{7,5},{8,10},{10,8},{12,... | collective-permute-start | bytes 884744 | tf_op jit(solution)/shard_map/ppermute | solution.py:515
  49.7 7.6 %collective-permute-start.17 = (bf16[4,64,128]{2,1,0:T(8,128)(2,1)S(1)}, bf16[4,64,128]{2,1,0:T(8,128)(2,1)S(1)}, u32[]{:S(2)}, u32[]{:S(2)}) collective-permute-start(bf16[4,64,128]{2,1,0:T(8,128)(2,1)S(1)} %shard_map.69), channel_id=1, source_target_pairs={{16,8},{17,9},{18,10},{19,11},{20,12},{21,13},{22,14},{23,15}} | collective-permute-start | bytes 196616 | tf_op jit(solution)/shard_map/ppermute | solution.py:604
  51.0 4.2 %collective-permute-start.12 = (bf16[2,64,576]{2,1,0:T(8,128)(2,1)S(1)}, bf16[2,64,576]{2,1,0:T(8,128)(2,1)S(1)}, u32[]{:S(2)}, u32[]{:S(2)}) collective-permute-start(bf16[2,64,576]{2,1,0:T(8,128)(2,1)S(1)} %add_convert_fusion.1), channel_id=1, source_target_pairs={{0,4},{1,5},{2,3},{3,2},{4,0},{5,1},{6,7},{7,6},{8,12},{9,13},{10,... | collective-permute-start | bytes 442376 | tf_op jit(solution)/shard_map/ppermute | solution.py:527
  52.5 11.8 %collective-permute-start.18 = (bf16[4,64,128]{2,1,0:T(8,128)(2,1)S(1)}, bf16[4,64,128]{2,1,0:T(8,128)(2,1)S(1)}, u32[]{:S(2)}, u32[]{:S(2)}) collective-permute-start(bf16[4,64,128]{2,1,0:T(8,128)(2,1)S(1)} %shard_map.70), channel_id=1, source_target_pairs={{16,8},{17,9},{18,10},{19,11},{20,12},{21,13},{22,14},{23,15}} | collective-permute-start | bytes 196616 | tf_op jit(solution)/shard_map/ppermute | solution.py:604
  55.3 4.7 %collective-permute-start.13 = (bf16[2,64,576]{2,1,0:T(8,128)(2,1)S(1)}, bf16[2,64,576]{2,1,0:T(8,128)(2,1)S(1)}, u32[]{:S(2)}, u32[]{:S(2)}) collective-permute-start(bf16[2,64,576]{2,1,0:T(8,128)(2,1)S(1)} %add_convert_fusion), channel_id=1, source_target_pairs={{0,1},{1,0},{2,6},{3,7},{4,5},{5,4},{6,2},{7,3},{8,9},{9,8},{10,14... | collective-permute-start | bytes 442376 | tf_op jit(solution)/shard_map/ppermute | solution.py:527
  57.5 7.7 %collective-permute-start.19 = (bf16[4,64,128]{2,1,0:T(8,128)(2,1)S(1)}, bf16[4,64,128]{2,1,0:T(8,128)(2,1)S(1)}, u32[]{:S(2)}, u32[]{:S(2)}) collective-permute-start(bf16[4,64,128]{2,1,0:T(8,128)(2,1)S(1)} %shard_map.71), channel_id=1, source_target_pairs={{8,0},{9,1},{10,2},{11,3},{12,4},{13,5},{14,6},{15,7}} | collective-permute-start | bytes 196616 | tf_op jit(solution)/shard_map/ppermute | solution.py:604
  60.0 5.5 %collective-permute-start.14 = (f32[2,64,576]{2,1,0:T(8,128)S(1)}, f32[2,64,576]{2,1,0:T(8,128)S(1)}, u32[]{:S(2)}, u32[]{:S(2)}) collective-permute-start(f32[2,64,576]{2,1,0:T(8,128)S(1)} %convert_add_fusion.half_ref), channel_id=1, source_target_pairs={{0,2},{2,0},{4,6},{6,4},{1,3},{3,1},{5,7},{7,5},{8,10},{10,8},{12,... | collective-permute-start | bytes 884744 | tf_op jit(solution)/shard_map/ppermute | solution.py:529
  64.5 0.7 %collective-permute-start.20 = (bf16[4,64,128]{2,1,0:T(8,128)(2,1)S(1)}, bf16[4,64,128]{2,1,0:T(8,128)(2,1)S(1)}, u32[]{:S(2)}, u32[]{:S(2)}) collective-permute-start(bf16[4,64,128]{2,1,0:T(8,128)(2,1)S(1)} %shard_map.72), channel_id=1, source_target_pairs={{8,0},{9,1},{10,2},{11,3},{12,4},{13,5},{14,6},{15,7}} | collective-permute-start | bytes 196616 | tf_op jit(solution)/shard_map/ppermute | solution.py:604

commit v11 on v10

--- a/solution.py
+++ b/solution.py
@@ -186,7 +186,7 @@
 
 
 def row_blocks(low, high, body):
-    turns = 1 if high - low <= 10 else 2
+    turns = 1 if high - low <= 32 else 2
     size, rest = divmod(high - low, turns)
 
     def turn(number, carry):

time: 67.8 us -> 64.8 us (0.956)
  Pallas kernels: 17.4 us -> 14.3 us
    pallas_call x1, Pallas kernels: 8.23 us -> 6.1 us  [local(): call(functools.partial(second_body, depth=depth, **sizes), (flat_f, tile_...]
    pallas_call x2, Pallas kernels: 3.16 us -> 2.21 us  [first(): call(functools.partial(first_body, depth=depth, sender=sender, **sizes),...]
  transfers between devices with their start and end apart: 21 -> 21, of which waited for: 7 -> 7; matrix products, arithmetic and copies ran while one was open for 4% -> 4% of each run, Pallas kernels for 9% -> 8%
where the time goes in v11:
time: 64.8 us; the launch traced here: 63.7 us
  starting transfers between devices  35.9 us (55%)
  Pallas kernels  14.3 us (22%)
  waiting for transfers between devices  9.57 us (15%)
  local copies, waits for them, and re-layouts  2.43 us (4%)
  between operations  1.19 us (2%)
    ppermute x12, starting transfers between devices, chain(): arrived = [lax.ppermute(sending, 'layer', [step]) for sending in sendings]  13 us
    ppermute x2, starting transfers between devices, exchanged(): lax.ppermute(to_pair, 'row', pairs)  9.31 us
    pallas_call x1, Pallas kernels, local(): call(functools.partial(second_body, depth=depth, **sizes), (flat_f, tile_...  6.1 us
    ppermute x1, starting transfers between devices, total_over_tiles(): return (value, lax.ppermute(value, 'row', pair))  4.35 us
    ppermute x12, waiting for transfers between devices, chain(): arrived = [lax.ppermute(sending, 'layer', [step]) for sending in sendings]  3.71 us
    ppermute x2, waiting for transfers between devices, total_over_tiles(): arrived = lax.ppermute(rounded, ('row', 'col'), pairs)  3.25 us
    ppermute x1, starting transfers between devices, total_over_tiles(): value = own + lax.ppermute(sent, 'row', pair)  3.25 us
    ppermute x2, starting transfers between devices, total_over_tiles(): arrived = lax.ppermute(rounded, ('row', 'col'), pairs)  3.19 us
  transfers between devices with their start and end apart: 21, of which 7 were waited for; matrix products, arithmetic and copies ran while one was open for 4% of the time, Pallas kernels for 8%

profile of v11, /device:TPU:19, one launch (start us, length us, event | category | flops | bytes accessed | tf_op | source)
XLA Modules:
  0.0 63.7 jit_solution(18158995246537569344)
XLA Ops:
  0.6 1.9 %shard_map.58 = bf16[64,256]{1,0:T(8,128)(2,1)} custom-call(f32[512,128]{1,0:T(8,128)} %bitcast.18, f32[512,128]{1,0:T(8,128)} %bitcast.28), custom_call_target="tpu_custom_call" | custom-call | tf_op jit(solution)/shard_map/pallas_call | solution.py:552
  2.6 1.3 %collective-permute-start = (bf16[64,256]{1,0:T(8,128)(2,1)}, bf16[64,256]{1,0:T(8,128)(2,1)S(1)}, u32[]{:S(2)}, u32[]{:S(2)}) collective-permute-start(bf16[64,256]{1,0:T(8,128)(2,1)} %shard_map.58), channel_id=1, source_target_pairs={{0,1},{1,0},{2,3},{3,2},{4,5},{5,4},{6,7},{7,6},{8,9},{9,8},{10,11... | collective-permute-start | bytes 98312 | tf_op jit(solution)/shard_map/ppermute | solution.py:502
  4.3 1.4 %collective-permute-done.left_ref.right_ref = bf16[64,256]{1,0:T(8,128)(2,1)S(1)} collective-permute-done((bf16[64,256]{1,0:T(8,128)(2,1)}, bf16[64,256]{1,0:T(8,128)(2,1)S(1)}, u32[]{:S(2)}, u32[]{:S(2)}) %collective-permute-start) | collective-permute-done | bytes 32800 | tf_op jit(solution)/shard_map/ppermute | solution.py:502
  5.9 0.7 %collective-permute-start.2 = (bf16[10,64,128]{2,1,0:T(8,128)(2,1)S(1)}, bf16[10,64,128]{2,1,0:T(8,128)(2,1)S(1)}, u32[]{:S(2)}, u32[]{:S(2)}) collective-permute-start(bf16[10,64,128]{2,1,0:T(8,128)(2,1)S(1)} %get-tuple-element.27), channel_id=1, source_target_pairs={{2,4},{4,2},{3,5},{5,3},{10,12},{12,10},{11,13},{13,11},{18,20},{2... | collective-permute-start | bytes 491528 | tf_op jit(solution)/shard_map/ppermute | solution.py:497
  6.6 3.1 %collective-permute-start.1 = (bf16[10,64,128]{2,1,0:T(8,128)(2,1)S(1)}, bf16[10,64,128]{2,1,0:T(8,128)(2,1)S(1)}, u32[]{:S(2)}, u32[]{:S(2)}) collective-permute-start(bf16[10,64,128]{2,1,0:T(8,128)(2,1)S(1)} %get-tuple-element.26), channel_id=1, source_target_pairs={{0,2},{2,0},{4,6},{6,4},{1,3},{3,1},{5,7},{7,5},{8,10},{10,8},{12,... | collective-permute-start | bytes 491528 | tf_op jit(solution)/shard_map/ppermute | solution.py:497
  11.8 0.7 %collective-permute-start.3 = (bf16[5,64,128]{2,1,0:T(8,128)(2,1)S(1)}, bf16[5,64,128]{2,1,0:T(8,128)(2,1)S(1)}, u32[]{:S(2)}, u32[]{:S(2)}) collective-permute-start(bf16[5,64,128]{2,1,0:T(8,128)(2,1)S(1)} %get-tuple-element.31), channel_id=1, source_target_pairs={{0,8},{1,9},{2,10},{3,11},{4,12},{5,13},{6,14},{7,15}} | collective-permute-start | bytes 245768 | tf_op jit(solution)/shard_map/ppermute | solution.py:604
  12.6 0.7 %collective-permute-start.4 = (bf16[4,64,128]{2,1,0:T(8,128)(2,1)S(1)}, bf16[4,64,128]{2,1,0:T(8,128)(2,1)S(1)}, u32[]{:S(2)}, u32[]{:S(2)}) collective-permute-start(bf16[4,64,128]{2,1,0:T(8,128)(2,1)S(1)} %get-tuple-element.32), channel_id=1, source_target_pairs={{0,8},{1,9},{2,10},{3,11},{4,12},{5,13},{6,14},{7,15}} | collective-permute-start | bytes 196616 | tf_op jit(solution)/shard_map/ppermute | solution.py:604
  13.3 2.2 %shard_map.61.refs_1_.refs_0_ = f32[9,64,128]{2,1,0:T(8,128)S(1)} custom-call(f32[512,128]{1,0:T(8,128)S(1)} %bitcast.21, bf16[10,64,128]{2,1,0:T(8,128)(2,1)S(1)} %collective-permute-done.1.pair_ref, bf16[10,64,128]{2,1,0:T(8,128)(2,1)S(1)} %collective-permute-done.2.cross_ref, bf16[64,256]{1,0:T(8,128)(2,1)S(1)} %get-tuple-element.36.side_ref, ...), custom_call_target="tpu_custom_call" | custom-call | flops 830472192 | tf_op jit(solution)/shard_map/pallas_call | solution.py:589
  15.7 1.3 %collective-permute-start.5 = (bf16[5,64,128]{2,1,0:T(8,128)(2,1)S(1)}, bf16[5,64,128]{2,1,0:T(8,128)(2,1)S(1)}, u32[]{:S(2)}, u32[]{:S(2)}) collective-permute-start(bf16[5,64,128]{2,1,0:T(8,128)(2,1)S(1)} %shard_map.62), channel_id=1, source_target_pairs={{8,16},{9,17},{10,18},{11,19},{12,20},{13,21},{14,22},{15,23}} | collective-permute-start | bytes 245768 | tf_op jit(solution)/shard_map/ppermute | solution.py:604
  17.2 1.3 %collective-permute-start.6 = (bf16[4,64,128]{2,1,0:T(8,128)(2,1)S(1)}, bf16[4,64,128]{2,1,0:T(8,128)(2,1)S(1)}, u32[]{:S(2)}, u32[]{:S(2)}) collective-permute-start(bf16[4,64,128]{2,1,0:T(8,128)(2,1)S(1)} %shard_map.63), channel_id=1, source_target_pairs={{8,16},{9,17},{10,18},{11,19},{12,20},{13,21},{14,22},{15,23}} | collective-permute-start | bytes 196616 | tf_op jit(solution)/shard_map/ppermute | solution.py:604
  18.5 2.4 %collective-permute-done.5.s_ref.refs_2_ = bf16[5,64,128]{2,1,0:T(8,128)(2,1)S(1)} collective-permute-done((bf16[5,64,128]{2,1,0:T(8,128)(2,1)S(1)}, bf16[5,64,128]{2,1,0:T(8,128)(2,1)S(1)}, u32[]{:S(2)}, u32[]{:S(2)}) %collective-permute-start.5) | collective-permute-done | bytes 81952 | tf_op jit(solution)/shard_map/ppermute | solution.py:604
  21.1 1.3 %collective-permute-start.7 = (bf16[5,64,128]{2,1,0:T(8,128)(2,1)S(1)}, bf16[5,64,128]{2,1,0:T(8,128)(2,1)S(1)}, u32[]{:S(2)}, u32[]{:S(2)}) collective-permute-start(bf16[5,64,128]{2,1,0:T(8,128)(2,1)S(1)} %shard_map.64), channel_id=1, source_target_pairs={{16,24},{17,25},{18,26},{19,27},{20,28},{21,29},{22,30},{23,31}} | collective-permute-start | bytes 245768 | tf_op jit(solution)/shard_map/ppermute | solution.py:604
  22.6 1.3 %collective-permute-start.8 = (bf16[4,64,128]{2,1,0:T(8,128)(2,1)S(1)}, bf16[4,64,128]{2,1,0:T(8,128)(2,1)S(1)}, u32[]{:S(2)}, u32[]{:S(2)}) collective-permute-start(bf16[4,64,128]{2,1,0:T(8,128)(2,1)S(1)} %shard_map.65), channel_id=1, source_target_pairs={{16,24},{17,25},{18,26},{19,27},{20,28},{21,29},{22,30},{23,31}} | collective-permute-start | bytes 196616 | tf_op jit(solution)/shard_map/ppermute | solution.py:604
  23.9 1.3 %collective-permute-done.8.refs_5_ = bf16[4,64,128]{2,1,0:T(8,128)(2,1)S(1)} collective-permute-done((bf16[4,64,128]{2,1,0:T(8,128)(2,1)S(1)}, bf16[4,64,128]{2,1,0:T(8,128)(2,1)S(1)}, u32[]{:S(2)}, u32[]{:S(2)}) %collective-permute-start.8) | collective-permute-done | bytes 65568 | tf_op jit(solution)/shard_map/ppermute | solution.py:604
  25.3 0.9 %collective-permute-start.10 = (bf16[9,64,128]{2,1,0:T(8,128)(2,1)S(1)}, bf16[9,64,128]{2,1,0:T(8,128)(2,1)S(1)}, u32[]{:S(2)}, u32[]{:S(2)}) collective-permute-start(bf16[9,64,128]{2,1,0:T(8,128)(2,1)S(1)} %shard_map.66.s_ref), channel_id=1, source_target_pairs={{2,4},{4,2},{3,5},{5,3},{10,12},{12,10},{11,13},{13,11},{18,20},{2... | collective-permute-start | bytes 442376 | tf_op jit(solution)/shard_map/ppermute | solution.py:497
  26.2 6.2 %collective-permute-start.9 = (bf16[9,64,128]{2,1,0:T(8,128)(2,1)S(1)}, bf16[9,64,128]{2,1,0:T(8,128)(2,1)S(1)}, u32[]{:S(2)}, u32[]{:S(2)}) collective-permute-start(bf16[9,64,128]{2,1,0:T(8,128)(2,1)S(1)} %shard_map.66.s_ref), channel_id=1, source_target_pairs={{0,2},{2,0},{4,6},{6,4},{1,3},{3,1},{5,7},{7,5},{8,10},{10,8},{12,... | collective-permute-start | bytes 442376 | tf_op jit(solution)/shard_map/ppermute | solution.py:497
  32.5 0.9 %collective-permute-done.9.s_pair_ref = bf16[9,64,128]{2,1,0:T(8,128)(2,1)S(1)} collective-permute-done((bf16[9,64,128]{2,1,0:T(8,128)(2,1)S(1)}, bf16[9,64,128]{2,1,0:T(8,128)(2,1)S(1)}, u32[]{:S(2)}, u32[]{:S(2)}) %collective-permute-start.9) | collective-permute-done | bytes 147488 | tf_op jit(solution)/shard_map/ppermute | solution.py:497
  33.3 6.1 %shard_map.67 = (f32[512,128]{1,0:T(8,128)}, f32[8,64,128]{2,1,0:T(8,128)S(1)}, bf16[4,64,128]{2,1,0:T(8,128)(2,1)S(1)}, bf16[4,64,128]{2,1,0:T(8,128)(2,1)S(1)}...) custom-call(f32[512,128]{1,0:T(8,128)S(1)} %bitcast.27, f32[512,128]{1,0:T(8,128)S(1)} %bitcast.30, ...), custom_call_target="tpu_custom_call" | custom-call | flops 2264924160 | tf_op jit(solution)/shard_map/pallas_call | solution.py:631
  39.5 1.3 %collective-permute-start.15 = (bf16[4,64,128]{2,1,0:T(8,128)(2,1)S(1)}, bf16[4,64,128]{2,1,0:T(8,128)(2,1)S(1)}, u32[]{:S(2)}, u32[]{:S(2)}) collective-permute-start(bf16[4,64,128]{2,1,0:T(8,128)(2,1)S(1)} %get-tuple-element.42), channel_id=1, source_target_pairs={{24,16},{25,17},{26,18},{27,19},{28,20},{29,21},{30,22},{31,23}} | collective-permute-start | bytes 196616 | tf_op jit(solution)/shard_map/ppermute | solution.py:604
  40.8 1.3 %collective-permute-start.16 = (bf16[4,64,128]{2,1,0:T(8,128)(2,1)S(1)}, bf16[4,64,128]{2,1,0:T(8,128)(2,1)S(1)}, u32[]{:S(2)}, u32[]{:S(2)}) collective-permute-start(bf16[4,64,128]{2,1,0:T(8,128)(2,1)S(1)} %get-tuple-element.43), channel_id=1, source_target_pairs={{24,16},{25,17},{26,18},{27,19},{28,20},{29,21},{30,22},{31,23}} | collective-permute-start | bytes 196616 | tf_op jit(solution)/shard_map/ppermute | solution.py:604
  42.1 1.1 %shard_map.68 = f32[4,64,576]{2,1,0:T(8,128)S(1)} custom-call(bf16[4,8,64,256]{3,2,1,0:T(8,128)(2,1)S(1)} %get-tuple-element.40.kept_ref, bf16[4,10,64,128]{3,2,1,0:T(8,128)(2,1)S(1)} %get-tuple-element.41.sent_ref), custom_call_target="tpu_custom_call" | custom-call | flops 1000000000 | tf_op jit(solution)/shard_map/pallas_call | solution.py:660
  43.2 3.2 %collective-permute-start.11 = (f32[2,64,576]{2,1,0:T(8,128)S(1)}, f32[2,64,576]{2,1,0:T(8,128)S(1)}, u32[]{:S(2)}, u32[]{:S(2)}) collective-permute-start(f32[2,64,576]{2,1,0:T(8,128)S(1)} %slice_select_fusion), channel_id=1, source_target_pairs={{0,2},{2,0},{4,6},{6,4},{1,3},{3,1},{5,7},{7,5},{8,10},{10,8},{12,... | collective-permute-start | bytes 884744 | tf_op jit(solution)/shard_map/ppermute | solution.py:515
  46.7 1.3 %collective-permute-start.17 = (bf16[4,64,128]{2,1,0:T(8,128)(2,1)S(1)}, bf16[4,64,128]{2,1,0:T(8,128)(2,1)S(1)}, u32[]{:S(2)}, u32[]{:S(2)}) collective-permute-start(bf16[4,64,128]{2,1,0:T(8,128)(2,1)S(1)} %shard_map.69), channel_id=1, source_target_pairs={{16,8},{17,9},{18,10},{19,11},{20,12},{21,13},{22,14},{23,15}} | collective-permute-start | bytes 196616 | tf_op jit(solution)/shard_map/ppermute | solution.py:604
  48.0 1.3 %collective-permute-start.12 = (bf16[2,64,576]{2,1,0:T(8,128)(2,1)S(1)}, bf16[2,64,576]{2,1,0:T(8,128)(2,1)S(1)}, u32[]{:S(2)}, u32[]{:S(2)}) collective-permute-start(bf16[2,64,576]{2,1,0:T(8,128)(2,1)S(1)} %add_convert_fusion.1), channel_id=1, source_target_pairs={{0,4},{1,5},{2,3},{3,2},{4,0},{5,1},{6,7},{7,6},{8,12},{9,13},{10,... | collective-permute-start | bytes 442376 | tf_op jit(solution)/shard_map/ppermute | solution.py:527
  49.5 1.3 %collective-permute-start.18 = (bf16[4,64,128]{2,1,0:T(8,128)(2,1)S(1)}, bf16[4,64,128]{2,1,0:T(8,128)(2,1)S(1)}, u32[]{:S(2)}, u32[]{:S(2)}) collective-permute-start(bf16[4,64,128]{2,1,0:T(8,128)(2,1)S(1)} %shard_map.70), channel_id=1, source_target_pairs={{16,8},{17,9},{18,10},{19,11},{20,12},{21,13},{22,14},{23,15}} | collective-permute-start | bytes 196616 | tf_op jit(solution)/shard_map/ppermute | solution.py:604
  50.8 1.4 %collective-permute-done.12 = bf16[2,64,576]{2,1,0:T(8,128)(2,1)S(1)} collective-permute-done((bf16[2,64,576]{2,1,0:T(8,128)(2,1)S(1)}, bf16[2,64,576]{2,1,0:T(8,128)(2,1)S(1)}, u32[]{:S(2)}, u32[]{:S(2)}) %collective-permute-start.12) | collective-permute-done | bytes 147488 | tf_op jit(solution)/shard_map/ppermute | solution.py:527
  52.3 1.9 %collective-permute-start.13 = (bf16[2,64,576]{2,1,0:T(8,128)(2,1)S(1)}, bf16[2,64,576]{2,1,0:T(8,128)(2,1)S(1)}, u32[]{:S(2)}, u32[]{:S(2)}) collective-permute-start(bf16[2,64,576]{2,1,0:T(8,128)(2,1)S(1)} %add_convert_fusion), channel_id=1, source_target_pairs={{0,1},{1,0},{2,6},{3,7},{4,5},{5,4},{6,2},{7,3},{8,9},{9,8},{10,14... | collective-permute-start | bytes 442376 | tf_op jit(solution)/shard_map/ppermute | solution.py:527
  54.4 0.7 %collective-permute-start.19 = (bf16[4,64,128]{2,1,0:T(8,128)(2,1)S(1)}, bf16[4,64,128]{2,1,0:T(8,128)(2,1)S(1)}, u32[]{:S(2)}, u32[]{:S(2)}) collective-permute-start(bf16[4,64,128]{2,1,0:T(8,128)(2,1)S(1)} %shard_map.71), channel_id=1, source_target_pairs={{8,0},{9,1},{10,2},{11,3},{12,4},{13,5},{14,6},{15,7}} | collective-permute-start | bytes 196616 | tf_op jit(solution)/shard_map/ppermute | solution.py:604
  55.1 1.8 %collective-permute-done.13 = bf16[2,64,576]{2,1,0:T(8,128)(2,1)S(1)} collective-permute-done((bf16[2,64,576]{2,1,0:T(8,128)(2,1)S(1)}, bf16[2,64,576]{2,1,0:T(8,128)(2,1)S(1)}, u32[]{:S(2)}, u32[]{:S(2)}) %collective-permute-start.13) | collective-permute-done | bytes 147488 | tf_op jit(solution)/shard_map/ppermute | solution.py:527
  56.9 4.4 %collective-permute-start.14 = (f32[2,64,576]{2,1,0:T(8,128)S(1)}, f32[2,64,576]{2,1,0:T(8,128)S(1)}, u32[]{:S(2)}, u32[]{:S(2)}) collective-permute-start(f32[2,64,576]{2,1,0:T(8,128)S(1)} %convert_add_fusion.half_ref), channel_id=1, source_target_pairs={{0,2},{2,0},{4,6},{6,4},{1,3},{3,1},{5,7},{7,5},{8,10},{10,8},{12,... | collective-permute-start | bytes 884744 | tf_op jit(solution)/shard_map/ppermute | solution.py:529
  61.5 0.7 %collective-permute-start.20 = (bf16[4,64,128]{2,1,0:T(8,128)(2,1)S(1)}, bf16[4,64,128]{2,1,0:T(8,128)(2,1)S(1)}, u32[]{:S(2)}, u32[]{:S(2)}) collective-permute-start(bf16[4,64,128]{2,1,0:T(8,128)(2,1)S(1)} %shard_map.72), channel_id=1, source_target_pairs={{8,0},{9,1},{10,2},{11,3},{12,4},{13,5},{14,6},{15,7}} | collective-permute-start | bytes 196616 | tf_op jit(solution)/shard_map/ppermute | solution.py:604
  62.5 1.0 %shard_map.73 = (f32[512,128]{1,0:T(8,128)}, f32[4,64,576]{2,1,0:T(8,128)}) custom-call(f32[512,128]{1,0:T(8,128)S(1)} %bitcast.35, f32[2,64,576]{2,1,0:T(8,128)S(1)} %convert_add_fusion.half_ref, f32[2,64,576]{2,1,0:T(8,128)S(1)} %collective-permute-done.14.other_ref, bf16[4,64,128]{2,1,0:T(8,128)(2,1)S(1)} %collective-permute-done.15.s_ref.refs_0_, ...), custom_call_target="tpu_custom_call" | custom-call | flops 10000000000 | tf_op jit(solution)/shard_map/pallas_call | solution.py:666
  (49 shorter events, 5.1 us)
Async XLA Ops:
  0.6 3.3 %copy-start.2 = (bf16[4,64,576]{2,1,0:T(8,128)(2,1)S(1)}, bf16[4,64,576]{2,1,0:T(8,128)(2,1)}, u32[]{:S(2)}) copy-start(bf16[4,64,576]{2,1,0:T(8,128)(2,1)} %param.5) | copy-start | bytes 884740
  2.6 3.0 %collective-permute-start = (bf16[64,256]{1,0:T(8,128)(2,1)}, bf16[64,256]{1,0:T(8,128)(2,1)S(1)}, u32[]{:S(2)}, u32[]{:S(2)}) collective-permute-start(bf16[64,256]{1,0:T(8,128)(2,1)} %shard_map.58), channel_id=1, source_target_pairs={{0,1},{1,0},{2,3},{3,2},{4,5},{5,4},{6,7},{7,6},{8,9},{9,8},{10,11... | collective-permute-start | bytes 98312 | tf_op jit(solution)/shard_map/ppermute | solution.py:502
  3.9 1.7 %copy-start.1 = (f32[1,64,8,128]{3,2,1,0:T(8,128)S(1)}, f32[1,64,8,128]{3,2,1,0:T(8,128)}, u32[]{:S(2)}) copy-start(f32[1,64,8,128]{3,2,1,0:T(8,128)} %param.4) | copy-start | bytes 786436
  4.2 1.4 %copy-start = (f32[1,64,8,128]{3,2,1,0:T(8,128)S(1)}, f32[1,64,8,128]{3,2,1,0:T(8,128)}, u32[]{:S(2)}) copy-start(f32[1,64,8,128]{3,2,1,0:T(8,128)} %param.3) | copy-start | bytes 786436
  5.9 5.9 %collective-permute-start.2 = (bf16[10,64,128]{2,1,0:T(8,128)(2,1)S(1)}, bf16[10,64,128]{2,1,0:T(8,128)(2,1)S(1)}, u32[]{:S(2)}, u32[]{:S(2)}) collective-permute-start(bf16[10,64,128]{2,1,0:T(8,128)(2,1)S(1)} %get-tuple-element.27), channel_id=1, source_target_pairs={{2,4},{4,2},{3,5},{5,3},{10,12},{12,10},{11,13},{13,11},{18,20},{2... | collective-permute-start | bytes 491528 | tf_op jit(solution)/shard_map/ppermute | solution.py:497
  6.6 5.2 %collective-permute-start.1 = (bf16[10,64,128]{2,1,0:T(8,128)(2,1)S(1)}, bf16[10,64,128]{2,1,0:T(8,128)(2,1)S(1)}, u32[]{:S(2)}, u32[]{:S(2)}) collective-permute-start(bf16[10,64,128]{2,1,0:T(8,128)(2,1)S(1)} %get-tuple-element.26), channel_id=1, source_target_pairs={{0,2},{2,0},{4,6},{6,4},{1,3},{3,1},{5,7},{7,5},{8,10},{10,8},{12,... | collective-permute-start | bytes 491528 | tf_op jit(solution)/shard_map/ppermute | solution.py:497
  11.8 3.6 %collective-permute-start.3 = (bf16[5,64,128]{2,1,0:T(8,128)(2,1)S(1)}, bf16[5,64,128]{2,1,0:T(8,128)(2,1)S(1)}, u32[]{:S(2)}, u32[]{:S(2)}) collective-permute-start(bf16[5,64,128]{2,1,0:T(8,128)(2,1)S(1)} %get-tuple-element.31), channel_id=1, source_target_pairs={{0,8},{1,9},{2,10},{3,11},{4,12},{5,13},{6,14},{7,15}} | collective-permute-start | bytes 245768 | tf_op jit(solution)/shard_map/ppermute | solution.py:604
  12.6 4.4 %collective-permute-start.4 = (bf16[4,64,128]{2,1,0:T(8,128)(2,1)S(1)}, bf16[4,64,128]{2,1,0:T(8,128)(2,1)S(1)}, u32[]{:S(2)}, u32[]{:S(2)}) collective-permute-start(bf16[4,64,128]{2,1,0:T(8,128)(2,1)S(1)} %get-tuple-element.32), channel_id=1, source_target_pairs={{0,8},{1,9},{2,10},{3,11},{4,12},{5,13},{6,14},{7,15}} | collective-permute-start | bytes 196616 | tf_op jit(solution)/shard_map/ppermute | solution.py:604
  15.7 5.2 %collective-permute-start.5 = (bf16[5,64,128]{2,1,0:T(8,128)(2,1)S(1)}, bf16[5,64,128]{2,1,0:T(8,128)(2,1)S(1)}, u32[]{:S(2)}, u32[]{:S(2)}) collective-permute-start(bf16[5,64,128]{2,1,0:T(8,128)(2,1)S(1)} %shard_map.62), channel_id=1, source_target_pairs={{8,16},{9,17},{10,18},{11,19},{12,20},{13,21},{14,22},{15,23}} | collective-permute-start | bytes 245768 | tf_op jit(solution)/shard_map/ppermute | solution.py:604
  17.2 5.2 %collective-permute-start.6 = (bf16[4,64,128]{2,1,0:T(8,128)(2,1)S(1)}, bf16[4,64,128]{2,1,0:T(8,128)(2,1)S(1)}, u32[]{:S(2)}, u32[]{:S(2)}) collective-permute-start(bf16[4,64,128]{2,1,0:T(8,128)(2,1)S(1)} %shard_map.63), channel_id=1, source_target_pairs={{8,16},{9,17},{10,18},{11,19},{12,20},{13,21},{14,22},{15,23}} | collective-permute-start | bytes 196616 | tf_op jit(solution)/shard_map/ppermute | solution.py:604
  21.1 4.1 %collective-permute-start.7 = (bf16[5,64,128]{2,1,0:T(8,128)(2,1)S(1)}, bf16[5,64,128]{2,1,0:T(8,128)(2,1)S(1)}, u32[]{:S(2)}, u32[]{:S(2)}) collective-permute-start(bf16[5,64,128]{2,1,0:T(8,128)(2,1)S(1)} %shard_map.64), channel_id=1, source_target_pairs={{16,24},{17,25},{18,26},{19,27},{20,28},{21,29},{22,30},{23,31}} | collective-permute-start | bytes 245768 | tf_op jit(solution)/shard_map/ppermute | solution.py:604
  22.6 2.6 %collective-permute-start.8 = (bf16[4,64,128]{2,1,0:T(8,128)(2,1)S(1)}, bf16[4,64,128]{2,1,0:T(8,128)(2,1)S(1)}, u32[]{:S(2)}, u32[]{:S(2)}) collective-permute-start(bf16[4,64,128]{2,1,0:T(8,128)(2,1)S(1)} %shard_map.65), channel_id=1, source_target_pairs={{16,24},{17,25},{18,26},{19,27},{20,28},{21,29},{22,30},{23,31}} | collective-permute-start | bytes 196616 | tf_op jit(solution)/shard_map/ppermute | solution.py:604
  25.3 7.1 %collective-permute-start.10 = (bf16[9,64,128]{2,1,0:T(8,128)(2,1)S(1)}, bf16[9,64,128]{2,1,0:T(8,128)(2,1)S(1)}, u32[]{:S(2)}, u32[]{:S(2)}) collective-permute-start(bf16[9,64,128]{2,1,0:T(8,128)(2,1)S(1)} %shard_map.66.s_ref), channel_id=1, source_target_pairs={{2,4},{4,2},{3,5},{5,3},{10,12},{12,10},{11,13},{13,11},{18,20},{2... | collective-permute-start | bytes 442376 | tf_op jit(solution)/shard_map/ppermute | solution.py:497
  26.2 7.2 %collective-permute-start.9 = (bf16[9,64,128]{2,1,0:T(8,128)(2,1)S(1)}, bf16[9,64,128]{2,1,0:T(8,128)(2,1)S(1)}, u32[]{:S(2)}, u32[]{:S(2)}) collective-permute-start(bf16[9,64,128]{2,1,0:T(8,128)(2,1)S(1)} %shard_map.66.s_ref), channel_id=1, source_target_pairs={{0,2},{2,0},{4,6},{6,4},{1,3},{3,1},{5,7},{7,5},{8,10},{10,8},{12,... | collective-permute-start | bytes 442376 | tf_op jit(solution)/shard_map/ppermute | solution.py:497
  39.5 7.0 %collective-permute-start.15 = (bf16[4,64,128]{2,1,0:T(8,128)(2,1)S(1)}, bf16[4,64,128]{2,1,0:T(8,128)(2,1)S(1)}, u32[]{:S(2)}, u32[]{:S(2)}) collective-permute-start(bf16[4,64,128]{2,1,0:T(8,128)(2,1)S(1)} %get-tuple-element.42), channel_id=1, source_target_pairs={{24,16},{25,17},{26,18},{27,19},{28,20},{29,21},{30,22},{31,23}} | collective-permute-start | bytes 196616 | tf_op jit(solution)/shard_map/ppermute | solution.py:604
  40.8 8.6 %collective-permute-start.16 = (bf16[4,64,128]{2,1,0:T(8,128)(2,1)S(1)}, bf16[4,64,128]{2,1,0:T(8,128)(2,1)S(1)}, u32[]{:S(2)}, u32[]{:S(2)}) collective-permute-start(bf16[4,64,128]{2,1,0:T(8,128)(2,1)S(1)} %get-tuple-element.43), channel_id=1, source_target_pairs={{24,16},{25,17},{26,18},{27,19},{28,20},{29,21},{30,22},{31,23}} | collective-permute-start | bytes 196616 | tf_op jit(solution)/shard_map/ppermute | solution.py:604
  43.2 4.8 %collective-permute-start.11 = (f32[2,64,576]{2,1,0:T(8,128)S(1)}, f32[2,64,576]{2,1,0:T(8,128)S(1)}, u32[]{:S(2)}, u32[]{:S(2)}) collective-permute-start(f32[2,64,576]{2,1,0:T(8,128)S(1)} %slice_select_fusion), channel_id=1, source_target_pairs={{0,2},{2,0},{4,6},{6,4},{1,3},{3,1},{5,7},{7,5},{8,10},{10,8},{12,... | collective-permute-start | bytes 884744 | tf_op jit(solution)/shard_map/ppermute | solution.py:515
  46.7 7.5 %collective-permute-start.17 = (bf16[4,64,128]{2,1,0:T(8,128)(2,1)S(1)}, bf16[4,64,128]{2,1,0:T(8,128)(2,1)S(1)}, u32[]{:S(2)}, u32[]{:S(2)}) collective-permute-start(bf16[4,64,128]{2,1,0:T(8,128)(2,1)S(1)} %shard_map.69), channel_id=1, source_target_pairs={{16,8},{17,9},{18,10},{19,11},{20,12},{21,13},{22,14},{23,15}} | collective-permute-start | bytes 196616 | tf_op jit(solution)/shard_map/ppermute | solution.py:604
  48.0 4.2 %collective-permute-start.12 = (bf16[2,64,576]{2,1,0:T(8,128)(2,1)S(1)}, bf16[2,64,576]{2,1,0:T(8,128)(2,1)S(1)}, u32[]{:S(2)}, u32[]{:S(2)}) collective-permute-start(bf16[2,64,576]{2,1,0:T(8,128)(2,1)S(1)} %add_convert_fusion.1), channel_id=1, source_target_pairs={{0,4},{1,5},{2,3},{3,2},{4,0},{5,1},{6,7},{7,6},{8,12},{9,13},{10,... | collective-permute-start | bytes 442376 | tf_op jit(solution)/shard_map/ppermute | solution.py:527
  49.5 11.8 %collective-permute-start.18 = (bf16[4,64,128]{2,1,0:T(8,128)(2,1)S(1)}, bf16[4,64,128]{2,1,0:T(8,128)(2,1)S(1)}, u32[]{:S(2)}, u32[]{:S(2)}) collective-permute-start(bf16[4,64,128]{2,1,0:T(8,128)(2,1)S(1)} %shard_map.70), channel_id=1, source_target_pairs={{16,8},{17,9},{18,10},{19,11},{20,12},{21,13},{22,14},{23,15}} | collective-permute-start | bytes 196616 | tf_op jit(solution)/shard_map/ppermute | solution.py:604
  52.3 4.6 %collective-permute-start.13 = (bf16[2,64,576]{2,1,0:T(8,128)(2,1)S(1)}, bf16[2,64,576]{2,1,0:T(8,128)(2,1)S(1)}, u32[]{:S(2)}, u32[]{:S(2)}) collective-permute-start(bf16[2,64,576]{2,1,0:T(8,128)(2,1)S(1)} %add_convert_fusion), channel_id=1, source_target_pairs={{0,1},{1,0},{2,6},{3,7},{4,5},{5,4},{6,2},{7,3},{8,9},{9,8},{10,14... | collective-permute-start | bytes 442376 | tf_op jit(solution)/shard_map/ppermute | solution.py:527
  54.4 7.8 %collective-permute-start.19 = (bf16[4,64,128]{2,1,0:T(8,128)(2,1)S(1)}, bf16[4,64,128]{2,1,0:T(8,128)(2,1)S(1)}, u32[]{:S(2)}, u32[]{:S(2)}) collective-permute-start(bf16[4,64,128]{2,1,0:T(8,128)(2,1)S(1)} %shard_map.71), channel_id=1, source_target_pairs={{8,0},{9,1},{10,2},{11,3},{12,4},{13,5},{14,6},{15,7}} | collective-permute-start | bytes 196616 | tf_op jit(solution)/shard_map/ppermute | solution.py:604
  56.9 5.6 %collective-permute-start.14 = (f32[2,64,576]{2,1,0:T(8,128)S(1)}, f32[2,64,576]{2,1,0:T(8,128)S(1)}, u32[]{:S(2)}, u32[]{:S(2)}) collective-permute-start(f32[2,64,576]{2,1,0:T(8,128)S(1)} %convert_add_fusion.half_ref), channel_id=1, source_target_pairs={{0,2},{2,0},{4,6},{6,4},{1,3},{3,1},{5,7},{7,5},{8,10},{10,8},{12,... | collective-permute-start | bytes 884744 | tf_op jit(solution)/shard_map/ppermute | solution.py:529
  61.5 0.7 %collective-permute-start.20 = (bf16[4,64,128]{2,1,0:T(8,128)(2,1)S(1)}, bf16[4,64,128]{2,1,0:T(8,128)(2,1)S(1)}, u32[]{:S(2)}, u32[]{:S(2)}) collective-permute-start(bf16[4,64,128]{2,1,0:T(8,128)(2,1)S(1)} %shard_map.72), channel_id=1, source_target_pairs={{8,0},{9,1},{10,2},{11,3},{12,4},{13,5},{14,6},{15,7}} | collective-permute-start | bytes 196616 | tf_op jit(solution)/shard_map/ppermute | solution.py:604

commit v12 on v11

--- a/solution.py
+++ b/solution.py
@@ -186,17 +186,7 @@
 
 
 def row_blocks(low, high, body):
-    turns = 1 if high - low <= 32 else 2
-    size, rest = divmod(high - low, turns)
-
-    def turn(number, carry):
-        body(low + size * number, size)
-        return carry
-
-    if size > 0:
-        lax.fori_loop(0, turns, turn, 0)
-    if rest > 0:
-        body(low + size * turns, rest)
+    body(low, high - low)
 
 
 def convolved_rows(weights, ref, first, count):
@@ -205,7 +195,9 @@
 
 
 def row_flag(index, halo, rows, up, down):
-    return jnp.where(index < halo, up, jnp.where(index >= halo + rows, down, 1.0))
+    if index < halo:
+        return up
+    return down if index >= halo + rows else 1.0
 
 
 def first_body(

time: 64.8 us -> 64.8 us (level)
  no operation moved by 1% of the time
where the time goes in v12:
time: 64.8 us; the launch traced here: 63.7 us
  starting transfers between devices  35.9 us (55%)
  Pallas kernels  14.3 us (22%)
  waiting for transfers between devices  9.57 us (15%)
  local copies, waits for them, and re-layouts  2.43 us (4%)
  between operations  1.19 us (2%)
    ppermute x12, starting transfers between devices, chain(): arrived = [lax.ppermute(sending, 'layer', [step]) for sending in sendings]  13 us
    ppermute x2, starting transfers between devices, exchanged(): lax.ppermute(to_pair, 'row', pairs)  9.31 us
    pallas_call x1, Pallas kernels, local(): call(functools.partial(second_body, depth=depth, **sizes), (flat_f, tile_...  6.1 us
    ppermute x1, starting transfers between devices, total_over_tiles(): return (value, lax.ppermute(value, 'row', pair))  4.35 us
    ppermute x12, waiting for transfers between devices, chain(): arrived = [lax.ppermute(sending, 'layer', [step]) for sending in sendings]  3.71 us
    ppermute x2, waiting for transfers between devices, total_over_tiles(): arrived = lax.ppermute(rounded, ('row', 'col'), pairs)  3.25 us
    ppermute x1, starting transfers between devices, total_over_tiles(): value = own + lax.ppermute(sent, 'row', pair)  3.25 us
    ppermute x2, starting transfers between devices, total_over_tiles(): arrived = lax.ppermute(rounded, ('row', 'col'), pairs)  3.19 us
  transfers between devices with their start and end apart: 21, of which 7 were waited for; matrix products, arithmetic and copies ran while one was open for 4% of the time, Pallas kernels for 8%

profile of v12, /device:TPU:19, one launch (start us, length us, event | category | flops | bytes accessed | tf_op | source)
XLA Modules:
  0.0 63.7 jit_solution(18158995246537569344)
XLA Ops:
  0.6 1.9 %shard_map.58 = bf16[64,256]{1,0:T(8,128)(2,1)} custom-call(f32[512,128]{1,0:T(8,128)} %bitcast.18, f32[512,128]{1,0:T(8,128)} %bitcast.28), custom_call_target="tpu_custom_call" | custom-call | tf_op jit(solution)/shard_map/pallas_call | solution.py:544
  2.6 1.3 %collective-permute-start = (bf16[64,256]{1,0:T(8,128)(2,1)}, bf16[64,256]{1,0:T(8,128)(2,1)S(1)}, u32[]{:S(2)}, u32[]{:S(2)}) collective-permute-start(bf16[64,256]{1,0:T(8,128)(2,1)} %shard_map.58), channel_id=1, source_target_pairs={{0,1},{1,0},{2,3},{3,2},{4,5},{5,4},{6,7},{7,6},{8,9},{9,8},{10,11... | collective-permute-start | bytes 98312 | tf_op jit(solution)/shard_map/ppermute | solution.py:494
  4.3 1.4 %collective-permute-done.left_ref.right_ref = bf16[64,256]{1,0:T(8,128)(2,1)S(1)} collective-permute-done((bf16[64,256]{1,0:T(8,128)(2,1)}, bf16[64,256]{1,0:T(8,128)(2,1)S(1)}, u32[]{:S(2)}, u32[]{:S(2)}) %collective-permute-start) | collective-permute-done | bytes 32800 | tf_op jit(solution)/shard_map/ppermute | solution.py:494
  5.9 0.7 %collective-permute-start.2 = (bf16[10,64,128]{2,1,0:T(8,128)(2,1)S(1)}, bf16[10,64,128]{2,1,0:T(8,128)(2,1)S(1)}, u32[]{:S(2)}, u32[]{:S(2)}) collective-permute-start(bf16[10,64,128]{2,1,0:T(8,128)(2,1)S(1)} %get-tuple-element.27), channel_id=1, source_target_pairs={{2,4},{4,2},{3,5},{5,3},{10,12},{12,10},{11,13},{13,11},{18,20},{2... | collective-permute-start | bytes 491528 | tf_op jit(solution)/shard_map/ppermute | solution.py:489
  6.6 3.1 %collective-permute-start.1 = (bf16[10,64,128]{2,1,0:T(8,128)(2,1)S(1)}, bf16[10,64,128]{2,1,0:T(8,128)(2,1)S(1)}, u32[]{:S(2)}, u32[]{:S(2)}) collective-permute-start(bf16[10,64,128]{2,1,0:T(8,128)(2,1)S(1)} %get-tuple-element.26), channel_id=1, source_target_pairs={{0,2},{2,0},{4,6},{6,4},{1,3},{3,1},{5,7},{7,5},{8,10},{10,8},{12,... | collective-permute-start | bytes 491528 | tf_op jit(solution)/shard_map/ppermute | solution.py:489
  11.8 0.7 %collective-permute-start.3 = (bf16[5,64,128]{2,1,0:T(8,128)(2,1)S(1)}, bf16[5,64,128]{2,1,0:T(8,128)(2,1)S(1)}, u32[]{:S(2)}, u32[]{:S(2)}) collective-permute-start(bf16[5,64,128]{2,1,0:T(8,128)(2,1)S(1)} %get-tuple-element.31), channel_id=1, source_target_pairs={{0,8},{1,9},{2,10},{3,11},{4,12},{5,13},{6,14},{7,15}} | collective-permute-start | bytes 245768 | tf_op jit(solution)/shard_map/ppermute | solution.py:596
  12.6 0.7 %collective-permute-start.4 = (bf16[4,64,128]{2,1,0:T(8,128)(2,1)S(1)}, bf16[4,64,128]{2,1,0:T(8,128)(2,1)S(1)}, u32[]{:S(2)}, u32[]{:S(2)}) collective-permute-start(bf16[4,64,128]{2,1,0:T(8,128)(2,1)S(1)} %get-tuple-element.32), channel_id=1, source_target_pairs={{0,8},{1,9},{2,10},{3,11},{4,12},{5,13},{6,14},{7,15}} | collective-permute-start | bytes 196616 | tf_op jit(solution)/shard_map/ppermute | solution.py:596
  13.3 2.2 %shard_map.61.refs_1_.refs_0_ = f32[9,64,128]{2,1,0:T(8,128)S(1)} custom-call(f32[512,128]{1,0:T(8,128)S(1)} %bitcast.21, bf16[10,64,128]{2,1,0:T(8,128)(2,1)S(1)} %collective-permute-done.1.pair_ref, bf16[10,64,128]{2,1,0:T(8,128)(2,1)S(1)} %collective-permute-done.2.cross_ref, bf16[64,256]{1,0:T(8,128)(2,1)S(1)} %get-tuple-element.36.side_ref, ...), custom_call_target="tpu_custom_call" | custom-call | flops 830472192 | tf_op jit(solution)/shard_map/pallas_call | solution.py:581
  15.7 1.3 %collective-permute-start.5 = (bf16[5,64,128]{2,1,0:T(8,128)(2,1)S(1)}, bf16[5,64,128]{2,1,0:T(8,128)(2,1)S(1)}, u32[]{:S(2)}, u32[]{:S(2)}) collective-permute-start(bf16[5,64,128]{2,1,0:T(8,128)(2,1)S(1)} %shard_map.62), channel_id=1, source_target_pairs={{8,16},{9,17},{10,18},{11,19},{12,20},{13,21},{14,22},{15,23}} | collective-permute-start | bytes 245768 | tf_op jit(solution)/shard_map/ppermute | solution.py:596
  17.2 1.3 %collective-permute-start.6 = (bf16[4,64,128]{2,1,0:T(8,128)(2,1)S(1)}, bf16[4,64,128]{2,1,0:T(8,128)(2,1)S(1)}, u32[]{:S(2)}, u32[]{:S(2)}) collective-permute-start(bf16[4,64,128]{2,1,0:T(8,128)(2,1)S(1)} %shard_map.63), channel_id=1, source_target_pairs={{8,16},{9,17},{10,18},{11,19},{12,20},{13,21},{14,22},{15,23}} | collective-permute-start | bytes 196616 | tf_op jit(solution)/shard_map/ppermute | solution.py:596
  18.5 2.4 %collective-permute-done.5.s_ref.refs_2_ = bf16[5,64,128]{2,1,0:T(8,128)(2,1)S(1)} collective-permute-done((bf16[5,64,128]{2,1,0:T(8,128)(2,1)S(1)}, bf16[5,64,128]{2,1,0:T(8,128)(2,1)S(1)}, u32[]{:S(2)}, u32[]{:S(2)}) %collective-permute-start.5) | collective-permute-done | bytes 81952 | tf_op jit(solution)/shard_map/ppermute | solution.py:596
  21.1 1.3 %collective-permute-start.7 = (bf16[5,64,128]{2,1,0:T(8,128)(2,1)S(1)}, bf16[5,64,128]{2,1,0:T(8,128)(2,1)S(1)}, u32[]{:S(2)}, u32[]{:S(2)}) collective-permute-start(bf16[5,64,128]{2,1,0:T(8,128)(2,1)S(1)} %shard_map.64), channel_id=1, source_target_pairs={{16,24},{17,25},{18,26},{19,27},{20,28},{21,29},{22,30},{23,31}} | collective-permute-start | bytes 245768 | tf_op jit(solution)/shard_map/ppermute | solution.py:596
  22.6 1.3 %collective-permute-start.8 = (bf16[4,64,128]{2,1,0:T(8,128)(2,1)S(1)}, bf16[4,64,128]{2,1,0:T(8,128)(2,1)S(1)}, u32[]{:S(2)}, u32[]{:S(2)}) collective-permute-start(bf16[4,64,128]{2,1,0:T(8,128)(2,1)S(1)} %shard_map.65), channel_id=1, source_target_pairs={{16,24},{17,25},{18,26},{19,27},{20,28},{21,29},{22,30},{23,31}} | collective-permute-start | bytes 196616 | tf_op jit(solution)/shard_map/ppermute | solution.py:596
  23.9 1.3 %collective-permute-done.8.refs_5_ = bf16[4,64,128]{2,1,0:T(8,128)(2,1)S(1)} collective-permute-done((bf16[4,64,128]{2,1,0:T(8,128)(2,1)S(1)}, bf16[4,64,128]{2,1,0:T(8,128)(2,1)S(1)}, u32[]{:S(2)}, u32[]{:S(2)}) %collective-permute-start.8) | collective-permute-done | bytes 65568 | tf_op jit(solution)/shard_map/ppermute | solution.py:596
  25.3 0.9 %collective-permute-start.10 = (bf16[9,64,128]{2,1,0:T(8,128)(2,1)S(1)}, bf16[9,64,128]{2,1,0:T(8,128)(2,1)S(1)}, u32[]{:S(2)}, u32[]{:S(2)}) collective-permute-start(bf16[9,64,128]{2,1,0:T(8,128)(2,1)S(1)} %shard_map.66.s_ref), channel_id=1, source_target_pairs={{2,4},{4,2},{3,5},{5,3},{10,12},{12,10},{11,13},{13,11},{18,20},{2... | collective-permute-start | bytes 442376 | tf_op jit(solution)/shard_map/ppermute | solution.py:489
  26.2 6.2 %collective-permute-start.9 = (bf16[9,64,128]{2,1,0:T(8,128)(2,1)S(1)}, bf16[9,64,128]{2,1,0:T(8,128)(2,1)S(1)}, u32[]{:S(2)}, u32[]{:S(2)}) collective-permute-start(bf16[9,64,128]{2,1,0:T(8,128)(2,1)S(1)} %shard_map.66.s_ref), channel_id=1, source_target_pairs={{0,2},{2,0},{4,6},{6,4},{1,3},{3,1},{5,7},{7,5},{8,10},{10,8},{12,... | collective-permute-start | bytes 442376 | tf_op jit(solution)/shard_map/ppermute | solution.py:489
  32.5 0.9 %collective-permute-done.9.s_pair_ref = bf16[9,64,128]{2,1,0:T(8,128)(2,1)S(1)} collective-permute-done((bf16[9,64,128]{2,1,0:T(8,128)(2,1)S(1)}, bf16[9,64,128]{2,1,0:T(8,128)(2,1)S(1)}, u32[]{:S(2)}, u32[]{:S(2)}) %collective-permute-start.9) | collective-permute-done | bytes 147488 | tf_op jit(solution)/shard_map/ppermute | solution.py:489
  33.3 6.1 %shard_map.67 = (f32[512,128]{1,0:T(8,128)}, f32[8,64,128]{2,1,0:T(8,128)S(1)}, bf16[4,64,128]{2,1,0:T(8,128)(2,1)S(1)}, bf16[4,64,128]{2,1,0:T(8,128)(2,1)S(1)}...) custom-call(f32[512,128]{1,0:T(8,128)S(1)} %bitcast.27, f32[512,128]{1,0:T(8,128)S(1)} %bitcast.30, ...), custom_call_target="tpu_custom_call" | custom-call | flops 2264924160 | tf_op jit(solution)/shard_map/pallas_call | solution.py:623
  39.5 1.3 %collective-permute-start.15 = (bf16[4,64,128]{2,1,0:T(8,128)(2,1)S(1)}, bf16[4,64,128]{2,1,0:T(8,128)(2,1)S(1)}, u32[]{:S(2)}, u32[]{:S(2)}) collective-permute-start(bf16[4,64,128]{2,1,0:T(8,128)(2,1)S(1)} %get-tuple-element.42), channel_id=1, source_target_pairs={{24,16},{25,17},{26,18},{27,19},{28,20},{29,21},{30,22},{31,23}} | collective-permute-start | bytes 196616 | tf_op jit(solution)/shard_map/ppermute | solution.py:596
  40.8 1.3 %collective-permute-start.16 = (bf16[4,64,128]{2,1,0:T(8,128)(2,1)S(1)}, bf16[4,64,128]{2,1,0:T(8,128)(2,1)S(1)}, u32[]{:S(2)}, u32[]{:S(2)}) collective-permute-start(bf16[4,64,128]{2,1,0:T(8,128)(2,1)S(1)} %get-tuple-element.43), channel_id=1, source_target_pairs={{24,16},{25,17},{26,18},{27,19},{28,20},{29,21},{30,22},{31,23}} | collective-permute-start | bytes 196616 | tf_op jit(solution)/shard_map/ppermute | solution.py:596
  42.1 1.1 %shard_map.68 = f32[4,64,576]{2,1,0:T(8,128)S(1)} custom-call(bf16[4,8,64,256]{3,2,1,0:T(8,128)(2,1)S(1)} %get-tuple-element.40.kept_ref, bf16[4,10,64,128]{3,2,1,0:T(8,128)(2,1)S(1)} %get-tuple-element.41.sent_ref), custom_call_target="tpu_custom_call" | custom-call | flops 1000000000 | tf_op jit(solution)/shard_map/pallas_call | solution.py:652
  43.2 3.2 %collective-permute-start.11 = (f32[2,64,576]{2,1,0:T(8,128)S(1)}, f32[2,64,576]{2,1,0:T(8,128)S(1)}, u32[]{:S(2)}, u32[]{:S(2)}) collective-permute-start(f32[2,64,576]{2,1,0:T(8,128)S(1)} %slice_select_fusion), channel_id=1, source_target_pairs={{0,2},{2,0},{4,6},{6,4},{1,3},{3,1},{5,7},{7,5},{8,10},{10,8},{12,... | collective-permute-start | bytes 884744 | tf_op jit(solution)/shard_map/ppermute | solution.py:507
  46.7 1.3 %collective-permute-start.17 = (bf16[4,64,128]{2,1,0:T(8,128)(2,1)S(1)}, bf16[4,64,128]{2,1,0:T(8,128)(2,1)S(1)}, u32[]{:S(2)}, u32[]{:S(2)}) collective-permute-start(bf16[4,64,128]{2,1,0:T(8,128)(2,1)S(1)} %shard_map.69), channel_id=1, source_target_pairs={{16,8},{17,9},{18,10},{19,11},{20,12},{21,13},{22,14},{23,15}} | collective-permute-start | bytes 196616 | tf_op jit(solution)/shard_map/ppermute | solution.py:596
  48.0 1.3 %collective-permute-start.12 = (bf16[2,64,576]{2,1,0:T(8,128)(2,1)S(1)}, bf16[2,64,576]{2,1,0:T(8,128)(2,1)S(1)}, u32[]{:S(2)}, u32[]{:S(2)}) collective-permute-start(bf16[2,64,576]{2,1,0:T(8,128)(2,1)S(1)} %add_convert_fusion.1), channel_id=1, source_target_pairs={{0,4},{1,5},{2,3},{3,2},{4,0},{5,1},{6,7},{7,6},{8,12},{9,13},{10,... | collective-permute-start | bytes 442376 | tf_op jit(solution)/shard_map/ppermute | solution.py:519
  49.5 1.3 %collective-permute-start.18 = (bf16[4,64,128]{2,1,0:T(8,128)(2,1)S(1)}, bf16[4,64,128]{2,1,0:T(8,128)(2,1)S(1)}, u32[]{:S(2)}, u32[]{:S(2)}) collective-permute-start(bf16[4,64,128]{2,1,0:T(8,128)(2,1)S(1)} %shard_map.70), channel_id=1, source_target_pairs={{16,8},{17,9},{18,10},{19,11},{20,12},{21,13},{22,14},{23,15}} | collective-permute-start | bytes 196616 | tf_op jit(solution)/shard_map/ppermute | solution.py:596
  50.8 1.4 %collective-permute-done.12 = bf16[2,64,576]{2,1,0:T(8,128)(2,1)S(1)} collective-permute-done((bf16[2,64,576]{2,1,0:T(8,128)(2,1)S(1)}, bf16[2,64,576]{2,1,0:T(8,128)(2,1)S(1)}, u32[]{:S(2)}, u32[]{:S(2)}) %collective-permute-start.12) | collective-permute-done | bytes 147488 | tf_op jit(solution)/shard_map/ppermute | solution.py:519
  52.3 1.9 %collective-permute-start.13 = (bf16[2,64,576]{2,1,0:T(8,128)(2,1)S(1)}, bf16[2,64,576]{2,1,0:T(8,128)(2,1)S(1)}, u32[]{:S(2)}, u32[]{:S(2)}) collective-permute-start(bf16[2,64,576]{2,1,0:T(8,128)(2,1)S(1)} %add_convert_fusion), channel_id=1, source_target_pairs={{0,1},{1,0},{2,6},{3,7},{4,5},{5,4},{6,2},{7,3},{8,9},{9,8},{10,14... | collective-permute-start | bytes 442376 | tf_op jit(solution)/shard_map/ppermute | solution.py:519
  54.4 0.7 %collective-permute-start.19 = (bf16[4,64,128]{2,1,0:T(8,128)(2,1)S(1)}, bf16[4,64,128]{2,1,0:T(8,128)(2,1)S(1)}, u32[]{:S(2)}, u32[]{:S(2)}) collective-permute-start(bf16[4,64,128]{2,1,0:T(8,128)(2,1)S(1)} %shard_map.71), channel_id=1, source_target_pairs={{8,0},{9,1},{10,2},{11,3},{12,4},{13,5},{14,6},{15,7}} | collective-permute-start | bytes 196616 | tf_op jit(solution)/shard_map/ppermute | solution.py:596
  55.1 1.8 %collective-permute-done.13 = bf16[2,64,576]{2,1,0:T(8,128)(2,1)S(1)} collective-permute-done((bf16[2,64,576]{2,1,0:T(8,128)(2,1)S(1)}, bf16[2,64,576]{2,1,0:T(8,128)(2,1)S(1)}, u32[]{:S(2)}, u32[]{:S(2)}) %collective-permute-start.13) | collective-permute-done | bytes 147488 | tf_op jit(solution)/shard_map/ppermute | solution.py:519
  56.9 4.4 %collective-permute-start.14 = (f32[2,64,576]{2,1,0:T(8,128)S(1)}, f32[2,64,576]{2,1,0:T(8,128)S(1)}, u32[]{:S(2)}, u32[]{:S(2)}) collective-permute-start(f32[2,64,576]{2,1,0:T(8,128)S(1)} %convert_add_fusion.half_ref), channel_id=1, source_target_pairs={{0,2},{2,0},{4,6},{6,4},{1,3},{3,1},{5,7},{7,5},{8,10},{10,8},{12,... | collective-permute-start | bytes 884744 | tf_op jit(solution)/shard_map/ppermute | solution.py:521
  61.5 0.7 %collective-permute-start.20 = (bf16[4,64,128]{2,1,0:T(8,128)(2,1)S(1)}, bf16[4,64,128]{2,1,0:T(8,128)(2,1)S(1)}, u32[]{:S(2)}, u32[]{:S(2)}) collective-permute-start(bf16[4,64,128]{2,1,0:T(8,128)(2,1)S(1)} %shard_map.72), channel_id=1, source_target_pairs={{8,0},{9,1},{10,2},{11,3},{12,4},{13,5},{14,6},{15,7}} | collective-permute-start | bytes 196616 | tf_op jit(solution)/shard_map/ppermute | solution.py:596
  62.5 1.0 %shard_map.73 = (f32[512,128]{1,0:T(8,128)}, f32[4,64,576]{2,1,0:T(8,128)}) custom-call(f32[512,128]{1,0:T(8,128)S(1)} %bitcast.35, f32[2,64,576]{2,1,0:T(8,128)S(1)} %convert_add_fusion.half_ref, f32[2,64,576]{2,1,0:T(8,128)S(1)} %collective-permute-done.14.other_ref, bf16[4,64,128]{2,1,0:T(8,128)(2,1)S(1)} %collective-permute-done.15.s_ref.refs_0_, ...), custom_call_target="tpu_custom_call" | custom-call | flops 10000000000 | tf_op jit(solution)/shard_map/pallas_call | solution.py:658
  (49 shorter events, 5.1 us)
Async XLA Ops:
  0.6 3.3 %copy-start.2 = (bf16[4,64,576]{2,1,0:T(8,128)(2,1)S(1)}, bf16[4,64,576]{2,1,0:T(8,128)(2,1)}, u32[]{:S(2)}) copy-start(bf16[4,64,576]{2,1,0:T(8,128)(2,1)} %param.5) | copy-start | bytes 884740
  2.6 3.0 %collective-permute-start = (bf16[64,256]{1,0:T(8,128)(2,1)}, bf16[64,256]{1,0:T(8,128)(2,1)S(1)}, u32[]{:S(2)}, u32[]{:S(2)}) collective-permute-start(bf16[64,256]{1,0:T(8,128)(2,1)} %shard_map.58), channel_id=1, source_target_pairs={{0,1},{1,0},{2,3},{3,2},{4,5},{5,4},{6,7},{7,6},{8,9},{9,8},{10,11... | collective-permute-start | bytes 98312 | tf_op jit(solution)/shard_map/ppermute | solution.py:494
  3.9 1.7 %copy-start.1 = (f32[1,64,8,128]{3,2,1,0:T(8,128)S(1)}, f32[1,64,8,128]{3,2,1,0:T(8,128)}, u32[]{:S(2)}) copy-start(f32[1,64,8,128]{3,2,1,0:T(8,128)} %param.4) | copy-start | bytes 786436
  4.2 1.4 %copy-start = (f32[1,64,8,128]{3,2,1,0:T(8,128)S(1)}, f32[1,64,8,128]{3,2,1,0:T(8,128)}, u32[]{:S(2)}) copy-start(f32[1,64,8,128]{3,2,1,0:T(8,128)} %param.3) | copy-start | bytes 786436
  5.9 5.9 %collective-permute-start.2 = (bf16[10,64,128]{2,1,0:T(8,128)(2,1)S(1)}, bf16[10,64,128]{2,1,0:T(8,128)(2,1)S(1)}, u32[]{:S(2)}, u32[]{:S(2)}) collective-permute-start(bf16[10,64,128]{2,1,0:T(8,128)(2,1)S(1)} %get-tuple-element.27), channel_id=1, source_target_pairs={{2,4},{4,2},{3,5},{5,3},{10,12},{12,10},{11,13},{13,11},{18,20},{2... | collective-permute-start | bytes 491528 | tf_op jit(solution)/shard_map/ppermute | solution.py:489
  6.6 5.2 %collective-permute-start.1 = (bf16[10,64,128]{2,1,0:T(8,128)(2,1)S(1)}, bf16[10,64,128]{2,1,0:T(8,128)(2,1)S(1)}, u32[]{:S(2)}, u32[]{:S(2)}) collective-permute-start(bf16[10,64,128]{2,1,0:T(8,128)(2,1)S(1)} %get-tuple-element.26), channel_id=1, source_target_pairs={{0,2},{2,0},{4,6},{6,4},{1,3},{3,1},{5,7},{7,5},{8,10},{10,8},{12,... | collective-permute-start | bytes 491528 | tf_op jit(solution)/shard_map/ppermute | solution.py:489
  11.8 3.6 %collective-permute-start.3 = (bf16[5,64,128]{2,1,0:T(8,128)(2,1)S(1)}, bf16[5,64,128]{2,1,0:T(8,128)(2,1)S(1)}, u32[]{:S(2)}, u32[]{:S(2)}) collective-permute-start(bf16[5,64,128]{2,1,0:T(8,128)(2,1)S(1)} %get-tuple-element.31), channel_id=1, source_target_pairs={{0,8},{1,9},{2,10},{3,11},{4,12},{5,13},{6,14},{7,15}} | collective-permute-start | bytes 245768 | tf_op jit(solution)/shard_map/ppermute | solution.py:596
  12.6 4.4 %collective-permute-start.4 = (bf16[4,64,128]{2,1,0:T(8,128)(2,1)S(1)}, bf16[4,64,128]{2,1,0:T(8,128)(2,1)S(1)}, u32[]{:S(2)}, u32[]{:S(2)}) collective-permute-start(bf16[4,64,128]{2,1,0:T(8,128)(2,1)S(1)} %get-tuple-element.32), channel_id=1, source_target_pairs={{0,8},{1,9},{2,10},{3,11},{4,12},{5,13},{6,14},{7,15}} | collective-permute-start | bytes 196616 | tf_op jit(solution)/shard_map/ppermute | solution.py:596
  15.7 5.2 %collective-permute-start.5 = (bf16[5,64,128]{2,1,0:T(8,128)(2,1)S(1)}, bf16[5,64,128]{2,1,0:T(8,128)(2,1)S(1)}, u32[]{:S(2)}, u32[]{:S(2)}) collective-permute-start(bf16[5,64,128]{2,1,0:T(8,128)(2,1)S(1)} %shard_map.62), channel_id=1, source_target_pairs={{8,16},{9,17},{10,18},{11,19},{12,20},{13,21},{14,22},{15,23}} | collective-permute-start | bytes 245768 | tf_op jit(solution)/shard_map/ppermute | solution.py:596
  17.2 5.2 %collective-permute-start.6 = (bf16[4,64,128]{2,1,0:T(8,128)(2,1)S(1)}, bf16[4,64,128]{2,1,0:T(8,128)(2,1)S(1)}, u32[]{:S(2)}, u32[]{:S(2)}) collective-permute-start(bf16[4,64,128]{2,1,0:T(8,128)(2,1)S(1)} %shard_map.63), channel_id=1, source_target_pairs={{8,16},{9,17},{10,18},{11,19},{12,20},{13,21},{14,22},{15,23}} | collective-permute-start | bytes 196616 | tf_op jit(solution)/shard_map/ppermute | solution.py:596
  21.1 4.1 %collective-permute-start.7 = (bf16[5,64,128]{2,1,0:T(8,128)(2,1)S(1)}, bf16[5,64,128]{2,1,0:T(8,128)(2,1)S(1)}, u32[]{:S(2)}, u32[]{:S(2)}) collective-permute-start(bf16[5,64,128]{2,1,0:T(8,128)(2,1)S(1)} %shard_map.64), channel_id=1, source_target_pairs={{16,24},{17,25},{18,26},{19,27},{20,28},{21,29},{22,30},{23,31}} | collective-permute-start | bytes 245768 | tf_op jit(solution)/shard_map/ppermute | solution.py:596
  22.6 2.6 %collective-permute-start.8 = (bf16[4,64,128]{2,1,0:T(8,128)(2,1)S(1)}, bf16[4,64,128]{2,1,0:T(8,128)(2,1)S(1)}, u32[]{:S(2)}, u32[]{:S(2)}) collective-permute-start(bf16[4,64,128]{2,1,0:T(8,128)(2,1)S(1)} %shard_map.65), channel_id=1, source_target_pairs={{16,24},{17,25},{18,26},{19,27},{20,28},{21,29},{22,30},{23,31}} | collective-permute-start | bytes 196616 | tf_op jit(solution)/shard_map/ppermute | solution.py:596
  25.3 7.1 %collective-permute-start.10 = (bf16[9,64,128]{2,1,0:T(8,128)(2,1)S(1)}, bf16[9,64,128]{2,1,0:T(8,128)(2,1)S(1)}, u32[]{:S(2)}, u32[]{:S(2)}) collective-permute-start(bf16[9,64,128]{2,1,0:T(8,128)(2,1)S(1)} %shard_map.66.s_ref), channel_id=1, source_target_pairs={{2,4},{4,2},{3,5},{5,3},{10,12},{12,10},{11,13},{13,11},{18,20},{2... | collective-permute-start | bytes 442376 | tf_op jit(solution)/shard_map/ppermute | solution.py:489
  26.2 7.2 %collective-permute-start.9 = (bf16[9,64,128]{2,1,0:T(8,128)(2,1)S(1)}, bf16[9,64,128]{2,1,0:T(8,128)(2,1)S(1)}, u32[]{:S(2)}, u32[]{:S(2)}) collective-permute-start(bf16[9,64,128]{2,1,0:T(8,128)(2,1)S(1)} %shard_map.66.s_ref), channel_id=1, source_target_pairs={{0,2},{2,0},{4,6},{6,4},{1,3},{3,1},{5,7},{7,5},{8,10},{10,8},{12,... | collective-permute-start | bytes 442376 | tf_op jit(solution)/shard_map/ppermute | solution.py:489
  39.5 7.0 %collective-permute-start.15 = (bf16[4,64,128]{2,1,0:T(8,128)(2,1)S(1)}, bf16[4,64,128]{2,1,0:T(8,128)(2,1)S(1)}, u32[]{:S(2)}, u32[]{:S(2)}) collective-permute-start(bf16[4,64,128]{2,1,0:T(8,128)(2,1)S(1)} %get-tuple-element.42), channel_id=1, source_target_pairs={{24,16},{25,17},{26,18},{27,19},{28,20},{29,21},{30,22},{31,23}} | collective-permute-start | bytes 196616 | tf_op jit(solution)/shard_map/ppermute | solution.py:596
  40.8 8.6 %collective-permute-start.16 = (bf16[4,64,128]{2,1,0:T(8,128)(2,1)S(1)}, bf16[4,64,128]{2,1,0:T(8,128)(2,1)S(1)}, u32[]{:S(2)}, u32[]{:S(2)}) collective-permute-start(bf16[4,64,128]{2,1,0:T(8,128)(2,1)S(1)} %get-tuple-element.43), channel_id=1, source_target_pairs={{24,16},{25,17},{26,18},{27,19},{28,20},{29,21},{30,22},{31,23}} | collective-permute-start | bytes 196616 | tf_op jit(solution)/shard_map/ppermute | solution.py:596
  43.2 4.8 %collective-permute-start.11 = (f32[2,64,576]{2,1,0:T(8,128)S(1)}, f32[2,64,576]{2,1,0:T(8,128)S(1)}, u32[]{:S(2)}, u32[]{:S(2)}) collective-permute-start(f32[2,64,576]{2,1,0:T(8,128)S(1)} %slice_select_fusion), channel_id=1, source_target_pairs={{0,2},{2,0},{4,6},{6,4},{1,3},{3,1},{5,7},{7,5},{8,10},{10,8},{12,... | collective-permute-start | bytes 884744 | tf_op jit(solution)/shard_map/ppermute | solution.py:507
  46.7 7.5 %collective-permute-start.17 = (bf16[4,64,128]{2,1,0:T(8,128)(2,1)S(1)}, bf16[4,64,128]{2,1,0:T(8,128)(2,1)S(1)}, u32[]{:S(2)}, u32[]{:S(2)}) collective-permute-start(bf16[4,64,128]{2,1,0:T(8,128)(2,1)S(1)} %shard_map.69), channel_id=1, source_target_pairs={{16,8},{17,9},{18,10},{19,11},{20,12},{21,13},{22,14},{23,15}} | collective-permute-start | bytes 196616 | tf_op jit(solution)/shard_map/ppermute | solution.py:596
  48.0 4.2 %collective-permute-start.12 = (bf16[2,64,576]{2,1,0:T(8,128)(2,1)S(1)}, bf16[2,64,576]{2,1,0:T(8,128)(2,1)S(1)}, u32[]{:S(2)}, u32[]{:S(2)}) collective-permute-start(bf16[2,64,576]{2,1,0:T(8,128)(2,1)S(1)} %add_convert_fusion.1), channel_id=1, source_target_pairs={{0,4},{1,5},{2,3},{3,2},{4,0},{5,1},{6,7},{7,6},{8,12},{9,13},{10,... | collective-permute-start | bytes 442376 | tf_op jit(solution)/shard_map/ppermute | solution.py:519
  49.5 11.8 %collective-permute-start.18 = (bf16[4,64,128]{2,1,0:T(8,128)(2,1)S(1)}, bf16[4,64,128]{2,1,0:T(8,128)(2,1)S(1)}, u32[]{:S(2)}, u32[]{:S(2)}) collective-permute-start(bf16[4,64,128]{2,1,0:T(8,128)(2,1)S(1)} %shard_map.70), channel_id=1, source_target_pairs={{16,8},{17,9},{18,10},{19,11},{20,12},{21,13},{22,14},{23,15}} | collective-permute-start | bytes 196616 | tf_op jit(solution)/shard_map/ppermute | solution.py:596
  52.3 4.6 %collective-permute-start.13 = (bf16[2,64,576]{2,1,0:T(8,128)(2,1)S(1)}, bf16[2,64,576]{2,1,0:T(8,128)(2,1)S(1)}, u32[]{:S(2)}, u32[]{:S(2)}) collective-permute-start(bf16[2,64,576]{2,1,0:T(8,128)(2,1)S(1)} %add_convert_fusion), channel_id=1, source_target_pairs={{0,1},{1,0},{2,6},{3,7},{4,5},{5,4},{6,2},{7,3},{8,9},{9,8},{10,14... | collective-permute-start | bytes 442376 | tf_op jit(solution)/shard_map/ppermute | solution.py:519
  54.4 7.8 %collective-permute-start.19 = (bf16[4,64,128]{2,1,0:T(8,128)(2,1)S(1)}, bf16[4,64,128]{2,1,0:T(8,128)(2,1)S(1)}, u32[]{:S(2)}, u32[]{:S(2)}) collective-permute-start(bf16[4,64,128]{2,1,0:T(8,128)(2,1)S(1)} %shard_map.71), channel_id=1, source_target_pairs={{8,0},{9,1},{10,2},{11,3},{12,4},{13,5},{14,6},{15,7}} | collective-permute-start | bytes 196616 | tf_op jit(solution)/shard_map/ppermute | solution.py:596
  56.9 5.6 %collective-permute-start.14 = (f32[2,64,576]{2,1,0:T(8,128)S(1)}, f32[2,64,576]{2,1,0:T(8,128)S(1)}, u32[]{:S(2)}, u32[]{:S(2)}) collective-permute-start(f32[2,64,576]{2,1,0:T(8,128)S(1)} %convert_add_fusion.half_ref), channel_id=1, source_target_pairs={{0,2},{2,0},{4,6},{6,4},{1,3},{3,1},{5,7},{7,5},{8,10},{10,8},{12,... | collective-permute-start | bytes 884744 | tf_op jit(solution)/shard_map/ppermute | solution.py:521
  61.5 0.7 %collective-permute-start.20 = (bf16[4,64,128]{2,1,0:T(8,128)(2,1)S(1)}, bf16[4,64,128]{2,1,0:T(8,128)(2,1)S(1)}, u32[]{:S(2)}, u32[]{:S(2)}) collective-permute-start(bf16[4,64,128]{2,1,0:T(8,128)(2,1)S(1)} %shard_map.72), channel_id=1, source_target_pairs={{8,0},{9,1},{10,2},{11,3},{12,4},{13,5},{14,6},{15,7}} | collective-permute-start | bytes 196616 | tf_op jit(solution)/shard_map/ppermute | solution.py:596

commit v13 on v12

--- a/solution.py
+++ b/solution.py
@@ -508,7 +508,7 @@
 
     flips = [(1 << bit, 0) for bit in range(1, rows.bit_length() - 1)]
     flips += [(0, 1 << bit) for bit in range(cols.bit_length() - 1)]
-    for even, uneven in zip(flips, flips[::-1]):
+    for even, uneven in zip(flips[::-1], flips):
         pairs = []
         for r in range(rows):
             row_by, col_by = uneven if r % 2 else even

time: 64.8 us -> 64.2 us (level); the launches traced: 63.7 us -> 63.9 us
  no operation moved by 1% of the time
where the time goes in v13:
time: 64.2 us; the launch traced here: 63.9 us
  starting transfers between devices  35.9 us (56%)
  Pallas kernels  14.3 us (22%)
  waiting for transfers between devices  9.77 us (15%)
  local copies, waits for them, and re-layouts  2.43 us (4%)
  between operations  1.19 us (2%)
    ppermute x12, starting transfers between devices, chain(): arrived = [lax.ppermute(sending, 'layer', [step]) for sending in sendings]  13 us
    ppermute x2, starting transfers between devices, exchanged(): lax.ppermute(to_pair, 'row', pairs)  9.31 us
    pallas_call x1, Pallas kernels, local(): call(functools.partial(second_body, depth=depth, **sizes), (flat_f, tile_...  6.1 us
    ppermute x1, starting transfers between devices, total_over_tiles(): return (value, lax.ppermute(value, 'row', pair))  4.58 us
    ppermute x12, waiting for transfers between devices, chain(): arrived = [lax.ppermute(sending, 'layer', [step]) for sending in sendings]  3.71 us
    ppermute x2, waiting for transfers between devices, total_over_tiles(): arrived = lax.ppermute(rounded, ('row', 'col'), pairs)  3.45 us
    ppermute x1, starting transfers between devices, total_over_tiles(): value = own + lax.ppermute(sent, 'row', pair)  3.25 us
    ppermute x2, starting transfers between devices, total_over_tiles(): arrived = lax.ppermute(rounded, ('row', 'col'), pairs)  2.91 us
  transfers between devices with their start and end apart: 21, of which 7 were waited for; matrix products, arithmetic and copies ran while one was open for 4% of the time, Pallas kernels for 8%

profile of v13, /device:TPU:19, one launch (start us, length us, event | category | flops | bytes accessed | tf_op | source)
XLA Modules:
  0.0 63.9 jit_solution(13075771094191133195)
XLA Ops:
  0.6 1.9 %shard_map.58 = bf16[64,256]{1,0:T(8,128)(2,1)} custom-call(f32[512,128]{1,0:T(8,128)} %bitcast.18, f32[512,128]{1,0:T(8,128)} %bitcast.28), custom_call_target="tpu_custom_call" | custom-call | tf_op jit(solution)/shard_map/pallas_call | solution.py:544
  2.6 1.3 %collective-permute-start = (bf16[64,256]{1,0:T(8,128)(2,1)}, bf16[64,256]{1,0:T(8,128)(2,1)S(1)}, u32[]{:S(2)}, u32[]{:S(2)}) collective-permute-start(bf16[64,256]{1,0:T(8,128)(2,1)} %shard_map.58), channel_id=1, source_target_pairs={{0,1},{1,0},{2,3},{3,2},{4,5},{5,4},{6,7},{7,6},{8,9},{9,8},{10,11... | collective-permute-start | bytes 98312 | tf_op jit(solution)/shard_map/ppermute | solution.py:494
  4.3 1.4 %collective-permute-done.left_ref.right_ref = bf16[64,256]{1,0:T(8,128)(2,1)S(1)} collective-permute-done((bf16[64,256]{1,0:T(8,128)(2,1)}, bf16[64,256]{1,0:T(8,128)(2,1)S(1)}, u32[]{:S(2)}, u32[]{:S(2)}) %collective-permute-start) | collective-permute-done | bytes 32800 | tf_op jit(solution)/shard_map/ppermute | solution.py:494
  5.9 0.7 %collective-permute-start.2 = (bf16[10,64,128]{2,1,0:T(8,128)(2,1)S(1)}, bf16[10,64,128]{2,1,0:T(8,128)(2,1)S(1)}, u32[]{:S(2)}, u32[]{:S(2)}) collective-permute-start(bf16[10,64,128]{2,1,0:T(8,128)(2,1)S(1)} %get-tuple-element.27), channel_id=1, source_target_pairs={{2,4},{4,2},{3,5},{5,3},{10,12},{12,10},{11,13},{13,11},{18,20},{2... | collective-permute-start | bytes 491528 | tf_op jit(solution)/shard_map/ppermute | solution.py:489
  6.6 3.1 %collective-permute-start.1 = (bf16[10,64,128]{2,1,0:T(8,128)(2,1)S(1)}, bf16[10,64,128]{2,1,0:T(8,128)(2,1)S(1)}, u32[]{:S(2)}, u32[]{:S(2)}) collective-permute-start(bf16[10,64,128]{2,1,0:T(8,128)(2,1)S(1)} %get-tuple-element.26), channel_id=1, source_target_pairs={{0,2},{2,0},{4,6},{6,4},{1,3},{3,1},{5,7},{7,5},{8,10},{10,8},{12,... | collective-permute-start | bytes 491528 | tf_op jit(solution)/shard_map/ppermute | solution.py:489
  11.8 0.7 %collective-permute-start.3 = (bf16[5,64,128]{2,1,0:T(8,128)(2,1)S(1)}, bf16[5,64,128]{2,1,0:T(8,128)(2,1)S(1)}, u32[]{:S(2)}, u32[]{:S(2)}) collective-permute-start(bf16[5,64,128]{2,1,0:T(8,128)(2,1)S(1)} %get-tuple-element.31), channel_id=1, source_target_pairs={{0,8},{1,9},{2,10},{3,11},{4,12},{5,13},{6,14},{7,15}} | collective-permute-start | bytes 245768 | tf_op jit(solution)/shard_map/ppermute | solution.py:596
  12.6 0.7 %collective-permute-start.4 = (bf16[4,64,128]{2,1,0:T(8,128)(2,1)S(1)}, bf16[4,64,128]{2,1,0:T(8,128)(2,1)S(1)}, u32[]{:S(2)}, u32[]{:S(2)}) collective-permute-start(bf16[4,64,128]{2,1,0:T(8,128)(2,1)S(1)} %get-tuple-element.32), channel_id=1, source_target_pairs={{0,8},{1,9},{2,10},{3,11},{4,12},{5,13},{6,14},{7,15}} | collective-permute-start | bytes 196616 | tf_op jit(solution)/shard_map/ppermute | solution.py:596
  13.3 2.2 %shard_map.61.refs_1_.refs_0_ = f32[9,64,128]{2,1,0:T(8,128)S(1)} custom-call(f32[512,128]{1,0:T(8,128)S(1)} %bitcast.21, bf16[10,64,128]{2,1,0:T(8,128)(2,1)S(1)} %collective-permute-done.1.pair_ref, bf16[10,64,128]{2,1,0:T(8,128)(2,1)S(1)} %collective-permute-done.2.cross_ref, bf16[64,256]{1,0:T(8,128)(2,1)S(1)} %get-tuple-element.36.side_ref, ...), custom_call_target="tpu_custom_call" | custom-call | flops 830472192 | tf_op jit(solution)/shard_map/pallas_call | solution.py:581
  15.7 1.3 %collective-permute-start.5 = (bf16[5,64,128]{2,1,0:T(8,128)(2,1)S(1)}, bf16[5,64,128]{2,1,0:T(8,128)(2,1)S(1)}, u32[]{:S(2)}, u32[]{:S(2)}) collective-permute-start(bf16[5,64,128]{2,1,0:T(8,128)(2,1)S(1)} %shard_map.62), channel_id=1, source_target_pairs={{8,16},{9,17},{10,18},{11,19},{12,20},{13,21},{14,22},{15,23}} | collective-permute-start | bytes 245768 | tf_op jit(solution)/shard_map/ppermute | solution.py:596
  17.2 1.3 %collective-permute-start.6 = (bf16[4,64,128]{2,1,0:T(8,128)(2,1)S(1)}, bf16[4,64,128]{2,1,0:T(8,128)(2,1)S(1)}, u32[]{:S(2)}, u32[]{:S(2)}) collective-permute-start(bf16[4,64,128]{2,1,0:T(8,128)(2,1)S(1)} %shard_map.63), channel_id=1, source_target_pairs={{8,16},{9,17},{10,18},{11,19},{12,20},{13,21},{14,22},{15,23}} | collective-permute-start | bytes 196616 | tf_op jit(solution)/shard_map/ppermute | solution.py:596
  18.5 2.4 %collective-permute-done.5.s_ref.refs_2_ = bf16[5,64,128]{2,1,0:T(8,128)(2,1)S(1)} collective-permute-done((bf16[5,64,128]{2,1,0:T(8,128)(2,1)S(1)}, bf16[5,64,128]{2,1,0:T(8,128)(2,1)S(1)}, u32[]{:S(2)}, u32[]{:S(2)}) %collective-permute-start.5) | collective-permute-done | bytes 81952 | tf_op jit(solution)/shard_map/ppermute | solution.py:596
  21.1 1.3 %collective-permute-start.7 = (bf16[5,64,128]{2,1,0:T(8,128)(2,1)S(1)}, bf16[5,64,128]{2,1,0:T(8,128)(2,1)S(1)}, u32[]{:S(2)}, u32[]{:S(2)}) collective-permute-start(bf16[5,64,128]{2,1,0:T(8,128)(2,1)S(1)} %shard_map.64), channel_id=1, source_target_pairs={{16,24},{17,25},{18,26},{19,27},{20,28},{21,29},{22,30},{23,31}} | collective-permute-start | bytes 245768 | tf_op jit(solution)/shard_map/ppermute | solution.py:596
  22.6 1.3 %collective-permute-start.8 = (bf16[4,64,128]{2,1,0:T(8,128)(2,1)S(1)}, bf16[4,64,128]{2,1,0:T(8,128)(2,1)S(1)}, u32[]{:S(2)}, u32[]{:S(2)}) collective-permute-start(bf16[4,64,128]{2,1,0:T(8,128)(2,1)S(1)} %shard_map.65), channel_id=1, source_target_pairs={{16,24},{17,25},{18,26},{19,27},{20,28},{21,29},{22,30},{23,31}} | collective-permute-start | bytes 196616 | tf_op jit(solution)/shard_map/ppermute | solution.py:596
  23.9 1.3 %collective-permute-done.8.refs_5_ = bf16[4,64,128]{2,1,0:T(8,128)(2,1)S(1)} collective-permute-done((bf16[4,64,128]{2,1,0:T(8,128)(2,1)S(1)}, bf16[4,64,128]{2,1,0:T(8,128)(2,1)S(1)}, u32[]{:S(2)}, u32[]{:S(2)}) %collective-permute-start.8) | collective-permute-done | bytes 65568 | tf_op jit(solution)/shard_map/ppermute | solution.py:596
  25.3 0.9 %collective-permute-start.10 = (bf16[9,64,128]{2,1,0:T(8,128)(2,1)S(1)}, bf16[9,64,128]{2,1,0:T(8,128)(2,1)S(1)}, u32[]{:S(2)}, u32[]{:S(2)}) collective-permute-start(bf16[9,64,128]{2,1,0:T(8,128)(2,1)S(1)} %shard_map.66.s_ref), channel_id=1, source_target_pairs={{2,4},{4,2},{3,5},{5,3},{10,12},{12,10},{11,13},{13,11},{18,20},{2... | collective-permute-start | bytes 442376 | tf_op jit(solution)/shard_map/ppermute | solution.py:489
  26.2 6.2 %collective-permute-start.9 = (bf16[9,64,128]{2,1,0:T(8,128)(2,1)S(1)}, bf16[9,64,128]{2,1,0:T(8,128)(2,1)S(1)}, u32[]{:S(2)}, u32[]{:S(2)}) collective-permute-start(bf16[9,64,128]{2,1,0:T(8,128)(2,1)S(1)} %shard_map.66.s_ref), channel_id=1, source_target_pairs={{0,2},{2,0},{4,6},{6,4},{1,3},{3,1},{5,7},{7,5},{8,10},{10,8},{12,... | collective-permute-start | bytes 442376 | tf_op jit(solution)/shard_map/ppermute | solution.py:489
  32.5 0.9 %collective-permute-done.9.s_pair_ref = bf16[9,64,128]{2,1,0:T(8,128)(2,1)S(1)} collective-permute-done((bf16[9,64,128]{2,1,0:T(8,128)(2,1)S(1)}, bf16[9,64,128]{2,1,0:T(8,128)(2,1)S(1)}, u32[]{:S(2)}, u32[]{:S(2)}) %collective-permute-start.9) | collective-permute-done | bytes 147488 | tf_op jit(solution)/shard_map/ppermute | solution.py:489
  33.3 6.1 %shard_map.67 = (f32[512,128]{1,0:T(8,128)}, f32[8,64,128]{2,1,0:T(8,128)S(1)}, bf16[4,64,128]{2,1,0:T(8,128)(2,1)S(1)}, bf16[4,64,128]{2,1,0:T(8,128)(2,1)S(1)}...) custom-call(f32[512,128]{1,0:T(8,128)S(1)} %bitcast.27, f32[512,128]{1,0:T(8,128)S(1)} %bitcast.30, ...), custom_call_target="tpu_custom_call" | custom-call | flops 2264924160 | tf_op jit(solution)/shard_map/pallas_call | solution.py:623
  39.5 1.3 %collective-permute-start.15 = (bf16[4,64,128]{2,1,0:T(8,128)(2,1)S(1)}, bf16[4,64,128]{2,1,0:T(8,128)(2,1)S(1)}, u32[]{:S(2)}, u32[]{:S(2)}) collective-permute-start(bf16[4,64,128]{2,1,0:T(8,128)(2,1)S(1)} %get-tuple-element.42), channel_id=1, source_target_pairs={{24,16},{25,17},{26,18},{27,19},{28,20},{29,21},{30,22},{31,23}} | collective-permute-start | bytes 196616 | tf_op jit(solution)/shard_map/ppermute | solution.py:596
  40.8 1.3 %collective-permute-start.16 = (bf16[4,64,128]{2,1,0:T(8,128)(2,1)S(1)}, bf16[4,64,128]{2,1,0:T(8,128)(2,1)S(1)}, u32[]{:S(2)}, u32[]{:S(2)}) collective-permute-start(bf16[4,64,128]{2,1,0:T(8,128)(2,1)S(1)} %get-tuple-element.43), channel_id=1, source_target_pairs={{24,16},{25,17},{26,18},{27,19},{28,20},{29,21},{30,22},{31,23}} | collective-permute-start | bytes 196616 | tf_op jit(solution)/shard_map/ppermute | solution.py:596
  42.1 1.1 %shard_map.68 = f32[4,64,576]{2,1,0:T(8,128)S(1)} custom-call(bf16[4,8,64,256]{3,2,1,0:T(8,128)(2,1)S(1)} %get-tuple-element.40.kept_ref, bf16[4,10,64,128]{3,2,1,0:T(8,128)(2,1)S(1)} %get-tuple-element.41.sent_ref), custom_call_target="tpu_custom_call" | custom-call | flops 1000000000 | tf_op jit(solution)/shard_map/pallas_call | solution.py:652
  43.2 3.2 %collective-permute-start.11 = (f32[2,64,576]{2,1,0:T(8,128)S(1)}, f32[2,64,576]{2,1,0:T(8,128)S(1)}, u32[]{:S(2)}, u32[]{:S(2)}) collective-permute-start(f32[2,64,576]{2,1,0:T(8,128)S(1)} %slice_select_fusion), channel_id=1, source_target_pairs={{0,2},{2,0},{4,6},{6,4},{1,3},{3,1},{5,7},{7,5},{8,10},{10,8},{12,... | collective-permute-start | bytes 884744 | tf_op jit(solution)/shard_map/ppermute | solution.py:507
  46.7 1.3 %collective-permute-start.17 = (bf16[4,64,128]{2,1,0:T(8,128)(2,1)S(1)}, bf16[4,64,128]{2,1,0:T(8,128)(2,1)S(1)}, u32[]{:S(2)}, u32[]{:S(2)}) collective-permute-start(bf16[4,64,128]{2,1,0:T(8,128)(2,1)S(1)} %shard_map.69), channel_id=1, source_target_pairs={{16,8},{17,9},{18,10},{19,11},{20,12},{21,13},{22,14},{23,15}} | collective-permute-start | bytes 196616 | tf_op jit(solution)/shard_map/ppermute | solution.py:596
  48.0 1.6 %collective-permute-start.12 = (bf16[2,64,576]{2,1,0:T(8,128)(2,1)S(1)}, bf16[2,64,576]{2,1,0:T(8,128)(2,1)S(1)}, u32[]{:S(2)}, u32[]{:S(2)}) collective-permute-start(bf16[2,64,576]{2,1,0:T(8,128)(2,1)S(1)} %add_convert_fusion.1), channel_id=1, source_target_pairs={{0,1},{1,0},{2,6},{3,7},{4,5},{5,4},{6,2},{7,3},{8,9},{9,8},{10,14... | collective-permute-start | bytes 442376 | tf_op jit(solution)/shard_map/ppermute | solution.py:519
  49.8 1.3 %collective-permute-start.18 = (bf16[4,64,128]{2,1,0:T(8,128)(2,1)S(1)}, bf16[4,64,128]{2,1,0:T(8,128)(2,1)S(1)}, u32[]{:S(2)}, u32[]{:S(2)}) collective-permute-start(bf16[4,64,128]{2,1,0:T(8,128)(2,1)S(1)} %shard_map.70), channel_id=1, source_target_pairs={{16,8},{17,9},{18,10},{19,11},{20,12},{21,13},{22,14},{23,15}} | collective-permute-start | bytes 196616 | tf_op jit(solution)/shard_map/ppermute | solution.py:596
  51.1 1.2 %collective-permute-done.12 = bf16[2,64,576]{2,1,0:T(8,128)(2,1)S(1)} collective-permute-done((bf16[2,64,576]{2,1,0:T(8,128)(2,1)S(1)}, bf16[2,64,576]{2,1,0:T(8,128)(2,1)S(1)}, u32[]{:S(2)}, u32[]{:S(2)}) %collective-permute-start.12) | collective-permute-done | bytes 147488 | tf_op jit(solution)/shard_map/ppermute | solution.py:519
  52.4 1.3 %collective-permute-start.13 = (bf16[2,64,576]{2,1,0:T(8,128)(2,1)S(1)}, bf16[2,64,576]{2,1,0:T(8,128)(2,1)S(1)}, u32[]{:S(2)}, u32[]{:S(2)}) collective-permute-start(bf16[2,64,576]{2,1,0:T(8,128)(2,1)S(1)} %add_convert_fusion), channel_id=1, source_target_pairs={{0,4},{1,5},{2,3},{3,2},{4,0},{5,1},{6,7},{7,6},{8,12},{9,13},{10,... | collective-permute-start | bytes 442376 | tf_op jit(solution)/shard_map/ppermute | solution.py:519
  53.9 0.7 %collective-permute-start.19 = (bf16[4,64,128]{2,1,0:T(8,128)(2,1)S(1)}, bf16[4,64,128]{2,1,0:T(8,128)(2,1)S(1)}, u32[]{:S(2)}, u32[]{:S(2)}) collective-permute-start(bf16[4,64,128]{2,1,0:T(8,128)(2,1)S(1)} %shard_map.71), channel_id=1, source_target_pairs={{8,0},{9,1},{10,2},{11,3},{12,4},{13,5},{14,6},{15,7}} | collective-permute-start | bytes 196616 | tf_op jit(solution)/shard_map/ppermute | solution.py:596
  54.6 2.3 %collective-permute-done.13 = bf16[2,64,576]{2,1,0:T(8,128)(2,1)S(1)} collective-permute-done((bf16[2,64,576]{2,1,0:T(8,128)(2,1)S(1)}, bf16[2,64,576]{2,1,0:T(8,128)(2,1)S(1)}, u32[]{:S(2)}, u32[]{:S(2)}) %collective-permute-start.13) | collective-permute-done | bytes 147488 | tf_op jit(solution)/shard_map/ppermute | solution.py:519
  56.9 4.6 %collective-permute-start.14 = (f32[2,64,576]{2,1,0:T(8,128)S(1)}, f32[2,64,576]{2,1,0:T(8,128)S(1)}, u32[]{:S(2)}, u32[]{:S(2)}) collective-permute-start(f32[2,64,576]{2,1,0:T(8,128)S(1)} %convert_add_fusion.half_ref), channel_id=1, source_target_pairs={{0,2},{2,0},{4,6},{6,4},{1,3},{3,1},{5,7},{7,5},{8,10},{10,8},{12,... | collective-permute-start | bytes 884744 | tf_op jit(solution)/shard_map/ppermute | solution.py:521
  61.6 0.7 %collective-permute-start.20 = (bf16[4,64,128]{2,1,0:T(8,128)(2,1)S(1)}, bf16[4,64,128]{2,1,0:T(8,128)(2,1)S(1)}, u32[]{:S(2)}, u32[]{:S(2)}) collective-permute-start(bf16[4,64,128]{2,1,0:T(8,128)(2,1)S(1)} %shard_map.72), channel_id=1, source_target_pairs={{8,0},{9,1},{10,2},{11,3},{12,4},{13,5},{14,6},{15,7}} | collective-permute-start | bytes 196616 | tf_op jit(solution)/shard_map/ppermute | solution.py:596
  62.7 1.0 %shard_map.73 = (f32[512,128]{1,0:T(8,128)}, f32[4,64,576]{2,1,0:T(8,128)}) custom-call(f32[512,128]{1,0:T(8,128)S(1)} %bitcast.35, f32[2,64,576]{2,1,0:T(8,128)S(1)} %convert_add_fusion.half_ref, f32[2,64,576]{2,1,0:T(8,128)S(1)} %collective-permute-done.14.other_ref, bf16[4,64,128]{2,1,0:T(8,128)(2,1)S(1)} %collective-permute-done.15.s_ref.refs_0_, ...), custom_call_target="tpu_custom_call" | custom-call | flops 10000000000 | tf_op jit(solution)/shard_map/pallas_call | solution.py:658
  (49 shorter events, 5.1 us)
Async XLA Ops:
  0.6 3.3 %copy-start.2 = (bf16[4,64,576]{2,1,0:T(8,128)(2,1)S(1)}, bf16[4,64,576]{2,1,0:T(8,128)(2,1)}, u32[]{:S(2)}) copy-start(bf16[4,64,576]{2,1,0:T(8,128)(2,1)} %param.5) | copy-start | bytes 884740
  2.6 3.0 %collective-permute-start = (bf16[64,256]{1,0:T(8,128)(2,1)}, bf16[64,256]{1,0:T(8,128)(2,1)S(1)}, u32[]{:S(2)}, u32[]{:S(2)}) collective-permute-start(bf16[64,256]{1,0:T(8,128)(2,1)} %shard_map.58), channel_id=1, source_target_pairs={{0,1},{1,0},{2,3},{3,2},{4,5},{5,4},{6,7},{7,6},{8,9},{9,8},{10,11... | collective-permute-start | bytes 98312 | tf_op jit(solution)/shard_map/ppermute | solution.py:494
  3.9 1.7 %copy-start.1 = (f32[1,64,8,128]{3,2,1,0:T(8,128)S(1)}, f32[1,64,8,128]{3,2,1,0:T(8,128)}, u32[]{:S(2)}) copy-start(f32[1,64,8,128]{3,2,1,0:T(8,128)} %param.4) | copy-start | bytes 786436
  4.2 1.4 %copy-start = (f32[1,64,8,128]{3,2,1,0:T(8,128)S(1)}, f32[1,64,8,128]{3,2,1,0:T(8,128)}, u32[]{:S(2)}) copy-start(f32[1,64,8,128]{3,2,1,0:T(8,128)} %param.3) | copy-start | bytes 786436
  5.9 5.9 %collective-permute-start.2 = (bf16[10,64,128]{2,1,0:T(8,128)(2,1)S(1)}, bf16[10,64,128]{2,1,0:T(8,128)(2,1)S(1)}, u32[]{:S(2)}, u32[]{:S(2)}) collective-permute-start(bf16[10,64,128]{2,1,0:T(8,128)(2,1)S(1)} %get-tuple-element.27), channel_id=1, source_target_pairs={{2,4},{4,2},{3,5},{5,3},{10,12},{12,10},{11,13},{13,11},{18,20},{2... | collective-permute-start | bytes 491528 | tf_op jit(solution)/shard_map/ppermute | solution.py:489
  6.6 5.2 %collective-permute-start.1 = (bf16[10,64,128]{2,1,0:T(8,128)(2,1)S(1)}, bf16[10,64,128]{2,1,0:T(8,128)(2,1)S(1)}, u32[]{:S(2)}, u32[]{:S(2)}) collective-permute-start(bf16[10,64,128]{2,1,0:T(8,128)(2,1)S(1)} %get-tuple-element.26), channel_id=1, source_target_pairs={{0,2},{2,0},{4,6},{6,4},{1,3},{3,1},{5,7},{7,5},{8,10},{10,8},{12,... | collective-permute-start | bytes 491528 | tf_op jit(solution)/shard_map/ppermute | solution.py:489
  11.8 3.6 %collective-permute-start.3 = (bf16[5,64,128]{2,1,0:T(8,128)(2,1)S(1)}, bf16[5,64,128]{2,1,0:T(8,128)(2,1)S(1)}, u32[]{:S(2)}, u32[]{:S(2)}) collective-permute-start(bf16[5,64,128]{2,1,0:T(8,128)(2,1)S(1)} %get-tuple-element.31), channel_id=1, source_target_pairs={{0,8},{1,9},{2,10},{3,11},{4,12},{5,13},{6,14},{7,15}} | collective-permute-start | bytes 245768 | tf_op jit(solution)/shard_map/ppermute | solution.py:596
  12.6 4.4 %collective-permute-start.4 = (bf16[4,64,128]{2,1,0:T(8,128)(2,1)S(1)}, bf16[4,64,128]{2,1,0:T(8,128)(2,1)S(1)}, u32[]{:S(2)}, u32[]{:S(2)}) collective-permute-start(bf16[4,64,128]{2,1,0:T(8,128)(2,1)S(1)} %get-tuple-element.32), channel_id=1, source_target_pairs={{0,8},{1,9},{2,10},{3,11},{4,12},{5,13},{6,14},{7,15}} | collective-permute-start | bytes 196616 | tf_op jit(solution)/shard_map/ppermute | solution.py:596
  15.7 5.2 %collective-permute-start.5 = (bf16[5,64,128]{2,1,0:T(8,128)(2,1)S(1)}, bf16[5,64,128]{2,1,0:T(8,128)(2,1)S(1)}, u32[]{:S(2)}, u32[]{:S(2)}) collective-permute-start(bf16[5,64,128]{2,1,0:T(8,128)(2,1)S(1)} %shard_map.62), channel_id=1, source_target_pairs={{8,16},{9,17},{10,18},{11,19},{12,20},{13,21},{14,22},{15,23}} | collective-permute-start | bytes 245768 | tf_op jit(solution)/shard_map/ppermute | solution.py:596
  17.2 5.2 %collective-permute-start.6 = (bf16[4,64,128]{2,1,0:T(8,128)(2,1)S(1)}, bf16[4,64,128]{2,1,0:T(8,128)(2,1)S(1)}, u32[]{:S(2)}, u32[]{:S(2)}) collective-permute-start(bf16[4,64,128]{2,1,0:T(8,128)(2,1)S(1)} %shard_map.63), channel_id=1, source_target_pairs={{8,16},{9,17},{10,18},{11,19},{12,20},{13,21},{14,22},{15,23}} | collective-permute-start | bytes 196616 | tf_op jit(solution)/shard_map/ppermute | solution.py:596
  21.1 4.1 %collective-permute-start.7 = (bf16[5,64,128]{2,1,0:T(8,128)(2,1)S(1)}, bf16[5,64,128]{2,1,0:T(8,128)(2,1)S(1)}, u32[]{:S(2)}, u32[]{:S(2)}) collective-permute-start(bf16[5,64,128]{2,1,0:T(8,128)(2,1)S(1)} %shard_map.64), channel_id=1, source_target_pairs={{16,24},{17,25},{18,26},{19,27},{20,28},{21,29},{22,30},{23,31}} | collective-permute-start | bytes 245768 | tf_op jit(solution)/shard_map/ppermute | solution.py:596
  22.6 2.6 %collective-permute-start.8 = (bf16[4,64,128]{2,1,0:T(8,128)(2,1)S(1)}, bf16[4,64,128]{2,1,0:T(8,128)(2,1)S(1)}, u32[]{:S(2)}, u32[]{:S(2)}) collective-permute-start(bf16[4,64,128]{2,1,0:T(8,128)(2,1)S(1)} %shard_map.65), channel_id=1, source_target_pairs={{16,24},{17,25},{18,26},{19,27},{20,28},{21,29},{22,30},{23,31}} | collective-permute-start | bytes 196616 | tf_op jit(solution)/shard_map/ppermute | solution.py:596
  25.3 7.1 %collective-permute-start.10 = (bf16[9,64,128]{2,1,0:T(8,128)(2,1)S(1)}, bf16[9,64,128]{2,1,0:T(8,128)(2,1)S(1)}, u32[]{:S(2)}, u32[]{:S(2)}) collective-permute-start(bf16[9,64,128]{2,1,0:T(8,128)(2,1)S(1)} %shard_map.66.s_ref), channel_id=1, source_target_pairs={{2,4},{4,2},{3,5},{5,3},{10,12},{12,10},{11,13},{13,11},{18,20},{2... | collective-permute-start | bytes 442376 | tf_op jit(solution)/shard_map/ppermute | solution.py:489
  26.2 7.2 %collective-permute-start.9 = (bf16[9,64,128]{2,1,0:T(8,128)(2,1)S(1)}, bf16[9,64,128]{2,1,0:T(8,128)(2,1)S(1)}, u32[]{:S(2)}, u32[]{:S(2)}) collective-permute-start(bf16[9,64,128]{2,1,0:T(8,128)(2,1)S(1)} %shard_map.66.s_ref), channel_id=1, source_target_pairs={{0,2},{2,0},{4,6},{6,4},{1,3},{3,1},{5,7},{7,5},{8,10},{10,8},{12,... | collective-permute-start | bytes 442376 | tf_op jit(solution)/shard_map/ppermute | solution.py:489
  39.5 7.0 %collective-permute-start.15 = (bf16[4,64,128]{2,1,0:T(8,128)(2,1)S(1)}, bf16[4,64,128]{2,1,0:T(8,128)(2,1)S(1)}, u32[]{:S(2)}, u32[]{:S(2)}) collective-permute-start(bf16[4,64,128]{2,1,0:T(8,128)(2,1)S(1)} %get-tuple-element.42), channel_id=1, source_target_pairs={{24,16},{25,17},{26,18},{27,19},{28,20},{29,21},{30,22},{31,23}} | collective-permute-start | bytes 196616 | tf_op jit(solution)/shard_map/ppermute | solution.py:596
  40.8 8.9 %collective-permute-start.16 = (bf16[4,64,128]{2,1,0:T(8,128)(2,1)S(1)}, bf16[4,64,128]{2,1,0:T(8,128)(2,1)S(1)}, u32[]{:S(2)}, u32[]{:S(2)}) collective-permute-start(bf16[4,64,128]{2,1,0:T(8,128)(2,1)S(1)} %get-tuple-element.43), channel_id=1, source_target_pairs={{24,16},{25,17},{26,18},{27,19},{28,20},{29,21},{30,22},{31,23}} | collective-permute-start | bytes 196616 | tf_op jit(solution)/shard_map/ppermute | solution.py:596
  43.2 4.8 %collective-permute-start.11 = (f32[2,64,576]{2,1,0:T(8,128)S(1)}, f32[2,64,576]{2,1,0:T(8,128)S(1)}, u32[]{:S(2)}, u32[]{:S(2)}) collective-permute-start(f32[2,64,576]{2,1,0:T(8,128)S(1)} %slice_select_fusion), channel_id=1, source_target_pairs={{0,2},{2,0},{4,6},{6,4},{1,3},{3,1},{5,7},{7,5},{8,10},{10,8},{12,... | collective-permute-start | bytes 884744 | tf_op jit(solution)/shard_map/ppermute | solution.py:507
  46.7 7.0 %collective-permute-start.17 = (bf16[4,64,128]{2,1,0:T(8,128)(2,1)S(1)}, bf16[4,64,128]{2,1,0:T(8,128)(2,1)S(1)}, u32[]{:S(2)}, u32[]{:S(2)}) collective-permute-start(bf16[4,64,128]{2,1,0:T(8,128)(2,1)S(1)} %shard_map.69), channel_id=1, source_target_pairs={{16,8},{17,9},{18,10},{19,11},{20,12},{21,13},{22,14},{23,15}} | collective-permute-start | bytes 196616 | tf_op jit(solution)/shard_map/ppermute | solution.py:596
  48.0 4.3 %collective-permute-start.12 = (bf16[2,64,576]{2,1,0:T(8,128)(2,1)S(1)}, bf16[2,64,576]{2,1,0:T(8,128)(2,1)S(1)}, u32[]{:S(2)}, u32[]{:S(2)}) collective-permute-start(bf16[2,64,576]{2,1,0:T(8,128)(2,1)S(1)} %add_convert_fusion.1), channel_id=1, source_target_pairs={{0,1},{1,0},{2,6},{3,7},{4,5},{5,4},{6,2},{7,3},{8,9},{9,8},{10,14... | collective-permute-start | bytes 442376 | tf_op jit(solution)/shard_map/ppermute | solution.py:519
  49.8 11.6 %collective-permute-start.18 = (bf16[4,64,128]{2,1,0:T(8,128)(2,1)S(1)}, bf16[4,64,128]{2,1,0:T(8,128)(2,1)S(1)}, u32[]{:S(2)}, u32[]{:S(2)}) collective-permute-start(bf16[4,64,128]{2,1,0:T(8,128)(2,1)S(1)} %shard_map.70), channel_id=1, source_target_pairs={{16,8},{17,9},{18,10},{19,11},{20,12},{21,13},{22,14},{23,15}} | collective-permute-start | bytes 196616 | tf_op jit(solution)/shard_map/ppermute | solution.py:596
  52.4 4.5 %collective-permute-start.13 = (bf16[2,64,576]{2,1,0:T(8,128)(2,1)S(1)}, bf16[2,64,576]{2,1,0:T(8,128)(2,1)S(1)}, u32[]{:S(2)}, u32[]{:S(2)}) collective-permute-start(bf16[2,64,576]{2,1,0:T(8,128)(2,1)S(1)} %add_convert_fusion), channel_id=1, source_target_pairs={{0,4},{1,5},{2,3},{3,2},{4,0},{5,1},{6,7},{7,6},{8,12},{9,13},{10,... | collective-permute-start | bytes 442376 | tf_op jit(solution)/shard_map/ppermute | solution.py:519
  53.9 8.4 %collective-permute-start.19 = (bf16[4,64,128]{2,1,0:T(8,128)(2,1)S(1)}, bf16[4,64,128]{2,1,0:T(8,128)(2,1)S(1)}, u32[]{:S(2)}, u32[]{:S(2)}) collective-permute-start(bf16[4,64,128]{2,1,0:T(8,128)(2,1)S(1)} %shard_map.71), channel_id=1, source_target_pairs={{8,0},{9,1},{10,2},{11,3},{12,4},{13,5},{14,6},{15,7}} | collective-permute-start | bytes 196616 | tf_op jit(solution)/shard_map/ppermute | solution.py:596
  56.9 5.8 %collective-permute-start.14 = (f32[2,64,576]{2,1,0:T(8,128)S(1)}, f32[2,64,576]{2,1,0:T(8,128)S(1)}, u32[]{:S(2)}, u32[]{:S(2)}) collective-permute-start(f32[2,64,576]{2,1,0:T(8,128)S(1)} %convert_add_fusion.half_ref), channel_id=1, source_target_pairs={{0,2},{2,0},{4,6},{6,4},{1,3},{3,1},{5,7},{7,5},{8,10},{10,8},{12,... | collective-permute-start | bytes 884744 | tf_op jit(solution)/shard_map/ppermute | solution.py:521
  61.6 0.7 %collective-permute-start.20 = (bf16[4,64,128]{2,1,0:T(8,128)(2,1)S(1)}, bf16[4,64,128]{2,1,0:T(8,128)(2,1)S(1)}, u32[]{:S(2)}, u32[]{:S(2)}) collective-permute-start(bf16[4,64,128]{2,1,0:T(8,128)(2,1)S(1)} %shard_map.72), channel_id=1, source_target_pairs={{8,0},{9,1},{10,2},{11,3},{12,4},{13,5},{14,6},{15,7}} | collective-permute-start | bytes 196616 | tf_op jit(solution)/shard_map/ppermute | solution.py:596

commit v14 on v13

--- a/solution.py
+++ b/solution.py
@@ -140,8 +140,7 @@
 
 
 def message_body(
-    c_ref, q_ref, left_ref, right_ref, pair_ref, cross_ref, side_ref, strip_ref,
-    *, channels, rows, depth,
+    c_ref, q_ref, left_ref, right_ref, pair_ref, cross_ref, side_ref, *, channels, rows, depth
 ):
     cols = c_ref.shape[1]
     _, _, left, right = flags()
@@ -149,9 +148,6 @@
     edges = ((c_edge, 0, middle), (q_edge, middle, 2 * cols))
     side = join_edges(left_ref[...], right_ref[...], left, right, edges).astype(bf16)
     side_ref[...] = side
-    wide = side.astype(f32)
-    image = [side_lanes(wide, c_edge, 0, row) for row in range(rows)]
-    strip_ref[...] = fold_edges(image, 2 * depth, 0, jnp.zeros(strip_ref.shape, f32))
     even = even_row()
     for which, ref in enumerate((c_ref, q_ref)):
         for row in range(depth):
@@ -179,6 +175,13 @@
         return jnp.where(
             self.even, self.pair[place].astype(f32), self.cross[place].astype(f32)
         )
+
+
+def halo_strip_body(side_ref, strip_ref, *, rows, depth):
+    (edge, low), _ = layout(rows, depth)
+    side = side_ref[...].astype(f32)
+    image = [side_lanes(side, edge, low, row) for row in range(rows)]
+    strip_ref[...] = fold_edges(image, 2 * depth, 0, jnp.zeros(strip_ref.shape, f32))
 
 
 def strips_of(get, depth):
@@ -302,10 +305,51 @@
         s_ref[row] = jnp.where(first, base[row], value).astype(bf16)
 
 
+def prepare_body(
+    c_ref, q_ref, s_ref, pair_ref, cross_ref, side_ref, state_hbm, adj_ref,
+    state_ref, left_here, *, channels, rows, depth,
+):
+    cols = c_ref.shape[1]
+    first = lax.axis_index("layer") == 0
+    for row in range(rows):
+        own = jnp.where(first, row_of(c_ref, row, channels, rows), s_ref[row].astype(f32))
+        state_ref[pl.ds(row, channels, stride=rows), :] = own
+    leaving = in_parts(state_ref, state_hbm, left_here, 0)
+    for copy in leaving:
+        copy.start()
+
+    def put_adj(index, own, beyond):
+        adj_ref[index, :, :cols] = own
+        adj_ref[index, :, cols:] = beyond
+
+    _, (edge, low) = layout(rows, depth)
+    own_side = side_ref[...].astype(f32)
+    beside = Beside(pair_ref, cross_ref)
+    above_side, below_side = strips_of(beside.above, depth), strips_of(beside.below, depth)
+    for row in range(rows):
+        put_adj(
+            depth + row, row_of(q_ref, row, channels, rows), side_lanes(own_side, edge, low, row)
+        )
+    for row in range(depth):
+        place = rows - depth + row
+        put_adj(
+            row,
+            beside.above(depth + row),
+            side_lanes(above_side, edge, low, place),
+        )
+        put_adj(
+            depth + rows + row,
+            beside.below(depth + row),
+            side_lanes(below_side, edge, low, row),
+        )
+    for copy in leaving:
+        copy.wait()
+
+
 def second_body(
-    c_ref, q_ref, s_ref, s_pair_ref, s_cross_ref, pair_ref, cross_ref, side_ref, w_ref, wt_ref,
-    state_hbm, g_ref, g_upper_ref, g_lower_ref, kept_ref, sent_ref,
-    x_ref, a_ref, a2_ref, slope_ref, adj_ref, src_ref, state_ref, left_here,
+    c_ref, s_ref, s_pair_ref, s_cross_ref, ready_ref, w_ref, wt_ref,
+    g_ref, g_upper_ref, g_lower_ref, kept_ref, sent_ref,
+    x_ref, a_ref, a2_ref, slope_ref, adj_ref, src_ref,
     *, channels, rows, depth,
 ):
     cols = c_ref.shape[1]
@@ -328,11 +372,7 @@
     above_side, below_side = beside.above(rows), beside.below(rows)
     for row in range(rows):
         own = jnp.where(first, row_of(c_ref, row, channels, rows), s_ref[row].astype(f32))
-        state_ref[pl.ds(row, channels, stride=rows), :] = own
         put(halo + row, own, side_lanes(own_side, edge, 0, row))
-    leaving = in_parts(state_ref, state_hbm, left_here, 0)
-    for copy in leaving:
-        copy.start()
     for row in range(halo):
         place = rows - halo + row
         put(
@@ -344,31 +384,6 @@
             halo + rows + row,
             beside.below(row),
             side_lanes(below_side, edge, 0, row),
-        )
-
-    def put_adj(index, own, beyond):
-        adj_ref[index, :, :cols] = own
-        adj_ref[index, :, cols:] = beyond
-
-    _, (edge, low) = layout(rows, depth)
-    own_side = side_ref[...].astype(f32)
-    beside = Beside(pair_ref, cross_ref)
-    above_side, below_side = strips_of(beside.above, depth), strips_of(beside.below, depth)
-    for row in range(rows):
-        put_adj(
-            halo + row, row_of(q_ref, row, channels, rows), side_lanes(own_side, edge, low, row)
-        )
-    for row in range(depth):
-        place = rows - depth + row
-        put_adj(
-            halo - depth + row,
-            beside.above(depth + row),
-            side_lanes(above_side, edge, low, place),
-        )
-        put_adj(
-            halo + rows + row,
-            beside.below(depth + row),
-            side_lanes(below_side, edge, low, row),
         )
 
     for layer in range(depth):
@@ -391,17 +406,23 @@
 
         row_blocks(layer + 1, total - layer - 1, step)
 
+    def before(layer, first, count):
+        if layer == depth - 1:
+            return ready_ref[pl.ds(first - (halo - depth), count)]
+        return adj_ref[pl.ds(first, count)]
+
     for layer in reversed(range(depth)):
         reach = layer + 1
 
         def source(first, count, layer=layer):
             part = pl.ds(first, count)
-            src_ref[part] = (adj_ref[part] * slope_ref[layer, part]).astype(bf16)
+            adjoints = before(layer, first, count)
+            src_ref[part] = (adjoints * slope_ref[layer, part]).astype(bf16)
 
         row_blocks(halo - reach, halo + rows + reach, source)
 
         def back(first, count, layer=layer):
-            adjoints = adj_ref[pl.ds(first, count)]
+            adjoints = before(layer, first, count)
             moved = convolved_rows(wt_ref[layer], src_ref, first, count)
             for place in range(count):
                 adj_ref[first + place] = adjoints[place] + moved[place]
@@ -413,8 +434,6 @@
         g_ref[row] = value
         ref, place = piece_of((g_upper_ref, g_lower_ref), row, rows)
         ref[place] = value.astype(bf16)
-    for copy in leaving:
-        copy.wait()
 
 
 def grad_body(kept_ref, sent_ref, grad_ref, *, channels, rows, depth):
@@ -554,11 +573,14 @@
         out_specs=HERE,
     )(c_flat, q_flat)
     left, right = from_sides(edges)
-    to_pair, to_cross, side, strip = call(
+    to_pair, to_cross, side = call(
         functools.partial(message_body, depth=depth, **sizes),
-        (message_b, message_b, wide_b, strip_f),
+        (message_b, message_b, wide_b),
     )(c_flat, q_flat, left, right)
     pair, cross = exchanged(to_pair, to_cross)
+    strip = call(
+        functools.partial(halo_strip_body, rows=rows, depth=depth), strip_f, flops=10**9
+    )(side)
 
     taps = weights.reshape(depth, channels, 3, 3, channels)
     w_fwd = jnp.transpose(taps, (0, 3, 1, 2, 4)).reshape(depth, 3 * channels, 3 * channels)
@@ -620,10 +642,17 @@
     s_pair, s_cross = exchanged(s, s)
 
     total = rows + 4 * depth
-    state, g, upper, lower, kept, sources = call(
+    held, _ = lax.optimization_barrier(((c_flat, q_flat), s))
+    state, ready = call(
+        functools.partial(prepare_body, depth=depth, **sizes),
+        (flat_f, jax.ShapeDtypeStruct((rows + 2 * depth, channels, lanes), f32)),
+        [pltpu.VMEM(flat, f32), pltpu.SemaphoreType.DMA((PARTS,))],
+        flops=2 * 10**9,
+        out_specs=(AWAY, HERE),
+    )(*held, s, pair, cross, side)
+    g, upper, lower, kept, sources = call(
         functools.partial(second_body, depth=depth, **sizes),
         (
-            flat_f,
             tile_f,
             lower_b,
             lower_b,
@@ -637,12 +666,9 @@
             pltpu.VMEM((depth, total, channels, lanes), f32),
             pltpu.VMEM((total, channels, lanes), f32),
             pltpu.VMEM((total, channels, lanes), bf16),
-            pltpu.VMEM(flat, f32),
-            pltpu.SemaphoreType.DMA((PARTS,)),
         ],
         flops=mac * 120,
-        out_specs=(AWAY, HERE, HERE, HERE, HERE, HERE),
-    )(c_flat, q_flat, s, s_pair, s_cross, pair, cross, side, w_fwd, w_back)
+    )(c_flat, s, s_pair, s_cross, ready, w_fwd, w_back)
     returned = chain(
         ((upper, 0, (q_flat,)), (lower, half, (q_flat,))),
         g,

time: 64.2 us -> 64.8 us (level)
  waiting for transfers between devices: 9.77 us -> 9.01 us
    ppermute x1, waiting for transfers between devices: 1.35 us -> 0.14 us  [from_sides(): other = lax.ppermute(array, 'col', [(0, 1), (1, 0)])]
    ppermute x12, waiting for transfers between devices: 3.71 us -> 4.86 us  [chain(): arrived = [lax.ppermute(sending, 'layer', [step]) for sending in sendings]]
    ppermute x2, waiting for transfers between devices: 0.89 us -> 0.01 us  [exchanged(): lax.ppermute(to_pair, 'row', pairs)]
    pallas_call x1 -> x3, Pallas kernels: 6.1 us -> 6.65 us  [the longest x1 5.45 us: local(): call(functools.partial(second_body, depth=depth, **sizes), (tile_f, lower...]
  transfers between devices with their start and end apart: 21 -> 21, of which waited for: 7 -> 7; matrix products, arithmetic and copies ran while one was open for 4% -> 4% of each run, Pallas kernels for 8% -> 9%
where the time goes in v14:
time: 64.8 us; the launch traced here: 64.4 us
  starting transfers between devices  36.3 us (56%)
  Pallas kernels  14.7 us (23%)
  waiting for transfers between devices  9.01 us (14%)
  local copies, waits for them, and re-layouts  2.85 us (4%)
  between operations  1.22 us (2%)
    ppermute x12, starting transfers between devices, chain(): arrived = [lax.ppermute(sending, 'layer', [step]) for sending in sendings]  13 us
    ppermute x2, starting transfers between devices, exchanged(): lax.ppermute(to_pair, 'row', pairs)  9.79 us
    pallas_call x1, Pallas kernels, local(): call(functools.partial(second_body, depth=depth, **sizes), (tile_f, lower...  5.45 us
    ppermute x12, waiting for transfers between devices, chain(): arrived = [lax.ppermute(sending, 'layer', [step]) for sending in sendings]  4.86 us
    ppermute x1, starting transfers between devices, total_over_tiles(): return (value, lax.ppermute(value, 'row', pair))  4.64 us
    ppermute x2, waiting for transfers between devices, total_over_tiles(): arrived = lax.ppermute(rounded, ('row', 'col'), pairs)  3.63 us
    ppermute x1, starting transfers between devices, total_over_tiles(): value = own + lax.ppermute(sent, 'row', pair)  3.34 us
    ppermute x2, starting transfers between devices, total_over_tiles(): arrived = lax.ppermute(rounded, ('row', 'col'), pairs)  2.73 us
  transfers between devices with their start and end apart: 21, of which 7 were waited for; matrix products, arithmetic and copies ran while one was open for 4% of the time, Pallas kernels for 9%

profile of v14, /device:TPU:19, one launch (start us, length us, event | category | flops | bytes accessed | tf_op | source)
XLA Modules:
  0.0 64.4 jit_solution(9772393427657995597)
XLA Ops:
  0.6 1.9 %shard_map.58 = bf16[64,256]{1,0:T(8,128)(2,1)} custom-call(f32[512,128]{1,0:T(8,128)} %bitcast.18, f32[512,128]{1,0:T(8,128)} %bitcast.29), custom_call_target="tpu_custom_call" | custom-call | tf_op jit(solution)/shard_map/pallas_call | solution.py:563
  2.6 1.3 %collective-permute-start = (bf16[64,256]{1,0:T(8,128)(2,1)}, bf16[64,256]{1,0:T(8,128)(2,1)S(1)}, u32[]{:S(2)}, u32[]{:S(2)}) collective-permute-start(bf16[64,256]{1,0:T(8,128)(2,1)} %shard_map.58), channel_id=1, source_target_pairs={{0,1},{1,0},{2,3},{3,2},{4,5},{5,4},{6,7},{7,6},{8,9},{9,8},{10,11... | collective-permute-start | bytes 98312 | tf_op jit(solution)/shard_map/ppermute | solution.py:513
  4.4 0.6 copy.13
  6.1 0.7 %collective-permute-start.2 = (bf16[10,64,128]{2,1,0:T(8,128)(2,1)S(1)}, bf16[10,64,128]{2,1,0:T(8,128)(2,1)S(1)}, u32[]{:S(2)}, u32[]{:S(2)}) collective-permute-start(bf16[10,64,128]{2,1,0:T(8,128)(2,1)S(1)} %get-tuple-element.29), channel_id=1, source_target_pairs={{2,4},{4,2},{3,5},{5,3},{10,12},{12,10},{11,13},{13,11},{18,20},{2... | collective-permute-start | bytes 491528 | tf_op jit(solution)/shard_map/ppermute | solution.py:508
  6.8 2.7 %collective-permute-start.1 = (bf16[10,64,128]{2,1,0:T(8,128)(2,1)S(1)}, bf16[10,64,128]{2,1,0:T(8,128)(2,1)S(1)}, u32[]{:S(2)}, u32[]{:S(2)}) collective-permute-start(bf16[10,64,128]{2,1,0:T(8,128)(2,1)S(1)} %get-tuple-element.28), channel_id=1, source_target_pairs={{0,2},{2,0},{4,6},{6,4},{1,3},{3,1},{5,7},{7,5},{8,10},{10,8},{12,... | collective-permute-start | bytes 491528 | tf_op jit(solution)/shard_map/ppermute | solution.py:508
  10.8 0.7 %collective-permute-start.3 = (bf16[5,64,128]{2,1,0:T(8,128)(2,1)S(1)}, bf16[5,64,128]{2,1,0:T(8,128)(2,1)S(1)}, u32[]{:S(2)}, u32[]{:S(2)}) collective-permute-start(bf16[5,64,128]{2,1,0:T(8,128)(2,1)S(1)} %get-tuple-element.32), channel_id=1, source_target_pairs={{0,8},{1,9},{2,10},{3,11},{4,12},{5,13},{6,14},{7,15}} | collective-permute-start | bytes 245768 | tf_op jit(solution)/shard_map/ppermute | solution.py:618
  11.5 0.7 %collective-permute-start.4 = (bf16[4,64,128]{2,1,0:T(8,128)(2,1)S(1)}, bf16[4,64,128]{2,1,0:T(8,128)(2,1)S(1)}, u32[]{:S(2)}, u32[]{:S(2)}) collective-permute-start(bf16[4,64,128]{2,1,0:T(8,128)(2,1)S(1)} %get-tuple-element.33), channel_id=1, source_target_pairs={{0,8},{1,9},{2,10},{3,11},{4,12},{5,13},{6,14},{7,15}} | collective-permute-start | bytes 196616 | tf_op jit(solution)/shard_map/ppermute | solution.py:618
  12.2 2.2 %shard_map.62.refs_1_.refs_0_ = f32[9,64,128]{2,1,0:T(8,128)S(1)} custom-call(f32[512,128]{1,0:T(8,128)S(1)} %bitcast.21, bf16[10,64,128]{2,1,0:T(8,128)(2,1)S(1)} %collective-permute-done.1.pair_ref, bf16[10,64,128]{2,1,0:T(8,128)(2,1)S(1)} %collective-permute-done.2.cross_ref, bf16[64,256]{1,0:T(8,128)(2,1)S(1)} %get-tuple-element.37.side_ref, ...), custom_call_target="tpu_custom_call" | custom-call | flops 830472192 | tf_op jit(solution)/shard_map/pallas_call | solution.py:603
  14.6 1.3 %collective-permute-start.6 = (bf16[4,64,128]{2,1,0:T(8,128)(2,1)S(1)}, bf16[4,64,128]{2,1,0:T(8,128)(2,1)S(1)}, u32[]{:S(2)}, u32[]{:S(2)}) collective-permute-start(bf16[4,64,128]{2,1,0:T(8,128)(2,1)S(1)} %shard_map.64), channel_id=1, source_target_pairs={{8,16},{9,17},{10,18},{11,19},{12,20},{13,21},{14,22},{15,23}} | collective-permute-start | bytes 196616 | tf_op jit(solution)/shard_map/ppermute | solution.py:618
  16.1 1.3 %collective-permute-start.5 = (bf16[5,64,128]{2,1,0:T(8,128)(2,1)S(1)}, bf16[5,64,128]{2,1,0:T(8,128)(2,1)S(1)}, u32[]{:S(2)}, u32[]{:S(2)}) collective-permute-start(bf16[5,64,128]{2,1,0:T(8,128)(2,1)S(1)} %shard_map.63), channel_id=1, source_target_pairs={{8,16},{9,17},{10,18},{11,19},{12,20},{13,21},{14,22},{15,23}} | collective-permute-start | bytes 245768 | tf_op jit(solution)/shard_map/ppermute | solution.py:618
  17.4 3.3 %collective-permute-done.6.s_ref.refs_3_ = bf16[4,64,128]{2,1,0:T(8,128)(2,1)S(1)} collective-permute-done((bf16[4,64,128]{2,1,0:T(8,128)(2,1)S(1)}, bf16[4,64,128]{2,1,0:T(8,128)(2,1)S(1)}, u32[]{:S(2)}, u32[]{:S(2)}) %collective-permute-start.6) | collective-permute-done | bytes 65568 | tf_op jit(solution)/shard_map/ppermute | solution.py:618
  20.9 1.3 %collective-permute-start.8 = (bf16[4,64,128]{2,1,0:T(8,128)(2,1)S(1)}, bf16[4,64,128]{2,1,0:T(8,128)(2,1)S(1)}, u32[]{:S(2)}, u32[]{:S(2)}) collective-permute-start(bf16[4,64,128]{2,1,0:T(8,128)(2,1)S(1)} %shard_map.66), channel_id=1, source_target_pairs={{16,24},{17,25},{18,26},{19,27},{20,28},{21,29},{22,30},{23,31}} | collective-permute-start | bytes 196616 | tf_op jit(solution)/shard_map/ppermute | solution.py:618
  22.6 1.3 %collective-permute-start.7 = (bf16[5,64,128]{2,1,0:T(8,128)(2,1)S(1)}, bf16[5,64,128]{2,1,0:T(8,128)(2,1)S(1)}, u32[]{:S(2)}, u32[]{:S(2)}) collective-permute-start(bf16[5,64,128]{2,1,0:T(8,128)(2,1)S(1)} %shard_map.65), channel_id=1, source_target_pairs={{16,24},{17,25},{18,26},{19,27},{20,28},{21,29},{22,30},{23,31}} | collective-permute-start | bytes 245768 | tf_op jit(solution)/shard_map/ppermute | solution.py:618
  24.0 1.4 %collective-permute-done.7.refs_4_ = bf16[5,64,128]{2,1,0:T(8,128)(2,1)S(1)} collective-permute-done((bf16[5,64,128]{2,1,0:T(8,128)(2,1)S(1)}, bf16[5,64,128]{2,1,0:T(8,128)(2,1)S(1)}, u32[]{:S(2)}, u32[]{:S(2)}) %collective-permute-start.7) | collective-permute-done | bytes 81952 | tf_op jit(solution)/shard_map/ppermute | solution.py:618
  25.4 0.9 %collective-permute-start.10 = (bf16[9,64,128]{2,1,0:T(8,128)(2,1)S(1)}, bf16[9,64,128]{2,1,0:T(8,128)(2,1)S(1)}, u32[]{:S(2)}, u32[]{:S(2)}) collective-permute-start(bf16[9,64,128]{2,1,0:T(8,128)(2,1)S(1)} %shard_map.67.s_ref), channel_id=1, source_target_pairs={{2,4},{4,2},{3,5},{5,3},{10,12},{12,10},{11,13},{13,11},{18,20},{2... | collective-permute-start | bytes 442376 | tf_op jit(solution)/shard_map/ppermute | solution.py:508
  26.3 7.1 %collective-permute-start.9 = (bf16[9,64,128]{2,1,0:T(8,128)(2,1)S(1)}, bf16[9,64,128]{2,1,0:T(8,128)(2,1)S(1)}, u32[]{:S(2)}, u32[]{:S(2)}) collective-permute-start(bf16[9,64,128]{2,1,0:T(8,128)(2,1)S(1)} %shard_map.67.s_ref), channel_id=1, source_target_pairs={{0,2},{2,0},{4,6},{6,4},{1,3},{3,1},{5,7},{7,5},{8,10},{10,8},{12,... | collective-permute-start | bytes 442376 | tf_op jit(solution)/shard_map/ppermute | solution.py:508
  33.4 1.0 %shard_map.68 = (f32[512,128]{1,0:T(8,128)}, f32[16,64,256]{2,1,0:T(8,128)S(1)}) custom-call(f32[512,128]{1,0:T(8,128)S(1)} %bitcast.27, f32[512,128]{1,0:T(8,128)S(1)} %bitcast.31, bf16[9,64,128]{2,1,0:T(8,128)(2,1)S(1)} %shard_map.67.s_ref, bf16[10,64,128]{2,1,0:T(8,128)(2,1)S(1)} %collective-permute-done.1.pair_ref, ...), custom_call_target="tpu_custom_call" | custom-call | flops 2000000000 | tf_op jit(solution)/shard_map/pallas_call | solution.py:646
  34.4 5.4 %shard_map.69 = (f32[8,64,128]{2,1,0:T(8,128)S(1)}, bf16[4,64,128]{2,1,0:T(8,128)(2,1)S(1)}, bf16[4,64,128]{2,1,0:T(8,128)(2,1)S(1)}, bf16[4,8,64,256]{3,2,1,0:T(8,128)(2,1)S(1)}, bf16[4,10,64,128]{3,2,1,0:T(8,128)(2,1)S(1)}) custom-call(f32[512,128]{1,0:T(8,128)S(1)} %bitcast.28, bf16[9,64,128]{2,1,0:T(8,128)(2,1)S(1)} %shard_map.67.s_ref, ...), custom_call_target="tpu_custom_call" | custom-call | flops 2264924160 | tf_op jit(solution)/shard_map/pallas_call | solution.py:653
  39.8 1.3 %collective-permute-start.15 = (bf16[4,64,128]{2,1,0:T(8,128)(2,1)S(1)}, bf16[4,64,128]{2,1,0:T(8,128)(2,1)S(1)}, u32[]{:S(2)}, u32[]{:S(2)}) collective-permute-start(bf16[4,64,128]{2,1,0:T(8,128)(2,1)S(1)} %get-tuple-element.46), channel_id=1, source_target_pairs={{24,16},{25,17},{26,18},{27,19},{28,20},{29,21},{30,22},{31,23}} | collective-permute-start | bytes 196616 | tf_op jit(solution)/shard_map/ppermute | solution.py:618
  41.1 1.3 %collective-permute-start.16 = (bf16[4,64,128]{2,1,0:T(8,128)(2,1)S(1)}, bf16[4,64,128]{2,1,0:T(8,128)(2,1)S(1)}, u32[]{:S(2)}, u32[]{:S(2)}) collective-permute-start(bf16[4,64,128]{2,1,0:T(8,128)(2,1)S(1)} %get-tuple-element.47), channel_id=1, source_target_pairs={{24,16},{25,17},{26,18},{27,19},{28,20},{29,21},{30,22},{31,23}} | collective-permute-start | bytes 196616 | tf_op jit(solution)/shard_map/ppermute | solution.py:618
  42.4 1.1 %shard_map.70 = f32[4,64,576]{2,1,0:T(8,128)S(1)} custom-call(bf16[4,8,64,256]{3,2,1,0:T(8,128)(2,1)S(1)} %get-tuple-element.44.kept_ref, bf16[4,10,64,128]{3,2,1,0:T(8,128)(2,1)S(1)} %get-tuple-element.45.sent_ref), custom_call_target="tpu_custom_call" | custom-call | flops 1000000000 | tf_op jit(solution)/shard_map/pallas_call | solution.py:678
  43.6 3.3 %collective-permute-start.11 = (f32[2,64,576]{2,1,0:T(8,128)S(1)}, f32[2,64,576]{2,1,0:T(8,128)S(1)}, u32[]{:S(2)}, u32[]{:S(2)}) collective-permute-start(f32[2,64,576]{2,1,0:T(8,128)S(1)} %slice_select_fusion), channel_id=1, source_target_pairs={{0,2},{2,0},{4,6},{6,4},{1,3},{3,1},{5,7},{7,5},{8,10},{10,8},{12,... | collective-permute-start | bytes 884744 | tf_op jit(solution)/shard_map/ppermute | solution.py:526
  47.1 1.3 %collective-permute-start.17 = (bf16[4,64,128]{2,1,0:T(8,128)(2,1)S(1)}, bf16[4,64,128]{2,1,0:T(8,128)(2,1)S(1)}, u32[]{:S(2)}, u32[]{:S(2)}) collective-permute-start(bf16[4,64,128]{2,1,0:T(8,128)(2,1)S(1)} %shard_map.71), channel_id=1, source_target_pairs={{16,8},{17,9},{18,10},{19,11},{20,12},{21,13},{22,14},{23,15}} | collective-permute-start | bytes 196616 | tf_op jit(solution)/shard_map/ppermute | solution.py:618
  48.5 1.4 %collective-permute-start.12 = (bf16[2,64,576]{2,1,0:T(8,128)(2,1)S(1)}, bf16[2,64,576]{2,1,0:T(8,128)(2,1)S(1)}, u32[]{:S(2)}, u32[]{:S(2)}) collective-permute-start(bf16[2,64,576]{2,1,0:T(8,128)(2,1)S(1)} %add_convert_fusion.1), channel_id=1, source_target_pairs={{0,1},{1,0},{2,6},{3,7},{4,5},{5,4},{6,2},{7,3},{8,9},{9,8},{10,14... | collective-permute-start | bytes 442376 | tf_op jit(solution)/shard_map/ppermute | solution.py:538
  50.1 1.3 %collective-permute-start.18 = (bf16[4,64,128]{2,1,0:T(8,128)(2,1)S(1)}, bf16[4,64,128]{2,1,0:T(8,128)(2,1)S(1)}, u32[]{:S(2)}, u32[]{:S(2)}) collective-permute-start(bf16[4,64,128]{2,1,0:T(8,128)(2,1)S(1)} %shard_map.72), channel_id=1, source_target_pairs={{16,8},{17,9},{18,10},{19,11},{20,12},{21,13},{22,14},{23,15}} | collective-permute-start | bytes 196616 | tf_op jit(solution)/shard_map/ppermute | solution.py:618
  51.4 1.3 %collective-permute-done.12 = bf16[2,64,576]{2,1,0:T(8,128)(2,1)S(1)} collective-permute-done((bf16[2,64,576]{2,1,0:T(8,128)(2,1)S(1)}, bf16[2,64,576]{2,1,0:T(8,128)(2,1)S(1)}, u32[]{:S(2)}, u32[]{:S(2)}) %collective-permute-start.12) | collective-permute-done | bytes 147488 | tf_op jit(solution)/shard_map/ppermute | solution.py:538
  52.8 1.3 %collective-permute-start.13 = (bf16[2,64,576]{2,1,0:T(8,128)(2,1)S(1)}, bf16[2,64,576]{2,1,0:T(8,128)(2,1)S(1)}, u32[]{:S(2)}, u32[]{:S(2)}) collective-permute-start(bf16[2,64,576]{2,1,0:T(8,128)(2,1)S(1)} %add_convert_fusion), channel_id=1, source_target_pairs={{0,4},{1,5},{2,3},{3,2},{4,0},{5,1},{6,7},{7,6},{8,12},{9,13},{10,... | collective-permute-start | bytes 442376 | tf_op jit(solution)/shard_map/ppermute | solution.py:538
  54.3 0.7 %collective-permute-start.19 = (bf16[4,64,128]{2,1,0:T(8,128)(2,1)S(1)}, bf16[4,64,128]{2,1,0:T(8,128)(2,1)S(1)}, u32[]{:S(2)}, u32[]{:S(2)}) collective-permute-start(bf16[4,64,128]{2,1,0:T(8,128)(2,1)S(1)} %shard_map.73), channel_id=1, source_target_pairs={{8,0},{9,1},{10,2},{11,3},{12,4},{13,5},{14,6},{15,7}} | collective-permute-start | bytes 196616 | tf_op jit(solution)/shard_map/ppermute | solution.py:618
  55.0 2.3 %collective-permute-done.13 = bf16[2,64,576]{2,1,0:T(8,128)(2,1)S(1)} collective-permute-done((bf16[2,64,576]{2,1,0:T(8,128)(2,1)S(1)}, bf16[2,64,576]{2,1,0:T(8,128)(2,1)S(1)}, u32[]{:S(2)}, u32[]{:S(2)}) %collective-permute-start.13) | collective-permute-done | bytes 147488 | tf_op jit(solution)/shard_map/ppermute | solution.py:538
  57.3 4.6 %collective-permute-start.14 = (f32[2,64,576]{2,1,0:T(8,128)S(1)}, f32[2,64,576]{2,1,0:T(8,128)S(1)}, u32[]{:S(2)}, u32[]{:S(2)}) collective-permute-start(f32[2,64,576]{2,1,0:T(8,128)S(1)} %convert_add_fusion.half_ref), channel_id=1, source_target_pairs={{0,2},{2,0},{4,6},{6,4},{1,3},{3,1},{5,7},{7,5},{8,10},{10,8},{12,... | collective-permute-start | bytes 884744 | tf_op jit(solution)/shard_map/ppermute | solution.py:540
  62.2 0.7 %collective-permute-start.20 = (bf16[4,64,128]{2,1,0:T(8,128)(2,1)S(1)}, bf16[4,64,128]{2,1,0:T(8,128)(2,1)S(1)}, u32[]{:S(2)}, u32[]{:S(2)}) collective-permute-start(bf16[4,64,128]{2,1,0:T(8,128)(2,1)S(1)} %shard_map.74), channel_id=1, source_target_pairs={{8,0},{9,1},{10,2},{11,3},{12,4},{13,5},{14,6},{15,7}} | collective-permute-start | bytes 196616 | tf_op jit(solution)/shard_map/ppermute | solution.py:618
  63.2 1.0 %shard_map.75 = (f32[512,128]{1,0:T(8,128)}, f32[4,64,576]{2,1,0:T(8,128)}) custom-call(f32[512,128]{1,0:T(8,128)S(1)} %bitcast.36, f32[2,64,576]{2,1,0:T(8,128)S(1)} %convert_add_fusion.half_ref, f32[2,64,576]{2,1,0:T(8,128)S(1)} %collective-permute-done.14.other_ref, bf16[4,64,128]{2,1,0:T(8,128)(2,1)S(1)} %collective-permute-done.15.s_ref.refs_0_, ...), custom_call_target="tpu_custom_call" | custom-call | flops 10000000000 | tf_op jit(solution)/shard_map/pallas_call | solution.py:684
  (51 shorter events, 5.4 us)
Async XLA Ops:
  0.6 3.3 %copy-start.2 = (bf16[4,64,576]{2,1,0:T(8,128)(2,1)S(1)}, bf16[4,64,576]{2,1,0:T(8,128)(2,1)}, u32[]{:S(2)}) copy-start(bf16[4,64,576]{2,1,0:T(8,128)(2,1)} %param.5) | copy-start | bytes 884740
  2.6 3.0 %collective-permute-start = (bf16[64,256]{1,0:T(8,128)(2,1)}, bf16[64,256]{1,0:T(8,128)(2,1)S(1)}, u32[]{:S(2)}, u32[]{:S(2)}) collective-permute-start(bf16[64,256]{1,0:T(8,128)(2,1)} %shard_map.58), channel_id=1, source_target_pairs={{0,1},{1,0},{2,3},{3,2},{4,5},{5,4},{6,7},{7,6},{8,9},{9,8},{10,11... | collective-permute-start | bytes 98312 | tf_op jit(solution)/shard_map/ppermute | solution.py:513
  5.0 1.0 %copy-start = (f32[1,64,8,128]{3,2,1,0:T(8,128)S(1)}, f32[1,64,8,128]{3,2,1,0:T(8,128)}, u32[]{:S(2)}) copy-start(f32[1,64,8,128]{3,2,1,0:T(8,128)} %param.3) | copy-start | bytes 786436
  5.0 1.0 %copy-start.1 = (f32[1,64,8,128]{3,2,1,0:T(8,128)S(1)}, f32[1,64,8,128]{3,2,1,0:T(8,128)}, u32[]{:S(2)}) copy-start(f32[1,64,8,128]{3,2,1,0:T(8,128)} %param.4) | copy-start | bytes 786436
  6.1 4.6 %collective-permute-start.2 = (bf16[10,64,128]{2,1,0:T(8,128)(2,1)S(1)}, bf16[10,64,128]{2,1,0:T(8,128)(2,1)S(1)}, u32[]{:S(2)}, u32[]{:S(2)}) collective-permute-start(bf16[10,64,128]{2,1,0:T(8,128)(2,1)S(1)} %get-tuple-element.29), channel_id=1, source_target_pairs={{2,4},{4,2},{3,5},{5,3},{10,12},{12,10},{11,13},{13,11},{18,20},{2... | collective-permute-start | bytes 491528 | tf_op jit(solution)/shard_map/ppermute | solution.py:508
  6.8 4.0 %collective-permute-start.1 = (bf16[10,64,128]{2,1,0:T(8,128)(2,1)S(1)}, bf16[10,64,128]{2,1,0:T(8,128)(2,1)S(1)}, u32[]{:S(2)}, u32[]{:S(2)}) collective-permute-start(bf16[10,64,128]{2,1,0:T(8,128)(2,1)S(1)} %get-tuple-element.28), channel_id=1, source_target_pairs={{0,2},{2,0},{4,6},{6,4},{1,3},{3,1},{5,7},{7,5},{8,10},{10,8},{12,... | collective-permute-start | bytes 491528 | tf_op jit(solution)/shard_map/ppermute | solution.py:508
  10.8 5.0 %collective-permute-start.3 = (bf16[5,64,128]{2,1,0:T(8,128)(2,1)S(1)}, bf16[5,64,128]{2,1,0:T(8,128)(2,1)S(1)}, u32[]{:S(2)}, u32[]{:S(2)}) collective-permute-start(bf16[5,64,128]{2,1,0:T(8,128)(2,1)S(1)} %get-tuple-element.32), channel_id=1, source_target_pairs={{0,8},{1,9},{2,10},{3,11},{4,12},{5,13},{6,14},{7,15}} | collective-permute-start | bytes 245768 | tf_op jit(solution)/shard_map/ppermute | solution.py:618
  11.5 2.9 %collective-permute-start.4 = (bf16[4,64,128]{2,1,0:T(8,128)(2,1)S(1)}, bf16[4,64,128]{2,1,0:T(8,128)(2,1)S(1)}, u32[]{:S(2)}, u32[]{:S(2)}) collective-permute-start(bf16[4,64,128]{2,1,0:T(8,128)(2,1)S(1)} %get-tuple-element.33), channel_id=1, source_target_pairs={{0,8},{1,9},{2,10},{3,11},{4,12},{5,13},{6,14},{7,15}} | collective-permute-start | bytes 196616 | tf_op jit(solution)/shard_map/ppermute | solution.py:618
  14.6 6.1 %collective-permute-start.6 = (bf16[4,64,128]{2,1,0:T(8,128)(2,1)S(1)}, bf16[4,64,128]{2,1,0:T(8,128)(2,1)S(1)}, u32[]{:S(2)}, u32[]{:S(2)}) collective-permute-start(bf16[4,64,128]{2,1,0:T(8,128)(2,1)S(1)} %shard_map.64), channel_id=1, source_target_pairs={{8,16},{9,17},{10,18},{11,19},{12,20},{13,21},{14,22},{15,23}} | collective-permute-start | bytes 196616 | tf_op jit(solution)/shard_map/ppermute | solution.py:618
  16.1 6.3 %collective-permute-start.5 = (bf16[5,64,128]{2,1,0:T(8,128)(2,1)S(1)}, bf16[5,64,128]{2,1,0:T(8,128)(2,1)S(1)}, u32[]{:S(2)}, u32[]{:S(2)}) collective-permute-start(bf16[5,64,128]{2,1,0:T(8,128)(2,1)S(1)} %shard_map.63), channel_id=1, source_target_pairs={{8,16},{9,17},{10,18},{11,19},{12,20},{13,21},{14,22},{15,23}} | collective-permute-start | bytes 245768 | tf_op jit(solution)/shard_map/ppermute | solution.py:618
  20.9 3.1 %collective-permute-start.8 = (bf16[4,64,128]{2,1,0:T(8,128)(2,1)S(1)}, bf16[4,64,128]{2,1,0:T(8,128)(2,1)S(1)}, u32[]{:S(2)}, u32[]{:S(2)}) collective-permute-start(bf16[4,64,128]{2,1,0:T(8,128)(2,1)S(1)} %shard_map.66), channel_id=1, source_target_pairs={{16,24},{17,25},{18,26},{19,27},{20,28},{21,29},{22,30},{23,31}} | collective-permute-start | bytes 196616 | tf_op jit(solution)/shard_map/ppermute | solution.py:618
  22.6 2.8 %collective-permute-start.7 = (bf16[5,64,128]{2,1,0:T(8,128)(2,1)S(1)}, bf16[5,64,128]{2,1,0:T(8,128)(2,1)S(1)}, u32[]{:S(2)}, u32[]{:S(2)}) collective-permute-start(bf16[5,64,128]{2,1,0:T(8,128)(2,1)S(1)} %shard_map.65), channel_id=1, source_target_pairs={{16,24},{17,25},{18,26},{19,27},{20,28},{21,29},{22,30},{23,31}} | collective-permute-start | bytes 245768 | tf_op jit(solution)/shard_map/ppermute | solution.py:618
  25.4 8.9 %collective-permute-start.10 = (bf16[9,64,128]{2,1,0:T(8,128)(2,1)S(1)}, bf16[9,64,128]{2,1,0:T(8,128)(2,1)S(1)}, u32[]{:S(2)}, u32[]{:S(2)}) collective-permute-start(bf16[9,64,128]{2,1,0:T(8,128)(2,1)S(1)} %shard_map.67.s_ref), channel_id=1, source_target_pairs={{2,4},{4,2},{3,5},{5,3},{10,12},{12,10},{11,13},{13,11},{18,20},{2... | collective-permute-start | bytes 442376 | tf_op jit(solution)/shard_map/ppermute | solution.py:508
  26.3 8.1 %collective-permute-start.9 = (bf16[9,64,128]{2,1,0:T(8,128)(2,1)S(1)}, bf16[9,64,128]{2,1,0:T(8,128)(2,1)S(1)}, u32[]{:S(2)}, u32[]{:S(2)}) collective-permute-start(bf16[9,64,128]{2,1,0:T(8,128)(2,1)S(1)} %shard_map.67.s_ref), channel_id=1, source_target_pairs={{0,2},{2,0},{4,6},{6,4},{1,3},{3,1},{5,7},{7,5},{8,10},{10,8},{12,... | collective-permute-start | bytes 442376 | tf_op jit(solution)/shard_map/ppermute | solution.py:508
  39.8 7.1 %collective-permute-start.15 = (bf16[4,64,128]{2,1,0:T(8,128)(2,1)S(1)}, bf16[4,64,128]{2,1,0:T(8,128)(2,1)S(1)}, u32[]{:S(2)}, u32[]{:S(2)}) collective-permute-start(bf16[4,64,128]{2,1,0:T(8,128)(2,1)S(1)} %get-tuple-element.46), channel_id=1, source_target_pairs={{24,16},{25,17},{26,18},{27,19},{28,20},{29,21},{30,22},{31,23}} | collective-permute-start | bytes 196616 | tf_op jit(solution)/shard_map/ppermute | solution.py:618
  41.1 8.8 %collective-permute-start.16 = (bf16[4,64,128]{2,1,0:T(8,128)(2,1)S(1)}, bf16[4,64,128]{2,1,0:T(8,128)(2,1)S(1)}, u32[]{:S(2)}, u32[]{:S(2)}) collective-permute-start(bf16[4,64,128]{2,1,0:T(8,128)(2,1)S(1)} %get-tuple-element.47), channel_id=1, source_target_pairs={{24,16},{25,17},{26,18},{27,19},{28,20},{29,21},{30,22},{31,23}} | collective-permute-start | bytes 196616 | tf_op jit(solution)/shard_map/ppermute | solution.py:618
  43.6 4.9 %collective-permute-start.11 = (f32[2,64,576]{2,1,0:T(8,128)S(1)}, f32[2,64,576]{2,1,0:T(8,128)S(1)}, u32[]{:S(2)}, u32[]{:S(2)}) collective-permute-start(f32[2,64,576]{2,1,0:T(8,128)S(1)} %slice_select_fusion), channel_id=1, source_target_pairs={{0,2},{2,0},{4,6},{6,4},{1,3},{3,1},{5,7},{7,5},{8,10},{10,8},{12,... | collective-permute-start | bytes 884744 | tf_op jit(solution)/shard_map/ppermute | solution.py:526
  47.1 7.0 %collective-permute-start.17 = (bf16[4,64,128]{2,1,0:T(8,128)(2,1)S(1)}, bf16[4,64,128]{2,1,0:T(8,128)(2,1)S(1)}, u32[]{:S(2)}, u32[]{:S(2)}) collective-permute-start(bf16[4,64,128]{2,1,0:T(8,128)(2,1)S(1)} %shard_map.71), channel_id=1, source_target_pairs={{16,8},{17,9},{18,10},{19,11},{20,12},{21,13},{22,14},{23,15}} | collective-permute-start | bytes 196616 | tf_op jit(solution)/shard_map/ppermute | solution.py:618
  48.5 4.2 %collective-permute-start.12 = (bf16[2,64,576]{2,1,0:T(8,128)(2,1)S(1)}, bf16[2,64,576]{2,1,0:T(8,128)(2,1)S(1)}, u32[]{:S(2)}, u32[]{:S(2)}) collective-permute-start(bf16[2,64,576]{2,1,0:T(8,128)(2,1)S(1)} %add_convert_fusion.1), channel_id=1, source_target_pairs={{0,1},{1,0},{2,6},{3,7},{4,5},{5,4},{6,2},{7,3},{8,9},{9,8},{10,14... | collective-permute-start | bytes 442376 | tf_op jit(solution)/shard_map/ppermute | solution.py:538
  50.1 11.8 %collective-permute-start.18 = (bf16[4,64,128]{2,1,0:T(8,128)(2,1)S(1)}, bf16[4,64,128]{2,1,0:T(8,128)(2,1)S(1)}, u32[]{:S(2)}, u32[]{:S(2)}) collective-permute-start(bf16[4,64,128]{2,1,0:T(8,128)(2,1)S(1)} %shard_map.72), channel_id=1, source_target_pairs={{16,8},{17,9},{18,10},{19,11},{20,12},{21,13},{22,14},{23,15}} | collective-permute-start | bytes 196616 | tf_op jit(solution)/shard_map/ppermute | solution.py:618
  52.8 4.5 %collective-permute-start.13 = (bf16[2,64,576]{2,1,0:T(8,128)(2,1)S(1)}, bf16[2,64,576]{2,1,0:T(8,128)(2,1)S(1)}, u32[]{:S(2)}, u32[]{:S(2)}) collective-permute-start(bf16[2,64,576]{2,1,0:T(8,128)(2,1)S(1)} %add_convert_fusion), channel_id=1, source_target_pairs={{0,4},{1,5},{2,3},{3,2},{4,0},{5,1},{6,7},{7,6},{8,12},{9,13},{10,... | collective-permute-start | bytes 442376 | tf_op jit(solution)/shard_map/ppermute | solution.py:538
  54.3 8.6 %collective-permute-start.19 = (bf16[4,64,128]{2,1,0:T(8,128)(2,1)S(1)}, bf16[4,64,128]{2,1,0:T(8,128)(2,1)S(1)}, u32[]{:S(2)}, u32[]{:S(2)}) collective-permute-start(bf16[4,64,128]{2,1,0:T(8,128)(2,1)S(1)} %shard_map.73), channel_id=1, source_target_pairs={{8,0},{9,1},{10,2},{11,3},{12,4},{13,5},{14,6},{15,7}} | collective-permute-start | bytes 196616 | tf_op jit(solution)/shard_map/ppermute | solution.py:618
  57.3 5.9 %collective-permute-start.14 = (f32[2,64,576]{2,1,0:T(8,128)S(1)}, f32[2,64,576]{2,1,0:T(8,128)S(1)}, u32[]{:S(2)}, u32[]{:S(2)}) collective-permute-start(f32[2,64,576]{2,1,0:T(8,128)S(1)} %convert_add_fusion.half_ref), channel_id=1, source_target_pairs={{0,2},{2,0},{4,6},{6,4},{1,3},{3,1},{5,7},{7,5},{8,10},{10,8},{12,... | collective-permute-start | bytes 884744 | tf_op jit(solution)/shard_map/ppermute | solution.py:540
  62.2 0.7 %collective-permute-start.20 = (bf16[4,64,128]{2,1,0:T(8,128)(2,1)S(1)}, bf16[4,64,128]{2,1,0:T(8,128)(2,1)S(1)}, u32[]{:S(2)}, u32[]{:S(2)}) collective-permute-start(bf16[4,64,128]{2,1,0:T(8,128)(2,1)S(1)} %shard_map.74), channel_id=1, source_target_pairs={{8,0},{9,1},{10,2},{11,3},{12,4},{13,5},{14,6},{15,7}} | collective-permute-start | bytes 196616 | tf_op jit(solution)/shard_map/ppermute | solution.py:618

commit v15 on v14

--- a/solution.py
+++ b/solution.py
@@ -140,7 +140,8 @@
 
 
 def message_body(
-    c_ref, q_ref, left_ref, right_ref, pair_ref, cross_ref, side_ref, *, channels, rows, depth
+    c_ref, q_ref, left_ref, right_ref, pair_ref, cross_ref, side_ref, strip_ref,
+    *, channels, rows, depth,
 ):
     cols = c_ref.shape[1]
     _, _, left, right = flags()
@@ -148,6 +149,9 @@
     edges = ((c_edge, 0, middle), (q_edge, middle, 2 * cols))
     side = join_edges(left_ref[...], right_ref[...], left, right, edges).astype(bf16)
     side_ref[...] = side
+    wide = side.astype(f32)
+    image = [side_lanes(wide, c_edge, 0, row) for row in range(rows)]
+    strip_ref[...] = fold_edges(image, 2 * depth, 0, jnp.zeros(strip_ref.shape, f32))
     even = even_row()
     for which, ref in enumerate((c_ref, q_ref)):
         for row in range(depth):
@@ -175,13 +179,6 @@
         return jnp.where(
             self.even, self.pair[place].astype(f32), self.cross[place].astype(f32)
         )
-
-
-def halo_strip_body(side_ref, strip_ref, *, rows, depth):
-    (edge, low), _ = layout(rows, depth)
-    side = side_ref[...].astype(f32)
-    image = [side_lanes(side, edge, low, row) for row in range(rows)]
-    strip_ref[...] = fold_edges(image, 2 * depth, 0, jnp.zeros(strip_ref.shape, f32))
 
 
 def strips_of(get, depth):
@@ -573,14 +570,11 @@
         out_specs=HERE,
     )(c_flat, q_flat)
     left, right = from_sides(edges)
-    to_pair, to_cross, side = call(
+    to_pair, to_cross, side, strip = call(
         functools.partial(message_body, depth=depth, **sizes),
-        (message_b, message_b, wide_b),
+        (message_b, message_b, wide_b, strip_f),
     )(c_flat, q_flat, left, right)
     pair, cross = exchanged(to_pair, to_cross)
-    strip = call(
-        functools.partial(halo_strip_body, rows=rows, depth=depth), strip_f, flops=10**9
-    )(side)
 
     taps = weights.reshape(depth, channels, 3, 3, channels)
     w_fwd = jnp.transpose(taps, (0, 3, 1, 2, 4)).reshape(depth, 3 * channels, 3 * channels)
@@ -611,21 +605,25 @@
             flops=mac * 44,
         )(*inputs)
 
-    def chain(pieces, target, matrix, order):
+    def chain(pieces, target, matrix, order, in_turn):
         sendings = [piece[0] for piece in pieces]
         arrivals = []
         for turn, step in enumerate(order):
             arrived = [lax.ppermute(sending, "layer", [step]) for sending in sendings]
             arrivals += arrived
             if turn < len(order) - 1:
-                sendings = [
-                    call(
-                        functools.partial(hop_body, start=start, **sizes),
-                        jax.ShapeDtypeStruct(value.shape, bf16),
-                        flops=10**10,
-                    )(value, *base, target, matrix)
-                    for value, (_, start, base) in zip(arrived, pieces)
-                ]
+                sendings = []
+                for value, (_, start, base) in zip(arrived, pieces):
+                    if in_turn and sendings:
+                        value = lax.optimization_barrier((value, sendings[0]))[0]
+                    size = len(base) - 1 + half
+                    sendings.append(
+                        call(
+                            functools.partial(hop_body, start=start, **sizes),
+                            jax.ShapeDtypeStruct((size, channels, cols), bf16),
+                            flops=10**10,
+                        )(value, *base, target, matrix)
+                    )
         return arrivals
 
     inputs = (c_flat, pair, cross, side, w_fwd)
@@ -637,6 +635,7 @@
         f,
         m_fwd,
         [(k, k + 1) for k in range(groups - 1)],
+        True,
     )
     s = call(functools.partial(settle_body, **sizes), more_b)(c_flat, strip, *arrivals)
     s_pair, s_cross = exchanged(s, s)
@@ -674,6 +673,7 @@
         g,
         m_back,
         [(k, k - 1) for k in range(groups - 1, 0, -1)],
+        False,
     )
     grads = call(
         functools.partial(grad_body, depth=depth, **sizes),

time: 64.8 us -> 63.8 us (0.985)
  other arithmetic: 0.31 us -> 1.52 us
  starting transfers between devices: 36.3 us -> 35.3 us
  waiting for transfers between devices: 9.01 us -> 8.35 us
    ppermute x12, waiting for transfers between devices: 4.86 us -> 3.6 us  [chain(): arrived = [lax.ppermute(sending, 'layer', [step]) for sending in sendings]]
    ppermute x2, starting transfers between devices: 9.79 us -> 8.6 us  [exchanged(): lax.ppermute(to_pair, 'row', pairs)]
  transfers between devices with their start and end apart: 21 -> 21, of which waited for: 7 -> 6; matrix products, arithmetic and copies ran while one was open for 4% -> 6% of each run, Pallas kernels for 9% -> 9%
where the time goes in v15:
time: 63.8 us; the launch traced here: 63.4 us
  starting transfers between devices  35.3 us (55%)
  Pallas kernels  14.6 us (23%)
  waiting for transfers between devices  8.35 us (13%)
  local copies, waits for them, and re-layouts  2.45 us (4%)
  other arithmetic  1.52 us (2%)
  between operations  1.24 us (2%)
    ppermute x12, starting transfers between devices, chain(): arrived = [lax.ppermute(sending, 'layer', [step]) for sending in sendings]  13.1 us
    ppermute x2, starting transfers between devices, exchanged(): lax.ppermute(to_pair, 'row', pairs)  8.6 us
    pallas_call x1, Pallas kernels, local(): call(functools.partial(second_body, depth=depth, **sizes), (tile_f, lower...  5.44 us
    ppermute x1, starting transfers between devices, total_over_tiles(): return (value, lax.ppermute(value, 'row', pair))  4.64 us
    ppermute x2, waiting for transfers between devices, total_over_tiles(): arrived = lax.ppermute(rounded, ('row', 'col'), pairs)  3.65 us
    ppermute x12, waiting for transfers between devices, chain(): arrived = [lax.ppermute(sending, 'layer', [step]) for sending in sendings]  3.6 us
    ppermute x1, starting transfers between devices, total_over_tiles(): value = own + lax.ppermute(sent, 'row', pair)  3.35 us
    ppermute x2, starting transfers between devices, total_over_tiles(): arrived = lax.ppermute(rounded, ('row', 'col'), pairs)  2.71 us
  transfers between devices with their start and end apart: 21, of which 6 were waited for; matrix products, arithmetic and copies ran while one was open for 6% of the time, Pallas kernels for 9%

profile of v15, /device:TPU:19, one launch (start us, length us, event | category | flops | bytes accessed | tf_op | source)
XLA Modules:
  0.0 63.4 jit_solution(3009900690545505123)
XLA Ops:
  0.6 1.9 %shard_map.58 = bf16[64,256]{1,0:T(8,128)(2,1)} custom-call(f32[512,128]{1,0:T(8,128)} %bitcast.18, f32[512,128]{1,0:T(8,128)} %bitcast.29), custom_call_target="tpu_custom_call" | custom-call | tf_op jit(solution)/shard_map/pallas_call | solution.py:560
  2.6 1.3 %collective-permute-start = (bf16[64,256]{1,0:T(8,128)(2,1)}, bf16[64,256]{1,0:T(8,128)(2,1)S(1)}, u32[]{:S(2)}, u32[]{:S(2)}) collective-permute-start(bf16[64,256]{1,0:T(8,128)(2,1)} %shard_map.58), channel_id=1, source_target_pairs={{0,1},{1,0},{2,3},{3,2},{4,5},{5,4},{6,7},{7,6},{8,9},{9,8},{10,11... | collective-permute-start | bytes 98312 | tf_op jit(solution)/shard_map/ppermute | solution.py:510
  4.9 0.7 %collective-permute-done.left_ref.right_ref = bf16[64,256]{1,0:T(8,128)(2,1)S(1)} collective-permute-done((bf16[64,256]{1,0:T(8,128)(2,1)}, bf16[64,256]{1,0:T(8,128)(2,1)S(1)}, u32[]{:S(2)}, u32[]{:S(2)}) %collective-permute-start) | collective-permute-done | bytes 32800 | tf_op jit(solution)/shard_map/ppermute | solution.py:510
  5.9 0.7 %collective-permute-start.2 = (bf16[10,64,128]{2,1,0:T(8,128)(2,1)S(1)}, bf16[10,64,128]{2,1,0:T(8,128)(2,1)S(1)}, u32[]{:S(2)}, u32[]{:S(2)}) collective-permute-start(bf16[10,64,128]{2,1,0:T(8,128)(2,1)S(1)} %get-tuple-element.32), channel_id=1, source_target_pairs={{2,4},{4,2},{3,5},{5,3},{10,12},{12,10},{11,13},{13,11},{18,20},{2... | collective-permute-start | bytes 491528 | tf_op jit(solution)/shard_map/ppermute | solution.py:505
  6.6 3.1 %collective-permute-start.1 = (bf16[10,64,128]{2,1,0:T(8,128)(2,1)S(1)}, bf16[10,64,128]{2,1,0:T(8,128)(2,1)S(1)}, u32[]{:S(2)}, u32[]{:S(2)}) collective-permute-start(bf16[10,64,128]{2,1,0:T(8,128)(2,1)S(1)} %get-tuple-element.31), channel_id=1, source_target_pairs={{0,2},{2,0},{4,6},{6,4},{1,3},{3,1},{5,7},{7,5},{8,10},{10,8},{12,... | collective-permute-start | bytes 491528 | tf_op jit(solution)/shard_map/ppermute | solution.py:505
  12.4 0.7 %collective-permute-start.3 = (bf16[5,64,128]{2,1,0:T(8,128)(2,1)S(1)}, bf16[5,64,128]{2,1,0:T(8,128)(2,1)S(1)}, u32[]{:S(2)}, u32[]{:S(2)}) collective-permute-start(bf16[5,64,128]{2,1,0:T(8,128)(2,1)S(1)} %get-tuple-element.36), channel_id=1, source_target_pairs={{0,8},{1,9},{2,10},{3,11},{4,12},{5,13},{6,14},{7,15}} | collective-permute-start | bytes 245768 | tf_op jit(solution)/shard_map/ppermute | solution.py:612
  13.2 0.7 %collective-permute-start.4 = (bf16[4,64,128]{2,1,0:T(8,128)(2,1)S(1)}, bf16[4,64,128]{2,1,0:T(8,128)(2,1)S(1)}, u32[]{:S(2)}, u32[]{:S(2)}) collective-permute-start(bf16[4,64,128]{2,1,0:T(8,128)(2,1)S(1)} %get-tuple-element.37), channel_id=1, source_target_pairs={{0,8},{1,9},{2,10},{3,11},{4,12},{5,13},{6,14},{7,15}} | collective-permute-start | bytes 196616 | tf_op jit(solution)/shard_map/ppermute | solution.py:612
  13.9 2.2 %shard_map.61.refs_1_.refs_0_ = f32[9,64,128]{2,1,0:T(8,128)S(1)} custom-call(f32[512,128]{1,0:T(8,128)S(1)} %bitcast.21, bf16[10,64,128]{2,1,0:T(8,128)(2,1)S(1)} %collective-permute-done.1.pair_ref, bf16[10,64,128]{2,1,0:T(8,128)(2,1)S(1)} %collective-permute-done.2.cross_ref, bf16[64,256]{1,0:T(8,128)(2,1)S(1)} %get-tuple-element.41.side_ref, ...), custom_call_target="tpu_custom_call" | custom-call | flops 830472192 | tf_op jit(solution)/shard_map/pallas_call | solution.py:597
  16.3 1.3 %collective-permute-start.5 = (bf16[5,64,128]{2,1,0:T(8,128)(2,1)S(1)}, bf16[5,64,128]{2,1,0:T(8,128)(2,1)S(1)}, u32[]{:S(2)}, u32[]{:S(2)}) collective-permute-start(bf16[5,64,128]{2,1,0:T(8,128)(2,1)S(1)} %shard_map.62), channel_id=1, source_target_pairs={{8,16},{9,17},{10,18},{11,19},{12,20},{13,21},{14,22},{15,23}} | collective-permute-start | bytes 245768 | tf_op jit(solution)/shard_map/ppermute | solution.py:612
  17.8 1.3 %collective-permute-start.6 = (bf16[4,64,128]{2,1,0:T(8,128)(2,1)S(1)}, bf16[4,64,128]{2,1,0:T(8,128)(2,1)S(1)}, u32[]{:S(2)}, u32[]{:S(2)}) collective-permute-start(bf16[4,64,128]{2,1,0:T(8,128)(2,1)S(1)} %shard_map.63), channel_id=1, source_target_pairs={{8,16},{9,17},{10,18},{11,19},{12,20},{13,21},{14,22},{15,23}} | collective-permute-start | bytes 196616 | tf_op jit(solution)/shard_map/ppermute | solution.py:612
  19.1 2.4 %collective-permute-done.5.s_ref.refs_2_ = bf16[5,64,128]{2,1,0:T(8,128)(2,1)S(1)} collective-permute-done((bf16[5,64,128]{2,1,0:T(8,128)(2,1)S(1)}, bf16[5,64,128]{2,1,0:T(8,128)(2,1)S(1)}, u32[]{:S(2)}, u32[]{:S(2)}) %collective-permute-start.5) | collective-permute-done | bytes 81952 | tf_op jit(solution)/shard_map/ppermute | solution.py:612
  21.7 1.4 %collective-permute-start.7 = (bf16[5,64,128]{2,1,0:T(8,128)(2,1)S(1)}, bf16[5,64,128]{2,1,0:T(8,128)(2,1)S(1)}, u32[]{:S(2)}, u32[]{:S(2)}) collective-permute-start(bf16[5,64,128]{2,1,0:T(8,128)(2,1)S(1)} %shard_map.64), channel_id=1, source_target_pairs={{16,24},{17,25},{18,26},{19,27},{20,28},{21,29},{22,30},{23,31}} | collective-permute-start | bytes 245768 | tf_op jit(solution)/shard_map/ppermute | solution.py:612
  23.4 1.3 %collective-permute-start.8 = (bf16[4,64,128]{2,1,0:T(8,128)(2,1)S(1)}, bf16[4,64,128]{2,1,0:T(8,128)(2,1)S(1)}, u32[]{:S(2)}, u32[]{:S(2)}) collective-permute-start(bf16[4,64,128]{2,1,0:T(8,128)(2,1)S(1)} %shard_map.65), channel_id=1, source_target_pairs={{16,24},{17,25},{18,26},{19,27},{20,28},{21,29},{22,30},{23,31}} | collective-permute-start | bytes 196616 | tf_op jit(solution)/shard_map/ppermute | solution.py:612
  24.8 1.2 %collective-permute-done.8.refs_5_ = bf16[4,64,128]{2,1,0:T(8,128)(2,1)S(1)} collective-permute-done((bf16[4,64,128]{2,1,0:T(8,128)(2,1)S(1)}, bf16[4,64,128]{2,1,0:T(8,128)(2,1)S(1)}, u32[]{:S(2)}, u32[]{:S(2)}) %collective-permute-start.8) | collective-permute-done | bytes 65568 | tf_op jit(solution)/shard_map/ppermute | solution.py:612
  26.1 0.9 %collective-permute-start.10 = (bf16[9,64,128]{2,1,0:T(8,128)(2,1)S(1)}, bf16[9,64,128]{2,1,0:T(8,128)(2,1)S(1)}, u32[]{:S(2)}, u32[]{:S(2)}) collective-permute-start(bf16[9,64,128]{2,1,0:T(8,128)(2,1)S(1)} %shard_map.66.s_ref), channel_id=1, source_target_pairs={{2,4},{4,2},{3,5},{5,3},{10,12},{12,10},{11,13},{13,11},{18,20},{2... | collective-permute-start | bytes 442376 | tf_op jit(solution)/shard_map/ppermute | solution.py:505
  26.9 5.5 %collective-permute-start.9 = (bf16[9,64,128]{2,1,0:T(8,128)(2,1)S(1)}, bf16[9,64,128]{2,1,0:T(8,128)(2,1)S(1)}, u32[]{:S(2)}, u32[]{:S(2)}) collective-permute-start(bf16[9,64,128]{2,1,0:T(8,128)(2,1)S(1)} %shard_map.66.s_ref), channel_id=1, source_target_pairs={{0,2},{2,0},{4,6},{6,4},{1,3},{3,1},{5,7},{7,5},{8,10},{10,8},{12,... | collective-permute-start | bytes 442376 | tf_op jit(solution)/shard_map/ppermute | solution.py:505
  32.4 1.0 %shard_map.67 = (f32[512,128]{1,0:T(8,128)}, f32[16,64,256]{2,1,0:T(8,128)S(1)}) custom-call(f32[512,128]{1,0:T(8,128)S(1)} %bitcast.27, f32[512,128]{1,0:T(8,128)S(1)} %bitcast.31, bf16[9,64,128]{2,1,0:T(8,128)(2,1)S(1)} %shard_map.66.s_ref, bf16[10,64,128]{2,1,0:T(8,128)(2,1)S(1)} %collective-permute-done.1.pair_ref, ...), custom_call_target="tpu_custom_call" | custom-call | flops 2000000000 | tf_op jit(solution)/shard_map/pallas_call | solution.py:645
  33.4 5.4 %shard_map.68 = (f32[8,64,128]{2,1,0:T(8,128)S(1)}, bf16[4,64,128]{2,1,0:T(8,128)(2,1)S(1)}, bf16[4,64,128]{2,1,0:T(8,128)(2,1)S(1)}, bf16[4,8,64,256]{3,2,1,0:T(8,128)(2,1)S(1)}, bf16[4,10,64,128]{3,2,1,0:T(8,128)(2,1)S(1)}) custom-call(f32[512,128]{1,0:T(8,128)S(1)} %bitcast.28, bf16[9,64,128]{2,1,0:T(8,128)(2,1)S(1)} %shard_map.66.s_ref, ...), custom_call_target="tpu_custom_call" | custom-call | flops 2264924160 | tf_op jit(solution)/shard_map/pallas_call | solution.py:652
  38.9 1.3 %collective-permute-start.15 = (bf16[4,64,128]{2,1,0:T(8,128)(2,1)S(1)}, bf16[4,64,128]{2,1,0:T(8,128)(2,1)S(1)}, u32[]{:S(2)}, u32[]{:S(2)}) collective-permute-start(bf16[4,64,128]{2,1,0:T(8,128)(2,1)S(1)} %get-tuple-element.52), channel_id=1, source_target_pairs={{24,16},{25,17},{26,18},{27,19},{28,20},{29,21},{30,22},{31,23}} | collective-permute-start | bytes 196616 | tf_op jit(solution)/shard_map/ppermute | solution.py:612
  40.2 1.3 %collective-permute-start.16 = (bf16[4,64,128]{2,1,0:T(8,128)(2,1)S(1)}, bf16[4,64,128]{2,1,0:T(8,128)(2,1)S(1)}, u32[]{:S(2)}, u32[]{:S(2)}) collective-permute-start(bf16[4,64,128]{2,1,0:T(8,128)(2,1)S(1)} %get-tuple-element.53), channel_id=1, source_target_pairs={{24,16},{25,17},{26,18},{27,19},{28,20},{29,21},{30,22},{31,23}} | collective-permute-start | bytes 196616 | tf_op jit(solution)/shard_map/ppermute | solution.py:612
  41.5 1.1 %shard_map.69 = f32[4,64,576]{2,1,0:T(8,128)S(1)} custom-call(bf16[4,8,64,256]{3,2,1,0:T(8,128)(2,1)S(1)} %get-tuple-element.50.kept_ref, bf16[4,10,64,128]{3,2,1,0:T(8,128)(2,1)S(1)} %get-tuple-element.51.sent_ref), custom_call_target="tpu_custom_call" | custom-call | flops 1000000000 | tf_op jit(solution)/shard_map/pallas_call | solution.py:678
  42.6 3.4 %collective-permute-start.11 = (f32[2,64,576]{2,1,0:T(8,128)S(1)}, f32[2,64,576]{2,1,0:T(8,128)S(1)}, u32[]{:S(2)}, u32[]{:S(2)}) collective-permute-start(f32[2,64,576]{2,1,0:T(8,128)S(1)} %slice_select_fusion), channel_id=1, source_target_pairs={{0,2},{2,0},{4,6},{6,4},{1,3},{3,1},{5,7},{7,5},{8,10},{10,8},{12,... | collective-permute-start | bytes 884744 | tf_op jit(solution)/shard_map/ppermute | solution.py:523
  46.2 1.3 %collective-permute-start.17 = (bf16[4,64,128]{2,1,0:T(8,128)(2,1)S(1)}, bf16[4,64,128]{2,1,0:T(8,128)(2,1)S(1)}, u32[]{:S(2)}, u32[]{:S(2)}) collective-permute-start(bf16[4,64,128]{2,1,0:T(8,128)(2,1)S(1)} %shard_map.70), channel_id=1, source_target_pairs={{16,8},{17,9},{18,10},{19,11},{20,12},{21,13},{22,14},{23,15}} | collective-permute-start | bytes 196616 | tf_op jit(solution)/shard_map/ppermute | solution.py:612
  47.5 1.4 %collective-permute-start.12 = (bf16[2,64,576]{2,1,0:T(8,128)(2,1)S(1)}, bf16[2,64,576]{2,1,0:T(8,128)(2,1)S(1)}, u32[]{:S(2)}, u32[]{:S(2)}) collective-permute-start(bf16[2,64,576]{2,1,0:T(8,128)(2,1)S(1)} %add_convert_fusion.1), channel_id=1, source_target_pairs={{0,1},{1,0},{2,6},{3,7},{4,5},{5,4},{6,2},{7,3},{8,9},{9,8},{10,14... | collective-permute-start | bytes 442376 | tf_op jit(solution)/shard_map/ppermute | solution.py:535
  49.2 1.3 %collective-permute-start.18 = (bf16[4,64,128]{2,1,0:T(8,128)(2,1)S(1)}, bf16[4,64,128]{2,1,0:T(8,128)(2,1)S(1)}, u32[]{:S(2)}, u32[]{:S(2)}) collective-permute-start(bf16[4,64,128]{2,1,0:T(8,128)(2,1)S(1)} %shard_map.71), channel_id=1, source_target_pairs={{16,8},{17,9},{18,10},{19,11},{20,12},{21,13},{22,14},{23,15}} | collective-permute-start | bytes 196616 | tf_op jit(solution)/shard_map/ppermute | solution.py:612
  50.5 1.3 %collective-permute-done.12 = bf16[2,64,576]{2,1,0:T(8,128)(2,1)S(1)} collective-permute-done((bf16[2,64,576]{2,1,0:T(8,128)(2,1)S(1)}, bf16[2,64,576]{2,1,0:T(8,128)(2,1)S(1)}, u32[]{:S(2)}, u32[]{:S(2)}) %collective-permute-start.12) | collective-permute-done | bytes 147488 | tf_op jit(solution)/shard_map/ppermute | solution.py:535
  51.8 1.3 %collective-permute-start.13 = (bf16[2,64,576]{2,1,0:T(8,128)(2,1)S(1)}, bf16[2,64,576]{2,1,0:T(8,128)(2,1)S(1)}, u32[]{:S(2)}, u32[]{:S(2)}) collective-permute-start(bf16[2,64,576]{2,1,0:T(8,128)(2,1)S(1)} %add_convert_fusion), channel_id=1, source_target_pairs={{0,4},{1,5},{2,3},{3,2},{4,0},{5,1},{6,7},{7,6},{8,12},{9,13},{10,... | collective-permute-start | bytes 442376 | tf_op jit(solution)/shard_map/ppermute | solution.py:535
  53.3 0.7 %collective-permute-start.19 = (bf16[4,64,128]{2,1,0:T(8,128)(2,1)S(1)}, bf16[4,64,128]{2,1,0:T(8,128)(2,1)S(1)}, u32[]{:S(2)}, u32[]{:S(2)}) collective-permute-start(bf16[4,64,128]{2,1,0:T(8,128)(2,1)S(1)} %shard_map.72), channel_id=1, source_target_pairs={{8,0},{9,1},{10,2},{11,3},{12,4},{13,5},{14,6},{15,7}} | collective-permute-start | bytes 196616 | tf_op jit(solution)/shard_map/ppermute | solution.py:612
  54.0 2.3 %collective-permute-done.13 = bf16[2,64,576]{2,1,0:T(8,128)(2,1)S(1)} collective-permute-done((bf16[2,64,576]{2,1,0:T(8,128)(2,1)S(1)}, bf16[2,64,576]{2,1,0:T(8,128)(2,1)S(1)}, u32[]{:S(2)}, u32[]{:S(2)}) %collective-permute-start.13) | collective-permute-done | bytes 147488 | tf_op jit(solution)/shard_map/ppermute | solution.py:535
  56.4 4.6 %collective-permute-start.14 = (f32[2,64,576]{2,1,0:T(8,128)S(1)}, f32[2,64,576]{2,1,0:T(8,128)S(1)}, u32[]{:S(2)}, u32[]{:S(2)}) collective-permute-start(f32[2,64,576]{2,1,0:T(8,128)S(1)} %convert_add_fusion.half_ref), channel_id=1, source_target_pairs={{0,2},{2,0},{4,6},{6,4},{1,3},{3,1},{5,7},{7,5},{8,10},{10,8},{12,... | collective-permute-start | bytes 884744 | tf_op jit(solution)/shard_map/ppermute | solution.py:537
  61.2 0.7 %collective-permute-start.20 = (bf16[4,64,128]{2,1,0:T(8,128)(2,1)S(1)}, bf16[4,64,128]{2,1,0:T(8,128)(2,1)S(1)}, u32[]{:S(2)}, u32[]{:S(2)}) collective-permute-start(bf16[4,64,128]{2,1,0:T(8,128)(2,1)S(1)} %shard_map.73), channel_id=1, source_target_pairs={{8,0},{9,1},{10,2},{11,3},{12,4},{13,5},{14,6},{15,7}} | collective-permute-start | bytes 196616 | tf_op jit(solution)/shard_map/ppermute | solution.py:612
  62.3 1.0 %shard_map.74 = (f32[512,128]{1,0:T(8,128)}, f32[4,64,576]{2,1,0:T(8,128)}) custom-call(f32[512,128]{1,0:T(8,128)S(1)} %bitcast.36, f32[2,64,576]{2,1,0:T(8,128)S(1)} %convert_add_fusion.half_ref, f32[2,64,576]{2,1,0:T(8,128)S(1)} %collective-permute-done.14.other_ref, bf16[4,64,128]{2,1,0:T(8,128)(2,1)S(1)} %collective-permute-done.15.s_ref.refs_0_, ...), custom_call_target="tpu_custom_call" | custom-call | flops 10000000000 | tf_op jit(solution)/shard_map/pallas_call | solution.py:684
  (54 shorter events, 6.3 us)
Async XLA Ops:
  0.6 3.3 %copy-start.2 = (bf16[4,64,576]{2,1,0:T(8,128)(2,1)S(1)}, bf16[4,64,576]{2,1,0:T(8,128)(2,1)}, u32[]{:S(2)}) copy-start(bf16[4,64,576]{2,1,0:T(8,128)(2,1)} %param.5) | copy-start | bytes 884740
  2.6 3.0 %collective-permute-start = (bf16[64,256]{1,0:T(8,128)(2,1)}, bf16[64,256]{1,0:T(8,128)(2,1)S(1)}, u32[]{:S(2)}, u32[]{:S(2)}) collective-permute-start(bf16[64,256]{1,0:T(8,128)(2,1)} %shard_map.58), channel_id=1, source_target_pairs={{0,1},{1,0},{2,3},{3,2},{4,5},{5,4},{6,7},{7,6},{8,9},{9,8},{10,11... | collective-permute-start | bytes 98312 | tf_op jit(solution)/shard_map/ppermute | solution.py:510
  4.2 1.4 %copy-start = (f32[1,64,8,128]{3,2,1,0:T(8,128)S(1)}, f32[1,64,8,128]{3,2,1,0:T(8,128)}, u32[]{:S(2)}) copy-start(f32[1,64,8,128]{3,2,1,0:T(8,128)} %param.3) | copy-start | bytes 786436
  4.2 1.4 %copy-start.1 = (f32[1,64,8,128]{3,2,1,0:T(8,128)S(1)}, f32[1,64,8,128]{3,2,1,0:T(8,128)}, u32[]{:S(2)}) copy-start(f32[1,64,8,128]{3,2,1,0:T(8,128)} %param.4) | copy-start | bytes 786436
  5.9 6.5 %collective-permute-start.2 = (bf16[10,64,128]{2,1,0:T(8,128)(2,1)S(1)}, bf16[10,64,128]{2,1,0:T(8,128)(2,1)S(1)}, u32[]{:S(2)}, u32[]{:S(2)}) collective-permute-start(bf16[10,64,128]{2,1,0:T(8,128)(2,1)S(1)} %get-tuple-element.32), channel_id=1, source_target_pairs={{2,4},{4,2},{3,5},{5,3},{10,12},{12,10},{11,13},{13,11},{18,20},{2... | collective-permute-start | bytes 491528 | tf_op jit(solution)/shard_map/ppermute | solution.py:505
  6.6 5.8 %collective-permute-start.1 = (bf16[10,64,128]{2,1,0:T(8,128)(2,1)S(1)}, bf16[10,64,128]{2,1,0:T(8,128)(2,1)S(1)}, u32[]{:S(2)}, u32[]{:S(2)}) collective-permute-start(bf16[10,64,128]{2,1,0:T(8,128)(2,1)S(1)} %get-tuple-element.31), channel_id=1, source_target_pairs={{0,2},{2,0},{4,6},{6,4},{1,3},{3,1},{5,7},{7,5},{8,10},{10,8},{12,... | collective-permute-start | bytes 491528 | tf_op jit(solution)/shard_map/ppermute | solution.py:505
  12.4 3.7 %collective-permute-start.3 = (bf16[5,64,128]{2,1,0:T(8,128)(2,1)S(1)}, bf16[5,64,128]{2,1,0:T(8,128)(2,1)S(1)}, u32[]{:S(2)}, u32[]{:S(2)}) collective-permute-start(bf16[5,64,128]{2,1,0:T(8,128)(2,1)S(1)} %get-tuple-element.36), channel_id=1, source_target_pairs={{0,8},{1,9},{2,10},{3,11},{4,12},{5,13},{6,14},{7,15}} | collective-permute-start | bytes 245768 | tf_op jit(solution)/shard_map/ppermute | solution.py:612
  13.2 4.4 %collective-permute-start.4 = (bf16[4,64,128]{2,1,0:T(8,128)(2,1)S(1)}, bf16[4,64,128]{2,1,0:T(8,128)(2,1)S(1)}, u32[]{:S(2)}, u32[]{:S(2)}) collective-permute-start(bf16[4,64,128]{2,1,0:T(8,128)(2,1)S(1)} %get-tuple-element.37), channel_id=1, source_target_pairs={{0,8},{1,9},{2,10},{3,11},{4,12},{5,13},{6,14},{7,15}} | collective-permute-start | bytes 196616 | tf_op jit(solution)/shard_map/ppermute | solution.py:612
  16.3 5.2 %collective-permute-start.5 = (bf16[5,64,128]{2,1,0:T(8,128)(2,1)S(1)}, bf16[5,64,128]{2,1,0:T(8,128)(2,1)S(1)}, u32[]{:S(2)}, u32[]{:S(2)}) collective-permute-start(bf16[5,64,128]{2,1,0:T(8,128)(2,1)S(1)} %shard_map.62), channel_id=1, source_target_pairs={{8,16},{9,17},{10,18},{11,19},{12,20},{13,21},{14,22},{15,23}} | collective-permute-start | bytes 245768 | tf_op jit(solution)/shard_map/ppermute | solution.py:612
  17.8 5.3 %collective-permute-start.6 = (bf16[4,64,128]{2,1,0:T(8,128)(2,1)S(1)}, bf16[4,64,128]{2,1,0:T(8,128)(2,1)S(1)}, u32[]{:S(2)}, u32[]{:S(2)}) collective-permute-start(bf16[4,64,128]{2,1,0:T(8,128)(2,1)S(1)} %shard_map.63), channel_id=1, source_target_pairs={{8,16},{9,17},{10,18},{11,19},{12,20},{13,21},{14,22},{15,23}} | collective-permute-start | bytes 196616 | tf_op jit(solution)/shard_map/ppermute | solution.py:612
  21.7 3.0 %copy-start.3 = (bf16[64,64]{1,0:T(8,128)(2,1)S(1)}, bf16[64,64]{1,0:T(8,128)(2,1)}, u32[]{:S(2)}) copy-start(bf16[64,64]{1,0:T(8,128)(2,1)} %get-tuple-element.57) | copy-start | bytes 24580
  21.7 3.0 %copy-start.4 = (bf16[64,64]{1,0:T(8,128)(2,1)S(1)}, bf16[64,64]{1,0:T(8,128)(2,1)}, u32[]{:S(2)}) copy-start(bf16[64,64]{1,0:T(8,128)(2,1)} %fusion) | copy-start | bytes 24580
  21.7 4.3 %collective-permute-start.7 = (bf16[5,64,128]{2,1,0:T(8,128)(2,1)S(1)}, bf16[5,64,128]{2,1,0:T(8,128)(2,1)S(1)}, u32[]{:S(2)}, u32[]{:S(2)}) collective-permute-start(bf16[5,64,128]{2,1,0:T(8,128)(2,1)S(1)} %shard_map.64), channel_id=1, source_target_pairs={{16,24},{17,25},{18,26},{19,27},{20,28},{21,29},{22,30},{23,31}} | collective-permute-start | bytes 245768 | tf_op jit(solution)/shard_map/ppermute | solution.py:612
  23.4 2.6 %collective-permute-start.8 = (bf16[4,64,128]{2,1,0:T(8,128)(2,1)S(1)}, bf16[4,64,128]{2,1,0:T(8,128)(2,1)S(1)}, u32[]{:S(2)}, u32[]{:S(2)}) collective-permute-start(bf16[4,64,128]{2,1,0:T(8,128)(2,1)S(1)} %shard_map.65), channel_id=1, source_target_pairs={{16,24},{17,25},{18,26},{19,27},{20,28},{21,29},{22,30},{23,31}} | collective-permute-start | bytes 196616 | tf_op jit(solution)/shard_map/ppermute | solution.py:612
  26.1 7.3 %collective-permute-start.10 = (bf16[9,64,128]{2,1,0:T(8,128)(2,1)S(1)}, bf16[9,64,128]{2,1,0:T(8,128)(2,1)S(1)}, u32[]{:S(2)}, u32[]{:S(2)}) collective-permute-start(bf16[9,64,128]{2,1,0:T(8,128)(2,1)S(1)} %shard_map.66.s_ref), channel_id=1, source_target_pairs={{2,4},{4,2},{3,5},{5,3},{10,12},{12,10},{11,13},{13,11},{18,20},{2... | collective-permute-start | bytes 442376 | tf_op jit(solution)/shard_map/ppermute | solution.py:505
  26.9 6.5 %collective-permute-start.9 = (bf16[9,64,128]{2,1,0:T(8,128)(2,1)S(1)}, bf16[9,64,128]{2,1,0:T(8,128)(2,1)S(1)}, u32[]{:S(2)}, u32[]{:S(2)}) collective-permute-start(bf16[9,64,128]{2,1,0:T(8,128)(2,1)S(1)} %shard_map.66.s_ref), channel_id=1, source_target_pairs={{0,2},{2,0},{4,6},{6,4},{1,3},{3,1},{5,7},{7,5},{8,10},{10,8},{12,... | collective-permute-start | bytes 442376 | tf_op jit(solution)/shard_map/ppermute | solution.py:505
  38.9 7.1 %collective-permute-start.15 = (bf16[4,64,128]{2,1,0:T(8,128)(2,1)S(1)}, bf16[4,64,128]{2,1,0:T(8,128)(2,1)S(1)}, u32[]{:S(2)}, u32[]{:S(2)}) collective-permute-start(bf16[4,64,128]{2,1,0:T(8,128)(2,1)S(1)} %get-tuple-element.52), channel_id=1, source_target_pairs={{24,16},{25,17},{26,18},{27,19},{28,20},{29,21},{30,22},{31,23}} | collective-permute-start | bytes 196616 | tf_op jit(solution)/shard_map/ppermute | solution.py:612
  40.2 8.8 %collective-permute-start.16 = (bf16[4,64,128]{2,1,0:T(8,128)(2,1)S(1)}, bf16[4,64,128]{2,1,0:T(8,128)(2,1)S(1)}, u32[]{:S(2)}, u32[]{:S(2)}) collective-permute-start(bf16[4,64,128]{2,1,0:T(8,128)(2,1)S(1)} %get-tuple-element.53), channel_id=1, source_target_pairs={{24,16},{25,17},{26,18},{27,19},{28,20},{29,21},{30,22},{31,23}} | collective-permute-start | bytes 196616 | tf_op jit(solution)/shard_map/ppermute | solution.py:612
  42.6 4.9 %collective-permute-start.11 = (f32[2,64,576]{2,1,0:T(8,128)S(1)}, f32[2,64,576]{2,1,0:T(8,128)S(1)}, u32[]{:S(2)}, u32[]{:S(2)}) collective-permute-start(f32[2,64,576]{2,1,0:T(8,128)S(1)} %slice_select_fusion), channel_id=1, source_target_pairs={{0,2},{2,0},{4,6},{6,4},{1,3},{3,1},{5,7},{7,5},{8,10},{10,8},{12,... | collective-permute-start | bytes 884744 | tf_op jit(solution)/shard_map/ppermute | solution.py:523
  46.2 6.9 %collective-permute-start.17 = (bf16[4,64,128]{2,1,0:T(8,128)(2,1)S(1)}, bf16[4,64,128]{2,1,0:T(8,128)(2,1)S(1)}, u32[]{:S(2)}, u32[]{:S(2)}) collective-permute-start(bf16[4,64,128]{2,1,0:T(8,128)(2,1)S(1)} %shard_map.70), channel_id=1, source_target_pairs={{16,8},{17,9},{18,10},{19,11},{20,12},{21,13},{22,14},{23,15}} | collective-permute-start | bytes 196616 | tf_op jit(solution)/shard_map/ppermute | solution.py:612
  47.5 4.2 %collective-permute-start.12 = (bf16[2,64,576]{2,1,0:T(8,128)(2,1)S(1)}, bf16[2,64,576]{2,1,0:T(8,128)(2,1)S(1)}, u32[]{:S(2)}, u32[]{:S(2)}) collective-permute-start(bf16[2,64,576]{2,1,0:T(8,128)(2,1)S(1)} %add_convert_fusion.1), channel_id=1, source_target_pairs={{0,1},{1,0},{2,6},{3,7},{4,5},{5,4},{6,2},{7,3},{8,9},{9,8},{10,14... | collective-permute-start | bytes 442376 | tf_op jit(solution)/shard_map/ppermute | solution.py:535
  49.2 11.9 %collective-permute-start.18 = (bf16[4,64,128]{2,1,0:T(8,128)(2,1)S(1)}, bf16[4,64,128]{2,1,0:T(8,128)(2,1)S(1)}, u32[]{:S(2)}, u32[]{:S(2)}) collective-permute-start(bf16[4,64,128]{2,1,0:T(8,128)(2,1)S(1)} %shard_map.71), channel_id=1, source_target_pairs={{16,8},{17,9},{18,10},{19,11},{20,12},{21,13},{22,14},{23,15}} | collective-permute-start | bytes 196616 | tf_op jit(solution)/shard_map/ppermute | solution.py:612
  51.8 4.5 %collective-permute-start.13 = (bf16[2,64,576]{2,1,0:T(8,128)(2,1)S(1)}, bf16[2,64,576]{2,1,0:T(8,128)(2,1)S(1)}, u32[]{:S(2)}, u32[]{:S(2)}) collective-permute-start(bf16[2,64,576]{2,1,0:T(8,128)(2,1)S(1)} %add_convert_fusion), channel_id=1, source_target_pairs={{0,4},{1,5},{2,3},{3,2},{4,0},{5,1},{6,7},{7,6},{8,12},{9,13},{10,... | collective-permute-start | bytes 442376 | tf_op jit(solution)/shard_map/ppermute | solution.py:535
  53.3 8.6 %collective-permute-start.19 = (bf16[4,64,128]{2,1,0:T(8,128)(2,1)S(1)}, bf16[4,64,128]{2,1,0:T(8,128)(2,1)S(1)}, u32[]{:S(2)}, u32[]{:S(2)}) collective-permute-start(bf16[4,64,128]{2,1,0:T(8,128)(2,1)S(1)} %shard_map.72), channel_id=1, source_target_pairs={{8,0},{9,1},{10,2},{11,3},{12,4},{13,5},{14,6},{15,7}} | collective-permute-start | bytes 196616 | tf_op jit(solution)/shard_map/ppermute | solution.py:612
  56.4 5.9 %collective-permute-start.14 = (f32[2,64,576]{2,1,0:T(8,128)S(1)}, f32[2,64,576]{2,1,0:T(8,128)S(1)}, u32[]{:S(2)}, u32[]{:S(2)}) collective-permute-start(f32[2,64,576]{2,1,0:T(8,128)S(1)} %convert_add_fusion.half_ref), channel_id=1, source_target_pairs={{0,2},{2,0},{4,6},{6,4},{1,3},{3,1},{5,7},{7,5},{8,10},{10,8},{12,... | collective-permute-start | bytes 884744 | tf_op jit(solution)/shard_map/ppermute | solution.py:537
  61.2 0.7 %collective-permute-start.20 = (bf16[4,64,128]{2,1,0:T(8,128)(2,1)S(1)}, bf16[4,64,128]{2,1,0:T(8,128)(2,1)S(1)}, u32[]{:S(2)}, u32[]{:S(2)}) collective-permute-start(bf16[4,64,128]{2,1,0:T(8,128)(2,1)S(1)} %shard_map.73), channel_id=1, source_target_pairs={{8,0},{9,1},{10,2},{11,3},{12,4},{13,5},{14,6},{15,7}} | collective-permute-start | bytes 196616 | tf_op jit(solution)/shard_map/ppermute | solution.py:612
